TPU v7x, 32 devices: a whole 2x2x4 slice. The times are simulated.
32 devices in a mesh: fsdp: 4 (over y, x), seq: 8 (over z, core).
Axes of the slice: x: 2, y: 2, z: 4, core: 2. Of those that a mesh axis runs over, the one named last changes fastest.
Arguments:
- tokens: bfloat16 [4096, 2048], P(('fsdp', 'seq')), may hold values from -6 to 6
- norm_gains: bfloat16 [4, 2048], replicated, may hold values from 0.25 to 1.75
- w_query: bfloat16 [2048, 2048], P('fsdp', 'seq'), may hold values from -0.125 to 0.125
- w_key: bfloat16 [2048, 2048], P('fsdp', 'seq'), may hold values from -0.125 to 0.125
- w_value: bfloat16 [2048, 2048], P('fsdp', 'seq'), may hold values from -0.125 to 0.125
- w_out: bfloat16 [2048, 2048], P('seq', 'fsdp'), may hold values from -1 to 1
- w_router: bfloat16 [2048, 32], replicated, may hold values from -0.0625 to 0.0625
- w_gate: bfloat16 [32, 2048, 1024], P('seq', 'fsdp'), may hold values from -0.125 to 0.125
- w_up: bfloat16 [32, 2048, 1024], P('seq', 'fsdp'), may hold values from -0.125 to 0.125
- w_down: bfloat16 [32, 1024, 2048], P('seq', None, 'fsdp'), may hold values from -0.5 to 0.5
- segment_ids: int32 [4096], P('fsdp'), may hold values from 0 to 4, as said below
- expert_ids: int32 [4096, 8], P(('fsdp', 'seq')), may hold values from 0 to 31, as said below
- expert_slots: int32 [4096, 8], P(('fsdp', 'seq')), may hold values from 0 to 40, as said below
- cotangent: bfloat16 [4096, 2048], P(('fsdp', 'seq')), may hold values from -6 to 6
Outputs:
- mixed: bfloat16 [4096, 2048], P(('fsdp', 'seq'))
- grad_tokens: float32 [4096, 2048], P(('fsdp', 'seq'))
- grad_gains: float32 [4, 2048], replicated
- grad_query: float32 [2048, 2048], P('fsdp', 'seq')
- grad_key: float32 [2048, 2048], P('fsdp', 'seq')
- grad_value: float32 [2048, 2048], P('fsdp', 'seq')
- grad_out: float32 [2048, 2048], P('seq', 'fsdp')
- grad_router: float32 [2048, 32], replicated
- grad_gate: float32 [32, 2048, 1024], P('seq', 'fsdp')
- grad_up: float32 [32, 2048, 1024], P('seq', 'fsdp')
- grad_down: float32 [32, 1024, 2048], P('seq', None, 'fsdp')
Inputs may be any that keep to these rules, and one draw needn't show every extreme that they name: `segment_ids`: within each sequence of 1024 rows the numbers start at 0, never fall and end at 4 (five documents); document 1 starts in the first 128 rows of the sequence and ends in its last 128 rows. `expert_ids`: each row names 8 different experts; in each sequence one expert is named by more than 40 rows of every block of 128 rows. `expert_slots`: within each block of 128 rows (one device's tokens), a pair's slot is its rank, in the order of rows and then of the row's choices, among the block's pairs that name the same expert, or 40 where that rank is 40 or more (the pair is dropped).
All inputs are finite; a program needn't handle non-finite values.
Results may differ from a plain program's by a relative error of at most 0.02.
Values may be sent and summed in bfloat16 or wider, within the bound.
A program may use at most 256 MiB of HBM per device.

v0:
```python
import math

import jax
import jax.numpy as jnp
from jax import lax
from jax.sharding import PartitionSpec as P

HEAD_DIM = 128
CAP = 40


EPSILON = 1e-06
THETA = 10000.0
MASKED = -1e30
HIGHEST = lax.Precision.HIGHEST


def rope_tables(positions, head_size):
    half_dim = head_size // 2
    frequency = THETA ** (-jnp.arange(half_dim, dtype=jnp.float32) / half_dim)
    angles = positions.astype(jnp.float32)[:, None] * frequency[None, :]
    return (jnp.cos(angles), jnp.sin(angles))


def rotate(values_in, cosine_table, sine_table, head_size):
    row_count = values_in.shape[0]
    pieces = values_in.reshape(row_count, -1, head_size)
    half_dim = head_size // 2
    former = pieces[..., :half_dim]
    latter = pieces[..., half_dim:]
    cosine_wide = cosine_table[:, None, :]
    sine_wide = sine_table[:, None, :]
    turned = jnp.concatenate(
        [former * cosine_wide - latter * sine_wide, latter * cosine_wide + former * sine_wide], -1
    )
    return turned.reshape(row_count, -1)


def inverse_rms(values_in):
    return lax.rsqrt(jnp.mean(values_in * values_in, -1, keepdims=True) + EPSILON)


def norm_back(grad_unit, unit_values, inverse):
    return inverse * (
        grad_unit - unit_values * jnp.mean(grad_unit * unit_values, -1, keepdims=True)
    )


def shards(
    tokens,
    norm_gains,
    w_query,
    w_key,
    w_value,
    w_out,
    w_router,
    w_gate,
    w_up,
    w_down,
    segment_ids,
    expert_ids,
    expert_slots,
    cotangent,
):
    half_type = jnp.bfloat16
    float_type = jnp.float32
    tok_rows = tokens.shape[0]
    model_width = tokens.shape[1]
    expert_total = w_router.shape[1]
    top_count = expert_ids.shape[1]
    head_size = HEAD_DIM
    local_width = w_query.shape[1]
    heads_local = local_width // head_size
    capacity = CAP
    column_start = lax.axis_index("seq") * local_width
    weights_full = (
        lax.all_gather(w_query, "fsdp", axis=0, tiled=True),
        lax.all_gather(w_key, "fsdp", axis=0, tiled=True),
        lax.all_gather(w_value, "fsdp", axis=0, tiled=True),
        lax.all_gather(w_out, "fsdp", axis=1, tiled=True),
        lax.all_gather(w_gate, "fsdp", axis=1, tiled=True),
        lax.all_gather(w_up, "fsdp", axis=1, tiled=True),
        lax.all_gather(w_down, "fsdp", axis=2, tiled=True),
    )
    query_cols, key_cols, value_cols, out_rows, gate_full, up_full, down_full = weights_full
    gain_rows = norm_gains.astype(float_type)
    gain_cols = lax.dynamic_slice_in_dim(gain_rows, column_start, local_width, 1)
    inputs = tokens.astype(float_type)
    inverse_first = inverse_rms(inputs)
    unit_first = inputs * inverse_first
    normed = (unit_first * gain_rows[0]).astype(half_type)
    normed_seq = lax.all_gather(normed, "seq", axis=0, tiled=True)
    length = normed_seq.shape[0]
    query_raw = jnp.dot(normed_seq, query_cols, preferred_element_type=float_type)
    key_raw = jnp.dot(normed_seq, key_cols, preferred_element_type=float_type)
    value_heads = jnp.dot(normed_seq, value_cols, preferred_element_type=float_type).astype(
        half_type
    )
    square_sums = lax.psum(
        (jnp.sum(query_raw * query_raw, -1), jnp.sum(key_raw * key_raw, -1)), "seq"
    )
    inverse_query = lax.rsqrt(square_sums[0] / model_width + EPSILON)[:, None]
    inverse_key = lax.rsqrt(square_sums[1] / model_width + EPSILON)[:, None]
    positions = jnp.arange(length, dtype=jnp.int32)
    cosine_table, sine_table = rope_tables(positions, head_size)
    unit_query = query_raw * inverse_query
    unit_key = key_raw * inverse_key
    query_heads = rotate(unit_query * gain_cols[2], cosine_table, sine_table, head_size).astype(
        half_type
    )
    key_heads = rotate(unit_key * gain_cols[3], cosine_table, sine_table, head_size).astype(
        half_type
    )
    block_rows = math.gcd(512, length)
    blocks = length // block_rows
    score_scale = head_size ** (-0.5)
    query_cube = query_heads.reshape(blocks, block_rows, heads_local, head_size)
    key_cube = key_heads.reshape(length, heads_local, head_size)
    value_cube = value_heads.reshape(length, heads_local, head_size)
    segment_blocks = segment_ids.reshape(blocks, block_rows)

    def block_scores(query_block, segment_block):
        scores = (
            jnp.einsum("qhd,khd->hqk", query_block, key_cube, preferred_element_type=float_type)
            * score_scale
        )
        visible = segment_block[:, None] == segment_ids[None, :]
        return jnp.where(visible[None], scores, MASKED)

    def attend(block_pair):
        query_block, segment_block = block_pair
        scores = block_scores(query_block, segment_block)
        row_peak = jnp.max(scores, -1, keepdims=True)
        exp_scores = jnp.exp(scores - row_peak)
        exp_total = jnp.sum(exp_scores, -1, keepdims=True)
        weights_soft = (exp_scores / exp_total).astype(half_type)
        mixed_block = jnp.einsum(
            "hqk,khd->qhd", weights_soft, value_cube, preferred_element_type=float_type
        )
        return (mixed_block.astype(half_type), (row_peak + jnp.log(exp_total))[..., 0])

    mixed_heads, log_sums = lax.map(attend, (query_cube, segment_blocks))
    attended_heads = mixed_heads.reshape(length, local_width)
    projected = lax.psum_scatter(
        jnp.dot(attended_heads, out_rows, preferred_element_type=float_type),
        "seq",
        scatter_dimension=0,
        tiled=True,
    )
    residual = inputs + projected
    inverse_second = inverse_rms(residual)
    unit_second = residual * inverse_second
    routed = (unit_second * gain_rows[1]).astype(half_type)
    logits = jnp.dot(routed, w_router, preferred_element_type=float_type)
    expert_range = jnp.arange(expert_total, dtype=jnp.int32)
    chosen = (expert_ids[:, :, None] == expert_range).astype(float_type)
    picked = jnp.einsum("tke,te->tk", chosen, logits, precision=HIGHEST)
    gate_weights = jax.nn.softmax(picked, axis=-1)
    places = jnp.where(expert_slots < capacity, expert_ids * capacity + expert_slots, -1)
    onehot = (places[:, :, None] == jnp.arange(expert_total * capacity, dtype=jnp.int32)).astype(
        half_type
    )
    outgoing = jnp.einsum("tkc,td->cd", onehot, routed, preferred_element_type=float_type).astype(
        half_type
    )
    expert_rows = lax.all_to_all(
        outgoing.reshape(expert_total, capacity, model_width),
        "seq",
        split_axis=0,
        concat_axis=1,
        tiled=True,
    )
    gate_pre = jnp.einsum("erd,edf->erf", expert_rows, gate_full, preferred_element_type=float_type)
    up_pre = jnp.einsum("erd,edf->erf", expert_rows, up_full, preferred_element_type=float_type)
    hidden = (jax.nn.silu(gate_pre) * up_pre).astype(half_type)
    returned = jnp.einsum(
        "erf,efd->erd", hidden, down_full, preferred_element_type=float_type
    ).astype(half_type)
    incoming = lax.all_to_all(returned, "seq", split_axis=1, concat_axis=0, tiled=True)
    onehot_flat = onehot.reshape(tok_rows * top_count, expert_total * capacity)
    picked_rows = jnp.dot(
        onehot_flat,
        incoming.reshape(expert_total * capacity, model_width),
        preferred_element_type=float_type,
    ).reshape(tok_rows, top_count, model_width)
    mixture = jnp.sum(gate_weights[:, :, None] * picked_rows, axis=1)
    output = (residual + mixture).astype(half_type)
    upstream = cotangent.astype(float_type)
    gate_grad = jnp.sum(upstream[:, None, :] * picked_rows, axis=-1)
    weighted = (gate_weights[:, :, None] * upstream[:, None, :]).astype(half_type)
    slot_grads = jnp.einsum(
        "tkc,tkd->cd", onehot, weighted, preferred_element_type=float_type
    ).astype(half_type)
    returned_grad = lax.all_to_all(
        slot_grads.reshape(expert_total, capacity, model_width),
        "seq",
        split_axis=0,
        concat_axis=1,
        tiled=True,
    )
    hidden_grad = jnp.einsum(
        "erd,efd->erf", returned_grad, down_full, preferred_element_type=float_type
    )
    gate_sigmoid = jax.nn.sigmoid(gate_pre)
    gate_pre_grad = (
        hidden_grad * up_pre * gate_sigmoid * (1.0 + gate_pre * (1.0 - gate_sigmoid))
    ).astype(half_type)
    up_pre_grad = (hidden_grad * gate_pre * gate_sigmoid).astype(half_type)
    grad_down_local = jnp.einsum(
        "erf,erd->efd", hidden, returned_grad, preferred_element_type=float_type
    )
    grad_gate_local = jnp.einsum(
        "erd,erf->edf", expert_rows, gate_pre_grad, preferred_element_type=float_type
    )
    grad_up_local = jnp.einsum(
        "erd,erf->edf", expert_rows, up_pre_grad, preferred_element_type=float_type
    )
    rows_grad = jnp.einsum(
        "erf,edf->erd", gate_pre_grad, gate_full, preferred_element_type=float_type
    )
    rows_grad = (
        rows_grad
        + jnp.einsum("erf,edf->erd", up_pre_grad, up_full, preferred_element_type=float_type)
    ).astype(half_type)
    sent_back = lax.all_to_all(rows_grad, "seq", split_axis=1, concat_axis=0, tiled=True)
    routed_grad = jnp.einsum(
        "tkc,cd->td",
        onehot,
        sent_back.reshape(expert_total * capacity, model_width),
        preferred_element_type=float_type,
    )
    mean_grad = jnp.sum(gate_weights * gate_grad, -1, keepdims=True)
    picked_grad = gate_weights * (gate_grad - mean_grad)
    logit_grad = jnp.einsum("tke,tk->te", chosen, picked_grad, precision=HIGHEST).astype(half_type)
    routed_grad = routed_grad + jnp.einsum(
        "te,de->td", logit_grad, w_router, preferred_element_type=float_type
    )
    grad_router_local = jnp.einsum(
        "td,te->de", routed, logit_grad, preferred_element_type=float_type
    )
    gain_second_grad = jnp.sum(routed_grad * unit_second, axis=0)
    residual_grad = upstream + norm_back(routed_grad * gain_rows[1], unit_second, inverse_second)
    out_grad = residual_grad.astype(half_type)
    out_grad_seq = lax.all_gather(out_grad, "seq", axis=0, tiled=True)
    grad_out_local = jnp.einsum(
        "th,td->hd", attended_heads, out_grad_seq, preferred_element_type=float_type
    )
    attended_grad = jnp.einsum(
        "td,hd->th", out_grad_seq, out_rows, preferred_element_type=float_type
    ).astype(half_type)
    grad_cube = attended_grad.reshape(blocks, block_rows, heads_local, head_size)

    def attend_back(running, pieces):
        key_acc, value_acc = running
        query_block, segment_block, grad_block, log_block = pieces
        scores = block_scores(query_block, segment_block)
        soft_values = jnp.exp(scores - log_block[..., None])
        prob_grad = jnp.einsum(
            "qhd,khd->hqk", grad_block, value_cube, preferred_element_type=float_type
        )
        center = jnp.sum(soft_values * prob_grad, -1, keepdims=True)
        score_grad = (soft_values * (prob_grad - center)).astype(half_type)
        query_grad = (
            jnp.einsum("hqk,khd->qhd", score_grad, key_cube, preferred_element_type=float_type)
            * score_scale
        )
        key_acc = (
            key_acc
            + jnp.einsum("hqk,qhd->khd", score_grad, query_block, preferred_element_type=float_type)
            * score_scale
        )
        value_acc = value_acc + jnp.einsum(
            "hqk,qhd->khd",
            soft_values.astype(half_type),
            grad_block,
            preferred_element_type=float_type,
        )
        return ((key_acc, value_acc), query_grad.astype(half_type))

    empty_acc = jnp.zeros((length, heads_local, head_size), float_type)
    (key_acc, value_acc), query_grads = lax.scan(
        attend_back, (empty_acc, empty_acc), (query_cube, segment_blocks, grad_cube, log_sums)
    )
    query_back = query_grads.reshape(length, local_width)
    key_back = key_acc.reshape(length, local_width).astype(half_type)
    value_back = value_acc.reshape(length, local_width).astype(half_type)
    query_unit_grad = rotate(query_back.astype(float_type), cosine_table, -sine_table, head_size)
    key_unit_grad = rotate(key_back.astype(float_type), cosine_table, -sine_table, head_size)
    gain_query_grad = jnp.sum(query_unit_grad * unit_query, axis=0)
    gain_key_grad = jnp.sum(key_unit_grad * unit_key, axis=0)
    query_scaled = query_unit_grad * gain_cols[2]
    key_scaled = key_unit_grad * gain_cols[3]
    centers = lax.psum(
        (jnp.sum(query_scaled * unit_query, -1), jnp.sum(key_scaled * unit_key, -1)), "seq"
    )
    query_raw_grad = (
        inverse_query * (query_scaled - unit_query * (centers[0] / model_width)[:, None])
    ).astype(half_type)
    key_raw_grad = (
        inverse_key * (key_scaled - unit_key * (centers[1] / model_width)[:, None])
    ).astype(half_type)
    normed_part = jnp.einsum(
        "th,dh->td", query_raw_grad, query_cols, preferred_element_type=float_type
    )
    normed_part = normed_part + jnp.einsum(
        "th,dh->td", key_raw_grad, key_cols, preferred_element_type=float_type
    )
    normed_part = normed_part + jnp.einsum(
        "th,dh->td", value_back, value_cols, preferred_element_type=float_type
    )
    normed_rows_back = lax.all_gather(normed, "seq", axis=0, tiled=True)
    grad_query_local = jnp.einsum(
        "td,th->dh", normed_rows_back, query_raw_grad, preferred_element_type=float_type
    )
    grad_key_local = jnp.einsum(
        "td,th->dh", normed_rows_back, key_raw_grad, preferred_element_type=float_type
    )
    grad_value_local = jnp.einsum(
        "td,th->dh", normed_rows_back, value_back, preferred_element_type=float_type
    )
    normed_grad = lax.psum_scatter(
        normed_part.astype(jnp.bfloat16), "seq", scatter_dimension=0, tiled=True
    ).astype(jnp.float32)
    gain_first_grad = jnp.sum(normed_grad * unit_first, axis=0)
    input_grad = residual_grad + norm_back(normed_grad * gain_rows[0], unit_first, inverse_first)
    zero_row = jnp.zeros((model_width,), float_type)
    gain_query_full = lax.dynamic_update_slice_in_dim(zero_row, gain_query_grad, column_start, 0)
    gain_key_full = lax.dynamic_update_slice_in_dim(zero_row, gain_key_grad, column_start, 0)
    gain_grads = jnp.stack([gain_first_grad, gain_second_grad, gain_query_full, gain_key_full])
    small_sums = lax.psum((gain_grads, grad_router_local), ("fsdp", "seq"))
    owned = (
        lax.psum_scatter(
            grad_query_local.astype(jnp.bfloat16), "fsdp", scatter_dimension=0, tiled=True
        ).astype(jnp.float32),
        lax.psum_scatter(
            grad_key_local.astype(jnp.bfloat16), "fsdp", scatter_dimension=0, tiled=True
        ).astype(jnp.float32),
        lax.psum_scatter(
            grad_value_local.astype(jnp.bfloat16), "fsdp", scatter_dimension=0, tiled=True
        ).astype(jnp.float32),
        lax.psum_scatter(
            grad_out_local.astype(jnp.bfloat16), "fsdp", scatter_dimension=1, tiled=True
        ).astype(jnp.float32),
        lax.psum_scatter(
            grad_gate_local.astype(jnp.bfloat16), "fsdp", scatter_dimension=1, tiled=True
        ).astype(jnp.float32),
        lax.psum_scatter(
            grad_up_local.astype(jnp.bfloat16), "fsdp", scatter_dimension=1, tiled=True
        ).astype(jnp.float32),
        lax.psum_scatter(
            grad_down_local.astype(jnp.bfloat16), "fsdp", scatter_dimension=2, tiled=True
        ).astype(jnp.float32),
    )
    return (
        output,
        input_grad,
        small_sums[0],
        owned[0],
        owned[1],
        owned[2],
        owned[3],
        small_sums[1],
        owned[4],
        owned[5],
        owned[6],
    )


def solution(mesh):
    in_specs = (
        P(("fsdp", "seq"), None),
        P(),
        P("fsdp", "seq"),
        P("fsdp", "seq"),
        P("fsdp", "seq"),
        P("seq", "fsdp"),
        P(),
        P("seq", "fsdp", None),
        P("seq", "fsdp", None),
        P("seq", None, "fsdp"),
        P("fsdp"),
        P(("fsdp", "seq"), None),
        P(("fsdp", "seq"), None),
        P(("fsdp", "seq"), None),
    )
    out_specs = (
        P(("fsdp", "seq"), None),
        P(("fsdp", "seq"), None),
        P(),
        P("fsdp", "seq"),
        P("fsdp", "seq"),
        P("fsdp", "seq"),
        P("seq", "fsdp"),
        P(),
        P("seq", "fsdp", None),
        P("seq", "fsdp", None),
        P("seq", None, "fsdp"),
    )
    return jax.shard_map(shards, mesh=mesh, in_specs=in_specs, out_specs=out_specs, check_vma=False)
```

profile of v0, /device:TPU:0, one launch (start us, length us, event | category | flops | bytes accessed | tf_op | source)
XLA Modules:
  0.0 1920.9 jit_solution(12459818908168976990)
XLA Ops:
  19.2 20.0 %all-gather.12.cloned.1.call-done = bf16[2048,256]{1,0:T(8,128)(2,1)} async-done(((bf16[512,256]{1,0:T(8,128)(2,1)}), bf16[2048,256]{1,0:T(8,128)(2,1)}) %all-gather.12.cloned.1.call-update) | async-done | bytes 1048592 | tf_op jit(solution)/shard_map/all_gather | solution.py:77
  39.2 49.3 %all-gather.10.cloned.1.call-done = bf16[1024,2048]{1,0:T(8,128)(2,1)} async-done(((bf16[128,2048]{1,0:T(8,128)(2,1)}), bf16[1024,2048]{1,0:T(8,128)(2,1)}) %all-gather.10.cloned.1.call-update) | async-done | bytes 4194320 | tf_op jit(solution)/shard_map/all_gather | solution.py:92
  92.4 23.4 %all-gather.14.cloned.1.call-done = bf16[2048,256]{1,0:T(8,128)(2,1)} async-done(((bf16[512,256]{1,0:T(8,128)(2,1)}), bf16[2048,256]{1,0:T(8,128)(2,1)}) %all-gather.14.cloned.1.call-update) | async-done | bytes 1048592 | tf_op jit(solution)/shard_map/all_gather | solution.py:78
  119.6 17.1 all-reduce.1
  180.8 87.2 %reduce-scatter.10.cloned.1.call-done = f32[128,2048]{1,0:T(8,128)} async-done(((f32[1024,2048]{1,0:T(8,128)}), f32[128,2048]{1,0:T(8,128)}) %reduce-scatter.10.cloned.1.call-update) | async-done | bytes 1048592 | tf_op jit(solution)/shard_map/reduce_scatter | solution.py:144
  287.6 111.9 %all-to-all-done.2 = bf16[32,40,2048]{2,1,0:T(8,128)(2,1)} async-done(((bf16[32,40,2048]{2,1,0:T(8,128)(2,1)}), bf16[32,40,2048]{2,1,0:T(8,128)(2,1)}, u32[]{:S(2)}, u32[]{:S(2)}) %all-to-all-start.2) | async-done | bytes 5242912 | tf_op jit(solution)/shard_map/all_to_all | solution.py:194
  409.8 110.8 %all-to-all-done = bf16[32,40,2048]{2,1,0:T(8,128)(2,1)} async-done(((bf16[32,40,2048]{2,1,0:T(8,128)(2,1)}), bf16[32,40,2048]{2,1,0:T(8,128)(2,1)}, u32[]{:S(2)}, u32[]{:S(2)}) %all-to-all-start) | async-done | bytes 5242912 | tf_op jit(solution)/shard_map/all_to_all | solution.py:166
  540.2 44.8 %all-gather.22.cloned.1.call-done = bf16[4,2048,1024]{2,1,0:T(8,128)(2,1)} async-done(((bf16[4,512,1024]{2,1,0:T(8,128)(2,1)}), bf16[4,2048,1024]{2,1,0:T(8,128)(2,1)}) %all-gather.22.cloned.1.call-update) | async-done | bytes 16777232 | tf_op jit(solution)/shard_map/all_gather | solution.py:82
  598.9 145.3 %all-gather.24.cloned.1.call-done = bf16[4,1024,2048]{2,1,0:T(8,128)(2,1)} async-done(((bf16[4,1024,512]{2,1,0:T(8,128)(2,1)}), bf16[4,1024,2048]{2,1,0:T(8,128)(2,1)}) %all-gather.24.cloned.1.call-update) | async-done | bytes 16777232 | tf_op jit(solution)/shard_map/all_gather | solution.py:83
  744.2 16.1 multiply_convert_fusion.2
  819.2 81.2 %all-to-all-done.1 = bf16[4,320,2048]{2,0,1:T(4,128)(2,1)} async-done(((bf16[4,320,2048]{2,0,1:T(4,128)(2,1)}), bf16[4,320,2048]{2,0,1:T(4,128)(2,1)}, u32[]{:S(2)}, u32[]{:S(2)}) %all-to-all-start.1) | async-done | bytes 5242912 | tf_op jit(solution)/shard_map/all_to_all | solution.py:179
  919.0 102.6 %all-to-all-done.3 = bf16[4,320,2048]{2,0,1:T(4,128)(2,1)} async-done(((bf16[4,320,2048]{2,0,1:T(4,128)(2,1)}), bf16[4,320,2048]{2,0,1:T(4,128)(2,1)}, u32[]{:S(2)}, u32[]{:S(2)}) %all-to-all-start.3) | async-done | bytes 5242912 | tf_op jit(solution)/shard_map/all_to_all | solution.py:225
  1031.7 44.9 %all-gather.26.cloned.1.call-done = bf16[1024,2048]{1,0:T(8,128)(2,1)} async-done(((bf16[128,2048]{1,0:T(8,128)(2,1)}), bf16[1024,2048]{1,0:T(8,128)(2,1)}) %all-gather.26.cloned.1.call-update) | async-done | bytes 4194320 | tf_op jit(solution)/shard_map/all_gather | solution.py:244
  1080.2 26.0 %while.28 = (s32[]{:T(128)}, f32[1024,2,128]{0,2,1:T(8,128)}, f32[1024,2,128]{0,2,1:T(8,128)}, bf16[2,512,2,128]{3,1,0,2:T(8,128)(2,1)}, bf16[2,512,2,128]{3,1,2...) while((s32[]{:T(128)}, f32[1024,2,128]{0,2,1:T(8,128)}, ...), condition=%wide.region_20.21_spmd.clone, body=%wide.region_18.20_spmd.clone.sunk | while | flops 1360002048 | bytes 81043248 | solution.py:281
  1164.7 14.9 convolution_convert_fusion
  1181.5 15.0 convolution_convert_fusion.2
  1198.3 14.9 convolution_convert_fusion.1
  1229.5 29.6 %reduce-scatter.18.cloned.1.call-done = bf16[512,256]{1,0:T(8,128)(2,1)} async-done(((bf16[2048,256]{1,0:T(8,128)(2,1)}), bf16[512,256]{1,0:T(8,128)(2,1)}) %reduce-scatter.18.cloned.1.call-update) | async-done | bytes 262160 | tf_op jit(solution)/shard_map/reduce_scatter | solution.py:338
  1260.9 51.0 %reduce-scatter.12.cloned.1.call-done = bf16[128,2048]{1,0:T(8,128)(2,1)} async-done(((bf16[1024,2048]{1,0:T(8,128)(2,1)}), bf16[128,2048]{1,0:T(8,128)(2,1)}) %reduce-scatter.12.cloned.1.call-update) | async-done | bytes 524304 | tf_op jit(solution)/shard_map/reduce_scatter | solution.py:321
  1316.4 39.1 %psum.46 = f32[4,2048]{1,0:T(4,128)} all-reduce(f32[4,2048]{1,0:T(4,128)S(1)} %pad_maximum_fusion.4), channel_id=1, replica_groups=mesh['fsdp'=4,'seq'=8] {'fsdp','seq'}, use_global_device_ids=true, to_apply=%region_31.32 | all-reduce | flops 8192 | bytes 65536 | tf_op jit(solution)/shard_map/psum | solution.py:330
  1355.5 112.3 %reduce-scatter.26.cloned.1.call-done = bf16[4,1024,512]{2,1,0:T(8,128)(2,1)} async-done(((bf16[4,1024,2048]{2,1,0:T(8,128)(2,1)}), bf16[4,1024,512]{2,1,0:T(8,128)(2,1)}) %reduce-scatter.26.cloned.1.call-update) | async-done | bytes 4194320 | tf_op jit(solution)/shard_map/reduce_scatter | solution.py:350
  1474.6 150.0 %reduce-scatter.22.cloned.1.call-done = bf16[4,512,1024]{2,1,0:T(8,128)(2,1)} async-done(((bf16[4,2048,1024]{2,1,0:T(8,128)(2,1)}), bf16[4,512,1024]{2,1,0:T(8,128)(2,1)}) %reduce-scatter.22.cloned.1.call-update) | async-done | bytes 4194320 | tf_op jit(solution)/shard_map/reduce_scatter | solution.py:344
  1631.3 150.1 %reduce-scatter.24.cloned.1.call-done = bf16[4,512,1024]{2,1,0:T(8,128)(2,1)} async-done(((bf16[4,2048,1024]{2,1,0:T(8,128)(2,1)}), bf16[4,512,1024]{2,1,0:T(8,128)(2,1)}) %reduce-scatter.24.cloned.1.call-update) | async-done | bytes 4194320 | tf_op jit(solution)/shard_map/reduce_scatter | solution.py:347
  1788.0 124.5 %all-reduce.4.cloned.1.call-done = f32[2048,32]{0,1:T(8,128)} async-done(((f32[2048,32]{0,1:T(8,128)}), f32[2048,32]{0,1:T(8,128)}) %all-reduce.4.cloned.1.call-update) | async-done | bytes 262160 | tf_op jit(solution)/shard_map/psum | solution.py:330
  (339 shorter events, 360.3 us)
Async XLA Ops:
  7.2 32.0 %all-gather.12.cloned.1.call-start = ((), (), s32[]{:S(2)}) async-start(), calls=%async_computation.14 | async-start | bytes 1310720 | tf_op jit(solution)/shard_map/all_gather | solution.py:77
  7.9 80.7 %all-gather.10.cloned.1.call-start = ((), (), s32[]{:S(2)}) async-start(), calls=%async_computation.13 | async-start | bytes 4718592 | tf_op jit(solution)/shard_map/all_gather | solution.py:92
  12.7 103.2 %all-gather.14.cloned.1.call-start = ((), (), s32[]{:S(2)}) async-start(), calls=%async_computation.15 | async-start | bytes 1310720 | tf_op jit(solution)/shard_map/all_gather | solution.py:78
  13.4 136.1 %all-gather.16.cloned.1.call-start = ((), (), s32[]{:S(2)}) async-start(), calls=%async_computation.16 | async-start | bytes 1310720 | tf_op jit(solution)/shard_map/all_gather | solution.py:79
  14.0 158.4 %all-gather.18.cloned.1.call-start = ((), (), s32[]{:S(2)}) async-start(), calls=%async_computation.17 | async-start | bytes 1310720 | tf_op jit(solution)/shard_map/all_gather | solution.py:80
  14.6 253.5 %reduce-scatter.10.cloned.1.call-start = ((), (), s32[]{:S(2)}) async-start(), calls=%async_computation.18 | async-start | bytes 9437184 | tf_op jit(solution)/shard_map/reduce_scatter | solution.py:144
  178.3 348.1 %all-gather.20.cloned.1.call-start = ((), (), s32[]{:S(2)}) async-start(), calls=%async_computation.19 | async-start | bytes 20971520 | tf_op jit(solution)/shard_map/all_gather | solution.py:81
  179.1 405.9 %all-gather.22.cloned.1.call-start = ((), (), s32[]{:S(2)}) async-start(), calls=%async_computation.20 | async-start | bytes 20971520 | tf_op jit(solution)/shard_map/all_gather | solution.py:82
  179.8 564.3 %all-gather.24.cloned.1.call-start = ((), (), s32[]{:S(2)}) async-start(), calls=%async_computation.21 | async-start | bytes 20971520 | tf_op jit(solution)/shard_map/all_gather | solution.py:83
  269.5 759.7 %copy-start.6 = (f32[128,2048]{1,0:T(8,128)}, f32[128,2048]{1,0:T(8,128)S(1)}, u32[]{:S(2)}) copy-start(f32[128,2048]{1,0:T(8,128)S(1)} %get-tuple-element.283) | copy-start | bytes 3145732
  278.1 121.4 %all-to-all-start.2 = ((bf16[32,40,2048]{2,1,0:T(8,128)(2,1)}), bf16[32,40,2048]{2,1,0:T(8,128)(2,1)}, u32[]{:S(2)}, u32[]{:S(2)}) async-start(bf16[32,40,2048]{2,1,0:T(8,128)(2,1)} %bitcast.224), calls=%async_computation.3 | async-start | bytes 10485760 | tf_op jit(solution)/shard_map/all_to_all | solution.py:194
  399.5 121.2 %all-to-all-start = ((bf16[32,40,2048]{2,1,0:T(8,128)(2,1)}), bf16[32,40,2048]{2,1,0:T(8,128)(2,1)}, u32[]{:S(2)}, u32[]{:S(2)}) async-start(bf16[32,40,2048]{2,1,0:T(8,128)(2,1)} %bitcast.215), calls=%async_computation.1 | async-start | bytes 10485760 | tf_op jit(solution)/shard_map/all_to_all | solution.py:166
  778.8 121.6 %all-to-all-start.1 = ((bf16[4,320,2048]{2,0,1:T(4,128)(2,1)}), bf16[4,320,2048]{2,0,1:T(4,128)(2,1)}, u32[]{:S(2)}, u32[]{:S(2)}) async-start(bf16[4,320,2048]{2,0,1:T(4,128)(2,1)} %copy.92), calls=%async_computation.2 | async-start | bytes 10485760 | tf_op jit(solution)/shard_map/all_to_all | solution.py:179
  900.4 121.2 %all-to-all-start.3 = ((bf16[4,320,2048]{2,0,1:T(4,128)(2,1)}), bf16[4,320,2048]{2,0,1:T(4,128)(2,1)}, u32[]{:S(2)}, u32[]{:S(2)}) async-start(bf16[4,320,2048]{2,0,1:T(4,128)(2,1)} %copy.95), calls=%async_computation.4 | async-start | bytes 10485760 | tf_op jit(solution)/shard_map/all_to_all | solution.py:225
  905.1 171.5 %all-gather.26.cloned.1.call-start = ((), (), s32[]{:S(2)}) async-start(), calls=%async_computation.22 | async-start | bytes 4718592 | tf_op jit(solution)/shard_map/all_gather | solution.py:244
  1031.4 184.0 %reduce-scatter.16.cloned.1.call-start = ((), (), s32[]{:S(2)}) async-start(), calls=%async_computation.25 | async-start | bytes 1310720 | tf_op jit(solution)/shard_map/reduce_scatter | solution.py:335
  1139.7 77.4 %reduce-scatter.20.cloned.1.call-start = ((), (), s32[]{:S(2)}) async-start(), calls=%async_computation.27 | async-start | bytes 1310720 | tf_op jit(solution)/shard_map/reduce_scatter | solution.py:341
  1144.7 83.1 %reduce-scatter.14.cloned.1.call-start = ((), (), s32[]{:S(2)}) async-start(), calls=%async_computation.24 | async-start | bytes 1310720 | tf_op jit(solution)/shard_map/reduce_scatter | solution.py:332
  1149.5 109.6 %reduce-scatter.18.cloned.1.call-start = ((), (), s32[]{:S(2)}) async-start(), calls=%async_computation.26 | async-start | bytes 1310720 | tf_op jit(solution)/shard_map/reduce_scatter | solution.py:338
  1155.5 156.3 %reduce-scatter.12.cloned.1.call-start = ((), (), s32[]{:S(2)}) async-start(), calls=%async_computation.23 | async-start | bytes 4718592 | tf_op jit(solution)/shard_map/reduce_scatter | solution.py:321
  1163.0 304.8 %reduce-scatter.26.cloned.1.call-start = ((), (), s32[]{:S(2)}) async-start(), calls=%async_computation.31 | async-start | bytes 20971520 | tf_op jit(solution)/shard_map/reduce_scatter | solution.py:350
  1179.7 444.9 %reduce-scatter.22.cloned.1.call-start = ((), (), s32[]{:S(2)}) async-start(), calls=%async_computation.29 | async-start | bytes 20971520 | tf_op jit(solution)/shard_map/reduce_scatter | solution.py:344
  1196.6 584.8 %reduce-scatter.24.cloned.1.call-start = ((), (), s32[]{:S(2)}) async-start(), calls=%async_computation.30 | async-start | bytes 20971520 | tf_op jit(solution)/shard_map/reduce_scatter | solution.py:347
  1213.3 699.2 %all-reduce.4.cloned.1.call-start = ((), (), s32[]{:S(2)}) async-start(), calls=%async_computation.28 | async-start | bytes 524288 | tf_op jit(solution)/shard_map/psum | solution.py:330
  (72 other events, 3225.0 us)
Sparse Core Ops, SparseCore 0:
  9.9 29.3 all-gather.11
  41.4 47.1 all-gather.9
  90.4 25.3 all-gather.13
  117.5 26.6 all-gather.15
  145.8 26.4 all-gather.17
  178.4 89.5 reduce-scatter.9
  269.9 155.7 all-gather.19
  427.5 157.4 all-gather.21
  586.8 157.2 all-gather.23
  1031.5 45.0 all-gather.25
  1139.9 25.8 reduce-scatter.15
  1168.8 27.7 reduce-scatter.19
  1200.0 27.7 reduce-scatter.13
  1231.3 27.7 reduce-scatter.17
  1261.8 50.0 reduce-scatter.11
  1314.8 152.9 reduce-scatter.25
  1470.7 153.8 reduce-scatter.21
  1627.5 153.8 reduce-scatter.23
  1787.5 124.9 all-reduce.3
where the time goes:
time: 1930 us; the launch traced here: 1920 us
  waiting for transfers between devices  1460 us (76%)
  matrix products  225 us (12%)
  blocking collectives  71.1 us (4%)
  local copies, waits for them, and re-layouts  66 us (3%)
  other arithmetic  62.6 us (3%)
  starting transfers between devices  21.2 us (1%)
    reduce_scatter x1, waiting for transfers between devices, shards(): lax.psum_scatter(grad_up_local.astype(jnp.bfloat16), 'fsdp', scatter_dime...  150 us
    reduce_scatter x1, waiting for transfers between devices, shards(): lax.psum_scatter(grad_gate_local.astype(jnp.bfloat16), 'fsdp', scatter_di...  150 us
    all_gather x1, waiting for transfers between devices, shards(): lax.all_gather(w_down, 'fsdp', axis=2, tiled=True)  145 us
    psum x1, waiting for transfers between devices, shards(): small_sums = lax.psum((gain_grads, grad_router_local), ('fsdp', 'seq'))  124 us
    reduce_scatter x1, waiting for transfers between devices, shards(): lax.psum_scatter(grad_down_local.astype(jnp.bfloat16), 'fsdp', scatter_di...  112 us
    all_to_all x1, waiting for transfers between devices, shards(): lax.all_to_all(slot_grads.reshape(expert_total, capacity, model_width), '...  112 us
    all_to_all x1, waiting for transfers between devices, shards(): lax.all_to_all(outgoing.reshape(expert_total, capacity, model_width), 'se...  111 us
    all_to_all x1, waiting for transfers between devices, shards(): lax.all_to_all(rows_grad, 'seq', split_axis=1, concat_axis=0, tiled=True)  103 us
  transfers between devices with their start and end apart: 23, of which 19 were waited for; matrix products, arithmetic and copies ran while one was open for 13% of the time, Pallas kernels for 0%

commit v1 on v0

--- a/solution.py
+++ b/solution.py
@@ -72,17 +72,51 @@
     local_width = w_query.shape[1]
     heads_local = local_width // head_size
     capacity = CAP
-    column_start = lax.axis_index("seq") * local_width
-    weights_full = (
-        lax.all_gather(w_query, "fsdp", axis=0, tiled=True),
-        lax.all_gather(w_key, "fsdp", axis=0, tiled=True),
-        lax.all_gather(w_value, "fsdp", axis=0, tiled=True),
-        lax.all_gather(w_out, "fsdp", axis=1, tiled=True),
-        lax.all_gather(w_gate, "fsdp", axis=1, tiled=True),
-        lax.all_gather(w_up, "fsdp", axis=1, tiled=True),
-        lax.all_gather(w_down, "fsdp", axis=2, tiled=True),
-    )
-    query_cols, key_cols, value_cols, out_rows, gate_full, up_full, down_full = weights_full
+    seq_index = lax.axis_index("seq")
+    column_start = seq_index * local_width
+    experts_local = w_gate.shape[0]
+    split = lax.axis_size("fsdp")
+    groups = split // experts_local
+    partners = None
+    if groups > 1:
+        partners = [
+            [group * experts_local + member for member in range(experts_local)]
+            for group in range(groups)
+        ]
+
+    def to_owner(weight, dim):
+        spread = jnp.concatenate([weight] * groups, 0) if groups > 1 else weight
+        return lax.all_to_all(spread, "fsdp", split_axis=0, concat_axis=dim, tiled=True)[0]
+
+    def to_shards(grad, dim):
+        parts = lax.all_to_all(
+            grad.astype(half_type)[None], "fsdp", split_axis=dim, concat_axis=0, tiled=True
+        ).astype(float_type)
+        if groups > 1:
+            parts = parts.reshape(groups, experts_local, *parts.shape[1:]).sum(0)
+        return parts
+
+    def exchange(rows):
+        return lax.all_to_all(
+            rows, "fsdp", split_axis=0, concat_axis=0, tiled=True, axis_index_groups=partners
+        )
+
+    qkv_cols = lax.all_gather(
+        jnp.concatenate([w_query, w_key, w_value], 1), "fsdp", axis=0, tiled=True
+    )
+    out_rows = lax.all_gather(w_out, "fsdp", axis=1, tiled=True)
+    gate_full = to_owner(w_gate, 1)
+    up_full = to_owner(w_up, 1)
+    down_full = to_owner(w_down, 2)
+    places = jnp.where(
+        expert_slots < capacity, expert_ids * capacity + expert_slots, -(10**6)
+    )
+    both_seq = lax.all_gather(
+        jnp.concatenate([expert_ids, places], 1), "seq", axis=0, tiled=True
+    )
+    ids_seq = both_seq[:, :top_count]
+    places_seq = both_seq[:, top_count:]
+    cotangent_seq = lax.all_gather(cotangent, "seq", axis=0, tiled=True)
     gain_rows = norm_gains.astype(float_type)
     gain_cols = lax.dynamic_slice_in_dim(gain_rows, column_start, local_width, 1)
     inputs = tokens.astype(float_type)
@@ -91,11 +125,10 @@
     normed = (unit_first * gain_rows[0]).astype(half_type)
     normed_seq = lax.all_gather(normed, "seq", axis=0, tiled=True)
     length = normed_seq.shape[0]
-    query_raw = jnp.dot(normed_seq, query_cols, preferred_element_type=float_type)
-    key_raw = jnp.dot(normed_seq, key_cols, preferred_element_type=float_type)
-    value_heads = jnp.dot(normed_seq, value_cols, preferred_element_type=float_type).astype(
-        half_type
-    )
+    raw = jnp.dot(normed_seq, qkv_cols, preferred_element_type=float_type)
+    query_raw = raw[:, :local_width]
+    key_raw = raw[:, local_width : 2 * local_width]
+    value_heads = raw[:, 2 * local_width :].astype(half_type)
     square_sums = lax.psum(
         (jnp.sum(query_raw * query_raw, -1), jnp.sum(key_raw * key_raw, -1)), "seq"
     )
@@ -142,93 +175,103 @@
     mixed_heads, log_sums = lax.map(attend, (query_cube, segment_blocks))
     attended_heads = mixed_heads.reshape(length, local_width)
     projected = lax.psum_scatter(
-        jnp.dot(attended_heads, out_rows, preferred_element_type=float_type),
+        jnp.dot(attended_heads, out_rows, preferred_element_type=float_type).astype(half_type),
         "seq",
         scatter_dimension=0,
         tiled=True,
-    )
+    ).astype(float_type)
     residual = inputs + projected
     inverse_second = inverse_rms(residual)
     unit_second = residual * inverse_second
     routed = (unit_second * gain_rows[1]).astype(half_type)
-    logits = jnp.dot(routed, w_router, preferred_element_type=float_type)
-    expert_range = jnp.arange(expert_total, dtype=jnp.int32)
-    chosen = (expert_ids[:, :, None] == expert_range).astype(float_type)
-    picked = jnp.einsum("tke,te->tk", chosen, logits, precision=HIGHEST)
-    gate_weights = jax.nn.softmax(picked, axis=-1)
-    places = jnp.where(expert_slots < capacity, expert_ids * capacity + expert_slots, -1)
-    onehot = (places[:, :, None] == jnp.arange(expert_total * capacity, dtype=jnp.int32)).astype(
-        half_type
-    )
-    outgoing = jnp.einsum("tkc,td->cd", onehot, routed, preferred_element_type=float_type).astype(
-        half_type
-    )
-    expert_rows = lax.all_to_all(
-        outgoing.reshape(expert_total, capacity, model_width),
-        "seq",
-        split_axis=0,
-        concat_axis=1,
-        tiled=True,
-    )
-    gate_pre = jnp.einsum("erd,edf->erf", expert_rows, gate_full, preferred_element_type=float_type)
-    up_pre = jnp.einsum("erd,edf->erf", expert_rows, up_full, preferred_element_type=float_type)
-    hidden = (jax.nn.silu(gate_pre) * up_pre).astype(half_type)
-    returned = jnp.einsum(
-        "erf,efd->erd", hidden, down_full, preferred_element_type=float_type
-    ).astype(half_type)
-    incoming = lax.all_to_all(returned, "seq", split_axis=1, concat_axis=0, tiled=True)
-    onehot_flat = onehot.reshape(tok_rows * top_count, expert_total * capacity)
-    picked_rows = jnp.dot(
-        onehot_flat,
-        incoming.reshape(expert_total * capacity, model_width),
-        preferred_element_type=float_type,
-    ).reshape(tok_rows, top_count, model_width)
-    mixture = jnp.sum(gate_weights[:, :, None] * picked_rows, axis=1)
+    routed_seq = lax.all_gather(routed, "seq", axis=0, tiled=True)
+    seq_size = length // tok_rows
+    slots = experts_local * capacity
+
+    def gates_of(rows, ids):
+        logits = jnp.dot(rows, w_router, preferred_element_type=float_type)
+        chosen = (ids[:, :, None] == jnp.arange(expert_total, dtype=jnp.int32)).astype(float_type)
+        picked = jnp.einsum("tke,te->tk", chosen, logits, precision=HIGHEST)
+        return chosen, jax.nn.softmax(picked, axis=-1)
+
+    chosen, gate_weights = gates_of(routed, expert_ids)
+    gates_seq = gates_of(routed_seq, ids_seq)[1]
+    mine = (places_seq - seq_index * slots).reshape(seq_size, tok_rows, top_count)
+    hits = mine[:, :, :, None] == jnp.arange(slots, dtype=jnp.int32)
+    onehot = jnp.any(hits, 2).astype(half_type)
+    combine = jnp.sum(
+        jnp.where(hits, gates_seq.reshape(seq_size, tok_rows, top_count)[..., None], 0.0), 2
+    )
+
+    def dispatch(rows):
+        placed = jnp.einsum(
+            "btc,btd->bcd",
+            onehot,
+            rows.reshape(seq_size, tok_rows, model_width),
+            preferred_element_type=float_type,
+        ).astype(half_type)
+        placed = placed.reshape(seq_size, experts_local, capacity, model_width)
+        return placed.transpose(1, 0, 2, 3)
+
+    def undispatch(rows):
+        rows = rows.reshape(experts_local, seq_size, capacity, model_width)
+        return rows.transpose(1, 0, 2, 3).reshape(seq_size, slots, model_width)
+
+    flat = experts_local * seq_size * capacity
+    expert_rows = exchange(dispatch(routed_seq)).reshape(flat, model_width)
+    upstream_slots = dispatch(cotangent_seq)
+    upstream_rows = exchange(upstream_slots).reshape(flat, model_width)
+    slot_gates = jnp.sum(combine, 1).reshape(seq_size, experts_local, capacity).transpose(1, 0, 2)
+    row_gates = exchange(slot_gates).reshape(flat)
+    gate_pre = jnp.dot(expert_rows, gate_full, preferred_element_type=float_type)
+    up_pre = jnp.dot(expert_rows, up_full, preferred_element_type=float_type)
+    gate_sigmoid = jax.nn.sigmoid(gate_pre)
+    hidden = (gate_pre * gate_sigmoid * up_pre).astype(half_type)
+    returned = jnp.dot(hidden, down_full, preferred_element_type=float_type).astype(half_type)
+    slot_dots = jnp.sum(
+        returned.astype(float_type) * upstream_rows.astype(float_type), -1
+    ).reshape(experts_local, seq_size, capacity)
+    slot_dots = exchange(slot_dots).transpose(1, 0, 2).reshape(seq_size, slots)
+    gate_grad_part = jnp.sum(jnp.where(hits, slot_dots[:, None, None, :], 0.0), -1)
+    gate_grad = lax.psum_scatter(
+        gate_grad_part.reshape(length, top_count), "seq", scatter_dimension=0, tiled=True
+    )
+    incoming = undispatch(exchange(returned.reshape(experts_local, seq_size, capacity, model_width)))
+    mixture_part = jnp.einsum(
+        "btc,bcd->btd", combine.astype(half_type), incoming, preferred_element_type=float_type
+    ).astype(half_type)
+    mixture = lax.psum_scatter(
+        mixture_part.reshape(length, model_width), "seq", scatter_dimension=0, tiled=True
+    ).astype(float_type)
     output = (residual + mixture).astype(half_type)
     upstream = cotangent.astype(float_type)
-    gate_grad = jnp.sum(upstream[:, None, :] * picked_rows, axis=-1)
-    weighted = (gate_weights[:, :, None] * upstream[:, None, :]).astype(half_type)
-    slot_grads = jnp.einsum(
-        "tkc,tkd->cd", onehot, weighted, preferred_element_type=float_type
-    ).astype(half_type)
-    returned_grad = lax.all_to_all(
-        slot_grads.reshape(expert_total, capacity, model_width),
-        "seq",
-        split_axis=0,
-        concat_axis=1,
-        tiled=True,
-    )
+    slot_grads = (row_gates[:, None] * upstream_rows.astype(float_type)).astype(half_type)
     hidden_grad = jnp.einsum(
-        "erd,efd->erf", returned_grad, down_full, preferred_element_type=float_type
-    )
-    gate_sigmoid = jax.nn.sigmoid(gate_pre)
+        "rd,fd->rf", slot_grads, down_full, preferred_element_type=float_type
+    )
     gate_pre_grad = (
         hidden_grad * up_pre * gate_sigmoid * (1.0 + gate_pre * (1.0 - gate_sigmoid))
     ).astype(half_type)
     up_pre_grad = (hidden_grad * gate_pre * gate_sigmoid).astype(half_type)
-    grad_down_local = jnp.einsum(
-        "erf,erd->efd", hidden, returned_grad, preferred_element_type=float_type
-    )
-    grad_gate_local = jnp.einsum(
-        "erd,erf->edf", expert_rows, gate_pre_grad, preferred_element_type=float_type
-    )
-    grad_up_local = jnp.einsum(
-        "erd,erf->edf", expert_rows, up_pre_grad, preferred_element_type=float_type
-    )
-    rows_grad = jnp.einsum(
-        "erf,edf->erd", gate_pre_grad, gate_full, preferred_element_type=float_type
-    )
+    rows_grad = jnp.einsum("rf,df->rd", gate_pre_grad, gate_full, preferred_element_type=float_type)
     rows_grad = (
         rows_grad
-        + jnp.einsum("erf,edf->erd", up_pre_grad, up_full, preferred_element_type=float_type)
-    ).astype(half_type)
-    sent_back = lax.all_to_all(rows_grad, "seq", split_axis=1, concat_axis=0, tiled=True)
-    routed_grad = jnp.einsum(
-        "tkc,cd->td",
-        onehot,
-        sent_back.reshape(expert_total * capacity, model_width),
-        preferred_element_type=float_type,
-    )
+        + jnp.einsum("rf,df->rd", up_pre_grad, up_full, preferred_element_type=float_type)
+    ).astype(half_type)
+    sent_back = undispatch(
+        exchange(rows_grad.reshape(experts_local, seq_size, capacity, model_width))
+    )
+    expert_part = jnp.einsum(
+        "btc,bcd->btd", onehot, sent_back, preferred_element_type=float_type
+    ).astype(half_type)
+    routed_grad = lax.psum_scatter(
+        expert_part.reshape(length, model_width), "seq", scatter_dimension=0, tiled=True
+    ).astype(float_type)
+    grad_down_full = jnp.einsum("rf,rd->fd", hidden, slot_grads, preferred_element_type=float_type)
+    grad_gate_full = jnp.einsum(
+        "rd,rf->df", expert_rows, gate_pre_grad, preferred_element_type=float_type
+    )
+    grad_up_full = jnp.einsum("rd,rf->df", expert_rows, up_pre_grad, preferred_element_type=float_type)
     mean_grad = jnp.sum(gate_weights * gate_grad, -1, keepdims=True)
     picked_grad = gate_weights * (gate_grad - mean_grad)
     logit_grad = jnp.einsum("tke,tk->te", chosen, picked_grad, precision=HIGHEST).astype(half_type)
@@ -236,7 +279,7 @@
         "te,de->td", logit_grad, w_router, preferred_element_type=float_type
     )
     grad_router_local = jnp.einsum(
-        "td,te->de", routed, logit_grad, preferred_element_type=float_type
+        "td,te->ed", routed, logit_grad, preferred_element_type=float_type
     )
     gain_second_grad = jnp.sum(routed_grad * unit_second, axis=0)
     residual_grad = upstream + norm_back(routed_grad * gain_rows[1], unit_second, inverse_second)
@@ -299,25 +342,9 @@
     key_raw_grad = (
         inverse_key * (key_scaled - unit_key * (centers[1] / model_width)[:, None])
     ).astype(half_type)
-    normed_part = jnp.einsum(
-        "th,dh->td", query_raw_grad, query_cols, preferred_element_type=float_type
-    )
-    normed_part = normed_part + jnp.einsum(
-        "th,dh->td", key_raw_grad, key_cols, preferred_element_type=float_type
-    )
-    normed_part = normed_part + jnp.einsum(
-        "th,dh->td", value_back, value_cols, preferred_element_type=float_type
-    )
-    normed_rows_back = lax.all_gather(normed, "seq", axis=0, tiled=True)
-    grad_query_local = jnp.einsum(
-        "td,th->dh", normed_rows_back, query_raw_grad, preferred_element_type=float_type
-    )
-    grad_key_local = jnp.einsum(
-        "td,th->dh", normed_rows_back, key_raw_grad, preferred_element_type=float_type
-    )
-    grad_value_local = jnp.einsum(
-        "td,th->dh", normed_rows_back, value_back, preferred_element_type=float_type
-    )
+    raw_grads = jnp.concatenate([query_raw_grad, key_raw_grad, value_back], 1)
+    normed_part = jnp.einsum("th,dh->td", raw_grads, qkv_cols, preferred_element_type=float_type)
+    grad_qkv_local = jnp.einsum("td,th->dh", normed_seq, raw_grads, preferred_element_type=float_type)
     normed_grad = lax.psum_scatter(
         normed_part.astype(jnp.bfloat16), "seq", scatter_dimension=0, tiled=True
     ).astype(jnp.float32)
@@ -327,42 +354,26 @@
     gain_query_full = lax.dynamic_update_slice_in_dim(zero_row, gain_query_grad, column_start, 0)
     gain_key_full = lax.dynamic_update_slice_in_dim(zero_row, gain_key_grad, column_start, 0)
     gain_grads = jnp.stack([gain_first_grad, gain_second_grad, gain_query_full, gain_key_full])
-    small_sums = lax.psum((gain_grads, grad_router_local), ("fsdp", "seq"))
-    owned = (
-        lax.psum_scatter(
-            grad_query_local.astype(jnp.bfloat16), "fsdp", scatter_dimension=0, tiled=True
-        ).astype(jnp.float32),
-        lax.psum_scatter(
-            grad_key_local.astype(jnp.bfloat16), "fsdp", scatter_dimension=0, tiled=True
-        ).astype(jnp.float32),
-        lax.psum_scatter(
-            grad_value_local.astype(jnp.bfloat16), "fsdp", scatter_dimension=0, tiled=True
-        ).astype(jnp.float32),
-        lax.psum_scatter(
-            grad_out_local.astype(jnp.bfloat16), "fsdp", scatter_dimension=1, tiled=True
-        ).astype(jnp.float32),
-        lax.psum_scatter(
-            grad_gate_local.astype(jnp.bfloat16), "fsdp", scatter_dimension=1, tiled=True
-        ).astype(jnp.float32),
-        lax.psum_scatter(
-            grad_up_local.astype(jnp.bfloat16), "fsdp", scatter_dimension=1, tiled=True
-        ).astype(jnp.float32),
-        lax.psum_scatter(
-            grad_down_local.astype(jnp.bfloat16), "fsdp", scatter_dimension=2, tiled=True
-        ).astype(jnp.float32),
-    )
+    router_grad = lax.psum(grad_router_local, ("fsdp", "seq")).T
+    gain_sums = lax.psum(gain_grads, ("fsdp", "seq"))
+    qkv_owned = lax.psum_scatter(
+        grad_qkv_local.astype(half_type), "fsdp", scatter_dimension=0, tiled=True
+    ).astype(float_type)
+    out_owned = lax.psum_scatter(
+        grad_out_local.astype(half_type), "fsdp", scatter_dimension=1, tiled=True
+    ).astype(float_type)
     return (
         output,
         input_grad,
-        small_sums[0],
-        owned[0],
-        owned[1],
-        owned[2],
-        owned[3],
-        small_sums[1],
-        owned[4],
-        owned[5],
-        owned[6],
+        gain_sums,
+        qkv_owned[:, :local_width],
+        qkv_owned[:, local_width : 2 * local_width],
+        qkv_owned[:, 2 * local_width :],
+        out_owned,
+        router_grad,
+        to_shards(grad_gate_full, 1),
+        to_shards(grad_up_full, 1),
+        to_shards(grad_down_full, 2),
     )
 
 

time: 1930 us -> 1200 us (0.62)
  waiting for transfers between devices: 1460 us -> 479 us
  local copies, waits for them, and re-layouts: 66 us -> 206 us
  blocking collectives: 71.1 us -> 148 us
  other arithmetic: 62.6 us -> 135 us
  matrix products: 225 us -> 154 us
  starting transfers between devices: 21.2 us -> 50.8 us
    reduce_scatter x7 -> x5, waiting for transfers between devices: 451 us -> 49.5 us  [the longest x1 49.5 us: shards(): lax.psum_scatter(expert_part.reshape(length, model_width), 'seq', scatter...]
    all_gather x7 -> x4, waiting for transfers between devices: 241 us -> 39.1 us  [the longest x1 39 us: shards(): lax.all_gather(jnp.concatenate([w_query, w_key, w_value], 1), 'fsdp', axi...]
    all_to_all x4 -> x10, waiting for transfers between devices: 407 us -> 219 us  [the longest x5 147 us: exchange(): lax.all_to_all(rows, 'fsdp', split_axis=0, concat_axis=0, tiled=True, axi...]
    psum x1, waiting for transfers between devices: 124 us -> 26.9 us  [shards(): router_grad = lax.psum(grad_router_local, ('fsdp', 'seq')).T]
    unnamed x3 -> x6, other arithmetic: 0.36 us -> 78.4 us
    broadcast_in_dim x0 -> x4, local copies, waits for them, and re-layouts: none -> 77.8 us  [the longest x3 77.7 us: to_shards(): grad.astype(half_type)[None]]
    unnamed x132 -> x130, local copies, waits for them, and re-layouts: 17.6 us -> 83.4 us
    dot_general x23 -> x18, matrix products: 180 us -> 121 us  [the longest x1 12.2 us: shards(): jnp.einsum('rd,fd->rf', slot_grads, down_full, preferred_element_type=flo...]
  transfers between devices with their start and end apart: 23 -> 24, of which waited for: 19 -> 14; matrix products, arithmetic and copies ran while one was open for 13% -> 34% of each run, Pallas kernels for 0% -> 0%
where the time goes in v1:
time: 1200 us; the launch traced here: 1190 us
  waiting for transfers between devices  479 us (40%)
  local copies, waits for them, and re-layouts  206 us (17%)
  matrix products  154 us (13%)
  blocking collectives  148 us (12%)
  other arithmetic  135 us (11%)
  starting transfers between devices  50.8 us (4%)
  between operations  15.5 us (1%)
    all_to_all x5, waiting for transfers between devices, exchange(): lax.all_to_all(rows, 'fsdp', split_axis=0, concat_axis=0, tiled=True, axi...  147 us
    unnamed x130, local copies, waits for them, and re-layouts  83.4 us
    unnamed x6, other arithmetic  78.4 us
    broadcast_in_dim x3, local copies, waits for them, and re-layouts, to_shards(): grad.astype(half_type)[None]  77.7 us
    all_to_all x2, waiting for transfers between devices, to_owner(): lax.all_to_all(spread, 'fsdp', split_axis=0, concat_axis=dim, tiled=True)[0]  58.4 us
    all_to_all x1, blocking collectives, to_owner(): lax.all_to_all(spread, 'fsdp', split_axis=0, concat_axis=dim, tiled=True)[0]  51.9 us
    reduce_scatter x1, waiting for transfers between devices, shards(): lax.psum_scatter(expert_part.reshape(length, model_width), 'seq', scatter...  49.5 us
    all_gather x1, waiting for transfers between devices, shards(): normed_seq = lax.all_gather(normed, 'seq', axis=0, tiled=True)  49.4 us
  transfers between devices with their start and end apart: 24, of which 14 were waited for; matrix products, arithmetic and copies ran while one was open for 34% of the time, Pallas kernels for 0%

profile of v1, /device:TPU:0, one launch (start us, length us, event | category | flops | bytes accessed | tf_op | source)
XLA Modules:
  0.0 1189.2 jit_solution(6531480711968059736)
XLA Ops:
  18.2 39.0 %all-gather.9.cloned.1.call-done = bf16[2048,768]{1,0:T(8,128)(2,1)} async-done(((bf16[512,768]{1,0:T(8,128)(2,1)}), bf16[2048,768]{1,0:T(8,128)(2,1)}) %all-gather.9.cloned.1.call-update) | async-done | bytes 3145744 | tf_op jit(solution)/shard_map/all_gather | solution.py:104
  57.2 49.4 %all-gather.7.cloned.1.call-done = bf16[1024,2048]{1,0:T(8,128)(2,1)} async-done(((bf16[128,2048]{1,0:T(8,128)(2,1)}), bf16[1024,2048]{1,0:T(8,128)(2,1)}) %all-gather.7.cloned.1.call-update) | async-done | bytes 4194320 | tf_op jit(solution)/shard_map/all_gather | solution.py:126
  114.8 14.8 %all-reduce.1 = (f32[1024]{0:T(1024)S(1)}, f32[1024]{0:T(1024)S(1)}) all-reduce(f32[1024]{0:T(1024)S(1)} %get-tuple-element.275, f32[1024]{0:T(1024)S(1)} %get-tuple-element.274), channel_id=1, replica_groups=mesh['fsdp'=4,'seq'=8] {'seq'}, use_global_device_ids=true, to_apply=%region_2.3 | all-reduce | flops 2048 | bytes 16384 | tf_op jit(solution)/shard_map/psum | solution.py:132
  158.9 48.2 %reduce-scatter.8.cloned.1.call-done = bf16[128,2048]{1,0:T(8,128)(2,1)} async-done(((bf16[1024,2048]{1,0:T(8,128)(2,1)}), bf16[128,2048]{1,0:T(8,128)(2,1)}) %reduce-scatter.8.cloned.1.call-update) | async-done | bytes 524304 | tf_op jit(solution)/shard_map/reduce_scatter | solution.py:177
  210.5 51.9 %all_to_all.90 = bf16[4,512,1024]{2,1,0:T(8,128)(2,1)} all-to-all(bf16[4,512,1024]{2,1,0:T(8,128)(2,1)} %param.25), channel_id=1, replica_groups=mesh['fsdp'=4,'seq'=8] {'fsdp'}, dimensions={0} | all-to-all | bytes 8388608 | tf_op jit(solution)/shard_map/all_to_all | solution.py:89
  274.1 37.3 %all-to-all-done.2 = bf16[4,512,1024]{2,1,0:T(8,128)(2,1)} async-done(((bf16[4,512,1024]{2,1,0:T(8,128)(2,1)}), bf16[4,512,1024]{2,1,0:T(8,128)(2,1)}, u32[]{:S(2)}, u32[]{:S(2)}) %all-to-all-start.2) | async-done | bytes 4194336 | tf_op jit(solution)/shard_map/all_to_all | solution.py:89
  316.3 17.9 %all_gather.24 = s32[1024,16]{0,1:T(8,128)S(1)} all-gather(s32[128,16]{0,1:T(8,128)S(1)} %pad_add_fusion), channel_id=1, replica_groups=mesh['fsdp'=4,'seq'=8] {'seq'}, dimensions={0}, use_global_device_ids=true | all-gather | bytes 73728 | tf_op jit(solution)/shard_map/all_gather | solution.py:114
  342.0 21.1 %all-to-all-done.3 = bf16[4,1024,512]{1,2,0:T(8,128)(2,1)} async-done(((bf16[4,1024,512]{1,2,0:T(8,128)(2,1)}), bf16[4,1024,512]{1,2,0:T(8,128)(2,1)}, u32[]{:S(2)}, u32[]{:S(2)}) %all-to-all-start.3) | async-done | bytes 4194336 | tf_op jit(solution)/shard_map/all_to_all | solution.py:89
  374.8 51.6 %all-to-all-done = bf16[4,8,40,2048]{3,2,1,0:T(8,128)(2,1)} async-done(((bf16[4,8,40,2048]{3,2,1,0:T(8,128)(2,1)}), bf16[4,8,40,2048]{3,2,1,0:T(8,128)(2,1)}, u32[]{:S(2)}, u32[]{:S(2)}) %all-to-all-start) | async-done | bytes 5242912 | tf_op jit(solution)/shard_map/all_to_all | solution.py:100
  457.7 32.1 %all-to-all-done.6 = bf16[4,8,40,2048]{3,2,1,0:T(8,128)(2,1)} async-done(((bf16[4,8,40,2048]{3,2,1,0:T(8,128)(2,1)}), bf16[4,8,40,2048]{3,2,1,0:T(8,128)(2,1)}, u32[]{:S(2)}, u32[]{:S(2)}) %all-to-all-start.6) | async-done | bytes 5242912 | tf_op jit(solution)/shard_map/all_to_all | solution.py:100
  558.7 54.8 %all-to-all-done.7 = bf16[4,8,40,2048]{3,2,1,0:T(8,128)(2,1)} async-done(((bf16[4,8,40,2048]{3,2,1,0:T(8,128)(2,1)}), bf16[4,8,40,2048]{3,2,1,0:T(8,128)(2,1)}, u32[]{:S(2)}, u32[]{:S(2)}) %all-to-all-start.7) | async-done | bytes 5242912 | tf_op jit(solution)/shard_map/all_to_all | solution.py:100
  623.8 49.5 %reduce-scatter.12.cloned.1.call-done = bf16[128,2048]{1,0:T(8,128)(2,1)} async-done(((bf16[1024,2048]{1,0:T(8,128)(2,1)}), bf16[128,2048]{1,0:T(8,128)(2,1)}) %reduce-scatter.12.cloned.1.call-update) | async-done | bytes 524304 | tf_op jit(solution)/shard_map/reduce_scatter | solution.py:267
  677.8 45.3 %all-gather.17.cloned.1.call-done = bf16[1024,2048]{1,0:T(8,128)(2,1)} async-done(((bf16[128,2048]{1,0:T(8,128)(2,1)}), bf16[1024,2048]{1,0:T(8,128)(2,1)}) %all-gather.17.cloned.1.call-update) | async-done | bytes 4194320 | tf_op jit(solution)/shard_map/all_gather | solution.py:287
  728.9 15.4 %while.28 = (s32[]{:T(128)}, f32[1024,2,128]{0,2,1:T(8,128)S(1)}, f32[1024,2,128]{0,2,1:T(8,128)}, bf16[2,512,2,128]{3,1,0,2:T(8,128)(2,1)}, bf16[2,512,2,128]{3...) while((s32[]{:T(128)}, f32[1024,2,128]{0,2,1:T(8,128)S(1)}, ...), condition=%wide.region_27.28_spmd.clone, body=%wide.region_25.27_spmd.clone.sunk | while | flops 1360002048 | bytes 53778708 | solution.py:324
  762.7 15.1 %all-reduce = (f32[1024]{0:T(1024)S(1)}, f32[1024]{0:T(1024)S(1)}) all-reduce(f32[1024]{0:T(1024)S(1)} %get-tuple-element.272, f32[1024]{0:T(1024)S(1)} %get-tuple-element.269), channel_id=1, replica_groups=mesh['fsdp'=4,'seq'=8] {'seq'}, use_global_device_ids=true, to_apply=%region_31.32 | all-reduce | flops 2048 | bytes 16384 | tf_op jit(solution)/shard_map/psum | solution.py:336
  807.7 28.7 %copy.232 = bf16[1,2048,1024]{2,0,1:T(2,128)(2,1)} copy(bf16[1,2048,1024]{2,1,0:T(8,128)(2,1)S(1)} %convert_bitcast_fusion.2) | data formatting | bytes 8388608 | tf_op jit(solution)/shard_map/broadcast_in_dim | solution.py:93
  836.9 26.0 %reduce.7 = bf16[2048,1024]{1,0:T(8,128)(2,1)} reduce(bf16[2048,1,1024]{2,1,0:T(2,128)(2,1)} %bitcast.249, bf16[]{:T(256)} %broadcast.251), dimensions={1}, to_apply=%bitcast.206.reduce_sub_computation | reduce | bytes 8388610
  893.7 28.7 %copy.231 = bf16[1,2048,1024]{2,0,1:T(2,128)(2,1)} copy(bf16[1,2048,1024]{2,1,0:T(8,128)(2,1)S(1)} %convert_bitcast_fusion.1) | data formatting | bytes 8388608 | tf_op jit(solution)/shard_map/broadcast_in_dim | solution.py:93
  922.4 26.0 %reduce.8 = bf16[2048,1024]{1,0:T(8,128)(2,1)} reduce(bf16[2048,1,1024]{2,1,0:T(2,128)(2,1)} %bitcast.251, bf16[]{:T(256)} %broadcast.251), dimensions={1}, to_apply=%bitcast.205.reduce_sub_computation | reduce | bytes 8388610
  971.2 20.3 %copy.180 = bf16[1,1024,2048]{1,0,2:T(2,128)(2,1)} copy(bf16[1,1024,2048]{2,1,0:T(8,128)(2,1)} %convert_bitcast_fusion) | data formatting | bytes 8388608 | tf_op jit(solution)/shard_map/broadcast_in_dim | solution.py:93
  991.4 26.0 %reduce.9 = bf16[2048,1024]{1,0:T(8,128)(2,1)} reduce(bf16[2048,1,1024]{2,1,0:T(2,128)(2,1)} %bitcast.250, bf16[]{:T(256)} %broadcast.251), dimensions={1}, to_apply=%bitcast.147.reduce_sub_computation | reduce | bytes 8388610
  1083.1 20.8 %copy.181 = f32[1,1024,4,512]{3,1,2,0:T(8,128)} copy(bf16[1,1024,4,512]{1,0,3,2:T(2,128)(2,1)} %bitcast.254) | data formatting | bytes 12582912 | tf_op jit(solution)/shard_map/convert_element_type | solution.py:94
  1113.1 40.6 %psum.46 = f32[4,2048]{1,0:T(4,128)} all-reduce(f32[4,2048]{1,0:T(4,128)S(1)} %pad_maximum_fusion.8), channel_id=1, replica_groups=mesh['fsdp'=4,'seq'=8] {'fsdp','seq'}, use_global_device_ids=true, to_apply=%region_38.39 | all-reduce | flops 8192 | bytes 65536 | tf_op jit(solution)/shard_map/psum | solution.py:358
  1153.7 26.9 %all-reduce.4.cloned.1.call-done = f32[2048,32]{0,1:T(8,128)} async-done(((f32[2048,32]{0,1:T(8,128)}), f32[2048,32]{0,1:T(8,128)}) %all-reduce.4.cloned.1.call-update) | async-done | bytes 262160 | tf_op jit(solution)/shard_map/psum | solution.py:357
  (343 shorter events, 410.5 us)
Async XLA Ops:
  7.2 50.0 %all-gather.9.cloned.1.call-start = ((), (), s32[]{:S(2)}) async-start(), calls=%async_computation.20 | async-start | bytes 3932160 | tf_op jit(solution)/shard_map/all_gather | solution.py:104
  9.3 97.2 %all-gather.7.cloned.1.call-start = ((), (), s32[]{:S(2)}) async-start(), calls=%async_computation.19 | async-start | bytes 4718592 | tf_op jit(solution)/shard_map/all_gather | solution.py:126
  13.5 140.0 %all-gather.11.cloned.1.call-start = ((), (), s32[]{:S(2)}) async-start(), calls=%async_computation.21 | async-start | bytes 1310720 | tf_op jit(solution)/shard_map/all_gather | solution.py:107
  14.2 192.9 %reduce-scatter.8.cloned.1.call-start = ((), (), s32[]{:S(2)}) async-start(), calls=%async_computation.22 | async-start | bytes 4718592 | tf_op jit(solution)/shard_map/reduce_scatter | solution.py:177
  158.9 176.6 %all-gather.13.cloned.1.call-start = ((), (), s32[]{:S(2)}) async-start(), calls=%async_computation.23 | async-start | bytes 4718592 | tf_op jit(solution)/shard_map/all_gather | solution.py:187
  262.5 48.9 %all-to-all-start.2 = ((bf16[4,512,1024]{2,1,0:T(8,128)(2,1)}), bf16[4,512,1024]{2,1,0:T(8,128)(2,1)}, u32[]{:S(2)}, u32[]{:S(2)}) async-start(bf16[4,512,1024]{2,1,0:T(8,128)(2,1)} %param.26), calls=%async_computation.3 | async-start | bytes 8388608 | tf_op jit(solution)/shard_map/all_to_all | solution.py:89
  267.3 100.9 %all-gather.15.cloned.1.call-start = ((), (), s32[]{:S(2)}) async-start(), calls=%async_computation.25 | async-start | bytes 4718592 | tf_op jit(solution)/shard_map/all_gather | solution.py:119
  311.4 51.7 %all-to-all-start.3 = ((bf16[4,1024,512]{1,2,0:T(8,128)(2,1)}), bf16[4,1024,512]{1,2,0:T(8,128)(2,1)}, u32[]{:S(2)}, u32[]{:S(2)}) async-start(bf16[4,1024,512]{1,2,0:T(8,128)(2,1)} %copy.164), calls=%async_computation.4 | async-start | bytes 8388608 | tf_op jit(solution)/shard_map/all_to_all | solution.py:89
  363.1 63.2 %all-to-all-start = ((bf16[4,8,40,2048]{3,2,1,0:T(8,128)(2,1)}), bf16[4,8,40,2048]{3,2,1,0:T(8,128)(2,1)}, u32[]{:S(2)}, u32[]{:S(2)}) async-start(bf16[4,8,40,2048]{3,2,1,0:T(8,128)(2,1)} %bitcast.259), calls=%async_computation.1 | async-start | bytes 10485760 | tf_op jit(solution)/shard_map/all_to_all | solution.py:100
  426.3 63.5 %all-to-all-start.6 = ((bf16[4,8,40,2048]{3,2,1,0:T(8,128)(2,1)}), bf16[4,8,40,2048]{3,2,1,0:T(8,128)(2,1)}, u32[]{:S(2)}, u32[]{:S(2)}) async-start(bf16[4,8,40,2048]{3,2,1,0:T(8,128)(2,1)} %bitcast.258), calls=%async_computation.8 | async-start | bytes 10485760 | tf_op jit(solution)/shard_map/all_to_all | solution.py:100
  501.4 7.9 all-to-all-start.8
  552.6 60.9 %all-to-all-start.7 = ((bf16[4,8,40,2048]{3,2,1,0:T(8,128)(2,1)}), bf16[4,8,40,2048]{3,2,1,0:T(8,128)(2,1)}, u32[]{:S(2)}, u32[]{:S(2)}) async-start(bf16[4,8,40,2048]{3,2,1,0:T(8,128)(2,1)} %bitcast.266), calls=%async_computation.9 | async-start | bytes 10485760 | tf_op jit(solution)/shard_map/all_to_all | solution.py:100
  557.6 64.0 %reduce-scatter.14.cloned.1.call-start = ((), (), s32[]{:S(2)}) async-start(), calls=%async_computation.27 | async-start | bytes 36864 | tf_op jit(solution)/shard_map/reduce_scatter | solution.py:236
  558.4 114.9 %reduce-scatter.12.cloned.1.call-start = ((), (), s32[]{:S(2)}) async-start(), calls=%async_computation.26 | async-start | bytes 4718592 | tf_op jit(solution)/shard_map/reduce_scatter | solution.py:267
  619.8 103.4 %all-gather.17.cloned.1.call-start = ((), (), s32[]{:S(2)}) async-start(), calls=%async_computation.28 | async-start | bytes 4718592 | tf_op jit(solution)/shard_map/all_gather | solution.py:287
  677.7 426.3 %reduce-scatter.20.cloned.1.call-start = ((), (), s32[]{:S(2)}) async-start(), calls=%async_computation.31 | async-start | bytes 1310720 | tf_op jit(solution)/shard_map/reduce_scatter | solution.py:362
  748.9 357.0 %reduce-scatter.18.cloned.1.call-start = ((), (), s32[]{:S(2)}) async-start(), calls=%async_computation.30 | async-start | bytes 3932160 | tf_op jit(solution)/shard_map/reduce_scatter | solution.py:359
  785.8 322.5 %reduce-scatter.16.cloned.1.call-start = ((), (), s32[]{:S(2)}) async-start(), calls=%async_computation.29 | async-start | bytes 4718592 | tf_op jit(solution)/shard_map/reduce_scatter | solution.py:348
  793.4 80.0 %all-to-all-start.4 = ((bf16[4,8,40,2048]{3,2,1,0:T(8,128)(2,1)}), bf16[4,8,40,2048]{3,2,1,0:T(8,128)(2,1)}, u32[]{:S(2)}, u32[]{:S(2)}) async-start(bf16[4,8,40,2048]{3,2,1,0:T(8,128)(2,1)} %bitcast.265), calls=%async_computation.5 | async-start | bytes 10485760 | tf_op jit(solution)/shard_map/all_to_all | solution.py:100
  873.4 81.3 %all-to-all-start.9 = ((bf16[4,2,262144]{2,1,0:T(2,128)(2,1)}), bf16[4,2,262144]{2,1,0:T(2,128)(2,1)}, u32[]{:S(2)}, u32[]{:S(2)}) async-start(bf16[4,2,262144]{2,1,0:T(2,128)(2,1)} %reshape.382), calls=%async_computation.16 | async-start | bytes 8388608 | tf_op jit(solution)/shard_map/all_to_all | solution.py:92
  878.3 231.6 %reduce-scatter.10.cloned.1.call-start = ((), (), s32[]{:S(2)}) async-start(), calls=%async_computation.24 | async-start | bytes 4718592 | tf_op jit(solution)/shard_map/reduce_scatter | solution.py:243
  954.7 69.0 %all-to-all-start.10 = ((bf16[4,2,262144]{2,1,0:T(2,128)(2,1)}), bf16[4,2,262144]{2,1,0:T(2,128)(2,1)}, u32[]{:S(2)}, u32[]{:S(2)}) async-start(bf16[4,2,262144]{2,1,0:T(2,128)(2,1)} %reshape.384), calls=%async_computation.17 | async-start | bytes 8388608 | tf_op jit(solution)/shard_map/all_to_all | solution.py:92
  1023.7 51.9 %all-to-all-start.11 = ((bf16[4,2,262144]{2,1,0:T(2,128)(2,1)}), bf16[4,2,262144]{2,1,0:T(2,128)(2,1)}, u32[]{:S(2)}, u32[]{:S(2)}) async-start(bf16[4,2,262144]{2,1,0:T(2,128)(2,1)} %reshape.386), calls=%async_computation.18 | async-start | bytes 8388608 | tf_op jit(solution)/shard_map/all_to_all | solution.py:92
  1028.8 151.7 %all-reduce.4.cloned.1.call-start = ((), (), s32[]{:S(2)}) async-start(), calls=%async_computation.32 | async-start | bytes 524288 | tf_op jit(solution)/shard_map/psum | solution.py:357
  (63 other events, 2722.1 us)
Sparse Core Ops, SparseCore 0:
  10.5 46.6 all-gather.8
  59.3 47.1 all-gather.6
  108.3 25.1 all-gather.10
  159.0 48.1 reduce-scatter.7
  210.7 45.3 all-gather.12
  269.5 48.0 all-gather.14
  561.3 34.6 reduce-scatter.13
  619.9 53.3 reduce-scatter.11
  677.9 45.2 all-gather.16
  749.1 26.4 reduce-scatter.19
  785.9 89.5 reduce-scatter.17
  877.6 49.9 reduce-scatter.15
  930.0 48.1 reduce-scatter.9
  1035.4 145.0 all-reduce.3

commit v2 on v1

--- a/solution.py
+++ b/solution.py
@@ -1,8 +1,11 @@
+import functools
 import math
 
 import jax
 import jax.numpy as jnp
 from jax import lax
+from jax.experimental import pallas as pl
+from jax.experimental.pallas import tpu as pltpu
 from jax.sharding import PartitionSpec as P
 
 HEAD_DIM = 128
@@ -44,6 +47,416 @@
     return inverse * (
         grad_unit - unit_values * jnp.mean(grad_unit * unit_values, -1, keepdims=True)
     )
+
+
+def greet_chain(chip, core, chips):
+    barrier = pltpu.get_barrier_semaphore()
+
+    def greet(target):
+        pl.semaphore_signal(barrier, inc=1, device_id={"seq": target})
+
+    greet(chip * 2 + 1 - core)
+
+    @pl.when(chip < chips - 1)
+    def _():
+        greet(chip * 2 + 2 + core)
+
+    @pl.when(chip > 0)
+    def _():
+        greet(chip * 2 - 2 + core)
+
+    inner = jnp.where(chip < chips - 1, 1, 0) + jnp.where(chip > 0, 1, 0)
+    pl.semaphore_wait(barrier, 1 + inner)
+
+
+def gather_kernel(chips, x_ref, out_ref, local_sem, up_sem, down_sem, side_sem, chain_sem, cross_sem):
+    me = lax.axis_index("seq")
+    chip, core = me // 2, lax.rem(me, 2)
+    rows = x_ref.shape[0]
+    greet_chain(chip, core, chips)
+
+    def block(source, source_core):
+        start = pl.multiple_of((source * 2 + source_core) * rows, rows)
+        return out_ref.at[pl.ds(start, rows)]
+
+    def hop(source, ref, target, sends, arrivals):
+        return pltpu.make_async_remote_copy(
+            src_ref=ref,
+            dst_ref=block(source, core),
+            send_sem=sends.at[source],
+            recv_sem=arrivals.at[source],
+            device_id={"seq": target},
+        )
+
+    def upward(source, ref):
+        return hop(source, ref, chip * 2 + 2 + core, up_sem, chain_sem)
+
+    def downward(source, ref):
+        return hop(source, ref, chip * 2 - 2 + core, down_sem, chain_sem)
+
+    def sideways(source, ref):
+        return hop(source, ref, chip * 2 + 1 - core, side_sem, cross_sem)
+
+    own = pltpu.make_async_copy(x_ref, block(chip, core), local_sem)
+
+    @pl.when(chip < chips - 1)
+    def _():
+        upward(chip, x_ref).start()
+
+    @pl.when(chip > 0)
+    def _():
+        downward(chip, x_ref).start()
+
+    sideways(chip, x_ref).start()
+    own.start()
+    for step in range(1, chips):
+        below, above = chip - step, chip + step
+
+        @pl.when(below >= 0)
+        def _():
+            landed = block(below, core)
+            upward(below, landed).wait_recv()
+
+            @pl.when(chip < chips - 1)
+            def _():
+                upward(below, landed).start()
+
+            sideways(below, landed).start()
+
+        @pl.when(above < chips)
+        def _():
+            landed = block(above, core)
+            downward(above, landed).wait_recv()
+
+            @pl.when(chip > 0)
+            def _():
+                downward(above, landed).start()
+
+            sideways(above, landed).start()
+
+    own.wait()
+    for source in range(chips):
+        sideways(source, block(source, core)).wait()
+
+        @pl.when((chip < chips - 1) & (source <= chip))
+        def _():
+            upward(source, block(source, core)).wait_send()
+
+        @pl.when((chip > 0) & (source >= chip))
+        def _():
+            downward(source, block(source, core)).wait_send()
+
+
+def seq_gather(x, size, which):
+    chips = size // 2
+    rows, width = x.shape
+    return pl.pallas_call(
+        functools.partial(gather_kernel, chips),
+        out_shape=jax.ShapeDtypeStruct((size * rows, width), x.dtype),
+        in_specs=[pl.BlockSpec(memory_space=pl.ANY)],
+        out_specs=pl.BlockSpec(memory_space=pl.ANY),
+        scratch_shapes=[pltpu.SemaphoreType.DMA] + [pltpu.SemaphoreType.DMA((chips,))] * 5,
+        compiler_params=pltpu.CompilerParams(collective_id=which, has_side_effects=True),
+        cost_estimate=pl.CostEstimate(
+            flops=0, bytes_accessed=40 * x.size * x.dtype.itemsize * chips, transcendentals=0
+        ),
+    )(x)
+
+
+def reduce_kernel(
+    chips,
+    shared,
+    turned,
+    a_ref,
+    b_ref,
+    o_ref,
+    side_out,
+    side_in,
+    chain_out,
+    chain_in,
+    total,
+    side_send,
+    side_recv,
+    chain_send,
+    chain_recv,
+):
+    me = lax.axis_index("seq")
+    chip, core = me // 2, lax.rem(me, 2)
+    rows, width = o_ref.shape
+    step_cols = min(512, width)
+    greet_chain(chip, core, chips)
+
+    def product(block, store):
+        left = a_ref[block]
+
+        @pl.loop(0, width // step_cols)
+        def _(index):
+            cols = pl.ds(pl.multiple_of(index * step_cols, step_cols), step_cols)
+            right_ref = b_ref if shared else b_ref.at[block]
+            if turned:
+                part = lax.dot_general(
+                    left,
+                    right_ref[cols, :],
+                    (((1,), (1,)), ((), ())),
+                    preferred_element_type=jnp.float32,
+                )
+            else:
+                part = jnp.dot(left, right_ref[:, cols], preferred_element_type=jnp.float32)
+            store(cols, part)
+
+    def side_copy(dest):
+        return pltpu.make_async_remote_copy(
+            src_ref=side_out.at[dest],
+            dst_ref=side_in.at[dest],
+            send_sem=side_send.at[dest],
+            recv_sem=side_recv.at[dest],
+            device_id={"seq": chip * 2 + 1 - core},
+        )
+
+    def chain_copy(way, dest, target):
+        return pltpu.make_async_remote_copy(
+            src_ref=chain_out.at[dest],
+            dst_ref=chain_in.at[way, dest],
+            send_sem=chain_send.at[dest],
+            recv_sem=chain_recv.at[way, dest],
+            device_id={"seq": target},
+        )
+
+    def place(index):
+        distance = chips - 1 - index // 2
+        sign = 1 - 2 * lax.rem(index, 2)
+        dest = chip + sign * distance
+        inside = (dest >= 0) & (dest < chips)
+        return dest, inside
+
+    @pl.loop(0, 2 * chips - 1)
+    def _(index):
+        dest, inside = place(index)
+
+        @pl.when(inside)
+        def _():
+            def store(cols, part):
+                side_out[dest, :, cols] = part.astype(side_out.dtype)
+
+            product(dest * 2 + 1 - core, store)
+            side_copy(dest).start()
+
+    @pl.loop(0, 2 * chips - 1)
+    def _(index):
+        dest, inside = place(index)
+
+        @pl.when(inside)
+        def _():
+            def store(cols, part):
+                total[:, cols] = part
+
+            product(dest * 2 + core, store)
+            side_copy(dest).wait_recv()
+            total[...] += side_in[dest].astype(jnp.float32)
+
+            @pl.when((dest >= chip) & (chip > 0))
+            def _():
+                chain_copy(0, dest, chip * 2 + 1 - core).wait_recv()
+                total[...] += chain_in[0, dest].astype(jnp.float32)
+
+            @pl.when((dest <= chip) & (chip < chips - 1))
+            def _():
+                chain_copy(1, dest, chip * 2 + 1 - core).wait_recv()
+                total[...] += chain_in[1, dest].astype(jnp.float32)
+
+            @pl.when(dest == chip)
+            def _():
+                o_ref[...] = total[...]
+
+            @pl.when(dest != chip)
+            def _():
+                chain_out[dest] = total[...].astype(chain_out.dtype)
+
+            @pl.when(dest > chip)
+            def _():
+                chain_copy(0, dest, chip * 2 + 2 + core).start()
+
+            @pl.when(dest < chip)
+            def _():
+                chain_copy(1, dest, chip * 2 - 2 + core).start()
+
+    @pl.loop(0, chips)
+    def _(dest):
+        side_copy(dest).wait_send()
+
+        @pl.when(dest != chip)
+        def _():
+            chain_copy(0, dest, chip * 2 + 1 - core).wait_send()
+
+
+def seq_reduce(a, b, width, turned, which):
+    size, rows, depth = a.shape
+    chips = size // 2
+    half = jnp.bfloat16
+    return pl.pallas_call(
+        functools.partial(reduce_kernel, chips, b.ndim == 2, turned),
+        out_shape=jax.ShapeDtypeStruct((rows, width), jnp.float32),
+        in_specs=[pl.BlockSpec(memory_space=pltpu.VMEM)] * 2,
+        out_specs=pl.BlockSpec(memory_space=pltpu.VMEM),
+        scratch_shapes=[
+            pltpu.VMEM((chips, rows, width), half),
+            pltpu.VMEM((chips, rows, width), half),
+            pltpu.VMEM((chips, rows, width), half),
+            pltpu.VMEM((2, chips, rows, width), half),
+            pltpu.VMEM((rows, width), jnp.float32),
+            pltpu.SemaphoreType.DMA((chips,)),
+            pltpu.SemaphoreType.DMA((chips,)),
+            pltpu.SemaphoreType.DMA((chips,)),
+            pltpu.SemaphoreType.DMA((2, chips)),
+        ],
+        compiler_params=pltpu.CompilerParams(
+            collective_id=which, has_side_effects=True, vmem_limit_bytes=56 * 2**20
+        ),
+        cost_estimate=pl.CostEstimate(
+            flops=2 * size * rows * depth * width,
+            bytes_accessed=40 * rows * width * size,
+            transcendentals=0,
+        ),
+    )(a, b)
+
+
+def swap_kernel(size, summed, x_ref, o_ref, landing, send_sem, recv_sem):
+    me = lax.axis_index("seq")
+    barrier = pltpu.get_barrier_semaphore()
+    for shift in range(1, size):
+        pl.semaphore_signal(barrier, inc=1, device_id={"seq": lax.rem(me + shift, size)})
+    pl.semaphore_wait(barrier, size - 1)
+
+    def copy(shift):
+        peer = lax.rem(me + shift, size)
+        return pltpu.make_async_remote_copy(
+            src_ref=x_ref if summed else x_ref.at[peer],
+            dst_ref=landing.at[me],
+            send_sem=send_sem.at[shift],
+            recv_sem=recv_sem.at[shift],
+            device_id={"seq": peer},
+        )
+
+    for shift in range(1, size):
+        copy(shift).start()
+    landing[me] = x_ref[...] if summed else x_ref[me]
+    for shift in range(1, size):
+        copy(shift).wait()
+    if summed:
+        o_ref[...] = jnp.sum(landing[...], 0)
+    else:
+        o_ref[...] = landing[...]
+
+
+def seq_swap(x, size, summed, which):
+    piece = x.shape if summed else x.shape[1:]
+    return pl.pallas_call(
+        functools.partial(swap_kernel, size, summed),
+        out_shape=jax.ShapeDtypeStruct(x.shape, x.dtype),
+        in_specs=[pl.BlockSpec(memory_space=pltpu.VMEM)],
+        out_specs=pl.BlockSpec(memory_space=pltpu.VMEM),
+        scratch_shapes=[
+            pltpu.VMEM((size, *piece), x.dtype),
+            pltpu.SemaphoreType.DMA((size,)),
+            pltpu.SemaphoreType.DMA((size,)),
+        ],
+        compiler_params=pltpu.CompilerParams(collective_id=which, has_side_effects=True),
+    )(x)
+
+
+def seq_sum(pair, size, which):
+    both = jnp.concatenate(pair).reshape(-1, 128)
+    return seq_swap(both, size, True, which).reshape(2, -1)
+
+
+def total_kernel(
+    size, split, x_ref, o_ref, first, second, final, send_one, recv_one, send_two, recv_two, send_three, recv_three
+):
+    me, mine = lax.axis_index("seq"), lax.axis_index("fsdp")
+    part = x_ref.shape[1] // size
+    barrier = pltpu.get_barrier_semaphore()
+    for shift in range(1, size):
+        pl.semaphore_signal(barrier, inc=1, device_id={"seq": lax.rem(me + shift, size)})
+    for shift in range(1, split):
+        pl.semaphore_signal(barrier, inc=1, device_id={"fsdp": lax.rem(mine + shift, split)})
+    pl.semaphore_wait(barrier, size + split - 2)
+
+    def columns(index):
+        return pl.ds(pl.multiple_of(index * part, part), part)
+
+    def scatter(shift):
+        peer = lax.rem(me + shift, size)
+        return pltpu.make_async_remote_copy(
+            src_ref=x_ref.at[:, columns(peer)],
+            dst_ref=first.at[me],
+            send_sem=send_one.at[shift],
+            recv_sem=recv_one.at[shift],
+            device_id={"seq": peer},
+        )
+
+    def share(shift):
+        return pltpu.make_async_remote_copy(
+            src_ref=second.at[mine],
+            dst_ref=second.at[mine],
+            send_sem=send_two.at[shift],
+            recv_sem=recv_two.at[shift],
+            device_id={"fsdp": lax.rem(mine + shift, split)},
+        )
+
+    def collect(shift):
+        return pltpu.make_async_remote_copy(
+            src_ref=final.at[me],
+            dst_ref=final.at[me],
+            send_sem=send_three.at[shift],
+            recv_sem=recv_three.at[shift],
+            device_id={"seq": lax.rem(me + shift, size)},
+        )
+
+    for shift in range(1, size):
+        scatter(shift).start()
+    first[me] = x_ref[:, columns(me)]
+    for shift in range(1, size):
+        scatter(shift).wait_recv()
+    second[mine] = jnp.sum(first[...], 0)
+    for shift in range(1, split):
+        share(shift).start()
+    for shift in range(1, split):
+        share(shift).wait_recv()
+    final[me] = jnp.sum(second[...], 0)
+    for shift in range(1, size):
+        collect(shift).start()
+    for shift in range(1, size):
+        scatter(shift).wait_send()
+    for shift in range(1, split):
+        share(shift).wait_send()
+    for shift in range(1, size):
+        collect(shift).wait()
+    for index in range(size):
+        o_ref[:, index * part : (index + 1) * part] = final[index]
+
+
+def total_sum(x, size, split, which):
+    rows, width = x.shape
+    part = width // size
+    kind = pltpu.SemaphoreType.DMA
+    return pl.pallas_call(
+        functools.partial(total_kernel, size, split),
+        out_shape=jax.ShapeDtypeStruct(x.shape, x.dtype),
+        in_specs=[pl.BlockSpec(memory_space=pltpu.VMEM)],
+        out_specs=pl.BlockSpec(memory_space=pltpu.VMEM),
+        scratch_shapes=[
+            pltpu.VMEM((size, rows, part), x.dtype),
+            pltpu.VMEM((split, rows, part), x.dtype),
+            pltpu.VMEM((size, rows, part), x.dtype),
+            kind((size,)),
+            kind((size,)),
+            kind((split,)),
+            kind((split,)),
+            kind((size,)),
+            kind((size,)),
+        ],
+        compiler_params=pltpu.CompilerParams(collective_id=which, has_side_effects=True),
+    )(x)
 
 
 def shards(
@@ -75,62 +488,91 @@
     seq_index = lax.axis_index("seq")
     column_start = seq_index * local_width
     experts_local = w_gate.shape[0]
+    seq_size = lax.axis_size("seq")
     split = lax.axis_size("fsdp")
     groups = split // experts_local
-    partners = None
-    if groups > 1:
-        partners = [
-            [group * experts_local + member for member in range(experts_local)]
-            for group in range(groups)
-        ]
+    shard_index = lax.axis_index("fsdp")
+    member = lax.rem(shard_index, experts_local)
+
+    def pick(stack, index):
+        return lax.dynamic_index_in_dim(stack, index, 0, keepdims=False)
 
     def to_owner(weight, dim):
-        spread = jnp.concatenate([weight] * groups, 0) if groups > 1 else weight
-        return lax.all_to_all(spread, "fsdp", split_axis=0, concat_axis=dim, tiled=True)[0]
+        pieces = []
+        for shift in range(split):
+            dest = lax.rem(shard_index + shift, split)
+            piece = pick(weight, lax.rem(dest, experts_local))
+            if shift:
+                links = [(one, (one + shift) % split) for one in range(split)]
+                piece = lax.ppermute(piece, "fsdp", links)
+            pieces.append(piece)
+        order = lax.rem(shard_index - jnp.arange(split) + split, split)
+        whole = jnp.stack(pieces)[order]
+        if dim == 0:
+            return whole.reshape(-1, whole.shape[2])
+        return whole.transpose(1, 0, 2).reshape(whole.shape[1], -1)
 
     def to_shards(grad, dim):
-        parts = lax.all_to_all(
-            grad.astype(half_type)[None], "fsdp", split_axis=dim, concat_axis=0, tiled=True
-        ).astype(float_type)
-        if groups > 1:
-            parts = parts.reshape(groups, experts_local, *parts.shape[1:]).sum(0)
-        return parts
-
-    def exchange(rows):
-        return lax.all_to_all(
-            rows, "fsdp", split_axis=0, concat_axis=0, tiled=True, axis_index_groups=partners
-        )
+        part = grad.shape[dim] // split
+        shape = [experts_local, *grad.shape]
+        shape[dim + 1] = part
+        owned = jnp.zeros(shape, float_type)
+        for shift in range(split):
+            dest = lax.rem(shard_index + shift, split)
+            piece = lax.dynamic_slice_in_dim(grad, dest * part, part, dim).astype(half_type)
+            if shift:
+                links = [(one, (one + shift) % split) for one in range(split)]
+                piece = lax.ppermute(piece, "fsdp", links)
+            expert = lax.rem(shard_index - shift + split, experts_local)
+            piece = piece.astype(float_type)
+            if groups > 1:
+                piece = piece + pick(owned, expert)
+            owned = lax.dynamic_update_index_in_dim(owned, piece, expert, 0)
+        return owned
+
+    def exchange(pieces, back):
+        moved = [pieces[0]]
+        for shift in range(1, experts_local):
+            turn = experts_local - shift if back else shift
+            links = [
+                (one, one - one % experts_local + (one + turn) % experts_local)
+                for one in range(split)
+            ]
+            moved.append(lax.ppermute(pieces[shift], "fsdp", links))
+        return moved
 
     qkv_cols = lax.all_gather(
         jnp.concatenate([w_query, w_key, w_value], 1), "fsdp", axis=0, tiled=True
     )
     out_rows = lax.all_gather(w_out, "fsdp", axis=1, tiled=True)
-    gate_full = to_owner(w_gate, 1)
-    up_full = to_owner(w_up, 1)
-    down_full = to_owner(w_down, 2)
+    gate_full = to_owner(w_gate, 0)
+    up_full = to_owner(w_up, 0)
+    down_full = to_owner(w_down, 1)
+    turned_ids = lax.rem(expert_ids - member + experts_local, experts_local)
+    turned_ids = turned_ids + expert_ids - lax.rem(expert_ids, experts_local)
     places = jnp.where(
-        expert_slots < capacity, expert_ids * capacity + expert_slots, -(10**6)
+        expert_slots < capacity, turned_ids * capacity + expert_slots, -(10**6)
     )
     both_seq = lax.all_gather(
         jnp.concatenate([expert_ids, places], 1), "seq", axis=0, tiled=True
     )
     ids_seq = both_seq[:, :top_count]
     places_seq = both_seq[:, top_count:]
-    cotangent_seq = lax.all_gather(cotangent, "seq", axis=0, tiled=True)
+    cotangent_seq = seq_gather(cotangent, seq_size, 0)
     gain_rows = norm_gains.astype(float_type)
     gain_cols = lax.dynamic_slice_in_dim(gain_rows, column_start, local_width, 1)
     inputs = tokens.astype(float_type)
     inverse_first = inverse_rms(inputs)
     unit_first = inputs * inverse_first
     normed = (unit_first * gain_rows[0]).astype(half_type)
-    normed_seq = lax.all_gather(normed, "seq", axis=0, tiled=True)
+    normed_seq = seq_gather(normed, seq_size, 0)
     length = normed_seq.shape[0]
     raw = jnp.dot(normed_seq, qkv_cols, preferred_element_type=float_type)
     query_raw = raw[:, :local_width]
     key_raw = raw[:, local_width : 2 * local_width]
     value_heads = raw[:, 2 * local_width :].astype(half_type)
-    square_sums = lax.psum(
-        (jnp.sum(query_raw * query_raw, -1), jnp.sum(key_raw * key_raw, -1)), "seq"
+    square_sums = seq_sum(
+        (jnp.sum(query_raw * query_raw, -1), jnp.sum(key_raw * key_raw, -1)), seq_size, 1
     )
     inverse_query = lax.rsqrt(square_sums[0] / model_width + EPSILON)[:, None]
     inverse_key = lax.rsqrt(square_sums[1] / model_width + EPSILON)[:, None]
@@ -174,18 +616,13 @@
 
     mixed_heads, log_sums = lax.map(attend, (query_cube, segment_blocks))
     attended_heads = mixed_heads.reshape(length, local_width)
-    projected = lax.psum_scatter(
-        jnp.dot(attended_heads, out_rows, preferred_element_type=float_type).astype(half_type),
-        "seq",
-        scatter_dimension=0,
-        tiled=True,
-    ).astype(float_type)
+    attended_blocks = attended_heads.reshape(seq_size, tok_rows, local_width)
+    projected = seq_reduce(attended_blocks, out_rows, model_width, False, 2)
     residual = inputs + projected
     inverse_second = inverse_rms(residual)
     unit_second = residual * inverse_second
     routed = (unit_second * gain_rows[1]).astype(half_type)
-    routed_seq = lax.all_gather(routed, "seq", axis=0, tiled=True)
-    seq_size = length // tok_rows
+    routed_seq = seq_gather(routed, seq_size, 0)
     slots = experts_local * capacity
 
     def gates_of(rows, ids):
@@ -204,45 +641,47 @@
     )
 
     def dispatch(rows):
-        placed = jnp.einsum(
-            "btc,btd->bcd",
-            onehot,
-            rows.reshape(seq_size, tok_rows, model_width),
-            preferred_element_type=float_type,
-        ).astype(half_type)
-        placed = placed.reshape(seq_size, experts_local, capacity, model_width)
-        return placed.transpose(1, 0, 2, 3)
-
-    def undispatch(rows):
-        rows = rows.reshape(experts_local, seq_size, capacity, model_width)
-        return rows.transpose(1, 0, 2, 3).reshape(seq_size, slots, model_width)
-
-    flat = experts_local * seq_size * capacity
-    expert_rows = exchange(dispatch(routed_seq)).reshape(flat, model_width)
-    upstream_slots = dispatch(cotangent_seq)
-    upstream_rows = exchange(upstream_slots).reshape(flat, model_width)
+        cube = rows.reshape(seq_size, tok_rows, model_width)
+        return [
+            jnp.einsum(
+                "btc,btd->bcd",
+                onehot[:, :, index * capacity : (index + 1) * capacity],
+                cube,
+                preferred_element_type=float_type,
+            )
+            .astype(half_type)
+            .reshape(seq_size * capacity, model_width)
+            for index in range(experts_local)
+        ]
+
+    def undispatch(pieces):
+        cubes = [piece.reshape(seq_size, capacity, model_width) for piece in pieces]
+        return jnp.concatenate(cubes, 1)
+
+    def parts_of(rows):
+        depth = rows.shape[0] // experts_local
+        return [rows[index * depth : (index + 1) * depth] for index in range(experts_local)]
+
+    expert_rows = jnp.concatenate(exchange(dispatch(routed_seq), False))
+    upstream_rows = jnp.concatenate(exchange(dispatch(cotangent_seq), False))
     slot_gates = jnp.sum(combine, 1).reshape(seq_size, experts_local, capacity).transpose(1, 0, 2)
-    row_gates = exchange(slot_gates).reshape(flat)
+    row_gates = jnp.concatenate(exchange(list(slot_gates.reshape(experts_local, -1)), False))
     gate_pre = jnp.dot(expert_rows, gate_full, preferred_element_type=float_type)
     up_pre = jnp.dot(expert_rows, up_full, preferred_element_type=float_type)
     gate_sigmoid = jax.nn.sigmoid(gate_pre)
     hidden = (gate_pre * gate_sigmoid * up_pre).astype(half_type)
     returned = jnp.dot(hidden, down_full, preferred_element_type=float_type).astype(half_type)
-    slot_dots = jnp.sum(
-        returned.astype(float_type) * upstream_rows.astype(float_type), -1
-    ).reshape(experts_local, seq_size, capacity)
-    slot_dots = exchange(slot_dots).transpose(1, 0, 2).reshape(seq_size, slots)
-    gate_grad_part = jnp.sum(jnp.where(hits, slot_dots[:, None, None, :], 0.0), -1)
-    gate_grad = lax.psum_scatter(
-        gate_grad_part.reshape(length, top_count), "seq", scatter_dimension=0, tiled=True
-    )
-    incoming = undispatch(exchange(returned.reshape(experts_local, seq_size, capacity, model_width)))
-    mixture_part = jnp.einsum(
-        "btc,bcd->btd", combine.astype(half_type), incoming, preferred_element_type=float_type
-    ).astype(half_type)
-    mixture = lax.psum_scatter(
-        mixture_part.reshape(length, model_width), "seq", scatter_dimension=0, tiled=True
-    ).astype(float_type)
+    row_dots = jnp.sum(returned.astype(float_type) * upstream_rows.astype(float_type), -1)
+    slot_dots = jnp.stack(exchange(parts_of(row_dots), True))
+    slot_dots = slot_dots.reshape(experts_local, seq_size, capacity).transpose(1, 0, 2)
+    slot_dots = slot_dots.reshape(seq_size, 1, slots)
+    padded = -(-slots // 128) * 128
+    slot_dots = jnp.pad(slot_dots, ((0, 0), (0, 7), (0, padded - slots)))
+    slot_dots = seq_swap(slot_dots, seq_size, False, 3)[:, 0, :slots].reshape(-1)
+    at_place = places[:, :, None] == jnp.arange(expert_total * capacity, dtype=jnp.int32)
+    gate_grad = jnp.sum(jnp.where(at_place, slot_dots, 0.0), -1)
+    incoming = undispatch(exchange(parts_of(returned), True))
+    mixture = seq_reduce(combine.astype(half_type), incoming, model_width, False, 4)
     output = (residual + mixture).astype(half_type)
     upstream = cotangent.astype(float_type)
     slot_grads = (row_gates[:, None] * upstream_rows.astype(float_type)).astype(half_type)
@@ -258,15 +697,8 @@
         rows_grad
         + jnp.einsum("rf,df->rd", up_pre_grad, up_full, preferred_element_type=float_type)
     ).astype(half_type)
-    sent_back = undispatch(
-        exchange(rows_grad.reshape(experts_local, seq_size, capacity, model_width))
-    )
-    expert_part = jnp.einsum(
-        "btc,bcd->btd", onehot, sent_back, preferred_element_type=float_type
-    ).astype(half_type)
-    routed_grad = lax.psum_scatter(
-        expert_part.reshape(length, model_width), "seq", scatter_dimension=0, tiled=True
-    ).astype(float_type)
+    sent_back = undispatch(exchange(parts_of(rows_grad), True))
+    routed_grad = seq_reduce(onehot, sent_back, model_width, False, 4)
     grad_down_full = jnp.einsum("rf,rd->fd", hidden, slot_grads, preferred_element_type=float_type)
     grad_gate_full = jnp.einsum(
         "rd,rf->df", expert_rows, gate_pre_grad, preferred_element_type=float_type
@@ -284,7 +716,7 @@
     gain_second_grad = jnp.sum(routed_grad * unit_second, axis=0)
     residual_grad = upstream + norm_back(routed_grad * gain_rows[1], unit_second, inverse_second)
     out_grad = residual_grad.astype(half_type)
-    out_grad_seq = lax.all_gather(out_grad, "seq", axis=0, tiled=True)
+    out_grad_seq = seq_gather(out_grad, seq_size, 0)
     grad_out_local = jnp.einsum(
         "th,td->hd", attended_heads, out_grad_seq, preferred_element_type=float_type
     )
@@ -333,8 +765,8 @@
     gain_key_grad = jnp.sum(key_unit_grad * unit_key, axis=0)
     query_scaled = query_unit_grad * gain_cols[2]
     key_scaled = key_unit_grad * gain_cols[3]
-    centers = lax.psum(
-        (jnp.sum(query_scaled * unit_query, -1), jnp.sum(key_scaled * unit_key, -1)), "seq"
+    centers = seq_sum(
+        (jnp.sum(query_scaled * unit_query, -1), jnp.sum(key_scaled * unit_key, -1)), seq_size, 1
     )
     query_raw_grad = (
         inverse_query * (query_scaled - unit_query * (centers[0] / model_width)[:, None])
@@ -343,19 +775,18 @@
         inverse_key * (key_scaled - unit_key * (centers[1] / model_width)[:, None])
     ).astype(half_type)
     raw_grads = jnp.concatenate([query_raw_grad, key_raw_grad, value_back], 1)
-    normed_part = jnp.einsum("th,dh->td", raw_grads, qkv_cols, preferred_element_type=float_type)
+    raw_blocks = raw_grads.reshape(seq_size, tok_rows, 3 * local_width)
+    normed_grad = seq_reduce(raw_blocks, qkv_cols, model_width, True, 5)
     grad_qkv_local = jnp.einsum("td,th->dh", normed_seq, raw_grads, preferred_element_type=float_type)
-    normed_grad = lax.psum_scatter(
-        normed_part.astype(jnp.bfloat16), "seq", scatter_dimension=0, tiled=True
-    ).astype(jnp.float32)
     gain_first_grad = jnp.sum(normed_grad * unit_first, axis=0)
     input_grad = residual_grad + norm_back(normed_grad * gain_rows[0], unit_first, inverse_first)
     zero_row = jnp.zeros((model_width,), float_type)
     gain_query_full = lax.dynamic_update_slice_in_dim(zero_row, gain_query_grad, column_start, 0)
     gain_key_full = lax.dynamic_update_slice_in_dim(zero_row, gain_key_grad, column_start, 0)
     gain_grads = jnp.stack([gain_first_grad, gain_second_grad, gain_query_full, gain_key_full])
-    router_grad = lax.psum(grad_router_local, ("fsdp", "seq")).T
-    gain_sums = lax.psum(gain_grads, ("fsdp", "seq"))
+    small = jnp.concatenate([gain_grads, jnp.zeros_like(gain_grads), grad_router_local])
+    small = total_sum(small, seq_size, split, 6)
+    gain_sums, router_grad = small[:4], small[8:].T
     qkv_owned = lax.psum_scatter(
         grad_qkv_local.astype(half_type), "fsdp", scatter_dimension=0, tiled=True
     ).astype(float_type)
@@ -371,9 +802,9 @@
         qkv_owned[:, 2 * local_width :],
         out_owned,
         router_grad,
-        to_shards(grad_gate_full, 1),
-        to_shards(grad_up_full, 1),
-        to_shards(grad_down_full, 2),
+        to_shards(grad_gate_full, 0),
+        to_shards(grad_up_full, 0),
+        to_shards(grad_down_full, 1),
     )
 
 

time: 1200 us -> 1030 us (0.86)
  Pallas kernels: 0 us -> 407 us
  waiting for transfers between devices: 479 us -> 188 us
  blocking collectives: 148 us -> 14.2 us
  local copies, waits for them, and re-layouts: 206 us -> 93.9 us
  other arithmetic: 135 us -> 87.2 us
  matrix products: 154 us -> 169 us
    pallas_call x0 -> x12, Pallas kernels: none -> 407 us  [the longest x4 194 us: seq_reduce(): pl.pallas_call(functools.partial(reduce_kernel, chips, b.ndim == 2, turne...]
    all_to_all x10 -> x0, waiting for transfers between devices: 219 us -> none  [the longest x5 147 us: exchange(): lax.all_to_all(rows, 'fsdp', split_axis=0, concat_axis=0, tiled=True, axi...]
    ppermute x0 -> x36, waiting for transfers between devices: none -> 188 us  [the longest x18 108 us: exchange(): moved.append(lax.ppermute(pieces[shift], 'fsdp', links))]
    reduce_scatter x5 -> x0, waiting for transfers between devices: 97.7 us -> none  [the longest x1 49.5 us: shards(): lax.psum_scatter(expert_part.reshape(length, model_width), 'seq', scatter...]
    all_gather x4 -> x0, waiting for transfers between devices: 94.7 us -> none  [the longest x1 49.4 us: shards(): normed_seq = lax.all_gather(normed, 'seq', axis=0, tiled=True)]
    unnamed x6 -> x3, other arithmetic: 78.4 us -> 0.36 us
    broadcast_in_dim x4 -> x2, local copies, waits for them, and re-layouts: 77.8 us -> 4.48 us  [the longest x1 4.47 us: to_shards(): owned = jnp.zeros(shape, float_type)]
    unnamed x130 -> x165, local copies, waits for them, and re-layouts: 83.4 us -> 10.6 us
  transfers between devices with their start and end apart: 24 -> 40, of which waited for: 14 -> 10; matrix products, arithmetic and copies ran while one was open for 34% -> 29% of each run, Pallas kernels for 0% -> 31%
where the time goes in v2:
time: 1030 us
  Pallas kernels  407 us (40%)
  waiting for transfers between devices  188 us (18%)
  matrix products  169 us (16%)
  local copies, waits for them, and re-layouts  93.9 us (9%)
  other arithmetic  87.2 us (8%)
  starting transfers between devices  49.8 us (5%)
  between operations  15.4 us (1%)
  blocking collectives  14.2 us (1%)
    pallas_call x4, Pallas kernels, seq_reduce(): pl.pallas_call(functools.partial(reduce_kernel, chips, b.ndim == 2, turne...  194 us
    pallas_call x4, Pallas kernels, seq_gather(): pl.pallas_call(functools.partial(gather_kernel, chips), out_shape=jax.Sha...  167 us
    ppermute x18, waiting for transfers between devices, exchange(): moved.append(lax.ppermute(pieces[shift], 'fsdp', links))  108 us
    ppermute x9, waiting for transfers between devices, to_shards(): piece = lax.ppermute(piece, 'fsdp', links)  66.1 us
    pallas_call x1, Pallas kernels, total_sum(): pl.pallas_call(functools.partial(total_kernel, size, split), out_shape=ja...  24.8 us
    ppermute x18, starting transfers between devices, exchange(): moved.append(lax.ppermute(pieces[shift], 'fsdp', links))  22.9 us
    dot_general x8, matrix products, dispatch(): jnp.einsum('btc,btd->bcd', onehot[:, :, index * capacity:(index + 1) * ca...  22.4 us
    pallas_call x3, Pallas kernels, seq_swap(): pl.pallas_call(functools.partial(swap_kernel, size, summed), out_shape=ja...  21.6 us
  transfers between devices with their start and end apart: 40, of which 10 were waited for; matrix products, arithmetic and copies ran while one was open for 29% of the time, Pallas kernels for 31%

profile of v2, /device:TPU:0, one launch (start us, length us, event | category | flops | bytes accessed | tf_op | source)
XLA Modules:
  0.0 1025.3 jit_solution(2365437986652388668)
XLA Ops:
  24.3 14.2 %all_gather.11 = s32[1024,16]{0,1:T(8,128)S(1)} all-gather(s32[128,16]{0,1:T(8,128)S(1)} %pad_add_fusion), channel_id=1, replica_groups=mesh['fsdp'=4,'seq'=8] {'seq'}, dimensions={0}, use_global_device_ids=true | all-gather | bytes 73728 | tf_op jit(solution)/shard_map/all_gather | solution.py:556
  40.3 43.1 %shard_map.226 = bf16[1024,2048]{1,0:T(8,128)(2,1)} custom-call(bf16[128,2048]{1,0:T(8,128)(2,1)} %x_ref.1), custom_call_target="tpu_custom_call" | custom-call | bytes 83886080 | tf_op jit(solution)/shard_map/pallas_call | solution.py:153
  115.0 43.0 %shard_map.221 = bf16[1024,2048]{1,0:T(8,128)(2,1)} custom-call(bf16[128,2048]{1,0:T(8,128)(2,1)} %fusion.50.x_ref), custom_call_target="tpu_custom_call" | custom-call | bytes 83886080 | tf_op jit(solution)/shard_map/pallas_call | solution.py:153
  237.9 14.4 %while.27 = (s32[]{:T(128)}, bf16[2,512,2,128]{3,2,1,0:T(2,128)(2,1)S(1)}, f32[2,2,512]{2,1,0:T(2,128)}, s32[2,512]{1,0:T(2,128)S(1)}, s32[1024]{0:T(1024)S(1)},...) while((s32[]{:T(128)}, ...), condition=%wide.region_6.7_spmd, body=%wide.region_3.6_spmd.sunk | while | flops 550108160 | bytes 16820340 | solution.py:617
  253.4 46.6 %shard_map.223 = f32[128,2048]{1,0:T(8,128)} custom-call(bf16[8,128,256]{2,1,0:T(8,128)(2,1)} %reshape_reshape.3.a_ref, bf16[256,2048]{1,0:T(8,128)(2,1)} %all-gather.5.cloned.1.call-done.b_ref), custom_call_target="tpu_custom_call" | custom-call | flops 1073741824 | bytes 83886080 | tf_op jit(solution)/shard_map/pallas_call | solution.py:296
  303.4 40.1 %shard_map.224 = bf16[1024,2048]{1,0:T(8,128)(2,1)} custom-call(bf16[128,2048]{1,0:T(8,128)(2,1)} %multiply_convert_fusion.6.x_ref), custom_call_target="tpu_custom_call" | custom-call | bytes 83886080 | tf_op jit(solution)/shard_map/pallas_call | solution.py:153
  363.8 46.8 %collective-permute-done.15 = f32[320]{0:T(512)S(1)} collective-permute-done((f32[320]{0:T(512)S(1)}, f32[320]{0:T(512)S(1)}, u32[]{:S(2)}, u32[]{:S(2)}) %collective-permute-start.15) | collective-permute-done | bytes 1312 | tf_op jit(solution)/shard_map/ppermute | solution.py:541
  418.0 11.9 %fusion.99 = f32[1280,1024]{1,0:T(8,128)} fusion(bf16[2048,1024]{1,0:T(8,128)(2,1)} %bitcast.299, bf16[320,2048]{1,0:T(8,128)(2,1)} %collective-permute-done.2, bf16[320,2048]{1,0:T(8,128)(2,1)} %collective-permute-done.1, bf16[320,2048]{1,0:T(8,128)(2,1)} %collective-permute-done, bf16[320,2048]{1,0:T(8,128)(2,1)S(1)} %bitcast.315), kind=kOutput, calls=%fused_computation.259 | convolution fusion | flops 5389680640 | bytes 14680064 | tf_op jit(solution)/shard_map/dot_general | solution.py:669
  430.0 10.6 %fusion.98 = f32[1280,1024]{1,0:T(8,128)} fusion(bf16[2048,1024]{1,0:T(8,128)(2,1)S(1)} %bitcast.303, bf16[320,2048]{1,0:T(8,128)(2,1)} %collective-permute-done.2, bf16[320,2048]{1,0:T(8,128)(2,1)} %collective-permute-done.1, bf16[320,2048]{1,0:T(8,128)(2,1)} %collective-permute-done, bf16[320,2048]{1,0:T(8,128)(2,1)} %bitcast.316), kind=kOutput, calls=%fused_computation.258 | convolution fusion | flops 5389680640 | bytes 14680064 | tf_op jit(solution)/shard_map/dot_general | solution.py:670
  446.0 26.8 %collective-permute-done.19 = bf16[320,2048]{1,0:T(8,128)(2,1)} collective-permute-done((bf16[320,2048]{1,0:T(8,128)(2,1)}, bf16[320,2048]{1,0:T(8,128)(2,1)}, u32[]{:S(2)}, u32[]{:S(2)}) %collective-permute-start.19) | collective-permute-done | bytes 1310752 | tf_op jit(solution)/shard_map/ppermute | solution.py:541
  473.9 15.2 %multiply_convert_fusion.1 = (bf16[1280,1024]{1,0:T(8,128)(2,1)}, bf16[1280,1024]{1,0:T(8,128)(2,1)}, bf16[1280,1024]{1,0:T(8,128)(2,1)}) fusion(f32[1280,1024]{1,0:T(8,128)} %fusion.99, f32[1280,1024]{1,0:T(8,128)} %fusion.98, bf16[1024,2048]{0,1:T(8,128)(2,1)S(1)} %bitcast.301, f32[1280]{0:T(1024)S(1)} %concatenate.67, ...), kind=kOutput, calls=%fused_computation.68 | convolution fusion | flops 5415895040 | bytes 27792384 | tf_op jit(solution)/shard_map/rd,fd->rf/dot_general | solution.py:688
  489.1 10.4 %fusion.111 = f32[1280,2048]{1,0:T(8,128)} fusion(bf16[1280,1024]{1,0:T(8,128)(2,1)} %get-tuple-element.333, bf16[2048,1024]{1,0:T(8,128)(2,1)S(1)} %bitcast.300), kind=kOutput, calls=%fused_computation.271 | convolution fusion | flops 5368709120 | bytes 17301504 | tf_op jit(solution)/shard_map/rf,df->rd/dot_general | solution.py:695
  514.0 8.6 fusion.40
  532.3 9.0 fusion.96
  545.6 23.1 %collective-permute-done.26 = f32[320]{0:T(512)S(1)} collective-permute-done((f32[320]{0:T(512)S(1)}, f32[320]{0:T(512)S(1)}, u32[]{:S(2)}, u32[]{:S(2)}) %collective-permute-start.26) | collective-permute-done | bytes 1312 | tf_op jit(solution)/shard_map/ppermute | solution.py:541
  593.2 47.7 %shard_map.227 = f32[128,2048]{1,0:T(8,128)} custom-call(bf16[8,128,160]{2,1,0:T(8,128)(2,1)} %copy.181.a_ref, bf16[8,160,2048]{2,1,0:T(8,128)(2,1)} %pad_maximum_fusion.3.b_ref), custom_call_target="tpu_custom_call" | custom-call | flops 671088640 | bytes 83886080 | tf_op jit(solution)/shard_map/pallas_call | solution.py:296
  657.5 48.4 %shard_map.225 = f32[128,2048]{1,0:T(8,128)} custom-call(bf16[8,128,160]{2,1,0:T(8,128)(2,1)} %copy.180.a_ref, bf16[8,160,2048]{2,1,0:T(8,128)(2,1)} %pad_maximum_fusion.1.b_ref), custom_call_target="tpu_custom_call" | custom-call | flops 671088640 | bytes 83886080 | tf_op jit(solution)/shard_map/pallas_call | solution.py:296
  709.0 40.4 %shard_map.229 = bf16[1024,2048]{1,0:T(8,128)(2,1)} custom-call(bf16[128,2048]{1,0:T(8,128)(2,1)} %get-tuple-element.324.x_ref), custom_call_target="tpu_custom_call" | custom-call | bytes 83886080 | tf_op jit(solution)/shard_map/pallas_call | solution.py:153
  753.9 31.1 %while.28 = (s32[]{:T(128)}, f32[1024,2,128]{0,2,1:T(8,128)}, f32[1024,2,128]{0,2,1:T(8,128)}, bf16[2,512,2,128]{3,1,0,2:T(8,128)(2,1)}, bf16[2,512,2,128]{3,1,2...) while((s32[]{:T(128)}, f32[1024,2,128]{0,2,1:T(8,128)}, ...), condition=%wide.region_21.22_spmd.clone, body=%wide.region_19.21_spmd.clone.sunk | while | flops 1360002048 | bytes 78944536 | solution.py:756
  857.3 16.4 %collective-permute-done.32 = bf16[512,1024]{1,0:T(8,128)(2,1)S(1)} collective-permute-done((bf16[512,1024]{1,0:T(8,128)(2,1)S(1)}, bf16[512,1024]{1,0:T(8,128)(2,1)S(1)}, u32[]{:S(2)}, u32[]{:S(2)}) %collective-permute-start.32) | collective-permute-done | bytes 1048608 | tf_op jit(solution)/shard_map/ppermute | solution.py:525
  874.1 31.5 %collective-permute-done.33 = bf16[1024,512]{1,0:T(8,128)(2,1)S(1)} collective-permute-done((bf16[1024,512]{1,0:T(8,128)(2,1)S(1)}, bf16[1024,512]{1,0:T(8,128)(2,1)S(1)}, u32[]{:S(2)}, u32[]{:S(2)}) %collective-permute-start.33) | collective-permute-done | bytes 1048608 | tf_op jit(solution)/shard_map/ppermute | solution.py:525
  908.8 18.2 %collective-permute-done.35 = bf16[1024,512]{1,0:T(8,128)(2,1)S(1)} collective-permute-done((bf16[1024,512]{1,0:T(8,128)(2,1)S(1)}, bf16[1024,512]{1,0:T(8,128)(2,1)S(1)}, u32[]{:S(2)}, u32[]{:S(2)}) %collective-permute-start.35) | collective-permute-done | bytes 1048608 | tf_op jit(solution)/shard_map/ppermute | solution.py:525
  930.4 51.5 %shard_map.231 = f32[128,2048]{1,0:T(8,128)} custom-call(bf16[8,128,768]{2,1,0:T(8,128)(2,1)} %bitcast.311, bf16[2048,768]{1,0:T(8,128)(2,1)} %all-gather.3.cloned.1.call-done.b_ref), custom_call_target="tpu_custom_call" | custom-call | flops 3221225472 | bytes 83886080 | tf_op jit(solution)/shard_map/pallas_call | solution.py:296
  985.1 24.8 %shard_map.232 = f32[40,2048]{1,0:T(8,128)} custom-call(f32[40,2048]{1,0:T(8,128)} %concatenate.76.x_ref), custom_call_target="tpu_custom_call" | custom-call | tf_op jit(solution)/shard_map/pallas_call | solution.py:442
  (450 shorter events, 381.4 us)
Async XLA Ops:
  7.2 195.2 %all-gather.3.cloned.1.call-start = ((), (), s32[]{:S(2)}) async-start(), calls=%async_computation.2 | async-start | bytes 3932160 | tf_op jit(solution)/shard_map/all_gather | solution.py:544
  9.4 244.0 %all-gather.5.cloned.1.call-start = ((), (), s32[]{:S(2)}) async-start(), calls=%async_computation.3 | async-start | bytes 1310720 | tf_op jit(solution)/shard_map/all_gather | solution.py:547
  13.6 86.3 %collective-permute-start.5 = (bf16[512,1024]{1,0:T(8,128)(2,1)}, bf16[512,1024]{1,0:T(8,128)(2,1)}, u32[]{:S(2)}, u32[]{:S(2)}) collective-permute-start(bf16[512,1024]{1,0:T(8,128)(2,1)} %get-tuple-element.358), channel_id=1, source_target_pairs={{0,24},{8,0},{16,8},{24,16},{1,25},{9,1},{17,9},{25,17},{2,26},{10... | collective-permute-start | bytes 3145736 | tf_op jit(solution)/shard_map/ppermute | solution.py:507
  17.5 84.2 %collective-permute-start.4 = (bf16[512,1024]{1,0:T(8,128)(2,1)}, bf16[512,1024]{1,0:T(8,128)(2,1)}, u32[]{:S(2)}, u32[]{:S(2)}) collective-permute-start(bf16[512,1024]{1,0:T(8,128)(2,1)} %get-tuple-element.359), channel_id=1, source_target_pairs={{0,16},{8,24},{16,0},{24,8},{1,17},{9,25},{17,1},{25,9},{2,18},{10... | collective-permute-start | bytes 3145736 | tf_op jit(solution)/shard_map/ppermute | solution.py:507
  18.0 86.6 %collective-permute-start.3 = (bf16[512,1024]{1,0:T(8,128)(2,1)}, bf16[512,1024]{1,0:T(8,128)(2,1)}, u32[]{:S(2)}, u32[]{:S(2)}) collective-permute-start(bf16[512,1024]{1,0:T(8,128)(2,1)} %get-tuple-element.357), channel_id=1, source_target_pairs={{0,8},{8,16},{16,24},{24,0},{1,9},{9,17},{17,25},{25,1},{2,10},{10... | collective-permute-start | bytes 3145736 | tf_op jit(solution)/shard_map/ppermute | solution.py:507
  20.3 91.2 %collective-permute-start.8 = (bf16[512,1024]{1,0:T(8,128)(2,1)}, bf16[512,1024]{1,0:T(8,128)(2,1)}, u32[]{:S(2)}, u32[]{:S(2)}) collective-permute-start(bf16[512,1024]{1,0:T(8,128)(2,1)} %get-tuple-element.362), channel_id=1, source_target_pairs={{0,24},{8,0},{16,8},{24,16},{1,25},{9,1},{17,9},{25,17},{2,26},{10... | collective-permute-start | bytes 3145736 | tf_op jit(solution)/shard_map/ppermute | solution.py:507
  22.7 148.3 %collective-permute-start.7 = (bf16[512,1024]{1,0:T(8,128)(2,1)}, bf16[512,1024]{1,0:T(8,128)(2,1)}, u32[]{:S(2)}, u32[]{:S(2)}) collective-permute-start(bf16[512,1024]{1,0:T(8,128)(2,1)} %get-tuple-element.363), channel_id=1, source_target_pairs={{0,16},{8,24},{16,0},{24,8},{1,17},{9,25},{17,1},{25,9},{2,18},{10... | collective-permute-start | bytes 3145736 | tf_op jit(solution)/shard_map/ppermute | solution.py:507
  24.2 990.3 %reduce-scatter.5.cloned.1.call-start = ((), (), s32[]{:S(2)}) async-start(), calls=%async_computation.5 | async-start | bytes 1310720 | tf_op jit(solution)/shard_map/reduce_scatter | solution.py:793
  99.9 71.1 %collective-permute-start.6 = (bf16[512,1024]{1,0:T(8,128)(2,1)}, bf16[512,1024]{1,0:T(8,128)(2,1)}, u32[]{:S(2)}, u32[]{:S(2)}) collective-permute-start(bf16[512,1024]{1,0:T(8,128)(2,1)} %get-tuple-element.361), channel_id=1, source_target_pairs={{0,8},{8,16},{16,24},{24,0},{1,9},{9,17},{17,25},{25,1},{2,10},{10... | collective-permute-start | bytes 3145736 | tf_op jit(solution)/shard_map/ppermute | solution.py:507
  101.6 78.0 %collective-permute-start.11 = (bf16[1024,512]{1,0:T(8,128)(2,1)}, bf16[1024,512]{1,0:T(8,128)(2,1)}, u32[]{:S(2)}, u32[]{:S(2)}) collective-permute-start(bf16[1024,512]{1,0:T(8,128)(2,1)} %get-tuple-element.354), channel_id=1, source_target_pairs={{0,24},{8,0},{16,8},{24,16},{1,25},{9,1},{17,9},{25,17},{2,26},{10... | collective-permute-start | bytes 3145736 | tf_op jit(solution)/shard_map/ppermute | solution.py:507
  104.5 75.1 %collective-permute-start.10 = (bf16[1024,512]{1,0:T(8,128)(2,1)}, bf16[1024,512]{1,0:T(8,128)(2,1)}, u32[]{:S(2)}, u32[]{:S(2)}) collective-permute-start(bf16[1024,512]{1,0:T(8,128)(2,1)} %get-tuple-element.355), channel_id=1, source_target_pairs={{0,16},{8,24},{16,0},{24,8},{1,17},{9,25},{17,1},{25,9},{2,18},{10... | collective-permute-start | bytes 3145736 | tf_op jit(solution)/shard_map/ppermute | solution.py:507
  111.6 75.9 %collective-permute-start.9 = (bf16[1024,512]{1,0:T(8,128)(2,1)}, bf16[1024,512]{1,0:T(8,128)(2,1)}, u32[]{:S(2)}, u32[]{:S(2)}) collective-permute-start(bf16[1024,512]{1,0:T(8,128)(2,1)} %get-tuple-element.353), channel_id=1, source_target_pairs={{0,8},{8,16},{16,24},{24,0},{1,9},{9,17},{17,25},{25,1},{2,10},{10... | collective-permute-start | bytes 3145736 | tf_op jit(solution)/shard_map/ppermute | solution.py:507
  510.1 73.2 %collective-permute-start.23 = (bf16[320,2048]{1,0:T(8,128)(2,1)}, bf16[320,2048]{1,0:T(8,128)(2,1)}, u32[]{:S(2)}, u32[]{:S(2)}) collective-permute-start(bf16[320,2048]{1,0:T(8,128)(2,1)} %get-tuple-element.336), channel_id=1, source_target_pairs={{0,8},{8,16},{16,24},{24,0},{1,9},{9,17},{17,25},{25,1},{2,10},{10... | collective-permute-start | bytes 3932168 | tf_op jit(solution)/shard_map/ppermute | solution.py:541
  510.4 76.2 %collective-permute-start.22 = (bf16[320,2048]{1,0:T(8,128)(2,1)}, bf16[320,2048]{1,0:T(8,128)(2,1)}, u32[]{:S(2)}, u32[]{:S(2)}) collective-permute-start(bf16[320,2048]{1,0:T(8,128)(2,1)} %get-tuple-element.337), channel_id=1, source_target_pairs={{0,16},{8,24},{16,0},{24,8},{1,17},{9,25},{17,1},{25,9},{2,18},{10... | collective-permute-start | bytes 3932168 | tf_op jit(solution)/shard_map/ppermute | solution.py:541
  511.9 74.7 %collective-permute-start.21 = (bf16[320,2048]{1,0:T(8,128)(2,1)}, bf16[320,2048]{1,0:T(8,128)(2,1)}, u32[]{:S(2)}, u32[]{:S(2)}) collective-permute-start(bf16[320,2048]{1,0:T(8,128)(2,1)} %get-tuple-element.338), channel_id=1, source_target_pairs={{0,24},{8,0},{16,8},{24,16},{1,25},{9,1},{17,9},{25,17},{2,26},{10... | collective-permute-start | bytes 3932168 | tf_op jit(solution)/shard_map/ppermute | solution.py:541
  572.3 71.0 %collective-permute-start.14 = (bf16[320,2048]{1,0:T(8,128)(2,1)}, bf16[320,2048]{1,0:T(8,128)(2,1)}, u32[]{:S(2)}, u32[]{:S(2)}) collective-permute-start(bf16[320,2048]{1,0:T(8,128)(2,1)} %get-tuple-element.340), channel_id=1, source_target_pairs={{0,8},{8,16},{16,24},{24,0},{1,9},{9,17},{17,25},{25,1},{2,10},{10... | collective-permute-start | bytes 3932168 | tf_op jit(solution)/shard_map/ppermute | solution.py:541
  572.7 79.2 %collective-permute-start.13 = (bf16[320,2048]{1,0:T(8,128)(2,1)}, bf16[320,2048]{1,0:T(8,128)(2,1)}, u32[]{:S(2)}, u32[]{:S(2)}) collective-permute-start(bf16[320,2048]{1,0:T(8,128)(2,1)} %get-tuple-element.341), channel_id=1, source_target_pairs={{0,16},{8,24},{16,0},{24,8},{1,17},{9,25},{17,1},{25,9},{2,18},{10... | collective-permute-start | bytes 3932168 | tf_op jit(solution)/shard_map/ppermute | solution.py:541
  586.5 255.8 %collective-permute-start.27 = (bf16[512,1024]{1,0:T(8,128)(2,1)}, bf16[512,1024]{1,0:T(8,128)(2,1)}, u32[]{:S(2)}, u32[]{:S(2)}) collective-permute-start(bf16[512,1024]{1,0:T(8,128)(2,1)} %get-tuple-element.351), channel_id=1, source_target_pairs={{0,8},{8,16},{16,24},{24,0},{1,9},{9,17},{17,25},{25,1},{2,10},{10... | collective-permute-start | bytes 3145736 | tf_op jit(solution)/shard_map/ppermute | solution.py:525
  586.6 262.5 %collective-permute-start.28 = (bf16[512,1024]{1,0:T(8,128)(2,1)}, bf16[512,1024]{1,0:T(8,128)(2,1)}, u32[]{:S(2)}, u32[]{:S(2)}) collective-permute-start(bf16[512,1024]{1,0:T(8,128)(2,1)} %get-tuple-element.350), channel_id=1, source_target_pairs={{0,16},{8,24},{16,0},{24,8},{1,17},{9,25},{17,1},{25,9},{2,18},{10... | collective-permute-start | bytes 3145736 | tf_op jit(solution)/shard_map/ppermute | solution.py:525
  643.3 212.6 %collective-permute-start.29 = (bf16[512,1024]{1,0:T(8,128)(2,1)}, bf16[512,1024]{1,0:T(8,128)(2,1)}, u32[]{:S(2)}, u32[]{:S(2)}) collective-permute-start(bf16[512,1024]{1,0:T(8,128)(2,1)} %get-tuple-element.349), channel_id=1, source_target_pairs={{0,24},{8,0},{16,8},{24,16},{1,25},{9,1},{17,9},{25,17},{2,26},{10... | collective-permute-start | bytes 3145736 | tf_op jit(solution)/shard_map/ppermute | solution.py:525
  651.9 195.6 %collective-permute-start.30 = (bf16[512,1024]{1,0:T(8,128)(2,1)}, bf16[512,1024]{1,0:T(8,128)(2,1)}, u32[]{:S(2)}, u32[]{:S(2)}) collective-permute-start(bf16[512,1024]{1,0:T(8,128)(2,1)} %get-tuple-element.348), channel_id=1, source_target_pairs={{0,8},{8,16},{16,24},{24,0},{1,9},{9,17},{17,25},{25,1},{2,10},{10... | collective-permute-start | bytes 3145736 | tf_op jit(solution)/shard_map/ppermute | solution.py:525
  651.9 199.2 %collective-permute-start.31 = (bf16[512,1024]{1,0:T(8,128)(2,1)}, bf16[512,1024]{1,0:T(8,128)(2,1)}, u32[]{:S(2)}, u32[]{:S(2)}) collective-permute-start(bf16[512,1024]{1,0:T(8,128)(2,1)} %get-tuple-element.347), channel_id=1, source_target_pairs={{0,16},{8,24},{16,0},{24,8},{1,17},{9,25},{17,1},{25,9},{2,18},{10... | collective-permute-start | bytes 3145736 | tf_op jit(solution)/shard_map/ppermute | solution.py:525
  794.6 221.7 %reduce-scatter.3.cloned.1.call-start = ((), (), s32[]{:S(2)}) async-start(), calls=%async_computation.4 | async-start | bytes 3932160 | tf_op jit(solution)/shard_map/reduce_scatter | solution.py:790
  851.2 75.8 %collective-permute-start.35 = (bf16[1024,512]{1,0:T(8,128)(2,1)S(1)}, bf16[1024,512]{1,0:T(8,128)(2,1)S(1)}, u32[]{:S(2)}, u32[]{:S(2)}) collective-permute-start(bf16[1024,512]{1,0:T(8,128)(2,1)S(1)} %get-tuple-element.343), channel_id=1, source_target_pairs={{0,24},{8,0},{16,8},{24,16},{1,25},{9,1},{17,9},{25,17},{2,26},{10... | collective-permute-start | bytes 3145736 | tf_op jit(solution)/shard_map/ppermute | solution.py:525
  (104 other events, 3071.6 us)
Sparse Core Ops, SparseCore 0:
  9.9 96.3 all-gather.2
  108.1 80.4 all-gather.4
  794.7 27.8 reduce-scatter.4
  825.7 78.2 reduce-scatter.2

commit v3 on v2

--- a/solution.py
+++ b/solution.py
@@ -69,82 +69,226 @@
     pl.semaphore_wait(barrier, 1 + inner)
 
 
-def gather_kernel(chips, x_ref, out_ref, local_sem, up_sem, down_sem, side_sem, chain_sem, cross_sem):
-    me = lax.axis_index("seq")
-    chip, core = me // 2, lax.rem(me, 2)
-    rows = x_ref.shape[0]
-    greet_chain(chip, core, chips)
-
-    def block(source, source_core):
-        start = pl.multiple_of((source * 2 + source_core) * rows, rows)
-        return out_ref.at[pl.ds(start, rows)]
-
-    def hop(source, ref, target, sends, arrivals):
+class ChainGather:
+    def __init__(self, chips, x_ref, out_ref, local_sem, sends, arrivals):
+        self.chips, self.x_ref, self.out_ref = chips, x_ref, out_ref
+        self.local_sem, self.sends, self.arrivals = local_sem, sends, arrivals
+        me = lax.axis_index("seq")
+        self.chip, self.core = me // 2, lax.rem(me, 2)
+        self.rows = x_ref.shape[0]
+
+    def block(self, source, core):
+        start = pl.multiple_of((source * 2 + core) * self.rows, self.rows)
+        return self.out_ref.at[pl.ds(start, self.rows)]
+
+    def hop(self, source, ref, target, way, lane):
         return pltpu.make_async_remote_copy(
             src_ref=ref,
-            dst_ref=block(source, core),
-            send_sem=sends.at[source],
-            recv_sem=arrivals.at[source],
+            dst_ref=self.block(source, self.core),
+            send_sem=self.sends.at[way, source],
+            recv_sem=self.arrivals.at[lane, source],
             device_id={"seq": target},
         )
 
-    def upward(source, ref):
-        return hop(source, ref, chip * 2 + 2 + core, up_sem, chain_sem)
-
-    def downward(source, ref):
-        return hop(source, ref, chip * 2 - 2 + core, down_sem, chain_sem)
-
-    def sideways(source, ref):
-        return hop(source, ref, chip * 2 + 1 - core, side_sem, cross_sem)
-
-    own = pltpu.make_async_copy(x_ref, block(chip, core), local_sem)
-
-    @pl.when(chip < chips - 1)
-    def _():
-        upward(chip, x_ref).start()
-
-    @pl.when(chip > 0)
-    def _():
-        downward(chip, x_ref).start()
-
-    sideways(chip, x_ref).start()
-    own.start()
-    for step in range(1, chips):
-        below, above = chip - step, chip + step
+    def upward(self, source, ref):
+        return self.hop(source, ref, self.chip * 2 + 2 + self.core, 0, 0)
+
+    def downward(self, source, ref):
+        return self.hop(source, ref, self.chip * 2 - 2 + self.core, 1, 0)
+
+    def sideways(self, source, ref):
+        return self.hop(source, ref, self.chip * 2 + 1 - self.core, 2, 1)
+
+    def own(self):
+        return pltpu.make_async_copy(
+            self.x_ref, self.block(self.chip, self.core), self.local_sem
+        )
+
+    def start(self):
+        @pl.when(self.chip < self.chips - 1)
+        def _():
+            self.upward(self.chip, self.x_ref).start()
+
+        @pl.when(self.chip > 0)
+        def _():
+            self.downward(self.chip, self.x_ref).start()
+
+        self.sideways(self.chip, self.x_ref).start()
+        self.own().start()
+
+    def step(self, distance):
+        below, above = self.chip - distance, self.chip + distance
 
         @pl.when(below >= 0)
         def _():
-            landed = block(below, core)
-            upward(below, landed).wait_recv()
-
-            @pl.when(chip < chips - 1)
+            landed = self.block(below, self.core)
+            self.upward(below, landed).wait_recv()
+
+            @pl.when(self.chip < self.chips - 1)
             def _():
-                upward(below, landed).start()
-
-            sideways(below, landed).start()
-
-        @pl.when(above < chips)
+                self.upward(below, landed).start()
+
+            self.sideways(below, landed).start()
+
+        @pl.when(above < self.chips)
         def _():
-            landed = block(above, core)
-            downward(above, landed).wait_recv()
-
-            @pl.when(chip > 0)
+            landed = self.block(above, self.core)
+            self.downward(above, landed).wait_recv()
+
+            @pl.when(self.chip > 0)
             def _():
-                downward(above, landed).start()
-
-            sideways(above, landed).start()
-
-    own.wait()
-    for source in range(chips):
-        sideways(source, block(source, core)).wait()
-
-        @pl.when((chip < chips - 1) & (source <= chip))
-        def _():
-            upward(source, block(source, core)).wait_send()
-
-        @pl.when((chip > 0) & (source >= chip))
-        def _():
-            downward(source, block(source, core)).wait_send()
+                self.downward(above, landed).start()
+
+            self.sideways(above, landed).start()
+
+    def steps(self):
+        for distance in range(1, self.chips):
+            self.step(distance)
+
+    def landed(self):
+        self.own().wait()
+        for source in range(self.chips):
+            self.sideways(source, self.block(source, self.core)).wait_recv()
+
+    def sent(self):
+        for source in range(self.chips):
+            ref = self.block(source, self.core)
+            self.sideways(source, ref).wait_send()
+
+            @pl.when((self.chip < self.chips - 1) & (source <= self.chip))
+            def _():
+                self.upward(source, ref).wait_send()
+
+            @pl.when((self.chip > 0) & (source >= self.chip))
+            def _():
+                self.downward(source, ref).wait_send()
+
+
+class ChainReduce:
+    def __init__(self, chips, rows, width, buffers):
+        (
+            self.side_out,
+            self.side_in,
+            self.chain_out,
+            self.chain_in,
+            self.total,
+            self.side_send,
+            self.side_recv,
+            self.chain_send,
+            self.chain_recv,
+        ) = buffers
+        self.chips = chips
+        me = lax.axis_index("seq")
+        self.chip, self.core = me // 2, lax.rem(me, 2)
+
+    @staticmethod
+    def scratch(chips, rows, width):
+        half = jnp.bfloat16
+        return [
+            pltpu.VMEM((chips, rows, width), half),
+            pltpu.VMEM((chips, rows, width), half),
+            pltpu.VMEM((chips, rows, width), half),
+            pltpu.VMEM((2, chips, rows, width), half),
+            pltpu.VMEM((rows, width), jnp.float32),
+            pltpu.SemaphoreType.DMA((chips,)),
+            pltpu.SemaphoreType.DMA((chips,)),
+            pltpu.SemaphoreType.DMA((chips,)),
+            pltpu.SemaphoreType.DMA((2, chips)),
+        ]
+
+    def side_copy(self, dest):
+        return pltpu.make_async_remote_copy(
+            src_ref=self.side_out.at[dest],
+            dst_ref=self.side_in.at[dest],
+            send_sem=self.side_send.at[dest],
+            recv_sem=self.side_recv.at[dest],
+            device_id={"seq": self.chip * 2 + 1 - self.core},
+        )
+
+    def chain_copy(self, way, dest, target):
+        return pltpu.make_async_remote_copy(
+            src_ref=self.chain_out.at[dest],
+            dst_ref=self.chain_in.at[way, dest],
+            send_sem=self.chain_send.at[dest],
+            recv_sem=self.chain_recv.at[way, dest],
+            device_id={"seq": target},
+        )
+
+    def place(self, index):
+        distance = self.chips - 1 - index // 2
+        dest = self.chip + (1 - 2 * lax.rem(index, 2)) * distance
+        return dest, (dest >= 0) & (dest < self.chips)
+
+    def run(self, product):
+        chips, chip, core, total = self.chips, self.chip, self.core, self.total
+        sibling = chip * 2 + 1 - core
+
+        @pl.loop(0, 2 * chips - 1)
+        def _(index):
+            dest, inside = self.place(index)
+
+            @pl.when(inside)
+            def _():
+                def store(cols, part):
+                    self.side_out[dest, :, cols] = part.astype(self.side_out.dtype)
+
+                product(dest * 2 + 1 - core, store)
+                self.side_copy(dest).start()
+
+        @pl.loop(0, 2 * chips - 1)
+        def _(index):
+            dest, inside = self.place(index)
+
+            @pl.when(inside)
+            def _():
+                def store(cols, part):
+                    total[:, cols] = part
+
+                product(dest * 2 + core, store)
+                self.side_copy(dest).wait_recv()
+                total[...] += self.side_in[dest].astype(jnp.float32)
+
+                @pl.when((dest >= chip) & (chip > 0))
+                def _():
+                    self.chain_copy(0, dest, sibling).wait_recv()
+                    total[...] += self.chain_in[0, dest].astype(jnp.float32)
+
+                @pl.when((dest <= chip) & (chip < chips - 1))
+                def _():
+                    self.chain_copy(1, dest, sibling).wait_recv()
+                    total[...] += self.chain_in[1, dest].astype(jnp.float32)
+
+                @pl.when(dest != chip)
+                def _():
+                    self.chain_out[dest] = total[...].astype(self.chain_out.dtype)
+
+                @pl.when(dest > chip)
+                def _():
+                    self.chain_copy(0, dest, chip * 2 + 2 + core).start()
+
+                @pl.when(dest < chip)
+                def _():
+                    self.chain_copy(1, dest, chip * 2 - 2 + core).start()
+
+    def sent(self):
+        sibling = self.chip * 2 + 1 - self.core
+
+        @pl.loop(0, self.chips)
+        def _(dest):
+            self.side_copy(dest).wait_send()
+
+            @pl.when(dest != self.chip)
+            def _():
+                self.chain_copy(0, dest, sibling).wait_send()
+
+
+def gather_kernel(chips, x_ref, out_ref, local_sem, sends, arrivals):
+    gather = ChainGather(chips, x_ref, out_ref, local_sem, sends, arrivals)
+    greet_chain(gather.chip, gather.core, chips)
+    gather.start()
+    gather.steps()
+    gather.landed()
+    gather.sent()
 
 
 def seq_gather(x, size, which):
@@ -155,7 +299,11 @@
         out_shape=jax.ShapeDtypeStruct((size * rows, width), x.dtype),
         in_specs=[pl.BlockSpec(memory_space=pl.ANY)],
         out_specs=pl.BlockSpec(memory_space=pl.ANY),
-        scratch_shapes=[pltpu.SemaphoreType.DMA] + [pltpu.SemaphoreType.DMA((chips,))] * 5,
+        scratch_shapes=[
+            pltpu.SemaphoreType.DMA,
+            pltpu.SemaphoreType.DMA((3, chips)),
+            pltpu.SemaphoreType.DMA((2, chips)),
+        ],
         compiler_params=pltpu.CompilerParams(collective_id=which, has_side_effects=True),
         cost_estimate=pl.CostEstimate(
             flops=0, bytes_accessed=40 * x.size * x.dtype.itemsize * chips, transcendentals=0
@@ -163,28 +311,11 @@
     )(x)
 
 
-def reduce_kernel(
-    chips,
-    shared,
-    turned,
-    a_ref,
-    b_ref,
-    o_ref,
-    side_out,
-    side_in,
-    chain_out,
-    chain_in,
-    total,
-    side_send,
-    side_recv,
-    chain_send,
-    chain_recv,
-):
-    me = lax.axis_index("seq")
-    chip, core = me // 2, lax.rem(me, 2)
+def reduce_kernel(chips, shared, turned, a_ref, b_ref, o_ref, *buffers):
     rows, width = o_ref.shape
     step_cols = min(512, width)
-    greet_chain(chip, core, chips)
+    reduce = ChainReduce(chips, rows, width, buffers)
+    greet_chain(reduce.chip, reduce.core, chips)
 
     def product(block, store):
         left = a_ref[block]
@@ -204,89 +335,9 @@
                 part = jnp.dot(left, right_ref[:, cols], preferred_element_type=jnp.float32)
             store(cols, part)
 
-    def side_copy(dest):
-        return pltpu.make_async_remote_copy(
-            src_ref=side_out.at[dest],
-            dst_ref=side_in.at[dest],
-            send_sem=side_send.at[dest],
-            recv_sem=side_recv.at[dest],
-            device_id={"seq": chip * 2 + 1 - core},
-        )
-
-    def chain_copy(way, dest, target):
-        return pltpu.make_async_remote_copy(
-            src_ref=chain_out.at[dest],
-            dst_ref=chain_in.at[way, dest],
-            send_sem=chain_send.at[dest],
-            recv_sem=chain_recv.at[way, dest],
-            device_id={"seq": target},
-        )
-
-    def place(index):
-        distance = chips - 1 - index // 2
-        sign = 1 - 2 * lax.rem(index, 2)
-        dest = chip + sign * distance
-        inside = (dest >= 0) & (dest < chips)
-        return dest, inside
-
-    @pl.loop(0, 2 * chips - 1)
-    def _(index):
-        dest, inside = place(index)
-
-        @pl.when(inside)
-        def _():
-            def store(cols, part):
-                side_out[dest, :, cols] = part.astype(side_out.dtype)
-
-            product(dest * 2 + 1 - core, store)
-            side_copy(dest).start()
-
-    @pl.loop(0, 2 * chips - 1)
-    def _(index):
-        dest, inside = place(index)
-
-        @pl.when(inside)
-        def _():
-            def store(cols, part):
-                total[:, cols] = part
-
-            product(dest * 2 + core, store)
-            side_copy(dest).wait_recv()
-            total[...] += side_in[dest].astype(jnp.float32)
-
-            @pl.when((dest >= chip) & (chip > 0))
-            def _():
-                chain_copy(0, dest, chip * 2 + 1 - core).wait_recv()
-                total[...] += chain_in[0, dest].astype(jnp.float32)
-
-            @pl.when((dest <= chip) & (chip < chips - 1))
-            def _():
-                chain_copy(1, dest, chip * 2 + 1 - core).wait_recv()
-                total[...] += chain_in[1, dest].astype(jnp.float32)
-
-            @pl.when(dest == chip)
-            def _():
-                o_ref[...] = total[...]
-
-            @pl.when(dest != chip)
-            def _():
-                chain_out[dest] = total[...].astype(chain_out.dtype)
-
-            @pl.when(dest > chip)
-            def _():
-                chain_copy(0, dest, chip * 2 + 2 + core).start()
-
-            @pl.when(dest < chip)
-            def _():
-                chain_copy(1, dest, chip * 2 - 2 + core).start()
-
-    @pl.loop(0, chips)
-    def _(dest):
-        side_copy(dest).wait_send()
-
-        @pl.when(dest != chip)
-        def _():
-            chain_copy(0, dest, chip * 2 + 1 - core).wait_send()
+    reduce.run(product)
+    o_ref[...] = reduce.total[...]
+    reduce.sent()
 
 
 def seq_reduce(a, b, width, turned, which):
@@ -298,17 +349,7 @@
         out_shape=jax.ShapeDtypeStruct((rows, width), jnp.float32),
         in_specs=[pl.BlockSpec(memory_space=pltpu.VMEM)] * 2,
         out_specs=pl.BlockSpec(memory_space=pltpu.VMEM),
-        scratch_shapes=[
-            pltpu.VMEM((chips, rows, width), half),
-            pltpu.VMEM((chips, rows, width), half),
-            pltpu.VMEM((chips, rows, width), half),
-            pltpu.VMEM((2, chips, rows, width), half),
-            pltpu.VMEM((rows, width), jnp.float32),
-            pltpu.SemaphoreType.DMA((chips,)),
-            pltpu.SemaphoreType.DMA((chips,)),
-            pltpu.SemaphoreType.DMA((chips,)),
-            pltpu.SemaphoreType.DMA((2, chips)),
-        ],
+        scratch_shapes=ChainReduce.scratch(chips, rows, width),
         compiler_params=pltpu.CompilerParams(
             collective_id=which, has_side_effects=True, vmem_limit_bytes=56 * 2**20
         ),
@@ -457,6 +498,396 @@
         ],
         compiler_params=pltpu.CompilerParams(collective_id=which, has_side_effects=True),
     )(x)
+
+def greet_all(size, split):
+    me, mine = lax.axis_index("seq"), lax.axis_index("fsdp")
+    barrier = pltpu.get_barrier_semaphore()
+    for shift in range(1, size):
+        pl.semaphore_signal(barrier, inc=1, device_id={"seq": lax.rem(me + shift, size)})
+    for shift in range(1, split):
+        pl.semaphore_signal(barrier, inc=1, device_id={"fsdp": lax.rem(mine + shift, split)})
+    pl.semaphore_wait(barrier, size + split - 2)
+
+
+def turned_halves(head):
+    return pltpu.roll(head, head.shape[-1] // 2, 1)
+
+
+def row_sums(values, pick):
+    return lax.dot_general(
+        pick, values, (((1,), (1,)), ((), ())), precision=HIGHEST, preferred_element_type=jnp.float32
+    )
+
+
+def column_of(row_form, pick):
+    return lax.dot_general(
+        row_form, pick, (((0,), (0,)), ((), ())), precision=HIGHEST, preferred_element_type=jnp.float32
+    )
+
+
+def front_kernel(
+    sizes,
+    tokens_ref,
+    gains_ref,
+    gain_cols_ref,
+    cos_ref,
+    sin_ref,
+    seg_col_ref,
+    seg_row_ref,
+    cotangent_ref,
+    wq_ref,
+    wk_ref,
+    wv_ref,
+    wo_ref,
+    w_gate_ref,
+    w_up_ref,
+    w_down_ref,
+    choice_ref,
+    normed_out,
+    qkv_out,
+    rows_out,
+    q_ref,
+    k_ref,
+    v_ref,
+    unit_ref,
+    sums_ref,
+    log_ref,
+    attended_ref,
+    residual_ref,
+    routed_out,
+    cotangent_out,
+    gate_full,
+    up_full,
+    down_full,
+    choices,
+    normed,
+    qkv,
+    rows_full,
+    routed_own,
+    raw,
+    sums_own,
+    sums_in,
+    gather_local,
+    gather_send,
+    gather_recv,
+    sums_send,
+    sums_recv,
+    choice_send,
+    choice_recv,
+    shard_local,
+    shard_send,
+    shard_recv,
+    expert_local,
+    expert_send,
+    expert_recv,
+    out_sem,
+    *reduce_buffers,
+):
+    size, split, chips, experts_local = sizes
+    f32, half = jnp.float32, jnp.bfloat16
+    me, mine = lax.axis_index("seq"), lax.axis_index("fsdp")
+    tok_rows, model_width = tokens_ref.shape
+    length, local_width = q_ref.shape
+    part = model_width // split
+    head = HEAD_DIM
+    heads = local_width // head
+
+    inputs = tokens_ref[...].astype(f32)
+    inverse = lax.rsqrt(jnp.mean(inputs * inputs, -1, keepdims=True) + EPSILON)
+    own_rows = pl.ds(pl.multiple_of(me * tok_rows, tok_rows), tok_rows)
+    routed_own[...] = (inputs * inverse * gains_ref[0:1, :]).astype(half)
+    greet_all(size, split)
+
+    def gather(index, x_ref, out_ref):
+        return ChainGather(
+            chips,
+            x_ref,
+            out_ref,
+            gather_local.at[index],
+            gather_send.at[index],
+            gather_recv.at[index],
+        )
+
+    first = gather(0, routed_own, normed)
+    first.start()
+
+    def choice_copy(shift):
+        return pltpu.make_async_remote_copy(
+            src_ref=choice_ref,
+            dst_ref=choices.at[me],
+            send_sem=choice_send.at[shift],
+            recv_sem=choice_recv.at[shift],
+            device_id={"seq": lax.rem(me + shift, size)},
+        )
+
+    own_part = pl.ds(pl.multiple_of(mine * part, part), part)
+    shard_pairs = (
+        (wq_ref, qkv.at[0, own_part]),
+        (wk_ref, qkv.at[1, own_part]),
+        (wv_ref, qkv.at[2, own_part]),
+        (wo_ref, rows_full.at[mine]),
+    )
+
+    def shard_copy(index, shift):
+        source, target = shard_pairs[index]
+        return pltpu.make_async_remote_copy(
+            src_ref=source,
+            dst_ref=target,
+            send_sem=shard_send.at[index, shift],
+            recv_sem=shard_recv.at[index, shift],
+            device_id={"fsdp": lax.rem(mine + shift, split)},
+        )
+
+    def shard_own(index):
+        source, target = shard_pairs[index]
+        return pltpu.make_async_copy(source, target, shard_local.at[index])
+
+    for index in range(4):
+        for shift in range(1, split):
+            shard_copy(index, shift).start()
+        shard_own(index).start()
+
+    def expert_pair(index, dest):
+        expert = lax.rem(dest, experts_local)
+        if index == 2:
+            return w_down_ref.at[expert], down_full.at[:, own_part]
+        source, target = ((w_gate_ref, gate_full), (w_up_ref, up_full))[index]
+        return source.at[expert], target.at[own_part]
+
+    def expert_copy(index, shift):
+        dest = lax.rem(mine + shift, split)
+        source, target = expert_pair(index, dest)
+        return pltpu.make_async_remote_copy(
+            src_ref=source,
+            dst_ref=target,
+            send_sem=expert_send.at[index, shift],
+            recv_sem=expert_recv.at[index, shift],
+            device_id={"fsdp": dest},
+        )
+
+    def expert_own(index):
+        source, target = expert_pair(index, mine)
+        return pltpu.make_async_copy(source, target, expert_local.at[index])
+
+    first.steps()
+    for index in range(4):
+        shard_own(index).wait()
+        for shift in range(1, split):
+            shard_copy(index, shift).wait_recv()
+    for index in range(3):
+        for shift in range(1, split):
+            expert_copy(index, shift).start()
+        expert_own(index).start()
+    first.landed()
+    for shift in range(1, size):
+        choice_copy(shift).start()
+    choices[me] = choice_ref[...]
+    second = gather(1, cotangent_ref, cotangent_out)
+    second.start()
+    keeps = [
+        pltpu.make_async_copy(normed, normed_out, out_sem.at[0]),
+        pltpu.make_async_copy(qkv, qkv_out, out_sem.at[1]),
+        pltpu.make_async_copy(rows_full, rows_out, out_sem.at[2]),
+    ]
+    for keep in keeps:
+        keep.start()
+
+    block = min(512, length)
+    lanes = lax.broadcasted_iota(jnp.int32, (8, local_width), 0)
+    first_row, second_row = (lanes == 0).astype(f32), (lanes == 1).astype(f32)
+
+    @pl.loop(0, length // block)
+    def _(step):
+        rows = pl.ds(pl.multiple_of(step * block, block), block)
+        left = normed[rows, :]
+        query = jnp.dot(left, qkv[0], preferred_element_type=f32)
+        raw[0, rows, :] = query
+        keys = jnp.dot(left, qkv[1], preferred_element_type=f32)
+        raw[1, rows, :] = keys
+        sums_own[:, rows] = row_sums(query * query, first_row) + row_sums(keys * keys, second_row)
+        v_ref[rows, :] = jnp.dot(left, qkv[2], preferred_element_type=f32).astype(half)
+
+    def sums_copy(shift):
+        return pltpu.make_async_remote_copy(
+            src_ref=sums_own,
+            dst_ref=sums_in.at[me],
+            send_sem=sums_send.at[shift],
+            recv_sem=sums_recv.at[shift],
+            device_id={"seq": lax.rem(me + shift, size)},
+        )
+
+    for shift in range(1, size):
+        sums_copy(shift).start()
+    sums_in[me] = sums_own[...]
+    for shift in range(1, size):
+        sums_copy(shift).wait()
+    sums_ref[...] = jnp.sum(sums_in[...], 0)
+
+    @pl.loop(0, length // block)
+    def _(step):
+        rows = pl.ds(pl.multiple_of(step * block, block), block)
+        square_sums = sums_ref[:, rows]
+        for index, pick, target in ((0, first_row, q_ref), (1, second_row, k_ref)):
+            scale = lax.rsqrt(column_of(square_sums, pick) / model_width + EPSILON)
+            unit = raw[index, rows, :] * scale
+            unit_ref[index, rows, :] = unit
+            scaled = unit * gain_cols_ref[2 + index : 3 + index, :]
+            for number in range(heads):
+                cols = slice(number * head, (number + 1) * head)
+                piece = scaled[:, cols]
+                target[rows, cols] = (
+                    piece * cos_ref[rows, :] + turned_halves(piece) * sin_ref[rows, :]
+                ).astype(half)
+
+    second.step(1)
+
+    wide = min(256, length)
+    for number in range(heads):
+        cols = slice(number * head, (number + 1) * head)
+
+        @pl.loop(0, length // wide)
+        def _(step):
+            rows = pl.ds(pl.multiple_of(step * wide, wide), wide)
+            scores = lax.dot_general(
+                q_ref[rows, cols],
+                k_ref[:, cols],
+                (((1,), (1,)), ((), ())),
+                preferred_element_type=f32,
+            )
+            scores = scores * (head**-0.5)
+            scores = jnp.where(seg_col_ref[rows, :] == seg_row_ref[...], scores, MASKED)
+            peak = jnp.max(scores, -1, keepdims=True)
+            grown = jnp.exp(scores - peak)
+            weight = jnp.sum(grown, -1, keepdims=True)
+            probs = (grown * (1.0 / weight)).astype(half)
+            attended_ref[rows, cols] = jnp.dot(
+                probs, v_ref[:, cols], preferred_element_type=f32
+            ).astype(half)
+            log_ref[rows, cols] = jnp.broadcast_to(peak + jnp.log(weight), (wide, head))
+
+        if number + 2 < chips:
+            second.step(number + 2)
+
+    for distance in range(heads + 2, chips):
+        second.step(distance)
+
+    reduce = ChainReduce(chips, tok_rows, model_width, reduce_buffers)
+
+    def product(index, store):
+        left = attended_ref[pl.ds(pl.multiple_of(index * tok_rows, tok_rows), tok_rows), :]
+        for piece in range(split):
+            cols = pl.ds(piece * part, part)
+            store(cols, jnp.dot(left, rows_full[piece], preferred_element_type=f32))
+
+    reduce.run(product)
+    residual = tokens_ref[...].astype(f32) + reduce.total[...]
+    residual_ref[...] = residual
+    inverse = lax.rsqrt(jnp.mean(residual * residual, -1, keepdims=True) + EPSILON)
+    first.sent()
+    routed_own[...] = (residual * inverse * gains_ref[1:2, :]).astype(half)
+    third = gather(2, routed_own, routed_out)
+    third.start()
+    third.steps()
+    third.landed()
+
+    second.landed()
+    reduce.sent()
+    second.sent()
+    third.sent()
+    for index in range(4):
+        for shift in range(1, split):
+            shard_copy(index, shift).wait_send()
+    for shift in range(1, size):
+        choice_copy(shift).wait()
+    for keep in keeps:
+        keep.wait()
+    for index in range(3):
+        expert_own(index).wait()
+        for shift in range(1, split):
+            expert_copy(index, shift).wait()
+
+
+def front(
+    sizes, tokens, gain_rows, gain_cols, cos, sin, segment_ids, cotangent, weights, choice, which
+):
+    size, split, chips, experts_local = sizes
+    w_query, w_key, w_value, w_out, w_gate, w_up, w_down = weights
+    tok_rows, model_width = tokens.shape
+    length = size * tok_rows
+    local_width = w_query.shape[1]
+    hidden_width = w_gate.shape[2]
+    f32, half = jnp.float32, jnp.bfloat16
+    vmem = pl.BlockSpec(memory_space=pltpu.VMEM)
+    anywhere = pl.BlockSpec(memory_space=pl.ANY)
+    kind = pltpu.SemaphoreType.DMA
+    shape = jax.ShapeDtypeStruct
+    return pl.pallas_call(
+        functools.partial(front_kernel, sizes),
+        out_shape=(
+            shape((length, model_width), half),
+            shape((3, model_width, local_width), half),
+            shape((split, *w_out.shape), half),
+            shape((length, local_width), half),
+            shape((length, local_width), half),
+            shape((length, local_width), half),
+            shape((2, length, local_width), f32),
+            shape((8, length), f32),
+            shape((length, local_width), f32),
+            shape((length, local_width), half),
+            shape((tok_rows, model_width), f32),
+            shape((length, model_width), half),
+            shape((length, model_width), half),
+            shape((model_width, hidden_width), half),
+            shape((model_width, hidden_width), half),
+            shape((hidden_width, model_width), half),
+            shape((size, *choice.shape), choice.dtype),
+        ),
+        in_specs=[vmem] * 7 + [anywhere] * 8 + [vmem],
+        out_specs=tuple([anywhere] * 3 + [vmem] * 8 + [anywhere] * 5 + [vmem]),
+        scratch_shapes=[
+            pltpu.VMEM((length, model_width), half),
+            pltpu.VMEM((3, model_width, local_width), half),
+            pltpu.VMEM((split, *w_out.shape), half),
+            pltpu.VMEM((tok_rows, model_width), half),
+            pltpu.VMEM((2, length, local_width), f32),
+            pltpu.VMEM((8, length), f32),
+            pltpu.VMEM((size, 8, length), f32),
+            kind((3,)),
+            kind((3, 3, chips)),
+            kind((3, 2, chips)),
+            kind((size,)),
+            kind((size,)),
+            kind((size,)),
+            kind((size,)),
+            kind((4,)),
+            kind((4, split)),
+            kind((4, split)),
+            kind((3,)),
+            kind((3, split)),
+            kind((3, split)),
+            kind((3,)),
+            *ChainReduce.scratch(chips, tok_rows, model_width),
+        ],
+        compiler_params=pltpu.CompilerParams(
+            collective_id=which, has_side_effects=True, vmem_limit_bytes=58 * 2**20
+        ),
+        cost_estimate=pl.CostEstimate(
+            flops=2 * length * model_width * local_width * 4,
+            bytes_accessed=500 * 2**20,
+            transcendentals=0,
+        ),
+    )(
+        tokens,
+        gain_rows,
+        gain_cols,
+        cos,
+        sin,
+        segment_ids.reshape(-1, 1),
+        segment_ids.reshape(1, -1),
+        cotangent,
+        *weights,
+        choice,
+    )
 
 
 def shards(
@@ -497,21 +928,6 @@
     def pick(stack, index):
         return lax.dynamic_index_in_dim(stack, index, 0, keepdims=False)
 
-    def to_owner(weight, dim):
-        pieces = []
-        for shift in range(split):
-            dest = lax.rem(shard_index + shift, split)
-            piece = pick(weight, lax.rem(dest, experts_local))
-            if shift:
-                links = [(one, (one + shift) % split) for one in range(split)]
-                piece = lax.ppermute(piece, "fsdp", links)
-            pieces.append(piece)
-        order = lax.rem(shard_index - jnp.arange(split) + split, split)
-        whole = jnp.stack(pieces)[order]
-        if dim == 0:
-            return whole.reshape(-1, whole.shape[2])
-        return whole.transpose(1, 0, 2).reshape(whole.shape[1], -1)
-
     def to_shards(grad, dim):
         part = grad.shape[dim] // split
         shape = [experts_local, *grad.shape]
@@ -541,51 +957,60 @@
             moved.append(lax.ppermute(pieces[shift], "fsdp", links))
         return moved
 
-    qkv_cols = lax.all_gather(
-        jnp.concatenate([w_query, w_key, w_value], 1), "fsdp", axis=0, tiled=True
-    )
-    out_rows = lax.all_gather(w_out, "fsdp", axis=1, tiled=True)
-    gate_full = to_owner(w_gate, 0)
-    up_full = to_owner(w_up, 0)
-    down_full = to_owner(w_down, 1)
     turned_ids = lax.rem(expert_ids - member + experts_local, experts_local)
     turned_ids = turned_ids + expert_ids - lax.rem(expert_ids, experts_local)
     places = jnp.where(
         expert_slots < capacity, turned_ids * capacity + expert_slots, -(10**6)
     )
-    both_seq = lax.all_gather(
-        jnp.concatenate([expert_ids, places], 1), "seq", axis=0, tiled=True
-    )
-    ids_seq = both_seq[:, :top_count]
-    places_seq = both_seq[:, top_count:]
-    cotangent_seq = seq_gather(cotangent, seq_size, 0)
     gain_rows = norm_gains.astype(float_type)
     gain_cols = lax.dynamic_slice_in_dim(gain_rows, column_start, local_width, 1)
     inputs = tokens.astype(float_type)
     inverse_first = inverse_rms(inputs)
     unit_first = inputs * inverse_first
-    normed = (unit_first * gain_rows[0]).astype(half_type)
-    normed_seq = seq_gather(normed, seq_size, 0)
-    length = normed_seq.shape[0]
-    raw = jnp.dot(normed_seq, qkv_cols, preferred_element_type=float_type)
-    query_raw = raw[:, :local_width]
-    key_raw = raw[:, local_width : 2 * local_width]
-    value_heads = raw[:, 2 * local_width :].astype(half_type)
-    square_sums = seq_sum(
-        (jnp.sum(query_raw * query_raw, -1), jnp.sum(key_raw * key_raw, -1)), seq_size, 1
-    )
+    length = seq_size * tok_rows
+    positions = jnp.arange(length, dtype=jnp.int32)
+    cosine_table, sine_table = rope_tables(positions, head_size)
+    cosine_wide = jnp.concatenate([cosine_table, cosine_table], 1)
+    sine_wide = jnp.concatenate([-sine_table, sine_table], 1)
+    (
+        normed_seq,
+        qkv_stack,
+        out_stack,
+        query_heads,
+        key_heads,
+        value_heads,
+        unit_pair,
+        square_sums,
+        log_wide,
+        attended_heads,
+        residual,
+        routed_seq,
+        cotangent_seq,
+        gate_full,
+        up_full,
+        down_full,
+        choices,
+    ) = front(
+        (seq_size, split, seq_size // 2, experts_local),
+        tokens,
+        gain_rows,
+        gain_cols,
+        cosine_wide,
+        sine_wide,
+        segment_ids,
+        cotangent,
+        (w_query, w_key, w_value, w_out, w_gate, w_up, w_down),
+        jnp.concatenate([expert_ids, places], 1).T,
+        0,
+    )
+    both_seq = choices.transpose(0, 2, 1).reshape(length, 2 * top_count)
+    ids_seq = both_seq[:, :top_count]
+    places_seq = both_seq[:, top_count:]
+    unit_query, unit_key = unit_pair[0], unit_pair[1]
     inverse_query = lax.rsqrt(square_sums[0] / model_width + EPSILON)[:, None]
     inverse_key = lax.rsqrt(square_sums[1] / model_width + EPSILON)[:, None]
-    positions = jnp.arange(length, dtype=jnp.int32)
-    cosine_table, sine_table = rope_tables(positions, head_size)
-    unit_query = query_raw * inverse_query
-    unit_key = key_raw * inverse_key
-    query_heads = rotate(unit_query * gain_cols[2], cosine_table, sine_table, head_size).astype(
-        half_type
-    )
-    key_heads = rotate(unit_key * gain_cols[3], cosine_table, sine_table, head_size).astype(
-        half_type
-    )
+    qkv_cols = jnp.concatenate([qkv_stack[0], qkv_stack[1], qkv_stack[2]], 1)
+    out_rows = out_stack.transpose(1, 0, 2).reshape(local_width, model_width)
     block_rows = math.gcd(512, length)
     blocks = length // block_rows
     score_scale = head_size ** (-0.5)
@@ -593,6 +1018,8 @@
     key_cube = key_heads.reshape(length, heads_local, head_size)
     value_cube = value_heads.reshape(length, heads_local, head_size)
     segment_blocks = segment_ids.reshape(blocks, block_rows)
+    log_sums = log_wide.reshape(blocks, block_rows, heads_local, head_size)[..., 0]
+    log_sums = log_sums.transpose(0, 2, 1)
 
     def block_scores(query_block, segment_block):
         scores = (
@@ -602,27 +1029,9 @@
         visible = segment_block[:, None] == segment_ids[None, :]
         return jnp.where(visible[None], scores, MASKED)
 
-    def attend(block_pair):
-        query_block, segment_block = block_pair
-        scores = block_scores(query_block, segment_block)
-        row_peak = jnp.max(scores, -1, keepdims=True)
-        exp_scores = jnp.exp(scores - row_peak)
-        exp_total = jnp.sum(exp_scores, -1, keepdims=True)
-        weights_soft = (exp_scores / exp_total).astype(half_type)
-        mixed_block = jnp.einsum(
-            "hqk,khd->qhd", weights_soft, value_cube, preferred_element_type=float_type
-        )
-        return (mixed_block.astype(half_type), (row_peak + jnp.log(exp_total))[..., 0])
-
-    mixed_heads, log_sums = lax.map(attend, (query_cube, segment_blocks))
-    attended_heads = mixed_heads.reshape(length, local_width)
-    attended_blocks = attended_heads.reshape(seq_size, tok_rows, local_width)
-    projected = seq_reduce(attended_blocks, out_rows, model_width, False, 2)
-    residual = inputs + projected
     inverse_second = inverse_rms(residual)
     unit_second = residual * inverse_second
     routed = (unit_second * gain_rows[1]).astype(half_type)
-    routed_seq = seq_gather(routed, seq_size, 0)
     slots = experts_local * capacity
 
     def gates_of(rows, ids):
@@ -716,7 +1125,7 @@
     gain_second_grad = jnp.sum(routed_grad * unit_second, axis=0)
     residual_grad = upstream + norm_back(routed_grad * gain_rows[1], unit_second, inverse_second)
     out_grad = residual_grad.astype(half_type)
-    out_grad_seq = seq_gather(out_grad, seq_size, 0)
+    out_grad_seq = seq_gather(out_grad, seq_size, 2)
     grad_out_local = jnp.einsum(
         "th,td->hd", attended_heads, out_grad_seq, preferred_element_type=float_type
     )

time: 1030 us -> 917 us (0.89)
  waiting for transfers between devices: 188 us -> 136 us
  local copies, waits for them, and re-layouts: 93.9 us -> 72.2 us
  matrix products: 169 us -> 154 us
  starting transfers between devices: 49.8 us -> 35.4 us
  blocking collectives: 14.2 us -> 0 us
  other arithmetic: 87.2 us -> 74.4 us
  Pallas kernels: 407 us -> 418 us
    pallas_call x0 -> x1, Pallas kernels: none -> 196 us  [front(): pl.pallas_call(functools.partial(front_kernel, sizes), out_shape=(shape((...]
    pallas_call x4 -> x1, Pallas kernels: 167 us -> 40.9 us  [seq_gather(): pl.pallas_call(functools.partial(gather_kernel, chips), out_shape=jax.Sha...]
    pallas_call x4 -> x3, Pallas kernels: 194 us -> 145 us  [seq_reduce(): pl.pallas_call(functools.partial(reduce_kernel, chips, b.ndim == 2, turne...]
    ppermute x18, waiting for transfers between devices: 108 us -> 74.3 us  [exchange(): moved.append(lax.ppermute(pieces[shift], 'fsdp', links))]
    gather x3 -> x0, local copies, waits for them, and re-layouts: 15.1 us -> none  [to_owner(): whole = jnp.stack(pieces)[order]]
    ppermute x9 -> x0, starting transfers between devices: 14.7 us -> none  [to_owner(): piece = lax.ppermute(piece, 'fsdp', links)]
    ppermute x9 -> x0, waiting for transfers between devices: 14.3 us -> none  [to_owner(): piece = lax.ppermute(piece, 'fsdp', links)]
    all_gather x1 -> x0, blocking collectives: 14.2 us -> none  [shards(): lax.all_gather(jnp.concatenate([expert_ids, places], 1), 'seq', axis=0, t...]
  transfers between devices with their start and end apart: 40 -> 29, of which waited for: 10 -> 9; matrix products, arithmetic and copies ran while one was open for 29% -> 27% of each run, Pallas kernels for 31% -> 24%
where the time goes in v3:
time: 917 us; the launch traced here: 906 us
  Pallas kernels  418 us (46%)
  matrix products  154 us (17%)
  waiting for transfers between devices  136 us (15%)
  other arithmetic  74.4 us (8%)
  local copies, waits for them, and re-layouts  72.2 us (8%)
  starting transfers between devices  35.4 us (4%)
  between operations  15.4 us (2%)
    pallas_call x1, Pallas kernels, front(): pl.pallas_call(functools.partial(front_kernel, sizes), out_shape=(shape((...  196 us
    pallas_call x3, Pallas kernels, seq_reduce(): pl.pallas_call(functools.partial(reduce_kernel, chips, b.ndim == 2, turne...  145 us
    ppermute x18, waiting for transfers between devices, exchange(): moved.append(lax.ppermute(pieces[shift], 'fsdp', links))  74.3 us
    ppermute x9, waiting for transfers between devices, to_shards(): piece = lax.ppermute(piece, 'fsdp', links)  61.2 us
    pallas_call x1, Pallas kernels, seq_gather(): pl.pallas_call(functools.partial(gather_kernel, chips), out_shape=jax.Sha...  40.9 us
    ppermute x18, starting transfers between devices, exchange(): moved.append(lax.ppermute(pieces[shift], 'fsdp', links))  22.4 us
    pallas_call x1, Pallas kernels, total_sum(): pl.pallas_call(functools.partial(total_kernel, size, split), out_shape=ja...  22.2 us
    dot_general x8, matrix products, dispatch(): jnp.einsum('btc,btd->bcd', onehot[:, :, index * capacity:(index + 1) * ca...  20.8 us
  transfers between devices with their start and end apart: 29, of which 9 were waited for; matrix products, arithmetic and copies ran while one was open for 27% of the time, Pallas kernels for 24%

profile of v3, /device:TPU:0, one launch (start us, length us, event | category | flops | bytes accessed | tf_op | source)
XLA Modules:
  0.0 905.6 jit_solution(9294493465007896088)
XLA Ops:
  17.0 196.4 %shard_map.221 = (bf16[1024,2048]{1,0:T(8,128)(2,1)}, bf16[3,2048,256]{2,1,0:T(8,128)(2,1)}, bf16[4,256,512]{2,1,0:T(8,128)(2,1)}, bf16[1024,256]{1,0:T(8,128)(2...) custom-call(bf16[128,2048]{1,0:T(8,128)(2,1)} %tokens_ref.1, ...), custom_call_target="tpu_custom_call" | custom-call | flops 4294967296 | bytes 524288000 | tf_op jit(solution)/shard_map/pallas_call | solution.py:824
  263.5 14.4 %collective-permute-done.6 = f32[320]{0:T(512)} collective-permute-done((f32[320]{0:T(512)}, f32[320]{0:T(512)}, u32[]{:S(2)}, u32[]{:S(2)}) %collective-permute-start.6) | collective-permute-done | bytes 1312 | tf_op jit(solution)/shard_map/ppermute | solution.py:957
  291.3 11.5 %fusion.88 = f32[1280,1024]{1,0:T(8,128)} fusion(bf16[2048,1024]{1,0:T(8,128)(2,1)} %get-tuple-element.90, bf16[320,2048]{1,0:T(8,128)(2,1)} %collective-permute-done.2, bf16[320,2048]{1,0:T(8,128)(2,1)} %collective-permute-done.1, bf16[320,2048]{1,0:T(8,128)(2,1)} %collective-permute-done, bf16[320,2048]{1,0:T(8,128)(2,1)S(1)} %bitcast.297), kind=kOutput, calls=%fused_computation.219 | convolution fusion | flops 5389680640 | bytes 14680064 | tf_op jit(solution)/shard_map/dot_general | solution.py:1078
  302.8 10.1 %fusion.87 = f32[1280,1024]{1,0:T(8,128)} fusion(bf16[2048,1024]{1,0:T(8,128)(2,1)S(1)} %copy-done.75, bf16[320,2048]{1,0:T(8,128)(2,1)} %collective-permute-done.2, bf16[320,2048]{1,0:T(8,128)(2,1)} %collective-permute-done.1, bf16[320,2048]{1,0:T(8,128)(2,1)} %collective-permute-done, bf16[320,2048]{1,0:T(8,128)(2,1)S(1)} %bitcast.298), kind=kOutput, calls=%fused_computation.218 | convolution fusion | flops 5389680640 | bytes 14680064 | tf_op jit(solution)/shard_map/dot_general | solution.py:1079
  319.8 26.8 %collective-permute-done.10 = bf16[320,2048]{1,0:T(8,128)(2,1)} collective-permute-done((bf16[320,2048]{1,0:T(8,128)(2,1)}, bf16[320,2048]{1,0:T(8,128)(2,1)}, u32[]{:S(2)}, u32[]{:S(2)}) %collective-permute-start.10) | collective-permute-done | bytes 1310752 | tf_op jit(solution)/shard_map/ppermute | solution.py:957
  346.5 16.1 %multiply_convert_fusion.1 = (bf16[1280,1024]{1,0:T(8,128)(2,1)}, bf16[1280,1024]{1,0:T(8,128)(2,1)}, bf16[1280,1024]{1,0:T(8,128)(2,1)}) fusion(f32[1280,1024]{1,0:T(8,128)} %fusion.88, f32[1280,1024]{1,0:T(8,128)} %fusion.87, bf16[1024,2048]{1,0:T(8,128)(2,1)} %get-tuple-element.92, f32[1280]{0:T(1024)S(1)} %concatenate.60, ...), kind=kOutput, calls=%fused_computation.43 | convolution fusion | flops 5415895040 | bytes 27792384 | tf_op jit(solution)/shard_map/rd,fd->rf/dot_general | solution.py:1097
  362.7 11.4 %fusion.97 = f32[1280,2048]{1,0:T(8,128)} fusion(bf16[1280,1024]{1,0:T(8,128)(2,1)} %get-tuple-element.241, bf16[2048,1024]{1,0:T(8,128)(2,1)} %get-tuple-element.90), kind=kOutput, calls=%fused_computation.228 | convolution fusion | flops 5368709120 | bytes 17301504 | tf_op jit(solution)/shard_map/rf,df->rd/dot_general | solution.py:1104
  374.1 8.5 add_convert_fusion
  387.9 8.6 fusion.23
  398.5 8.4 fusion.86
  406.9 9.0 fusion.85
  420.7 20.8 %collective-permute-done.17 = f32[320]{0:T(512)S(1)} collective-permute-done((f32[320]{0:T(512)S(1)}, f32[320]{0:T(512)S(1)}, u32[]{:S(2)}, u32[]{:S(2)}) %collective-permute-start.17) | collective-permute-done | bytes 1312 | tf_op jit(solution)/shard_map/ppermute | solution.py:957
  447.4 7.1 shard_map.224
  466.1 46.4 %shard_map.223 = f32[128,2048]{1,0:T(8,128)} custom-call(bf16[8,128,160]{2,1,0:T(8,128)(2,1)} %copy.152.a_ref, bf16[8,160,2048]{2,1,0:T(8,128)(2,1)} %pad_maximum_fusion.3.b_ref), custom_call_target="tpu_custom_call" | custom-call | flops 671088640 | bytes 83886080 | tf_op jit(solution)/shard_map/pallas_call | solution.py:347
  528.0 46.5 %shard_map.222 = f32[128,2048]{1,0:T(8,128)} custom-call(bf16[8,128,160]{2,1,0:T(8,128)(2,1)} %copy.151.a_ref, bf16[8,160,2048]{2,1,0:T(8,128)(2,1)} %pad_maximum_fusion.1.b_ref), custom_call_target="tpu_custom_call" | custom-call | flops 671088640 | bytes 83886080 | tf_op jit(solution)/shard_map/pallas_call | solution.py:347
  577.7 40.9 %shard_map.225 = bf16[1024,2048]{1,0:T(8,128)(2,1)} custom-call(bf16[128,2048]{1,0:T(8,128)(2,1)} %get-tuple-element.234.x_ref), custom_call_target="tpu_custom_call" | custom-call | bytes 83886080 | tf_op jit(solution)/shard_map/pallas_call | solution.py:297
  623.0 32.8 %while.15 = (s32[]{:T(128)}, f32[1024,2,128]{0,2,1:T(8,128)}, f32[1024,2,128]{0,2,1:T(8,128)}, bf16[2,512,2,128]{3,1,0,2:T(8,128)(2,1)}, bf16[2,512,2,128]{3,2,1...) while((s32[]{:T(128)}, f32[1024,2,128]{0,2,1:T(8,128)}, ...), condition=%wide.region_15.16_spmd.clone, body=%wide.region_13.15_spmd.clone.sunk | while | flops 1360002048 | bytes 79468808 | solution.py:1165
  684.8 7.0 shard_map.226
  703.0 8.6 fusion.25
  739.9 20.0 %collective-permute-done.23 = bf16[512,1024]{1,0:T(8,128)(2,1)S(1)} collective-permute-done((bf16[512,1024]{1,0:T(8,128)(2,1)S(1)}, bf16[512,1024]{1,0:T(8,128)(2,1)S(1)}, u32[]{:S(2)}, u32[]{:S(2)}) %collective-permute-start.23) | collective-permute-done | bytes 1048608 | tf_op jit(solution)/shard_map/ppermute | solution.py:941
  760.1 23.1 %collective-permute-done.24 = bf16[1024,512]{1,0:T(8,128)(2,1)S(1)} collective-permute-done((bf16[1024,512]{1,0:T(8,128)(2,1)S(1)}, bf16[1024,512]{1,0:T(8,128)(2,1)S(1)}, u32[]{:S(2)}, u32[]{:S(2)}) %collective-permute-start.24) | collective-permute-done | bytes 1048608 | tf_op jit(solution)/shard_map/ppermute | solution.py:941
  788.0 16.6 %collective-permute-done.26 = bf16[1024,512]{1,0:T(8,128)(2,1)S(1)} collective-permute-done((bf16[1024,512]{1,0:T(8,128)(2,1)S(1)}, bf16[1024,512]{1,0:T(8,128)(2,1)S(1)}, u32[]{:S(2)}, u32[]{:S(2)}) %collective-permute-start.26) | collective-permute-done | bytes 1048608 | tf_op jit(solution)/shard_map/ppermute | solution.py:941
  812.8 51.7 %shard_map.227 = f32[128,2048]{1,0:T(8,128)} custom-call(bf16[8,128,768]{2,1,0:T(8,128)(2,1)} %pad_maximum_fusion.5.a_ref, bf16[2048,768]{1,0:T(8,128)(2,1)} %pad_maximum_fusion.4.b_ref), custom_call_target="tpu_custom_call" | custom-call | flops 3221225472 | bytes 83886080 | tf_op jit(solution)/shard_map/pallas_call | solution.py:347
  867.8 22.2 %shard_map.228 = f32[40,2048]{1,0:T(8,128)} custom-call(f32[40,2048]{1,0:T(8,128)} %concatenate.72.x_ref), custom_call_target="tpu_custom_call" | custom-call | tf_op jit(solution)/shard_map/pallas_call | solution.py:483
  (386 shorter events, 257.9 us)
Async XLA Ops:
  7.2 887.3 %reduce-scatter.5.cloned.1.call-start = ((), (), s32[]{:S(2)}) async-start(), calls=%async_computation.3 | async-start | bytes 1310720 | tf_op jit(solution)/shard_map/reduce_scatter | solution.py:1202
  219.5 70.4 %collective-permute-start.2 = (bf16[320,2048]{1,0:T(8,128)(2,1)}, bf16[320,2048]{1,0:T(8,128)(2,1)}, u32[]{:S(2)}, u32[]{:S(2)}) collective-permute-start(bf16[320,2048]{1,0:T(8,128)(2,1)} %bitcast.12), channel_id=1, source_target_pairs={{0,24},{8,0},{16,8},{24,16},{1,25},{9,1},{17,9},{25,17},{2,26},{10... | collective-permute-start | bytes 3932168 | tf_op jit(solution)/shard_map/ppermute | solution.py:957
  222.8 68.5 %collective-permute-start.1 = (bf16[320,2048]{1,0:T(8,128)(2,1)}, bf16[320,2048]{1,0:T(8,128)(2,1)}, u32[]{:S(2)}, u32[]{:S(2)}) collective-permute-start(bf16[320,2048]{1,0:T(8,128)(2,1)} %bitcast.11), channel_id=1, source_target_pairs={{0,16},{8,24},{16,0},{24,8},{1,17},{9,25},{17,1},{25,9},{2,18},{10... | collective-permute-start | bytes 3932168 | tf_op jit(solution)/shard_map/ppermute | solution.py:957
  226.1 65.2 %collective-permute-start = (bf16[320,2048]{1,0:T(8,128)(2,1)}, bf16[320,2048]{1,0:T(8,128)(2,1)}, u32[]{:S(2)}, u32[]{:S(2)}) collective-permute-start(bf16[320,2048]{1,0:T(8,128)(2,1)} %bitcast.10), channel_id=1, source_target_pairs={{0,8},{8,16},{16,24},{24,0},{1,9},{9,17},{17,25},{25,1},{2,10},{10... | collective-permute-start | bytes 3932168 | tf_op jit(solution)/shard_map/ppermute | solution.py:957
  229.9 48.0 %collective-permute-start.6 = (f32[320]{0:T(512)}, f32[320]{0:T(512)}, u32[]{:S(2)}, u32[]{:S(2)}) collective-permute-start(f32[320]{0:T(512)} %unstack.27), channel_id=1, source_target_pairs={{0,8},{8,16},{16,24},{24,0},{1,9},{9,17},{17,25},{25,1},{2,10},{10... | collective-permute-start | bytes 3848 | tf_op jit(solution)/shard_map/ppermute | solution.py:957
  232.5 55.2 %collective-permute-start.7 = (f32[320]{0:T(512)}, f32[320]{0:T(512)}, u32[]{:S(2)}, u32[]{:S(2)}) collective-permute-start(f32[320]{0:T(512)} %unstack.29), channel_id=1, source_target_pairs={{0,16},{8,24},{16,0},{24,8},{1,17},{9,25},{17,1},{25,9},{2,18},{10... | collective-permute-start | bytes 3848 | tf_op jit(solution)/shard_map/ppermute | solution.py:957
  289.1 57.4 %collective-permute-start.10 = (bf16[320,2048]{1,0:T(8,128)(2,1)}, bf16[320,2048]{1,0:T(8,128)(2,1)}, u32[]{:S(2)}, u32[]{:S(2)}) collective-permute-start(bf16[320,2048]{1,0:T(8,128)(2,1)} %bitcast.303), channel_id=1, source_target_pairs={{0,16},{8,24},{16,0},{24,8},{1,17},{9,25},{17,1},{25,9},{2,18},{10... | collective-permute-start | bytes 3932168 | tf_op jit(solution)/shard_map/ppermute | solution.py:957
  289.9 56.6 %collective-permute-start.9 = (bf16[320,2048]{1,0:T(8,128)(2,1)}, bf16[320,2048]{1,0:T(8,128)(2,1)}, u32[]{:S(2)}, u32[]{:S(2)}) collective-permute-start(bf16[320,2048]{1,0:T(8,128)(2,1)} %bitcast.302), channel_id=1, source_target_pairs={{0,8},{8,16},{16,24},{24,0},{1,9},{9,17},{17,25},{25,1},{2,10},{10... | collective-permute-start | bytes 3932168 | tf_op jit(solution)/shard_map/ppermute | solution.py:957
  384.7 71.6 %collective-permute-start.14 = (bf16[320,2048]{1,0:T(8,128)(2,1)}, bf16[320,2048]{1,0:T(8,128)(2,1)}, u32[]{:S(2)}, u32[]{:S(2)}) collective-permute-start(bf16[320,2048]{1,0:T(8,128)(2,1)} %get-tuple-element.244), channel_id=1, source_target_pairs={{0,8},{8,16},{16,24},{24,0},{1,9},{9,17},{17,25},{25,1},{2,10},{10... | collective-permute-start | bytes 3932168 | tf_op jit(solution)/shard_map/ppermute | solution.py:957
  385.0 74.7 %collective-permute-start.13 = (bf16[320,2048]{1,0:T(8,128)(2,1)}, bf16[320,2048]{1,0:T(8,128)(2,1)}, u32[]{:S(2)}, u32[]{:S(2)}) collective-permute-start(bf16[320,2048]{1,0:T(8,128)(2,1)} %get-tuple-element.245), channel_id=1, source_target_pairs={{0,16},{8,24},{16,0},{24,8},{1,17},{9,25},{17,1},{25,9},{2,18},{10... | collective-permute-start | bytes 3932168 | tf_op jit(solution)/shard_map/ppermute | solution.py:957
  385.6 74.1 %collective-permute-start.12 = (bf16[320,2048]{1,0:T(8,128)(2,1)}, bf16[320,2048]{1,0:T(8,128)(2,1)}, u32[]{:S(2)}, u32[]{:S(2)}) collective-permute-start(bf16[320,2048]{1,0:T(8,128)(2,1)} %get-tuple-element.246), channel_id=1, source_target_pairs={{0,24},{8,0},{16,8},{24,16},{1,25},{9,1},{17,9},{25,17},{2,26},{10... | collective-permute-start | bytes 3932168 | tf_op jit(solution)/shard_map/ppermute | solution.py:957
  397.0 48.2 %collective-permute-start.16 = (f32[320]{0:T(512)S(1)}, f32[320]{0:T(512)S(1)}, u32[]{:S(2)}, u32[]{:S(2)}) collective-permute-start(f32[320]{0:T(512)S(1)} %get-tuple-element.291), channel_id=1, source_target_pairs={{0,16},{8,24},{16,0},{24,8},{1,17},{9,25},{17,1},{25,9},{2,18},{10... | collective-permute-start | bytes 3848 | tf_op jit(solution)/shard_map/ppermute | solution.py:957
  445.1 69.6 %collective-permute-start.5 = (bf16[320,2048]{1,0:T(8,128)(2,1)}, bf16[320,2048]{1,0:T(8,128)(2,1)}, u32[]{:S(2)}, u32[]{:S(2)}) collective-permute-start(bf16[320,2048]{1,0:T(8,128)(2,1)} %get-tuple-element.248), channel_id=1, source_target_pairs={{0,8},{8,16},{16,24},{24,0},{1,9},{9,17},{17,25},{25,1},{2,10},{10... | collective-permute-start | bytes 3932168 | tf_op jit(solution)/shard_map/ppermute | solution.py:957
  445.6 77.3 %collective-permute-start.4 = (bf16[320,2048]{1,0:T(8,128)(2,1)}, bf16[320,2048]{1,0:T(8,128)(2,1)}, u32[]{:S(2)}, u32[]{:S(2)}) collective-permute-start(bf16[320,2048]{1,0:T(8,128)(2,1)} %get-tuple-element.249), channel_id=1, source_target_pairs={{0,16},{8,24},{16,0},{24,8},{1,17},{9,25},{17,1},{25,9},{2,18},{10... | collective-permute-start | bytes 3932168 | tf_op jit(solution)/shard_map/ppermute | solution.py:957
  456.3 66.7 %collective-permute-start.3 = (bf16[320,2048]{1,0:T(8,128)(2,1)}, bf16[320,2048]{1,0:T(8,128)(2,1)}, u32[]{:S(2)}, u32[]{:S(2)}) collective-permute-start(bf16[320,2048]{1,0:T(8,128)(2,1)} %get-tuple-element.250), channel_id=1, source_target_pairs={{0,24},{8,0},{16,8},{24,16},{1,25},{9,1},{17,9},{25,17},{2,26},{10... | collective-permute-start | bytes 3932168 | tf_op jit(solution)/shard_map/ppermute | solution.py:957
  459.7 263.7 %collective-permute-start.18 = (bf16[512,1024]{1,0:T(8,128)(2,1)}, bf16[512,1024]{1,0:T(8,128)(2,1)}, u32[]{:S(2)}, u32[]{:S(2)}) collective-permute-start(bf16[512,1024]{1,0:T(8,128)(2,1)} %get-tuple-element.259), channel_id=1, source_target_pairs={{0,8},{8,16},{16,24},{24,0},{1,9},{9,17},{17,25},{25,1},{2,10},{10... | collective-permute-start | bytes 3145736 | tf_op jit(solution)/shard_map/ppermute | solution.py:941
  459.8 270.7 %collective-permute-start.19 = (bf16[512,1024]{1,0:T(8,128)(2,1)}, bf16[512,1024]{1,0:T(8,128)(2,1)}, u32[]{:S(2)}, u32[]{:S(2)}) collective-permute-start(bf16[512,1024]{1,0:T(8,128)(2,1)} %get-tuple-element.258), channel_id=1, source_target_pairs={{0,16},{8,24},{16,0},{24,8},{1,17},{9,25},{17,1},{25,9},{2,18},{10... | collective-permute-start | bytes 3145736 | tf_op jit(solution)/shard_map/ppermute | solution.py:941
  514.8 223.4 %collective-permute-start.20 = (bf16[512,1024]{1,0:T(8,128)(2,1)}, bf16[512,1024]{1,0:T(8,128)(2,1)}, u32[]{:S(2)}, u32[]{:S(2)}) collective-permute-start(bf16[512,1024]{1,0:T(8,128)(2,1)} %get-tuple-element.257), channel_id=1, source_target_pairs={{0,24},{8,0},{16,8},{24,16},{1,25},{9,1},{17,9},{25,17},{2,26},{10... | collective-permute-start | bytes 3145736 | tf_op jit(solution)/shard_map/ppermute | solution.py:941
  523.0 205.3 %collective-permute-start.21 = (bf16[512,1024]{1,0:T(8,128)(2,1)}, bf16[512,1024]{1,0:T(8,128)(2,1)}, u32[]{:S(2)}, u32[]{:S(2)}) collective-permute-start(bf16[512,1024]{1,0:T(8,128)(2,1)} %get-tuple-element.256), channel_id=1, source_target_pairs={{0,8},{8,16},{16,24},{24,0},{1,9},{9,17},{17,25},{25,1},{2,10},{10... | collective-permute-start | bytes 3145736 | tf_op jit(solution)/shard_map/ppermute | solution.py:941
  523.0 210.6 %collective-permute-start.22 = (bf16[512,1024]{1,0:T(8,128)(2,1)}, bf16[512,1024]{1,0:T(8,128)(2,1)}, u32[]{:S(2)}, u32[]{:S(2)}) collective-permute-start(bf16[512,1024]{1,0:T(8,128)(2,1)} %get-tuple-element.255), channel_id=1, source_target_pairs={{0,16},{8,24},{16,0},{24,8},{1,17},{9,25},{17,1},{25,9},{2,18},{10... | collective-permute-start | bytes 3145736 | tf_op jit(solution)/shard_map/ppermute | solution.py:941
  663.0 233.3 %reduce-scatter.3.cloned.1.call-start = ((), (), s32[]{:S(2)}) async-start(), calls=%async_computation.2 | async-start | bytes 3932160 | tf_op jit(solution)/shard_map/reduce_scatter | solution.py:1199
  728.3 55.0 %collective-permute-start.24 = (bf16[1024,512]{1,0:T(8,128)(2,1)S(1)}, bf16[1024,512]{1,0:T(8,128)(2,1)S(1)}, u32[]{:S(2)}, u32[]{:S(2)}) collective-permute-start(bf16[1024,512]{1,0:T(8,128)(2,1)S(1)} %get-tuple-element.253), channel_id=1, source_target_pairs={{0,8},{8,16},{16,24},{24,0},{1,9},{9,17},{17,25},{25,1},{2,10},{10... | collective-permute-start | bytes 3145736 | tf_op jit(solution)/shard_map/ppermute | solution.py:941
  730.5 55.8 %collective-permute-start.25 = (bf16[1024,512]{1,0:T(8,128)(2,1)S(1)}, bf16[1024,512]{1,0:T(8,128)(2,1)S(1)}, u32[]{:S(2)}, u32[]{:S(2)}) collective-permute-start(bf16[1024,512]{1,0:T(8,128)(2,1)S(1)} %get-tuple-element.252), channel_id=1, source_target_pairs={{0,16},{8,24},{16,0},{24,8},{1,17},{9,25},{17,1},{25,9},{2,18},{10... | collective-permute-start | bytes 3145736 | tf_op jit(solution)/shard_map/ppermute | solution.py:941
  733.6 71.0 %collective-permute-start.26 = (bf16[1024,512]{1,0:T(8,128)(2,1)S(1)}, bf16[1024,512]{1,0:T(8,128)(2,1)S(1)}, u32[]{:S(2)}, u32[]{:S(2)}) collective-permute-start(bf16[1024,512]{1,0:T(8,128)(2,1)S(1)} %get-tuple-element.251), channel_id=1, source_target_pairs={{0,24},{8,0},{16,8},{24,16},{1,25},{9,1},{17,9},{25,17},{2,26},{10... | collective-permute-start | bytes 3145736 | tf_op jit(solution)/shard_map/ppermute | solution.py:941
  (88 other events, 1986.9 us)
Sparse Core Ops, SparseCore 0:
  663.1 27.6 reduce-scatter.4
  703.1 55.8 reduce-scatter.2

commit v4 on v3

--- a/solution.py
+++ b/solution.py
@@ -165,13 +165,12 @@
 
 
 class ChainReduce:
-    def __init__(self, chips, rows, width, buffers):
+    def __init__(self, chips, total, buffers):
+        self.total = total
         (
             self.side_out,
             self.side_in,
-            self.chain_out,
             self.chain_in,
-            self.total,
             self.side_send,
             self.side_recv,
             self.chain_send,
@@ -187,9 +186,7 @@
         return [
             pltpu.VMEM((chips, rows, width), half),
             pltpu.VMEM((chips, rows, width), half),
-            pltpu.VMEM((chips, rows, width), half),
-            pltpu.VMEM((2, chips, rows, width), half),
-            pltpu.VMEM((rows, width), jnp.float32),
+            pltpu.VMEM((chips + 1, rows, width), half),
             pltpu.SemaphoreType.DMA((chips,)),
             pltpu.SemaphoreType.DMA((chips,)),
             pltpu.SemaphoreType.DMA((chips,)),
@@ -207,12 +204,15 @@
 
     def chain_copy(self, way, dest, target):
         return pltpu.make_async_remote_copy(
-            src_ref=self.chain_out.at[dest],
-            dst_ref=self.chain_in.at[way, dest],
+            src_ref=self.side_out.at[dest],
+            dst_ref=self.chain_in.at[self.slot(way, dest, target // 2)],
             send_sem=self.chain_send.at[dest],
             recv_sem=self.chain_recv.at[way, dest],
             device_id={"seq": target},
         )
+
+    def slot(self, way, dest, holder):
+        return jnp.where(dest == holder, self.chips, dest) if way else dest
 
     def place(self, index):
         distance = self.chips - 1 - index // 2
@@ -251,16 +251,18 @@
                 @pl.when((dest >= chip) & (chip > 0))
                 def _():
                     self.chain_copy(0, dest, sibling).wait_recv()
-                    total[...] += self.chain_in[0, dest].astype(jnp.float32)
+                    total[...] += self.chain_in[dest].astype(jnp.float32)
 
                 @pl.when((dest <= chip) & (chip < chips - 1))
                 def _():
                     self.chain_copy(1, dest, sibling).wait_recv()
-                    total[...] += self.chain_in[1, dest].astype(jnp.float32)
+                    total[...] += self.chain_in[self.slot(1, dest, chip)].astype(jnp.float32)
+
+                self.side_copy(dest).wait_send()
 
                 @pl.when(dest != chip)
                 def _():
-                    self.chain_out[dest] = total[...].astype(self.chain_out.dtype)
+                    self.side_out[dest] = total[...].astype(self.side_out.dtype)
 
                 @pl.when(dest > chip)
                 def _():
@@ -275,8 +277,6 @@
 
         @pl.loop(0, self.chips)
         def _(dest):
-            self.side_copy(dest).wait_send()
-
             @pl.when(dest != self.chip)
             def _():
                 self.chain_copy(0, dest, sibling).wait_send()
@@ -314,7 +314,7 @@
 def reduce_kernel(chips, shared, turned, a_ref, b_ref, o_ref, *buffers):
     rows, width = o_ref.shape
     step_cols = min(512, width)
-    reduce = ChainReduce(chips, rows, width, buffers)
+    reduce = ChainReduce(chips, o_ref, buffers)
     greet_chain(reduce.chip, reduce.core, chips)
 
     def product(block, store):
@@ -336,7 +336,6 @@
             store(cols, part)
 
     reduce.run(product)
-    o_ref[...] = reduce.total[...]
     reduce.sent()
 
 
@@ -498,6 +497,15 @@
         ],
         compiler_params=pltpu.CompilerParams(collective_id=which, has_side_effects=True),
     )(x)
+
+def partner_of(index, move):
+    turned, bit = index, 1
+    while bit <= move:
+        if move // bit % 2:
+            turned = turned + bit - 2 * bit * lax.rem(index // bit, 2)
+        bit *= 2
+    return turned
+
 
 def greet_all(size, split):
     me, mine = lax.axis_index("seq"), lax.axis_index("fsdp")
@@ -555,15 +563,18 @@
     attended_ref,
     residual_ref,
     routed_out,
-    cotangent_out,
+    cotangent_rows,
     gate_full,
     up_full,
     down_full,
     choices,
+    onehot_ref,
     normed,
     qkv,
     rows_full,
     routed_own,
+    cotangent_all,
+    placed,
     raw,
     sums_own,
     sums_in,
@@ -574,6 +585,9 @@
     sums_recv,
     choice_send,
     choice_recv,
+    placed_local,
+    placed_send,
+    placed_recv,
     shard_local,
     shard_send,
     shard_recv,
@@ -682,7 +696,7 @@
     for shift in range(1, size):
         choice_copy(shift).start()
     choices[me] = choice_ref[...]
-    second = gather(1, cotangent_ref, cotangent_out)
+    second = gather(1, cotangent_ref, cotangent_all)
     second.start()
     keeps = [
         pltpu.make_async_copy(normed, normed_out, out_sem.at[0]),
@@ -771,7 +785,7 @@
     for distance in range(heads + 2, chips):
         second.step(distance)
 
-    reduce = ChainReduce(chips, tok_rows, model_width, reduce_buffers)
+    reduce = ChainReduce(chips, residual_ref, reduce_buffers)
 
     def product(index, store):
         left = attended_ref[pl.ds(pl.multiple_of(index * tok_rows, tok_rows), tok_rows), :]
@@ -791,16 +805,59 @@
     third.landed()
 
     second.landed()
+    for shift in range(1, size):
+        choice_copy(shift).wait()
+    double = 2 * CAP
+    member = lax.rem(mine, experts_local)
+    top_count = choice_ref.shape[0] // 2
+    slot_row = lax.broadcasted_iota(jnp.int32, (double, tok_rows), 0)
+
+    @pl.loop(0, size // 2)
+    def _(pair):
+        for move in range(experts_local):
+            base = (me * experts_local + partner_of(member, move)) * CAP
+            for side in range(2):
+                want = jnp.where(slot_row // CAP == side, slot_row - side * CAP + base, -1)
+                places = choices[pair * 2 + side]
+                hit = want == places[top_count : top_count + 1, :]
+                for choice in range(1, top_count):
+                    hit = hit | (want == places[top_count + choice : top_count + choice + 1, :])
+                cols = slice(side * tok_rows, (side + 1) * tok_rows)
+                onehot_ref[pair, move * double : (move + 1) * double, cols] = jnp.where(
+                    hit, 1.0, 0.0
+                ).astype(half)
+        start = pl.multiple_of(pair * 2 * tok_rows, 2 * tok_rows)
+        made = jnp.dot(
+            onehot_ref[pair], cotangent_all[pl.ds(start, 2 * tok_rows), :], preferred_element_type=f32
+        ).astype(half)
+        for move in range(experts_local):
+            placed[move, pair] = made[move * double : (move + 1) * double]
+
+    def placed_copy(move):
+        return pltpu.make_async_remote_copy(
+            src_ref=placed.at[move],
+            dst_ref=cotangent_rows.at[move],
+            send_sem=placed_send.at[move],
+            recv_sem=placed_recv.at[move],
+            device_id={"fsdp": partner_of(mine, move)},
+        )
+
+    for move in range(experts_local - 1, 0, -1):
+        placed_copy(move).start()
+    placed_own = pltpu.make_async_copy(placed.at[0], cotangent_rows.at[0], placed_local)
+    placed_own.start()
+
     reduce.sent()
     second.sent()
     third.sent()
     for index in range(4):
         for shift in range(1, split):
             shard_copy(index, shift).wait_send()
-    for shift in range(1, size):
-        choice_copy(shift).wait()
     for keep in keeps:
         keep.wait()
+    placed_own.wait()
+    for move in range(1, experts_local):
+        placed_copy(move).wait()
     for index in range(3):
         expert_own(index).wait()
         for shift in range(1, split):
@@ -836,19 +893,22 @@
             shape((length, local_width), half),
             shape((tok_rows, model_width), f32),
             shape((length, model_width), half),
-            shape((length, model_width), half),
+            shape((experts_local, size // 2, 2 * CAP, model_width), half),
             shape((model_width, hidden_width), half),
             shape((model_width, hidden_width), half),
             shape((hidden_width, model_width), half),
             shape((size, *choice.shape), choice.dtype),
+            shape((size // 2, experts_local * 2 * CAP, 2 * tok_rows), half),
         ),
         in_specs=[vmem] * 7 + [anywhere] * 8 + [vmem],
-        out_specs=tuple([anywhere] * 3 + [vmem] * 8 + [anywhere] * 5 + [vmem]),
+        out_specs=tuple([anywhere] * 3 + [vmem] * 8 + [anywhere] * 5 + [vmem] * 2),
         scratch_shapes=[
             pltpu.VMEM((length, model_width), half),
             pltpu.VMEM((3, model_width, local_width), half),
             pltpu.VMEM((split, *w_out.shape), half),
             pltpu.VMEM((tok_rows, model_width), half),
+            pltpu.VMEM((length, model_width), half),
+            pltpu.VMEM((experts_local, size // 2, 2 * CAP, model_width), half),
             pltpu.VMEM((2, length, local_width), f32),
             pltpu.VMEM((8, length), f32),
             pltpu.VMEM((size, 8, length), f32),
@@ -859,6 +919,9 @@
             kind((size,)),
             kind((size,)),
             kind((size,)),
+            kind,
+            kind((experts_local,)),
+            kind((experts_local,)),
             kind((4,)),
             kind((4, split)),
             kind((4, split)),
@@ -889,6 +952,484 @@
         choice,
     )
 
+def experts_kernel(
+    sizes,
+    routed_ref,
+    choices_ref,
+    onehot_ref,
+    cotangent_rows_ref,
+    router_ref,
+    gains_ref,
+    residual_ref,
+    cotangent_ref,
+    gate_ref,
+    up_ref,
+    down_ref,
+    residual_grad_ref,
+    out_grad_ref,
+    gain_ref,
+    router_grad_ref,
+    combine_ref,
+    hidden_out,
+    grad_gate_ref,
+    grad_up_ref,
+    grad_down_ref,
+    gate_full,
+    up_full,
+    down_full,
+    upstream,
+    pair_rows,
+    outgoing,
+    arrived,
+    hidden,
+    gate_grad,
+    up_grad,
+    back,
+    gates,
+    gates_out,
+    gates_in,
+    dots_out,
+    dots_in,
+    token_out,
+    token_in,
+    scales,
+    load_sem,
+    pair_sem,
+    keep_sem,
+    rows_send,
+    rows_recv,
+    gates_send,
+    gates_recv,
+    back_send,
+    back_recv,
+    dots_send,
+    dots_recv,
+    token_send,
+    token_recv,
+    *reduce_buffers,
+):
+    size, split, chips, experts_local = sizes
+    f32, half = jnp.float32, jnp.bfloat16
+    me, mine = lax.axis_index("seq"), lax.axis_index("fsdp")
+    tok_rows, model_width = residual_ref.shape
+    pairs = size // 2
+    double = 2 * CAP
+    wide = 2 * tok_rows
+    hidden_width = gate_full.shape[1]
+    rows_of = pairs * double
+    part = model_width // split
+    member = lax.rem(mine, experts_local)
+
+    loads = [
+        pltpu.make_async_copy(source, target, load_sem.at[index])
+        for index, (source, target) in enumerate(
+            (
+                (gate_ref, gate_full),
+                (up_ref, up_full),
+                (down_ref, down_full),
+                (cotangent_rows_ref, upstream),
+            )
+        )
+    ]
+
+    slots = pair_rows.shape[0]
+
+    def pair_load(pair):
+        slot = lax.rem(pair, slots)
+        start = pl.multiple_of(pair * wide, wide)
+        return pltpu.make_async_copy(
+            routed_ref.at[pl.ds(start, wide)], pair_rows.at[slot], pair_sem.at[slot]
+        )
+
+    pair_load(0).start()
+    for load in loads:
+        load.start()
+    greet_all(size, split)
+
+    padded = size * 8
+    expert_row = lax.broadcasted_iota(jnp.int32, (padded, tok_rows), 0)
+    inner = lax.rem(expert_row, 8)
+    expert_row = jnp.where(inner < experts_local, expert_row // 8 * experts_local + inner, -1)
+    ones = jnp.ones((8, wide), f32)
+    top_count = choices_ref.shape[1] // 2
+
+    @pl.loop(0, pairs)
+    def _(pair):
+        pair_load(pair).wait()
+
+        @pl.when((pair + 1 < pairs) & (slots > 1))
+        def _():
+            pair_load(pair + 1).start()
+
+        rows = pair_rows[lax.rem(pair, slots)]
+        logits = lax.dot_general(
+            router_ref[...], rows, (((1,), (1,)), ((), ())), preferred_element_type=f32
+        )
+        for side in range(2):
+            ids = choices_ref[pair * 2 + side]
+            chosen = expert_row == ids[0:1, :]
+            for choice in range(1, top_count):
+                chosen = chosen | (expert_row == ids[choice : choice + 1, :])
+            own = jnp.where(chosen, logits[:, side * tok_rows : (side + 1) * tok_rows], MASKED)
+            grown = jnp.where(chosen, jnp.exp(own - jnp.max(own, 0, keepdims=True)), 0.0)
+            gates[pair * 2 + side] = grown / jnp.sum(grown, 0, keepdims=True)
+        placed = jnp.dot(onehot_ref[pair], rows, preferred_element_type=f32).astype(half)
+        for move in range(experts_local):
+            piece = placed[move * double : (move + 1) * double]
+            if move:
+                outgoing[move - 1, pair] = piece
+            else:
+                arrived[0, pair] = piece
+            row = me * 8 + partner_of(member, move)
+            weights = jnp.concatenate(
+                [gates[pair * 2, pl.ds(row, 1), :], gates[pair * 2 + 1, pl.ds(row, 1), :]], 1
+            )
+            slot_rows = pl.ds(move * double, double)
+            weighted = onehot_ref[pair, slot_rows, :].astype(f32) * weights
+            combine_ref[pair, slot_rows, :] = weighted.astype(half)
+            gates_out[move, pair] = row_sums(weighted, ones)
+
+        @pl.when((pair + 1 < pairs) & (slots == 1))
+        def _():
+            pair_load(pair + 1).start()
+
+    def mate(move):
+        return {"fsdp": partner_of(mine, move)}
+
+    def rows_copy(move):
+        return pltpu.make_async_remote_copy(
+            src_ref=outgoing.at[move - 1],
+            dst_ref=arrived.at[move],
+            send_sem=rows_send.at[move],
+            recv_sem=rows_recv.at[move],
+            device_id=mate(move),
+        )
+
+    def gates_copy(move):
+        return pltpu.make_async_remote_copy(
+            src_ref=gates_out.at[move],
+            dst_ref=gates_in.at[move],
+            send_sem=gates_send.at[move],
+            recv_sem=gates_recv.at[move],
+            device_id=mate(move),
+        )
+
+    def back_rows(move):
+        return back.at[:, pl.ds(move * double, double), :]
+
+    def back_copy(move):
+        return pltpu.make_async_remote_copy(
+            src_ref=outgoing.at[move - 1],
+            dst_ref=back_rows(move),
+            send_sem=back_send.at[move],
+            recv_sem=back_recv.at[move],
+            device_id=mate(move),
+        )
+
+    def dots_copy(move):
+        return pltpu.make_async_remote_copy(
+            src_ref=dots_out.at[move],
+            dst_ref=dots_in.at[move],
+            send_sem=dots_send.at[move],
+            recv_sem=dots_recv.at[move],
+            device_id=mate(move),
+        )
+
+    order = list(range(experts_local - 1, 0, -1))
+    for move in order:
+        gates_copy(move).start()
+        rows_copy(move).start()
+    gates_in[0] = gates_out[0]
+    for load in loads:
+        load.wait()
+
+    cols_step = min(256, hidden_width)
+    width_step = min(512, model_width)
+    spread = (lax.broadcasted_iota(jnp.int32, (8, 128), 0) == 0).astype(f32)
+    for move in [0] + order:
+        if move:
+            gates_copy(move).wait()
+            rows_copy(move).wait()
+        for pair in range(pairs):
+            scales[pair * double : (pair + 1) * double, :] = column_of(
+                gates_in[move, pair], spread
+            )
+        dots_out[move] = jnp.zeros_like(dots_out[move])
+
+        @pl.loop(0, hidden_width // cols_step)
+        def _(index):
+            cols = pl.ds(pl.multiple_of(index * cols_step, cols_step), cols_step)
+            rows = arrived[move].reshape(rows_of, model_width)
+            pre = jnp.dot(rows, gate_full[:, cols], preferred_element_type=f32)
+            up = jnp.dot(rows, up_full[:, cols], preferred_element_type=f32)
+            plain = lax.dot_general(
+                upstream[move].reshape(rows_of, model_width),
+                down_full[cols, :],
+                (((1,), (1,)), ((), ())),
+                preferred_element_type=f32,
+            )
+            sigmoid = 1.0 / (1.0 + jnp.exp(-pre))
+            active = pre * sigmoid
+            made = (active * up).astype(half)
+            hidden[move, :, :, cols] = made.reshape(pairs, double, cols_step)
+            dots = made.astype(f32) * plain
+            for pair in range(pairs):
+                dots_out[move, pair] += row_sums(
+                    dots[pair * double : (pair + 1) * double], jnp.ones((8, cols_step), f32)
+                )
+            scaled = plain * scales[:, 0:1]
+            gate_back = scaled * up * sigmoid * (1.0 + pre * (1.0 - sigmoid))
+            gate_grad[move, :, :, cols] = gate_back.astype(half).reshape(pairs, double, cols_step)
+            up_grad[move, :, :, cols] = (
+                (scaled * active).astype(half).reshape(pairs, double, cols_step)
+            )
+
+        for pair in range(pairs):
+            scale = scales[pair * double : (pair + 1) * double, 0:1]
+            upstream[move, pair] = (upstream[move, pair].astype(f32) * scale).astype(half)
+
+        if move:
+            dots_copy(move).start()
+        else:
+            dots_in[0] = dots_out[0]
+
+        @pl.loop(0, model_width // width_step)
+        def _(index):
+            cols = pl.ds(pl.multiple_of(index * width_step, width_step), width_step)
+            rows_grad = lax.dot_general(
+                gate_grad[move].reshape(rows_of, hidden_width),
+                gate_full[cols, :],
+                (((1,), (1,)), ((), ())),
+                preferred_element_type=f32,
+            )
+            rows_grad = rows_grad + lax.dot_general(
+                up_grad[move].reshape(rows_of, hidden_width),
+                up_full[cols, :],
+                (((1,), (1,)), ((), ())),
+                preferred_element_type=f32,
+            )
+            rows_grad = rows_grad.astype(half).reshape(pairs, double, width_step)
+            if move:
+                outgoing[move - 1, :, :, cols] = rows_grad
+            else:
+                back[:, 0:double, cols] = rows_grad
+
+        if move:
+            back_copy(move).start()
+
+    own_rows = pl.ds(pl.multiple_of(me * tok_rows, tok_rows), tok_rows)
+    own_load = pltpu.make_async_copy(
+        routed_ref.at[own_rows], pair_rows.at[0, pl.ds(0, tok_rows)], pair_sem.at[0]
+    )
+    own_load.start()
+    hidden_keep = pltpu.make_async_copy(hidden, hidden_out, keep_sem)
+    hidden_keep.start()
+
+    total_rows = experts_local * rows_of
+
+    def flat(ref, cols):
+        return ref[:, :, :, cols].reshape(total_rows, -1)
+
+    def turned_dot(left, right):
+        return lax.dot_general(
+            left, right, (((0,), (0,)), ((), ())), preferred_element_type=f32
+        )
+
+    every = pl.ds(0, hidden_width)
+
+    @pl.loop(0, split)
+    def _(piece):
+        cols = pl.ds(pl.multiple_of(piece * part, part), part)
+        gate_full[cols, :] = turned_dot(flat(arrived, cols), flat(gate_grad, every)).astype(half)
+        up_full[cols, :] = turned_dot(flat(arrived, cols), flat(up_grad, every)).astype(half)
+        down_full[:, cols] = turned_dot(flat(hidden, every), flat(upstream, cols)).astype(half)
+
+    grad_keeps = [
+        pltpu.make_async_copy(source, target, load_sem.at[index])
+        for index, (source, target) in enumerate(
+            ((gate_full, grad_gate_ref), (up_full, grad_up_ref), (down_full, grad_down_ref))
+        )
+    ]
+    for keep in grad_keeps:
+        keep.start()
+
+    for move in order:
+        dots_copy(move).wait()
+    token_out[...] = jnp.zeros_like(token_out)
+
+    @pl.loop(0, pairs)
+    def _(pair):
+        for move in range(experts_local):
+            found = jnp.dot(
+                dots_in[move, pair],
+                onehot_ref[pair, pl.ds(move * double, double), :].astype(f32),
+                precision=HIGHEST,
+                preferred_element_type=f32,
+            )
+            row = partner_of(member, move)
+            for side in range(2):
+                token_out[pair * 2 + side, pl.ds(row, 1), :] = found[
+                    0:1, side * tok_rows : (side + 1) * tok_rows
+                ]
+
+    def token_copy(shift):
+        peer = lax.rem(me + shift, size)
+        return pltpu.make_async_remote_copy(
+            src_ref=token_out.at[peer],
+            dst_ref=token_in.at[me],
+            send_sem=token_send.at[shift],
+            recv_sem=token_recv.at[shift],
+            device_id={"seq": peer},
+        )
+
+    for shift in range(1, size):
+        token_copy(shift).start()
+    token_in[me] = token_out[me]
+    for move in order:
+        back_copy(move).wait()
+
+    reduce = ChainReduce(chips, residual_grad_ref, reduce_buffers)
+
+    def product(index, store):
+        side = pl.ds(pl.multiple_of(lax.rem(index, 2) * tok_rows, tok_rows), tok_rows)
+        left = onehot_ref[index // 2, :, side]
+
+        @pl.loop(0, model_width // width_step)
+        def _(step):
+            cols = pl.ds(pl.multiple_of(step * width_step, width_step), width_step)
+            store(cols, turned_dot(left, back[index // 2, :, cols]))
+
+    reduce.run(product)
+
+    for shift in range(1, size):
+        token_copy(shift).wait()
+    own_gates = gates[me]
+    grads = token_in[...].reshape(padded, tok_rows)
+    mean = jnp.sum(own_gates * grads, 0, keepdims=True)
+    logit_grad = (own_gates * (grads - mean)).astype(half)
+    routed_grad = reduce.total[...] + turned_dot(logit_grad, router_ref[...])
+    own_load.wait()
+    router_grad_ref[...] = jnp.dot(
+        logit_grad, pair_rows[0, 0:tok_rows, :], preferred_element_type=f32
+    )
+    residual = residual_ref[...]
+    inverse = lax.rsqrt(jnp.mean(residual * residual, -1, keepdims=True) + EPSILON)
+    unit = residual * inverse
+    gain_ref[...] = jnp.broadcast_to(
+        jnp.sum(routed_grad * unit, 0, keepdims=True), gain_ref.shape
+    )
+    routed_grad = routed_grad * gains_ref[1:2, :]
+    routed_grad = inverse * (
+        routed_grad - unit * jnp.mean(routed_grad * unit, -1, keepdims=True)
+    )
+    residual_grad = cotangent_ref[...].astype(f32) + routed_grad
+    residual_grad_ref[...] = residual_grad
+    out_grad_ref[...] = residual_grad.astype(half)
+    reduce.sent()
+    hidden_keep.wait()
+    for keep in grad_keeps:
+        keep.wait()
+
+
+def experts(
+    sizes,
+    routed_seq,
+    choices,
+    onehot,
+    cotangent_rows,
+    router_rows,
+    gain_rows,
+    residual,
+    cotangent,
+    weights,
+    which,
+):
+    size, split, chips, experts_local = sizes
+    gate_full, up_full, down_full = weights
+    model_width, hidden_width = gate_full.shape
+    tok_rows = residual.shape[0]
+    pairs, double = size // 2, 2 * CAP
+    f32, half = jnp.float32, jnp.bfloat16
+    vmem = pl.BlockSpec(memory_space=pltpu.VMEM)
+    anywhere = pl.BlockSpec(memory_space=pl.ANY)
+    kind = pltpu.SemaphoreType.DMA
+    shape = jax.ShapeDtypeStruct
+    few = kind((experts_local,))
+    wide_rows = (experts_local, pairs, double, model_width)
+    narrow_rows = (experts_local, pairs, double, hidden_width)
+    flags = (experts_local, pairs, 8, double)
+    return pl.pallas_call(
+        functools.partial(experts_kernel, sizes),
+        out_shape=(
+            shape((tok_rows, model_width), f32),
+            shape((tok_rows, model_width), half),
+            shape((8, model_width), f32),
+            shape((size * 8, model_width), f32),
+            shape(onehot.shape, half),
+            shape(narrow_rows, half),
+            shape(gate_full.shape, half),
+            shape(up_full.shape, half),
+            shape(down_full.shape, half),
+        ),
+        in_specs=[anywhere, vmem, vmem, anywhere] + [vmem] * 4 + [anywhere] * 3,
+        out_specs=tuple([vmem] * 5 + [anywhere] * 4),
+        scratch_shapes=[
+            pltpu.VMEM(gate_full.shape, half),
+            pltpu.VMEM(up_full.shape, half),
+            pltpu.VMEM(down_full.shape, half),
+            pltpu.VMEM(wide_rows, half),
+            pltpu.VMEM((2 if chips < 8 else 1, 2 * tok_rows, model_width), half),
+            pltpu.VMEM((max(experts_local - 1, 1), *wide_rows[1:]), half),
+            pltpu.VMEM(wide_rows, half),
+            pltpu.VMEM(narrow_rows, half),
+            pltpu.VMEM(narrow_rows, half),
+            pltpu.VMEM(narrow_rows, half),
+            pltpu.VMEM((pairs, experts_local * double, model_width), half),
+            pltpu.VMEM((size, size * 8, tok_rows), f32),
+            pltpu.VMEM(flags, f32),
+            pltpu.VMEM(flags, f32),
+            pltpu.VMEM(flags, f32),
+            pltpu.VMEM(flags, f32),
+            pltpu.VMEM((size, 8, tok_rows), f32),
+            pltpu.VMEM((size, 8, tok_rows), f32),
+            pltpu.VMEM((pairs * double, 128), f32),
+            kind((4,)),
+            kind((2,)),
+            kind,
+            few,
+            few,
+            few,
+            few,
+            few,
+            few,
+            few,
+            few,
+            kind((size,)),
+            kind((size,)),
+            *ChainReduce.scratch(chips, tok_rows, model_width),
+        ],
+        compiler_params=pltpu.CompilerParams(
+            collective_id=which, has_side_effects=True, vmem_limit_bytes=63 * 2**20
+        ),
+        cost_estimate=pl.CostEstimate(
+            flops=2 * experts_local * pairs * double * model_width * hidden_width * 8,
+            bytes_accessed=500 * 2**20,
+            transcendentals=0,
+        ),
+    )(
+        routed_seq,
+        choices,
+        onehot,
+        cotangent_rows,
+        router_rows,
+        gain_rows,
+        residual,
+        cotangent,
+        gate_full,
+        up_full,
+        down_full,
+    )
+
 
 def shards(
     tokens,
@@ -916,14 +1457,12 @@
     local_width = w_query.shape[1]
     heads_local = local_width // head_size
     capacity = CAP
-    seq_index = lax.axis_index("seq")
-    column_start = seq_index * local_width
+    column_start = lax.axis_index("seq") * local_width
     experts_local = w_gate.shape[0]
     seq_size = lax.axis_size("seq")
     split = lax.axis_size("fsdp")
     groups = split // experts_local
     shard_index = lax.axis_index("fsdp")
-    member = lax.rem(shard_index, experts_local)
 
     def pick(stack, index):
         return lax.dynamic_index_in_dim(stack, index, 0, keepdims=False)
@@ -946,28 +1485,14 @@
             owned = lax.dynamic_update_index_in_dim(owned, piece, expert, 0)
         return owned
 
-    def exchange(pieces, back):
-        moved = [pieces[0]]
-        for shift in range(1, experts_local):
-            turn = experts_local - shift if back else shift
-            links = [
-                (one, one - one % experts_local + (one + turn) % experts_local)
-                for one in range(split)
-            ]
-            moved.append(lax.ppermute(pieces[shift], "fsdp", links))
-        return moved
-
-    turned_ids = lax.rem(expert_ids - member + experts_local, experts_local)
-    turned_ids = turned_ids + expert_ids - lax.rem(expert_ids, experts_local)
-    places = jnp.where(
-        expert_slots < capacity, turned_ids * capacity + expert_slots, -(10**6)
-    )
+    places = jnp.where(expert_slots < capacity, expert_ids * capacity + expert_slots, -(10**6))
     gain_rows = norm_gains.astype(float_type)
     gain_cols = lax.dynamic_slice_in_dim(gain_rows, column_start, local_width, 1)
     inputs = tokens.astype(float_type)
     inverse_first = inverse_rms(inputs)
     unit_first = inputs * inverse_first
     length = seq_size * tok_rows
+    sizes = (seq_size, split, seq_size // 2, experts_local)
     positions = jnp.arange(length, dtype=jnp.int32)
     cosine_table, sine_table = rope_tables(positions, head_size)
     cosine_wide = jnp.concatenate([cosine_table, cosine_table], 1)
@@ -985,13 +1510,14 @@
         attended_heads,
         residual,
         routed_seq,
-        cotangent_seq,
+        cotangent_rows,
         gate_full,
         up_full,
         down_full,
         choices,
+        onehot,
     ) = front(
-        (seq_size, split, seq_size // 2, experts_local),
+        sizes,
         tokens,
         gain_rows,
         gain_cols,
@@ -1003,9 +1529,6 @@
         jnp.concatenate([expert_ids, places], 1).T,
         0,
     )
-    both_seq = choices.transpose(0, 2, 1).reshape(length, 2 * top_count)
-    ids_seq = both_seq[:, :top_count]
-    places_seq = both_seq[:, top_count:]
     unit_query, unit_key = unit_pair[0], unit_pair[1]
     inverse_query = lax.rsqrt(square_sums[0] / model_width + EPSILON)[:, None]
     inverse_key = lax.rsqrt(square_sums[1] / model_width + EPSILON)[:, None]
@@ -1029,102 +1552,57 @@
         visible = segment_block[:, None] == segment_ids[None, :]
         return jnp.where(visible[None], scores, MASKED)
 
-    inverse_second = inverse_rms(residual)
-    unit_second = residual * inverse_second
-    routed = (unit_second * gain_rows[1]).astype(half_type)
-    slots = experts_local * capacity
-
-    def gates_of(rows, ids):
-        logits = jnp.dot(rows, w_router, preferred_element_type=float_type)
-        chosen = (ids[:, :, None] == jnp.arange(expert_total, dtype=jnp.int32)).astype(float_type)
-        picked = jnp.einsum("tke,te->tk", chosen, logits, precision=HIGHEST)
-        return chosen, jax.nn.softmax(picked, axis=-1)
-
-    chosen, gate_weights = gates_of(routed, expert_ids)
-    gates_seq = gates_of(routed_seq, ids_seq)[1]
-    mine = (places_seq - seq_index * slots).reshape(seq_size, tok_rows, top_count)
-    hits = mine[:, :, :, None] == jnp.arange(slots, dtype=jnp.int32)
-    onehot = jnp.any(hits, 2).astype(half_type)
-    combine = jnp.sum(
-        jnp.where(hits, gates_seq.reshape(seq_size, tok_rows, top_count)[..., None], 0.0), 2
-    )
-
-    def dispatch(rows):
-        cube = rows.reshape(seq_size, tok_rows, model_width)
-        return [
-            jnp.einsum(
-                "btc,btd->bcd",
-                onehot[:, :, index * capacity : (index + 1) * capacity],
-                cube,
-                preferred_element_type=float_type,
-            )
-            .astype(half_type)
-            .reshape(seq_size * capacity, model_width)
-            for index in range(experts_local)
-        ]
-
-    def undispatch(pieces):
-        cubes = [piece.reshape(seq_size, capacity, model_width) for piece in pieces]
-        return jnp.concatenate(cubes, 1)
-
-    def parts_of(rows):
-        depth = rows.shape[0] // experts_local
-        return [rows[index * depth : (index + 1) * depth] for index in range(experts_local)]
-
-    expert_rows = jnp.concatenate(exchange(dispatch(routed_seq), False))
-    upstream_rows = jnp.concatenate(exchange(dispatch(cotangent_seq), False))
-    slot_gates = jnp.sum(combine, 1).reshape(seq_size, experts_local, capacity).transpose(1, 0, 2)
-    row_gates = jnp.concatenate(exchange(list(slot_gates.reshape(experts_local, -1)), False))
-    gate_pre = jnp.dot(expert_rows, gate_full, preferred_element_type=float_type)
-    up_pre = jnp.dot(expert_rows, up_full, preferred_element_type=float_type)
-    gate_sigmoid = jax.nn.sigmoid(gate_pre)
-    hidden = (gate_pre * gate_sigmoid * up_pre).astype(half_type)
-    returned = jnp.dot(hidden, down_full, preferred_element_type=float_type).astype(half_type)
-    row_dots = jnp.sum(returned.astype(float_type) * upstream_rows.astype(float_type), -1)
-    slot_dots = jnp.stack(exchange(parts_of(row_dots), True))
-    slot_dots = slot_dots.reshape(experts_local, seq_size, capacity).transpose(1, 0, 2)
-    slot_dots = slot_dots.reshape(seq_size, 1, slots)
-    padded = -(-slots // 128) * 128
-    slot_dots = jnp.pad(slot_dots, ((0, 0), (0, 7), (0, padded - slots)))
-    slot_dots = seq_swap(slot_dots, seq_size, False, 3)[:, 0, :slots].reshape(-1)
-    at_place = places[:, :, None] == jnp.arange(expert_total * capacity, dtype=jnp.int32)
-    gate_grad = jnp.sum(jnp.where(at_place, slot_dots, 0.0), -1)
-    incoming = undispatch(exchange(parts_of(returned), True))
-    mixture = seq_reduce(combine.astype(half_type), incoming, model_width, False, 4)
+    router_rows = jnp.zeros((seq_size, 8, model_width), half_type)
+    router_rows = router_rows.at[:, :experts_local].set(
+        w_router.T.reshape(seq_size, experts_local, model_width)
+    )
+    router_rows = router_rows.reshape(seq_size * 8, model_width)
+    (
+        residual_grad,
+        out_grad,
+        gain_second_grad,
+        router_grad_rows,
+        combine,
+        hidden,
+        grad_gate_full,
+        grad_up_full,
+        grad_down_full,
+    ) = experts(
+        sizes,
+        routed_seq,
+        choices,
+        onehot,
+        cotangent_rows,
+        router_rows,
+        gain_rows,
+        residual,
+        cotangent,
+        (gate_full, up_full, down_full),
+        1,
+    )
+    gain_second_grad = gain_second_grad[0]
+    grad_router_local = router_grad_rows.reshape(seq_size, 8, model_width)[:, :experts_local]
+    grad_router_local = grad_router_local.reshape(expert_total, model_width)
+    pairs = seq_size // 2
+    returned = jnp.einsum(
+        "mpsf,fd->mpsd", hidden, down_full, preferred_element_type=float_type
+    ).astype(half_type)
+    incoming = []
+    for move in range(experts_local):
+        piece = returned[move]
+        if move:
+            piece = lax.ppermute(piece, "fsdp", [(one, one ^ move) for one in range(split)])
+        incoming.append(piece)
+    mixture = jnp.einsum(
+        "pst,psd->ptd",
+        combine,
+        jnp.concatenate(incoming, 1),
+        preferred_element_type=float_type,
+    ).astype(half_type)
+    mixture = lax.psum_scatter(
+        mixture.reshape(length, model_width), "seq", scatter_dimension=0, tiled=True
+    ).astype(float_type)
     output = (residual + mixture).astype(half_type)
-    upstream = cotangent.astype(float_type)
-    slot_grads = (row_gates[:, None] * upstream_rows.astype(float_type)).astype(half_type)
-    hidden_grad = jnp.einsum(
-        "rd,fd->rf", slot_grads, down_full, preferred_element_type=float_type
-    )
-    gate_pre_grad = (
-        hidden_grad * up_pre * gate_sigmoid * (1.0 + gate_pre * (1.0 - gate_sigmoid))
-    ).astype(half_type)
-    up_pre_grad = (hidden_grad * gate_pre * gate_sigmoid).astype(half_type)
-    rows_grad = jnp.einsum("rf,df->rd", gate_pre_grad, gate_full, preferred_element_type=float_type)
-    rows_grad = (
-        rows_grad
-        + jnp.einsum("rf,df->rd", up_pre_grad, up_full, preferred_element_type=float_type)
-    ).astype(half_type)
-    sent_back = undispatch(exchange(parts_of(rows_grad), True))
-    routed_grad = seq_reduce(onehot, sent_back, model_width, False, 4)
-    grad_down_full = jnp.einsum("rf,rd->fd", hidden, slot_grads, preferred_element_type=float_type)
-    grad_gate_full = jnp.einsum(
-        "rd,rf->df", expert_rows, gate_pre_grad, preferred_element_type=float_type
-    )
-    grad_up_full = jnp.einsum("rd,rf->df", expert_rows, up_pre_grad, preferred_element_type=float_type)
-    mean_grad = jnp.sum(gate_weights * gate_grad, -1, keepdims=True)
-    picked_grad = gate_weights * (gate_grad - mean_grad)
-    logit_grad = jnp.einsum("tke,tk->te", chosen, picked_grad, precision=HIGHEST).astype(half_type)
-    routed_grad = routed_grad + jnp.einsum(
-        "te,de->td", logit_grad, w_router, preferred_element_type=float_type
-    )
-    grad_router_local = jnp.einsum(
-        "td,te->ed", routed, logit_grad, preferred_element_type=float_type
-    )
-    gain_second_grad = jnp.sum(routed_grad * unit_second, axis=0)
-    residual_grad = upstream + norm_back(routed_grad * gain_rows[1], unit_second, inverse_second)
-    out_grad = residual_grad.astype(half_type)
     out_grad_seq = seq_gather(out_grad, seq_size, 2)
     grad_out_local = jnp.einsum(
         "th,td->hd", attended_heads, out_grad_seq, preferred_element_type=float_type
@@ -1175,7 +1653,7 @@
     query_scaled = query_unit_grad * gain_cols[2]
     key_scaled = key_unit_grad * gain_cols[3]
     centers = seq_sum(
-        (jnp.sum(query_scaled * unit_query, -1), jnp.sum(key_scaled * unit_key, -1)), seq_size, 1
+        (jnp.sum(query_scaled * unit_query, -1), jnp.sum(key_scaled * unit_key, -1)), seq_size, 3
     )
     query_raw_grad = (
         inverse_query * (query_scaled - unit_query * (centers[0] / model_width)[:, None])

time: 917 us -> 889 us (0.969)
  Pallas kernels: 418 us -> 561 us
  matrix products: 154 us -> 49.2 us
  starting transfers between devices: 35.4 us -> 14.8 us
  other arithmetic: 74.4 us -> 58.7 us
  local copies, waits for them, and re-layouts: 72.2 us -> 57.4 us
    pallas_call x0 -> x1, Pallas kernels: none -> 176 us  [experts(): pl.pallas_call(functools.partial(experts_kernel, sizes), out_shape=(shape...]
    dot_general x21 -> x2, matrix products: 118 us -> 12.2 us  [the longest x1 8.19 us: shards(): jnp.einsum('mpsf,fd->mpsd', hidden, down_full, preferred_element_type=flo...]
    pallas_call x3 -> x1, Pallas kernels: 145 us -> 61.8 us  [seq_reduce(): pl.pallas_call(functools.partial(reduce_kernel, chips, b.ndim == 2, turne...]
    pallas_call x1, Pallas kernels: 196 us -> 253 us  [front(): pl.pallas_call(functools.partial(front_kernel, sizes), out_shape=(shape((...]
    ppermute x18 -> x3, starting transfers between devices: 22.4 us -> 3.55 us  [shards(): lax.ppermute(piece, 'fsdp', [(one, one ^ move) for one in range(split)])]
    concatenate x2 -> x0, other arithmetic: 10 us -> none  [undispatch(): return jnp.concatenate(cubes, 1)]
    ppermute x18 -> x3, waiting for transfers between devices: 74.3 us -> 73.8 us  [shards(): lax.ppermute(piece, 'fsdp', [(one, one ^ move) for one in range(split)])]
  transfers between devices with their start and end apart: 29 -> 15, of which waited for: 9 -> 6; matrix products, arithmetic and copies ran while one was open for 27% -> 16% of each run, Pallas kernels for 24% -> 10%
where the time goes in v4:
time: 889 us; the launch traced here: 884 us
  Pallas kernels  561 us (63%)
  waiting for transfers between devices  128 us (14%)
  other arithmetic  58.7 us (7%)
  local copies, waits for them, and re-layouts  57.4 us (6%)
  matrix products  49.2 us (6%)
  starting transfers between devices  14.8 us (2%)
  between operations  14.7 us (2%)
    pallas_call x1, Pallas kernels, front(): pl.pallas_call(functools.partial(front_kernel, sizes), out_shape=(shape((...  253 us
    pallas_call x1, Pallas kernels, experts(): pl.pallas_call(functools.partial(experts_kernel, sizes), out_shape=(shape...  176 us
    ppermute x3, waiting for transfers between devices, shards(): lax.ppermute(piece, 'fsdp', [(one, one ^ move) for one in range(split)])  73.8 us
    pallas_call x1, Pallas kernels, seq_reduce(): pl.pallas_call(functools.partial(reduce_kernel, chips, b.ndim == 2, turne...  61.8 us
    ppermute x9, waiting for transfers between devices, to_shards(): piece = lax.ppermute(piece, 'fsdp', links)  54.4 us
    pallas_call x1, Pallas kernels, seq_gather(): pl.pallas_call(functools.partial(gather_kernel, chips), out_shape=jax.Sha...  40.7 us
    pallas_call x1, Pallas kernels, total_sum(): pl.pallas_call(functools.partial(total_kernel, size, split), out_shape=ja...  22.3 us
  transfers between devices with their start and end apart: 15, of which 6 were waited for; matrix products, arithmetic and copies ran while one was open for 16% of the time, Pallas kernels for 10%

profile of v4, /device:TPU:0, one launch (start us, length us, event | category | flops | bytes accessed | tf_op | source)
XLA Modules:
  0.0 883.9 jit_solution(546213323006102816)
XLA Ops:
  18.7 252.9 %shard_map.221 = (bf16[1024,2048]{1,0:T(8,128)(2,1)}, bf16[3,2048,256]{2,1,0:T(8,128)(2,1)}, bf16[4,256,512]{2,1,0:T(8,128)(2,1)}, bf16[1024,256]{1,0:T(8,128)(2...) custom-call(bf16[128,2048]{1,0:T(8,128)(2,1)} %tokens_ref.1, ...), custom_call_target="tpu_custom_call" | custom-call | flops 4294967296 | bytes 524288000 | tf_op jit(solution)/shard_map/pallas_call | solution.py:881
  271.6 175.9 %shard_map.222 = (f32[128,2048]{1,0:T(8,128)}, bf16[128,2048]{1,0:T(8,128)(2,1)}, f32[8,2048]{1,0:T(8,128)}, f32[64,2048]{1,0:T(8,128)}, bf16[4,320,256]{2,1,0:T...) custom-call(bf16[1024,2048]{1,0:T(8,128)(2,1)} %get-tuple-element.11, ...), custom_call_target="tpu_custom_call" | custom-call | flops 42949672960 | bytes 524288000 | tf_op jit(solution)/shard_map/pallas_call | solution.py:1361
  447.5 40.7 %shard_map.223 = bf16[1024,2048]{1,0:T(8,128)(2,1)} custom-call(bf16[128,2048]{1,0:T(8,128)(2,1)} %get-tuple-element.124.x_ref), custom_call_target="tpu_custom_call" | custom-call | bytes 83886080 | tf_op jit(solution)/shard_map/pallas_call | solution.py:297
  488.2 4.6 convolution_convert_fusion.1
  496.3 3.7 convolution_convert_fusion.2
  501.7 33.0 %while.16 = (s32[]{:T(128)}, f32[1024,2,128]{0,2,1:T(8,128)}, f32[1024,2,128]{0,2,1:T(8,128)}, bf16[2,512,2,128]{3,1,0,2:T(8,128)(2,1)}, bf16[2,512,2,128]{3,2,1...) while((s32[]{:T(128)}, f32[1024,2,128]{0,2,1:T(8,128)}, ...), condition=%wide.region_4.5_spmd.clone, body=%wide.region_2.0_spmd.clone.sunk | while | flops 1360002048 | bytes 79468808 | solution.py:1643
  505.3 3.1 multiply_reduce_fusion.4
  520.9 3.1 multiply_reduce_fusion.4
  528.2 3.7 fusion.105
  547.6 3.0 concatenate.55
  550.6 3.2 multiply_reduce_fusion.1
  558.2 6.9 shard_map.224
  572.0 5.1 convolution_convert_fusion
  577.1 8.2 fusion.32
  589.7 40.2 %collective-permute-done.2 = bf16[4,80,2048]{2,1,0:T(8,128)(2,1)S(1)} collective-permute-done((bf16[4,80,2048]{2,1,0:T(8,128)(2,1)S(1)}, bf16[4,80,2048]{2,1,0:T(8,128)(2,1)S(1)}, u32[]{:S(2)}, u32[]{:S(2)}) %collective-permute-start.2) | collective-permute-done | bytes 1310752 | tf_op jit(solution)/shard_map/ppermute | solution.py:1594
  629.9 33.5 %collective-permute-done.1 = bf16[4,80,2048]{2,1,0:T(8,128)(2,1)S(1)} collective-permute-done((bf16[4,80,2048]{2,1,0:T(8,128)(2,1)S(1)}, bf16[4,80,2048]{2,1,0:T(8,128)(2,1)S(1)}, u32[]{:S(2)}, u32[]{:S(2)}) %collective-permute-start.1) | collective-permute-done | bytes 1310752 | tf_op jit(solution)/shard_map/ppermute | solution.py:1594
  663.5 4.0 fusion.35
  667.5 3.8 constant_dynamic-slice_fusion.9
  693.9 61.8 %shard_map.225 = f32[128,2048]{1,0:T(8,128)} custom-call(bf16[8,128,768]{2,1,0:T(8,128)(2,1)} %pad_maximum_fusion.1.a_ref, bf16[2048,768]{1,0:T(8,128)(2,1)} %pad_maximum_fusion.b_ref), custom_call_target="tpu_custom_call" | custom-call | flops 3221225472 | bytes 83886080 | tf_op jit(solution)/shard_map/pallas_call | solution.py:346
  758.8 22.3 %shard_map.226 = f32[40,2048]{1,0:T(8,128)} custom-call(f32[40,2048]{1,0:T(8,128)} %concatenate.57.x_ref), custom_call_target="tpu_custom_call" | custom-call | tf_op jit(solution)/shard_map/pallas_call | solution.py:482
  792.5 4.5 broadcast_in_dim.148
  811.5 12.9 %collective-permute-done.8 = bf16[512,1024]{1,0:T(8,128)(2,1)S(1)} collective-permute-done((bf16[512,1024]{1,0:T(8,128)(2,1)S(1)}, bf16[512,1024]{1,0:T(8,128)(2,1)S(1)}, u32[]{:S(2)}, u32[]{:S(2)}) %collective-permute-start.8) | collective-permute-done | bytes 1048608 | tf_op jit(solution)/shard_map/ppermute | solution.py:1480
  824.7 22.4 %collective-permute-done.9 = bf16[1024,512]{1,0:T(8,128)(2,1)S(1)} collective-permute-done((bf16[1024,512]{1,0:T(8,128)(2,1)S(1)}, bf16[1024,512]{1,0:T(8,128)(2,1)S(1)}, u32[]{:S(2)}, u32[]{:S(2)}) %collective-permute-start.9) | collective-permute-done | bytes 1048608 | tf_op jit(solution)/shard_map/ppermute | solution.py:1480
  853.3 16.1 %collective-permute-done.11 = bf16[1024,512]{1,0:T(8,128)(2,1)S(1)} collective-permute-done((bf16[1024,512]{1,0:T(8,128)(2,1)S(1)}, bf16[1024,512]{1,0:T(8,128)(2,1)S(1)}, u32[]{:S(2)}, u32[]{:S(2)}) %collective-permute-start.11) | collective-permute-done | bytes 1048608 | tf_op jit(solution)/shard_map/ppermute | solution.py:1480
  (216 shorter events, 133.4 us)
Async XLA Ops:
  7.2 11.5 %copy-start.32 = (s32[1024]{0:T(1024)S(1)}, s32[1024]{0:T(1024)}, u32[]{:S(2)}) copy-start(s32[1024]{0:T(1024)} %param.28) | copy-start | bytes 12292
  7.2 863.8 %reduce-scatter.8.cloned.1.call-start = ((), (), s32[]{:S(2)}) async-start(), calls=%async_computation.5 | async-start | bytes 1310720 | tf_op jit(solution)/shard_map/reduce_scatter | solution.py:1680
  8.0 10.7 %copy-start.33 = (f32[4,2048]{1,0:T(4,128)}, f32[4,2048]{1,0:T(4,128)S(1)}, u32[]{:S(2)}) copy-start(f32[4,2048]{1,0:T(4,128)S(1)} %convert_element_type.123.gains_ref) | copy-start | bytes 98308
  9.9 261.7 %copy-start.11 = (f32[1024,64]{1,0:T(8,128)}, f32[1024,64]{1,0:T(8,128)S(1)}, u32[]{:S(2)}) copy-start(f32[1024,64]{1,0:T(8,128)S(1)} %get-tuple-element.266) | copy-start | bytes 786436
  447.5 40.8 %copy-start.36 = (bf16[1024,256]{1,0:T(8,128)(2,1)S(1)}, bf16[1024,256]{1,0:T(8,128)(2,1)}, u32[]{:S(2)}) copy-start(bf16[1024,256]{1,0:T(8,128)(2,1)} %get-tuple-element.135) | copy-start | bytes 1572868
  492.9 380.0 %reduce-scatter.6.cloned.1.call-start = ((), (), s32[]{:S(2)}) async-start(), calls=%async_computation.4 | async-start | bytes 3932160 | tf_op jit(solution)/shard_map/reduce_scatter | solution.py:1677
  577.0 298.1 %reduce-scatter.4.cloned.1.call-start = ((), (), s32[]{:S(2)}) async-start(), calls=%async_computation.3 | async-start | bytes 4718592 | tf_op jit(solution)/shard_map/reduce_scatter | solution.py:1602
  585.3 78.2 %copy-start.38 = (bf16[4,320,256]{2,1,0:T(8,128)(2,1)S(1)}, bf16[4,320,256]{2,1,0:T(8,128)(2,1)}, u32[]{:S(2)}) copy-start(bf16[4,320,256]{2,1,0:T(8,128)(2,1)} %get-tuple-element.117) | copy-start | bytes 1966084
  586.2 43.8 %collective-permute-start.2 = (bf16[4,80,2048]{2,1,0:T(8,128)(2,1)S(1)}, bf16[4,80,2048]{2,1,0:T(8,128)(2,1)S(1)}, u32[]{:S(2)}, u32[]{:S(2)}) collective-permute-start(bf16[4,80,2048]{2,1,0:T(8,128)(2,1)S(1)} %get-tuple-element.230), channel_id=1, source_target_pairs={{0,24},{8,16},{16,8},{24,0},{1,25},{9,17},{17,9},{25,1},{2,26},{10... | collective-permute-start | bytes 3932168 | tf_op jit(solution)/shard_map/ppermute | solution.py:1594
  587.6 75.8 %collective-permute-start.1 = (bf16[4,80,2048]{2,1,0:T(8,128)(2,1)S(1)}, bf16[4,80,2048]{2,1,0:T(8,128)(2,1)S(1)}, u32[]{:S(2)}, u32[]{:S(2)}) collective-permute-start(bf16[4,80,2048]{2,1,0:T(8,128)(2,1)S(1)} %get-tuple-element.231), channel_id=1, source_target_pairs={{0,16},{8,24},{16,0},{24,8},{1,17},{9,25},{17,1},{25,9},{2,18},{10... | collective-permute-start | bytes 3932168 | tf_op jit(solution)/shard_map/ppermute | solution.py:1594
  587.7 75.7 %collective-permute-start = (bf16[4,80,2048]{2,1,0:T(8,128)(2,1)S(1)}, bf16[4,80,2048]{2,1,0:T(8,128)(2,1)S(1)}, u32[]{:S(2)}, u32[]{:S(2)}) collective-permute-start(bf16[4,80,2048]{2,1,0:T(8,128)(2,1)S(1)} %get-tuple-element.232), channel_id=1, source_target_pairs={{0,8},{8,0},{16,24},{24,16},{1,9},{9,1},{17,25},{25,17},{2,10},{10... | collective-permute-start | bytes 3932168 | tf_op jit(solution)/shard_map/ppermute | solution.py:1594
  671.3 127.2 %collective-permute-start.3 = (bf16[512,1024]{1,0:T(8,128)(2,1)}, bf16[512,1024]{1,0:T(8,128)(2,1)}, u32[]{:S(2)}, u32[]{:S(2)}) collective-permute-start(bf16[512,1024]{1,0:T(8,128)(2,1)} %get-tuple-element.241), channel_id=1, source_target_pairs={{0,8},{8,16},{16,24},{24,0},{1,9},{9,17},{17,25},{25,1},{2,10},{10... | collective-permute-start | bytes 3145736 | tf_op jit(solution)/shard_map/ppermute | solution.py:1480
  672.7 130.9 %collective-permute-start.4 = (bf16[512,1024]{1,0:T(8,128)(2,1)}, bf16[512,1024]{1,0:T(8,128)(2,1)}, u32[]{:S(2)}, u32[]{:S(2)}) collective-permute-start(bf16[512,1024]{1,0:T(8,128)(2,1)} %get-tuple-element.240), channel_id=1, source_target_pairs={{0,16},{8,24},{16,0},{24,8},{1,17},{9,25},{17,1},{25,9},{2,18},{10... | collective-permute-start | bytes 3145736 | tf_op jit(solution)/shard_map/ppermute | solution.py:1480
  673.3 136.8 %collective-permute-start.5 = (bf16[512,1024]{1,0:T(8,128)(2,1)}, bf16[512,1024]{1,0:T(8,128)(2,1)}, u32[]{:S(2)}, u32[]{:S(2)}) collective-permute-start(bf16[512,1024]{1,0:T(8,128)(2,1)} %get-tuple-element.239), channel_id=1, source_target_pairs={{0,24},{8,0},{16,8},{24,16},{1,25},{9,1},{17,9},{25,17},{2,26},{10... | collective-permute-start | bytes 3145736 | tf_op jit(solution)/shard_map/ppermute | solution.py:1480
  677.4 123.7 %collective-permute-start.6 = (bf16[512,1024]{1,0:T(8,128)(2,1)}, bf16[512,1024]{1,0:T(8,128)(2,1)}, u32[]{:S(2)}, u32[]{:S(2)}) collective-permute-start(bf16[512,1024]{1,0:T(8,128)(2,1)} %get-tuple-element.238), channel_id=1, source_target_pairs={{0,8},{8,16},{16,24},{24,0},{1,9},{9,17},{17,25},{25,1},{2,10},{10... | collective-permute-start | bytes 3145736 | tf_op jit(solution)/shard_map/ppermute | solution.py:1480
  677.4 128.7 %collective-permute-start.7 = (bf16[512,1024]{1,0:T(8,128)(2,1)}, bf16[512,1024]{1,0:T(8,128)(2,1)}, u32[]{:S(2)}, u32[]{:S(2)}) collective-permute-start(bf16[512,1024]{1,0:T(8,128)(2,1)} %get-tuple-element.237), channel_id=1, source_target_pairs={{0,16},{8,24},{16,0},{24,8},{1,17},{9,25},{17,1},{25,9},{2,18},{10... | collective-permute-start | bytes 3145736 | tf_op jit(solution)/shard_map/ppermute | solution.py:1480
  693.9 87.2 %copy-start.24 = (f32[128,2048]{1,0:T(8,128)S(1)}, f32[128,2048]{1,0:T(8,128)}, u32[]{:S(2)}) copy-start(f32[128,2048]{1,0:T(8,128)} %get-tuple-element.119) | copy-start | bytes 3145732
  798.5 25.9 %collective-permute-start.8 = (bf16[512,1024]{1,0:T(8,128)(2,1)S(1)}, bf16[512,1024]{1,0:T(8,128)(2,1)S(1)}, u32[]{:S(2)}, u32[]{:S(2)}) collective-permute-start(bf16[512,1024]{1,0:T(8,128)(2,1)S(1)} %copy-done.25), channel_id=1, source_target_pairs={{0,24},{8,0},{16,8},{24,16},{1,25},{9,1},{17,9},{25,17},{2,26},{10... | collective-permute-start | bytes 3145736 | tf_op jit(solution)/shard_map/ppermute | solution.py:1480
  801.1 46.0 %collective-permute-start.9 = (bf16[1024,512]{1,0:T(8,128)(2,1)S(1)}, bf16[1024,512]{1,0:T(8,128)(2,1)S(1)}, u32[]{:S(2)}, u32[]{:S(2)}) collective-permute-start(bf16[1024,512]{1,0:T(8,128)(2,1)S(1)} %get-tuple-element.235), channel_id=1, source_target_pairs={{0,8},{8,16},{16,24},{24,0},{1,9},{9,17},{17,25},{25,1},{2,10},{10... | collective-permute-start | bytes 3145736 | tf_op jit(solution)/shard_map/ppermute | solution.py:1480
  803.5 48.1 %collective-permute-start.10 = (bf16[1024,512]{1,0:T(8,128)(2,1)S(1)}, bf16[1024,512]{1,0:T(8,128)(2,1)S(1)}, u32[]{:S(2)}, u32[]{:S(2)}) collective-permute-start(bf16[1024,512]{1,0:T(8,128)(2,1)S(1)} %get-tuple-element.234), channel_id=1, source_target_pairs={{0,16},{8,24},{16,0},{24,8},{1,17},{9,25},{17,1},{25,9},{2,18},{10... | collective-permute-start | bytes 3145736 | tf_op jit(solution)/shard_map/ppermute | solution.py:1480
  806.1 63.3 %collective-permute-start.11 = (bf16[1024,512]{1,0:T(8,128)(2,1)S(1)}, bf16[1024,512]{1,0:T(8,128)(2,1)S(1)}, u32[]{:S(2)}, u32[]{:S(2)}) collective-permute-start(bf16[1024,512]{1,0:T(8,128)(2,1)S(1)} %get-tuple-element.233), channel_id=1, source_target_pairs={{0,24},{8,0},{16,8},{24,16},{1,25},{9,1},{17,9},{25,17},{2,26},{10... | collective-permute-start | bytes 3145736 | tf_op jit(solution)/shard_map/ppermute | solution.py:1480
  811.5 41.8 %copy-start.8 = (f32[4,512,1024]{2,1,0:T(8,128)}, f32[4,512,1024]{2,1,0:T(8,128)S(1)}, u32[]{:S(2)}) copy-start(f32[4,512,1024]{2,1,0:T(8,128)S(1)} %convert_dynamic-update-slice_fusion.8) | copy-start | bytes 25165828
  824.7 44.7 %copy-start.9 = (f32[4,512,1024]{2,1,0:T(8,128)}, f32[4,512,1024]{2,1,0:T(8,128)S(1)}, u32[]{:S(2)}) copy-start(f32[4,512,1024]{2,1,0:T(8,128)S(1)} %convert_dynamic-update-slice_fusion.4) | copy-start | bytes 25165828
  853.3 21.8 %copy-start.21 = (f32[128,2048]{1,0:T(8,128)S(1)}, f32[128,2048]{1,0:T(8,128)}, u32[]{:S(2)}) copy-start(f32[128,2048]{1,0:T(8,128)} %get-tuple-element.109.residual_ref) | copy-start | bytes 3145732
  (34 other events, 138.5 us)
Sparse Core Ops, SparseCore 0:
  493.0 25.6 reduce-scatter.7
  577.2 89.4 reduce-scatter.5
  669.1 58.0 reduce-scatter.3

commit v5 on v4

--- a/solution.py
+++ b/solution.py
@@ -1,5 +1,4 @@
 import functools
-import math
 
 import jax
 import jax.numpy as jnp
@@ -23,50 +22,6 @@
     frequency = THETA ** (-jnp.arange(half_dim, dtype=jnp.float32) / half_dim)
     angles = positions.astype(jnp.float32)[:, None] * frequency[None, :]
     return (jnp.cos(angles), jnp.sin(angles))
-
-
-def rotate(values_in, cosine_table, sine_table, head_size):
-    row_count = values_in.shape[0]
-    pieces = values_in.reshape(row_count, -1, head_size)
-    half_dim = head_size // 2
-    former = pieces[..., :half_dim]
-    latter = pieces[..., half_dim:]
-    cosine_wide = cosine_table[:, None, :]
-    sine_wide = sine_table[:, None, :]
-    turned = jnp.concatenate(
-        [former * cosine_wide - latter * sine_wide, latter * cosine_wide + former * sine_wide], -1
-    )
-    return turned.reshape(row_count, -1)
-
-
-def inverse_rms(values_in):
-    return lax.rsqrt(jnp.mean(values_in * values_in, -1, keepdims=True) + EPSILON)
-
-
-def norm_back(grad_unit, unit_values, inverse):
-    return inverse * (
-        grad_unit - unit_values * jnp.mean(grad_unit * unit_values, -1, keepdims=True)
-    )
-
-
-def greet_chain(chip, core, chips):
-    barrier = pltpu.get_barrier_semaphore()
-
-    def greet(target):
-        pl.semaphore_signal(barrier, inc=1, device_id={"seq": target})
-
-    greet(chip * 2 + 1 - core)
-
-    @pl.when(chip < chips - 1)
-    def _():
-        greet(chip * 2 + 2 + core)
-
-    @pl.when(chip > 0)
-    def _():
-        greet(chip * 2 - 2 + core)
-
-    inner = jnp.where(chip < chips - 1, 1, 0) + jnp.where(chip > 0, 1, 0)
-    pl.semaphore_wait(barrier, 1 + inner)
 
 
 class ChainGather:
@@ -219,7 +174,7 @@
         dest = self.chip + (1 - 2 * lax.rem(index, 2)) * distance
         return dest, (dest >= 0) & (dest < self.chips)
 
-    def run(self, product):
+    def run(self, product, between=None):
         chips, chip, core, total = self.chips, self.chip, self.core, self.total
         sibling = chip * 2 + 1 - core
 
@@ -234,6 +189,9 @@
 
                 product(dest * 2 + 1 - core, store)
                 self.side_copy(dest).start()
+
+        if between:
+            between()
 
         @pl.loop(0, 2 * chips - 1)
         def _(index):
@@ -281,222 +239,6 @@
             def _():
                 self.chain_copy(0, dest, sibling).wait_send()
 
-
-def gather_kernel(chips, x_ref, out_ref, local_sem, sends, arrivals):
-    gather = ChainGather(chips, x_ref, out_ref, local_sem, sends, arrivals)
-    greet_chain(gather.chip, gather.core, chips)
-    gather.start()
-    gather.steps()
-    gather.landed()
-    gather.sent()
-
-
-def seq_gather(x, size, which):
-    chips = size // 2
-    rows, width = x.shape
-    return pl.pallas_call(
-        functools.partial(gather_kernel, chips),
-        out_shape=jax.ShapeDtypeStruct((size * rows, width), x.dtype),
-        in_specs=[pl.BlockSpec(memory_space=pl.ANY)],
-        out_specs=pl.BlockSpec(memory_space=pl.ANY),
-        scratch_shapes=[
-            pltpu.SemaphoreType.DMA,
-            pltpu.SemaphoreType.DMA((3, chips)),
-            pltpu.SemaphoreType.DMA((2, chips)),
-        ],
-        compiler_params=pltpu.CompilerParams(collective_id=which, has_side_effects=True),
-        cost_estimate=pl.CostEstimate(
-            flops=0, bytes_accessed=40 * x.size * x.dtype.itemsize * chips, transcendentals=0
-        ),
-    )(x)
-
-
-def reduce_kernel(chips, shared, turned, a_ref, b_ref, o_ref, *buffers):
-    rows, width = o_ref.shape
-    step_cols = min(512, width)
-    reduce = ChainReduce(chips, o_ref, buffers)
-    greet_chain(reduce.chip, reduce.core, chips)
-
-    def product(block, store):
-        left = a_ref[block]
-
-        @pl.loop(0, width // step_cols)
-        def _(index):
-            cols = pl.ds(pl.multiple_of(index * step_cols, step_cols), step_cols)
-            right_ref = b_ref if shared else b_ref.at[block]
-            if turned:
-                part = lax.dot_general(
-                    left,
-                    right_ref[cols, :],
-                    (((1,), (1,)), ((), ())),
-                    preferred_element_type=jnp.float32,
-                )
-            else:
-                part = jnp.dot(left, right_ref[:, cols], preferred_element_type=jnp.float32)
-            store(cols, part)
-
-    reduce.run(product)
-    reduce.sent()
-
-
-def seq_reduce(a, b, width, turned, which):
-    size, rows, depth = a.shape
-    chips = size // 2
-    half = jnp.bfloat16
-    return pl.pallas_call(
-        functools.partial(reduce_kernel, chips, b.ndim == 2, turned),
-        out_shape=jax.ShapeDtypeStruct((rows, width), jnp.float32),
-        in_specs=[pl.BlockSpec(memory_space=pltpu.VMEM)] * 2,
-        out_specs=pl.BlockSpec(memory_space=pltpu.VMEM),
-        scratch_shapes=ChainReduce.scratch(chips, rows, width),
-        compiler_params=pltpu.CompilerParams(
-            collective_id=which, has_side_effects=True, vmem_limit_bytes=56 * 2**20
-        ),
-        cost_estimate=pl.CostEstimate(
-            flops=2 * size * rows * depth * width,
-            bytes_accessed=40 * rows * width * size,
-            transcendentals=0,
-        ),
-    )(a, b)
-
-
-def swap_kernel(size, summed, x_ref, o_ref, landing, send_sem, recv_sem):
-    me = lax.axis_index("seq")
-    barrier = pltpu.get_barrier_semaphore()
-    for shift in range(1, size):
-        pl.semaphore_signal(barrier, inc=1, device_id={"seq": lax.rem(me + shift, size)})
-    pl.semaphore_wait(barrier, size - 1)
-
-    def copy(shift):
-        peer = lax.rem(me + shift, size)
-        return pltpu.make_async_remote_copy(
-            src_ref=x_ref if summed else x_ref.at[peer],
-            dst_ref=landing.at[me],
-            send_sem=send_sem.at[shift],
-            recv_sem=recv_sem.at[shift],
-            device_id={"seq": peer},
-        )
-
-    for shift in range(1, size):
-        copy(shift).start()
-    landing[me] = x_ref[...] if summed else x_ref[me]
-    for shift in range(1, size):
-        copy(shift).wait()
-    if summed:
-        o_ref[...] = jnp.sum(landing[...], 0)
-    else:
-        o_ref[...] = landing[...]
-
-
-def seq_swap(x, size, summed, which):
-    piece = x.shape if summed else x.shape[1:]
-    return pl.pallas_call(
-        functools.partial(swap_kernel, size, summed),
-        out_shape=jax.ShapeDtypeStruct(x.shape, x.dtype),
-        in_specs=[pl.BlockSpec(memory_space=pltpu.VMEM)],
-        out_specs=pl.BlockSpec(memory_space=pltpu.VMEM),
-        scratch_shapes=[
-            pltpu.VMEM((size, *piece), x.dtype),
-            pltpu.SemaphoreType.DMA((size,)),
-            pltpu.SemaphoreType.DMA((size,)),
-        ],
-        compiler_params=pltpu.CompilerParams(collective_id=which, has_side_effects=True),
-    )(x)
-
-
-def seq_sum(pair, size, which):
-    both = jnp.concatenate(pair).reshape(-1, 128)
-    return seq_swap(both, size, True, which).reshape(2, -1)
-
-
-def total_kernel(
-    size, split, x_ref, o_ref, first, second, final, send_one, recv_one, send_two, recv_two, send_three, recv_three
-):
-    me, mine = lax.axis_index("seq"), lax.axis_index("fsdp")
-    part = x_ref.shape[1] // size
-    barrier = pltpu.get_barrier_semaphore()
-    for shift in range(1, size):
-        pl.semaphore_signal(barrier, inc=1, device_id={"seq": lax.rem(me + shift, size)})
-    for shift in range(1, split):
-        pl.semaphore_signal(barrier, inc=1, device_id={"fsdp": lax.rem(mine + shift, split)})
-    pl.semaphore_wait(barrier, size + split - 2)
-
-    def columns(index):
-        return pl.ds(pl.multiple_of(index * part, part), part)
-
-    def scatter(shift):
-        peer = lax.rem(me + shift, size)
-        return pltpu.make_async_remote_copy(
-            src_ref=x_ref.at[:, columns(peer)],
-            dst_ref=first.at[me],
-            send_sem=send_one.at[shift],
-            recv_sem=recv_one.at[shift],
-            device_id={"seq": peer},
-        )
-
-    def share(shift):
-        return pltpu.make_async_remote_copy(
-            src_ref=second.at[mine],
-            dst_ref=second.at[mine],
-            send_sem=send_two.at[shift],
-            recv_sem=recv_two.at[shift],
-            device_id={"fsdp": lax.rem(mine + shift, split)},
-        )
-
-    def collect(shift):
-        return pltpu.make_async_remote_copy(
-            src_ref=final.at[me],
-            dst_ref=final.at[me],
-            send_sem=send_three.at[shift],
-            recv_sem=recv_three.at[shift],
-            device_id={"seq": lax.rem(me + shift, size)},
-        )
-
-    for shift in range(1, size):
-        scatter(shift).start()
-    first[me] = x_ref[:, columns(me)]
-    for shift in range(1, size):
-        scatter(shift).wait_recv()
-    second[mine] = jnp.sum(first[...], 0)
-    for shift in range(1, split):
-        share(shift).start()
-    for shift in range(1, split):
-        share(shift).wait_recv()
-    final[me] = jnp.sum(second[...], 0)
-    for shift in range(1, size):
-        collect(shift).start()
-    for shift in range(1, size):
-        scatter(shift).wait_send()
-    for shift in range(1, split):
-        share(shift).wait_send()
-    for shift in range(1, size):
-        collect(shift).wait()
-    for index in range(size):
-        o_ref[:, index * part : (index + 1) * part] = final[index]
-
-
-def total_sum(x, size, split, which):
-    rows, width = x.shape
-    part = width // size
-    kind = pltpu.SemaphoreType.DMA
-    return pl.pallas_call(
-        functools.partial(total_kernel, size, split),
-        out_shape=jax.ShapeDtypeStruct(x.shape, x.dtype),
-        in_specs=[pl.BlockSpec(memory_space=pltpu.VMEM)],
-        out_specs=pl.BlockSpec(memory_space=pltpu.VMEM),
-        scratch_shapes=[
-            pltpu.VMEM((size, rows, part), x.dtype),
-            pltpu.VMEM((split, rows, part), x.dtype),
-            pltpu.VMEM((size, rows, part), x.dtype),
-            kind((size,)),
-            kind((size,)),
-            kind((split,)),
-            kind((split,)),
-            kind((size,)),
-            kind((size,)),
-        ],
-        compiler_params=pltpu.CompilerParams(collective_id=which, has_side_effects=True),
-    )(x)
 
 def partner_of(index, move):
     turned, bit = index, 1
@@ -952,6 +694,50 @@
         choice,
     )
 
+class ShardSend:
+    def __init__(self, split, source, landing, local_sem, sends, arrivals):
+        self.split, self.source, self.landing = split, source, landing
+        self.local_sem, self.sends, self.arrivals = local_sem, sends, arrivals
+        self.mine = lax.axis_index("fsdp")
+
+    def copy(self, shift):
+        dest = lax.rem(self.mine + shift, self.split)
+        return pltpu.make_async_remote_copy(
+            src_ref=self.source(dest),
+            dst_ref=self.landing.at[self.mine],
+            send_sem=self.sends.at[shift],
+            recv_sem=self.arrivals.at[shift],
+            device_id={"fsdp": dest},
+        )
+
+    def own(self):
+        return pltpu.make_async_copy(
+            self.source(self.mine), self.landing.at[self.mine], self.local_sem
+        )
+
+    def start(self):
+        for shift in range(1, self.split):
+            self.copy(shift).start()
+        self.own().start()
+
+    def wait(self):
+        for shift in range(1, self.split):
+            self.copy(shift).wait()
+        self.own().wait()
+
+
+def turned_dot(left, right):
+    return lax.dot_general(
+        left, right, (((0,), (0,)), ((), ())), preferred_element_type=jnp.float32
+    )
+
+
+def cross_dot(left, right):
+    return lax.dot_general(
+        left, right, (((1,), (1,)), ((), ())), preferred_element_type=jnp.float32
+    )
+
+
 def experts_kernel(
     sizes,
     routed_ref,
@@ -973,7 +759,7 @@
     hidden_out,
     grad_gate_ref,
     grad_up_ref,
-    grad_down_ref,
+    down_landing,
     gate_full,
     up_full,
     down_full,
@@ -1006,6 +792,8 @@
     dots_recv,
     token_send,
     token_recv,
+    down_send,
+    down_recv,
     *reduce_buffers,
 ):
     size, split, chips, experts_local = sizes
@@ -1230,11 +1018,6 @@
     def flat(ref, cols):
         return ref[:, :, :, cols].reshape(total_rows, -1)
 
-    def turned_dot(left, right):
-        return lax.dot_general(
-            left, right, (((0,), (0,)), ((), ())), preferred_element_type=f32
-        )
-
     every = pl.ds(0, hidden_width)
 
     @pl.loop(0, split)
@@ -1247,11 +1030,19 @@
     grad_keeps = [
         pltpu.make_async_copy(source, target, load_sem.at[index])
         for index, (source, target) in enumerate(
-            ((gate_full, grad_gate_ref), (up_full, grad_up_ref), (down_full, grad_down_ref))
+            ((gate_full, grad_gate_ref), (up_full, grad_up_ref))
         )
     ]
     for keep in grad_keeps:
         keep.start()
+    down_send_all = ShardSend(
+        split,
+        lambda dest: down_full.at[:, pl.ds(pl.multiple_of(dest * part, part), part)],
+        down_landing,
+        load_sem.at[2],
+        down_send,
+        down_recv,
+    )
 
     for move in order:
         dots_copy(move).wait()
@@ -1287,6 +1078,7 @@
     token_in[me] = token_out[me]
     for move in order:
         back_copy(move).wait()
+    down_send_all.start()
 
     reduce = ChainReduce(chips, residual_grad_ref, reduce_buffers)
 
@@ -1309,9 +1101,11 @@
     logit_grad = (own_gates * (grads - mean)).astype(half)
     routed_grad = reduce.total[...] + turned_dot(logit_grad, router_ref[...])
     own_load.wait()
-    router_grad_ref[...] = jnp.dot(
-        logit_grad, pair_rows[0, 0:tok_rows, :], preferred_element_type=f32
-    )
+    router_grad = jnp.dot(logit_grad, pair_rows[0, 0:tok_rows, :], preferred_element_type=f32)
+    for device in range(size):
+        router_grad_ref[device * experts_local : (device + 1) * experts_local, :] = router_grad[
+            device * 8 : device * 8 + experts_local
+        ]
     residual = residual_ref[...]
     inverse = lax.rsqrt(jnp.mean(residual * residual, -1, keepdims=True) + EPSILON)
     unit = residual * inverse
@@ -1329,6 +1123,7 @@
     hidden_keep.wait()
     for keep in grad_keeps:
         keep.wait()
+    down_send_all.wait()
 
 
 def experts(
@@ -1364,12 +1159,12 @@
             shape((tok_rows, model_width), f32),
             shape((tok_rows, model_width), half),
             shape((8, model_width), f32),
-            shape((size * 8, model_width), f32),
+            shape((size * experts_local, model_width), f32),
             shape(onehot.shape, half),
             shape(narrow_rows, half),
             shape(gate_full.shape, half),
             shape(up_full.shape, half),
-            shape(down_full.shape, half),
+            shape((split, hidden_width, model_width // split), half),
         ),
         in_specs=[anywhere, vmem, vmem, anywhere] + [vmem] * 4 + [anywhere] * 3,
         out_specs=tuple([vmem] * 5 + [anywhere] * 4),
@@ -1406,6 +1201,8 @@
             few,
             kind((size,)),
             kind((size,)),
+            kind((split,)),
+            kind((split,)),
             *ChainReduce.scratch(chips, tok_rows, model_width),
         ],
         compiler_params=pltpu.CompilerParams(
@@ -1429,6 +1226,534 @@
         up_full,
         down_full,
     )
+
+def back_kernel(
+    sizes,
+    out_grad_ref,
+    tokens_ref,
+    residual_grad_ref,
+    gains_ref,
+    gain_cols_ref,
+    second_gain_ref,
+    cos_ref,
+    sin_ref,
+    seg_col_ref,
+    seg_row_ref,
+    q_ref,
+    k_ref,
+    v_ref,
+    unit_ref,
+    sums_ref,
+    log_ref,
+    attended_ref,
+    qkv_ref,
+    rows_full_ref,
+    normed_ref,
+    hidden_ref,
+    down_ref,
+    grad_gate_ref,
+    input_grad_ref,
+    gains_out_ref,
+    qkv_grad_ref,
+    out_w_grad_ref,
+    mixed_rows,
+    gate_landing,
+    down_full,
+    out_grads,
+    attended_grad,
+    hidden,
+    returned,
+    key_total,
+    value_total,
+    scaled,
+    raw_grads,
+    centers_own,
+    centers_in,
+    qkv_stage,
+    qkv_landing,
+    out_stage,
+    out_landing,
+    load_sem,
+    gather_local,
+    gather_send,
+    gather_recv,
+    gate_local,
+    gate_send,
+    gate_recv,
+    rows_local,
+    rows_send,
+    rows_recv,
+    centers_send,
+    centers_recv,
+    qkv_local,
+    qkv_send,
+    qkv_recv,
+    out_local,
+    out_send,
+    out_recv,
+    *reduce_buffers,
+):
+    size, split, chips, experts_local = sizes
+    f32, half = jnp.float32, jnp.bfloat16
+    me, mine = lax.axis_index("seq"), lax.axis_index("fsdp")
+    tok_rows, model_width = tokens_ref.shape
+    length, local_width = q_ref.shape
+    hidden_width = down_ref.shape[0]
+    part = model_width // split
+    head = HEAD_DIM
+    heads = local_width // head
+    double = 2 * CAP
+    pairs = size // 2
+    rows_of = pairs * double
+
+    down_load = pltpu.make_async_copy(down_ref, down_full, load_sem.at[0])
+    hidden_load = pltpu.make_async_copy(hidden_ref, hidden, load_sem.at[1])
+    down_load.start()
+    hidden_load.start()
+    greet_all(size, split)
+    gather = ChainGather(chips, out_grad_ref, out_grads, gather_local, gather_send, gather_recv)
+    gather.start()
+    gate_send_all = ShardSend(
+        split,
+        lambda dest: grad_gate_ref.at[pl.ds(pl.multiple_of(dest * part, part), part)],
+        gate_landing,
+        gate_local,
+        gate_send,
+        gate_recv,
+    )
+
+    down_load.wait()
+    hidden_load.wait()
+    width_step = min(512, model_width)
+
+    def rows_target(move):
+        return mixed_rows.at[:, pl.ds(move * double, double), :]
+
+    def rows_copy(move):
+        return pltpu.make_async_remote_copy(
+            src_ref=returned.at[move],
+            dst_ref=rows_target(move),
+            send_sem=rows_send.at[move],
+            recv_sem=rows_recv.at[move],
+            device_id={"fsdp": partner_of(mine, move)},
+        )
+
+    own_rows = pltpu.make_async_copy(returned.at[0], rows_target(0), rows_local)
+    for move in range(experts_local - 1, -1, -1):
+
+        @pl.loop(0, model_width // width_step)
+        def _(index):
+            cols = pl.ds(pl.multiple_of(index * width_step, width_step), width_step)
+            made = jnp.dot(
+                hidden[move].reshape(rows_of, hidden_width),
+                down_full[:, cols],
+                preferred_element_type=f32,
+            )
+            returned[move, :, :, cols] = made.astype(half).reshape(pairs, double, width_step)
+
+        if move:
+            rows_copy(move).start()
+    own_rows.start()
+    gate_send_all.start()
+    gather.steps()
+    gather.landed()
+
+    block = min(512, length)
+
+    @pl.loop(0, length // block)
+    def _(step):
+        rows = pl.ds(pl.multiple_of(step * block, block), block)
+        total = cross_dot(out_grads[rows, 0:part], rows_full_ref[0])
+        for piece in range(1, split):
+            total += cross_dot(
+                out_grads[rows, piece * part : (piece + 1) * part], rows_full_ref[piece]
+            )
+        attended_grad[rows, :] = total.astype(half)
+
+    @pl.loop(0, split)
+    def _(piece):
+        cols = pl.ds(pl.multiple_of(piece * part, part), part)
+        out_stage[piece] = turned_dot(attended_ref[...], out_grads[:, cols]).astype(half)
+
+    out_send_all = ShardSend(
+        split, lambda dest: out_stage.at[dest], out_landing, out_local, out_send, out_recv
+    )
+    out_send_all.start()
+    gather.sent()
+    normed_load = pltpu.make_async_copy(normed_ref, out_grads, load_sem.at[0])
+    normed_load.start()
+
+    wide = min(256, length) if length <= 1024 else 128
+    scale = head**-0.5
+    for number in range(heads):
+        cols = slice(number * head, (number + 1) * head)
+        key_total[...] = jnp.zeros_like(key_total)
+        value_total[...] = jnp.zeros_like(value_total)
+
+        @pl.loop(0, length // wide)
+        def _(step):
+            rows = pl.ds(pl.multiple_of(step * wide, wide), wide)
+            scores = cross_dot(q_ref[rows, cols], k_ref[:, cols]) * scale
+            scores = jnp.where(seg_col_ref[rows, :] == seg_row_ref[...], scores, MASKED)
+            probs = jnp.exp(scores - log_ref[rows, cols][:, 0:1])
+            grads = attended_grad[rows, cols]
+            prob_grad = cross_dot(grads, v_ref[:, cols])
+            center = jnp.sum(probs * prob_grad, -1, keepdims=True)
+            score_grad = (probs * (prob_grad - center)).astype(half)
+            query_grad = jnp.dot(score_grad, k_ref[:, cols], preferred_element_type=f32) * scale
+            raw_grads[0, rows, cols] = query_grad.astype(half)
+            key_total[...] += turned_dot(score_grad, q_ref[rows, cols])
+            value_total[...] += turned_dot(probs.astype(half), grads)
+
+        raw_grads[1, :, cols] = (key_total[...] * scale).astype(half)
+        raw_grads[2, :, cols] = value_total[...].astype(half)
+
+    lanes = lax.broadcasted_iota(jnp.int32, (8, local_width), 0)
+    first_row, second_row = (lanes == 0).astype(f32), (lanes == 1).astype(f32)
+    gains_out_ref[...] = jnp.zeros_like(gains_out_ref)
+    own_cols = pl.ds(pl.multiple_of(me * local_width, local_width), local_width)
+    gains_out_ref[1:2, :] = second_gain_ref[0:1, :]
+
+    @pl.loop(0, length // block)
+    def _(step):
+        rows = pl.ds(pl.multiple_of(step * block, block), block)
+        found = jnp.zeros((8, block), f32)
+        for index, pick in ((0, first_row), (1, second_row)):
+            unit = unit_ref[index, rows, :]
+            pieces = []
+            for number in range(heads):
+                cols = slice(number * head, (number + 1) * head)
+                piece = raw_grads[index, rows, cols].astype(f32)
+                pieces.append(piece * cos_ref[rows, :] - turned_halves(piece) * sin_ref[rows, :])
+            unit_grad = pieces[0] if heads == 1 else jnp.concatenate(pieces, 1)
+            gains_out_ref[2 + index : 3 + index, own_cols] += jnp.sum(
+                unit_grad * unit, 0, keepdims=True
+            )
+            grown = unit_grad * gain_cols_ref[2 + index : 3 + index, :]
+            scaled[index, rows, :] = grown
+            found += row_sums(grown * unit, pick)
+        centers_own[:, rows] = found
+
+    def centers_copy(shift):
+        return pltpu.make_async_remote_copy(
+            src_ref=centers_own,
+            dst_ref=centers_in.at[me],
+            send_sem=centers_send.at[shift],
+            recv_sem=centers_recv.at[shift],
+            device_id={"seq": lax.rem(me + shift, size)},
+        )
+
+    for shift in range(1, size):
+        centers_copy(shift).start()
+    centers_in[me] = centers_own[...]
+    for shift in range(1, size):
+        centers_copy(shift).wait()
+    centers_own[...] = jnp.sum(centers_in[...], 0) * (1.0 / model_width)
+
+    @pl.loop(0, length // block)
+    def _(step):
+        rows = pl.ds(pl.multiple_of(step * block, block), block)
+        for index, pick in ((0, first_row), (1, second_row)):
+            inverse = lax.rsqrt(column_of(sums_ref[:, rows], pick) / model_width + EPSILON)
+            center = column_of(centers_own[:, rows], pick)
+            raw_grads[index, rows, :] = (
+                inverse * (scaled[index, rows, :] - unit_ref[index, rows, :] * center)
+            ).astype(half)
+
+    reduce = ChainReduce(chips, input_grad_ref, reduce_buffers)
+
+    def product(index, store):
+        rows = pl.ds(pl.multiple_of(index * tok_rows, tok_rows), tok_rows)
+
+        @pl.loop(0, model_width // width_step)
+        def _(step):
+            cols = pl.ds(pl.multiple_of(step * width_step, width_step), width_step)
+            total = cross_dot(raw_grads[0, rows, :], qkv_ref[0, cols, :])
+            total += cross_dot(raw_grads[1, rows, :], qkv_ref[1, cols, :])
+            total += cross_dot(raw_grads[2, rows, :], qkv_ref[2, cols, :])
+            store(cols, total)
+
+    qkv_send_all = ShardSend(
+        split, lambda dest: qkv_stage.at[dest], qkv_landing, qkv_local, qkv_send, qkv_recv
+    )
+
+    def between():
+        normed_load.wait()
+
+        @pl.loop(0, split)
+        def _(piece):
+            cols = pl.ds(pl.multiple_of(piece * part, part), part)
+            left = out_grads[:, cols]
+            for index in range(3):
+                qkv_stage[piece, index] = turned_dot(left, raw_grads[index]).astype(half)
+
+        qkv_send_all.start()
+
+    reduce.run(product, between)
+
+    inputs = tokens_ref[...].astype(f32)
+    inverse = lax.rsqrt(jnp.mean(inputs * inputs, -1, keepdims=True) + EPSILON)
+    unit = inputs * inverse
+    grads = input_grad_ref[...]
+    gains_out_ref[0:1, :] = jnp.sum(grads * unit, 0, keepdims=True)
+    grads = grads * gains_ref[0:1, :]
+    input_grad_ref[...] = residual_grad_ref[...] + inverse * (
+        grads - unit * jnp.mean(grads * unit, -1, keepdims=True)
+    )
+
+    out_send_all.wait()
+    total = out_landing[0].astype(f32)
+    for index in range(1, split):
+        total += out_landing[index].astype(f32)
+    out_w_grad_ref[...] = total
+    qkv_send_all.wait()
+    for index in range(3):
+        total = qkv_landing[0, index].astype(f32)
+        for piece in range(1, split):
+            total += qkv_landing[piece, index].astype(f32)
+        qkv_grad_ref[index] = total
+    reduce.sent()
+    own_rows.wait()
+    for move in range(1, experts_local):
+        rows_copy(move).wait()
+    gate_send_all.wait()
+
+
+def back(sizes, out_grad, tokens, residual_grad, gains, kept, big_ones, which):
+    size, split, chips, experts_local = sizes
+    f32, half = jnp.float32, jnp.bfloat16
+    tok_rows, model_width = tokens.shape
+    query_heads, qkv_stack, out_stack = kept[4], kept[11], kept[12]
+    length, local_width = query_heads.shape
+    normed_seq, hidden, down_full, grad_gate = big_ones
+    hidden_width = down_full.shape[0]
+    part = model_width // split
+    vmem = pl.BlockSpec(memory_space=pltpu.VMEM)
+    anywhere = pl.BlockSpec(memory_space=pl.ANY)
+    kind = pltpu.SemaphoreType.DMA
+    shape = jax.ShapeDtypeStruct
+    few, fsdp = kind((experts_local,)), kind((split,))
+    return pl.pallas_call(
+        functools.partial(back_kernel, sizes),
+        out_shape=(
+            shape((tok_rows, model_width), f32),
+            shape((8, model_width), f32),
+            shape((3, part, local_width), f32),
+            shape((local_width, part), f32),
+            shape((size // 2, experts_local * 2 * CAP, model_width), half),
+            shape((split, part, hidden_width), half),
+        ),
+        in_specs=[vmem] * 19 + [anywhere] * 4,
+        out_specs=tuple([vmem] * 4 + [anywhere] * 2),
+        scratch_shapes=[
+            pltpu.VMEM(down_full.shape, half),
+            pltpu.VMEM((length, model_width), half),
+            pltpu.VMEM((length, local_width), half),
+            pltpu.VMEM(hidden.shape, half),
+            pltpu.VMEM((experts_local, size // 2, 2 * CAP, model_width), half),
+            pltpu.VMEM((length, HEAD_DIM), f32),
+            pltpu.VMEM((length, HEAD_DIM), f32),
+            pltpu.VMEM((2, length, local_width), f32),
+            pltpu.VMEM((3, length, local_width), half),
+            pltpu.VMEM((8, length), f32),
+            pltpu.VMEM((size, 8, length), f32),
+            pltpu.VMEM((split, 3, part, local_width), half),
+            pltpu.VMEM((split, 3, part, local_width), half),
+            pltpu.VMEM((split, local_width, part), half),
+            pltpu.VMEM((split, local_width, part), half),
+            kind((2,)),
+            kind,
+            kind((3, chips)),
+            kind((2, chips)),
+            kind,
+            fsdp,
+            fsdp,
+            kind,
+            few,
+            few,
+            kind((size,)),
+            kind((size,)),
+            kind,
+            fsdp,
+            fsdp,
+            kind,
+            fsdp,
+            fsdp,
+            *ChainReduce.scratch(chips, tok_rows, model_width),
+        ],
+        compiler_params=pltpu.CompilerParams(
+            collective_id=which, has_side_effects=True, vmem_limit_bytes=63 * 2**20
+        ),
+        cost_estimate=pl.CostEstimate(
+            flops=2 * length * model_width * local_width * 8,
+            bytes_accessed=500 * 2**20,
+            transcendentals=0,
+        ),
+    )(out_grad, tokens, residual_grad, *gains, *kept, *big_ones)
+
+
+def close_kernel(
+    sizes,
+    mixed_rows_ref,
+    combine_ref,
+    residual_ref,
+    gains_ref,
+    router_ref,
+    grad_up_ref,
+    output_ref,
+    small_ref,
+    up_landing,
+    total,
+    small,
+    first,
+    second,
+    final,
+    up_local,
+    up_send,
+    up_recv,
+    send_one,
+    recv_one,
+    send_two,
+    recv_two,
+    send_three,
+    recv_three,
+    *reduce_buffers,
+):
+    size, split, chips, experts_local = sizes
+    f32 = jnp.float32
+    me, mine = lax.axis_index("seq"), lax.axis_index("fsdp")
+    tok_rows, model_width = residual_ref.shape
+    part = model_width // split
+    slice_width = model_width // size
+    experts_all = router_ref.shape[0]
+    small[0:8, :] = gains_ref[...]
+    small[8 : 8 + experts_all, :] = router_ref[...]
+    greet_all(size, split)
+    up_send_all = ShardSend(
+        split,
+        lambda dest: grad_up_ref.at[pl.ds(pl.multiple_of(dest * part, part), part)],
+        up_landing,
+        up_local,
+        up_send,
+        up_recv,
+    )
+    up_send_all.start()
+
+    def columns(index):
+        return pl.ds(pl.multiple_of(index * slice_width, slice_width), slice_width)
+
+    def scatter(shift):
+        peer = lax.rem(me + shift, size)
+        return pltpu.make_async_remote_copy(
+            src_ref=small.at[:, columns(peer)],
+            dst_ref=first.at[me],
+            send_sem=send_one.at[shift],
+            recv_sem=recv_one.at[shift],
+            device_id={"seq": peer},
+        )
+
+    def share(shift):
+        return pltpu.make_async_remote_copy(
+            src_ref=second.at[mine],
+            dst_ref=second.at[mine],
+            send_sem=send_two.at[shift],
+            recv_sem=recv_two.at[shift],
+            device_id={"fsdp": lax.rem(mine + shift, split)},
+        )
+
+    def collect(shift):
+        return pltpu.make_async_remote_copy(
+            src_ref=final.at[me],
+            dst_ref=final.at[me],
+            send_sem=send_three.at[shift],
+            recv_sem=recv_three.at[shift],
+            device_id={"seq": lax.rem(me + shift, size)},
+        )
+
+    for shift in range(1, size):
+        scatter(shift).start()
+    first[me] = small[:, columns(me)]
+
+    reduce = ChainReduce(chips, total, reduce_buffers)
+    width_step = min(512, model_width)
+
+    def product(index, store):
+        side = pl.ds(pl.multiple_of(lax.rem(index, 2) * tok_rows, tok_rows), tok_rows)
+        left = combine_ref[index // 2, :, side]
+
+        @pl.loop(0, model_width // width_step)
+        def _(step):
+            cols = pl.ds(pl.multiple_of(step * width_step, width_step), width_step)
+            store(cols, turned_dot(left, mixed_rows_ref[index // 2, :, cols]))
+
+    def between():
+        for shift in range(1, size):
+            scatter(shift).wait_recv()
+        second[mine] = jnp.sum(first[...], 0)
+        for shift in range(1, split):
+            share(shift).start()
+
+    reduce.run(product, between)
+    for shift in range(1, split):
+        share(shift).wait_recv()
+    final[me] = jnp.sum(second[...], 0)
+    for shift in range(1, size):
+        collect(shift).start()
+    output_ref[...] = (residual_ref[...] + total[...]).astype(output_ref.dtype)
+    for shift in range(1, size):
+        scatter(shift).wait_send()
+    for shift in range(1, split):
+        share(shift).wait_send()
+    for shift in range(1, size):
+        collect(shift).wait()
+    for index in range(size):
+        small_ref[:, index * slice_width : (index + 1) * slice_width] = final[index]
+    reduce.sent()
+    up_send_all.wait()
+
+
+def close(sizes, mixed_rows, combine, residual, gains, router_grad, grad_up, which):
+    size, split, chips, experts_local = sizes
+    f32, half = jnp.float32, jnp.bfloat16
+    tok_rows, model_width = residual.shape
+    hidden_width = grad_up.shape[1]
+    part, slice_width = model_width // split, model_width // size
+    rows = 8 + router_grad.shape[0]
+    vmem = pl.BlockSpec(memory_space=pltpu.VMEM)
+    anywhere = pl.BlockSpec(memory_space=pl.ANY)
+    kind = pltpu.SemaphoreType.DMA
+    shape = jax.ShapeDtypeStruct
+    seq, fsdp = kind((size,)), kind((split,))
+    return pl.pallas_call(
+        functools.partial(close_kernel, sizes),
+        out_shape=(
+            shape((tok_rows, model_width), half),
+            shape((rows, model_width), f32),
+            shape((split, part, hidden_width), half),
+        ),
+        in_specs=[vmem] * 5 + [anywhere],
+        out_specs=(vmem, vmem, anywhere),
+        scratch_shapes=[
+            pltpu.VMEM((tok_rows, model_width), f32),
+            pltpu.VMEM((rows, model_width), f32),
+            pltpu.VMEM((size, rows, slice_width), f32),
+            pltpu.VMEM((split, rows, slice_width), f32),
+            pltpu.VMEM((size, rows, slice_width), f32),
+            kind,
+            fsdp,
+            fsdp,
+            seq,
+            seq,
+            fsdp,
+            fsdp,
+            seq,
+            seq,
+            *ChainReduce.scratch(chips, tok_rows, model_width),
+        ],
+        compiler_params=pltpu.CompilerParams(
+            collective_id=which, has_side_effects=True, vmem_limit_bytes=56 * 2**20
+        ),
+    )(mixed_rows, combine, residual, gains, router_grad, grad_up)
 
 
 def shards(
@@ -1455,42 +1780,14 @@
     top_count = expert_ids.shape[1]
     head_size = HEAD_DIM
     local_width = w_query.shape[1]
-    heads_local = local_width // head_size
     capacity = CAP
     column_start = lax.axis_index("seq") * local_width
     experts_local = w_gate.shape[0]
     seq_size = lax.axis_size("seq")
     split = lax.axis_size("fsdp")
-    groups = split // experts_local
-    shard_index = lax.axis_index("fsdp")
-
-    def pick(stack, index):
-        return lax.dynamic_index_in_dim(stack, index, 0, keepdims=False)
-
-    def to_shards(grad, dim):
-        part = grad.shape[dim] // split
-        shape = [experts_local, *grad.shape]
-        shape[dim + 1] = part
-        owned = jnp.zeros(shape, float_type)
-        for shift in range(split):
-            dest = lax.rem(shard_index + shift, split)
-            piece = lax.dynamic_slice_in_dim(grad, dest * part, part, dim).astype(half_type)
-            if shift:
-                links = [(one, (one + shift) % split) for one in range(split)]
-                piece = lax.ppermute(piece, "fsdp", links)
-            expert = lax.rem(shard_index - shift + split, experts_local)
-            piece = piece.astype(float_type)
-            if groups > 1:
-                piece = piece + pick(owned, expert)
-            owned = lax.dynamic_update_index_in_dim(owned, piece, expert, 0)
-        return owned
-
     places = jnp.where(expert_slots < capacity, expert_ids * capacity + expert_slots, -(10**6))
     gain_rows = norm_gains.astype(float_type)
     gain_cols = lax.dynamic_slice_in_dim(gain_rows, column_start, local_width, 1)
-    inputs = tokens.astype(float_type)
-    inverse_first = inverse_rms(inputs)
-    unit_first = inputs * inverse_first
     length = seq_size * tok_rows
     sizes = (seq_size, split, seq_size // 2, experts_local)
     positions = jnp.arange(length, dtype=jnp.int32)
@@ -1529,29 +1826,6 @@
         jnp.concatenate([expert_ids, places], 1).T,
         0,
     )
-    unit_query, unit_key = unit_pair[0], unit_pair[1]
-    inverse_query = lax.rsqrt(square_sums[0] / model_width + EPSILON)[:, None]
-    inverse_key = lax.rsqrt(square_sums[1] / model_width + EPSILON)[:, None]
-    qkv_cols = jnp.concatenate([qkv_stack[0], qkv_stack[1], qkv_stack[2]], 1)
-    out_rows = out_stack.transpose(1, 0, 2).reshape(local_width, model_width)
-    block_rows = math.gcd(512, length)
-    blocks = length // block_rows
-    score_scale = head_size ** (-0.5)
-    query_cube = query_heads.reshape(blocks, block_rows, heads_local, head_size)
-    key_cube = key_heads.reshape(length, heads_local, head_size)
-    value_cube = value_heads.reshape(length, heads_local, head_size)
-    segment_blocks = segment_ids.reshape(blocks, block_rows)
-    log_sums = log_wide.reshape(blocks, block_rows, heads_local, head_size)[..., 0]
-    log_sums = log_sums.transpose(0, 2, 1)
-
-    def block_scores(query_block, segment_block):
-        scores = (
-            jnp.einsum("qhd,khd->hqk", query_block, key_cube, preferred_element_type=float_type)
-            * score_scale
-        )
-        visible = segment_block[:, None] == segment_ids[None, :]
-        return jnp.where(visible[None], scores, MASKED)
-
     router_rows = jnp.zeros((seq_size, 8, model_width), half_type)
     router_rows = router_rows.at[:, :experts_local].set(
         w_router.T.reshape(seq_size, experts_local, model_width)
@@ -1561,12 +1835,12 @@
         residual_grad,
         out_grad,
         gain_second_grad,
-        router_grad_rows,
+        router_grad,
         combine,
         hidden,
         grad_gate_full,
         grad_up_full,
-        grad_down_full,
+        down_landing,
     ) = experts(
         sizes,
         routed_seq,
@@ -1580,118 +1854,50 @@
         (gate_full, up_full, down_full),
         1,
     )
-    gain_second_grad = gain_second_grad[0]
-    grad_router_local = router_grad_rows.reshape(seq_size, 8, model_width)[:, :experts_local]
-    grad_router_local = grad_router_local.reshape(expert_total, model_width)
-    pairs = seq_size // 2
-    returned = jnp.einsum(
-        "mpsf,fd->mpsd", hidden, down_full, preferred_element_type=float_type
-    ).astype(half_type)
-    incoming = []
-    for move in range(experts_local):
-        piece = returned[move]
-        if move:
-            piece = lax.ppermute(piece, "fsdp", [(one, one ^ move) for one in range(split)])
-        incoming.append(piece)
-    mixture = jnp.einsum(
-        "pst,psd->ptd",
-        combine,
-        jnp.concatenate(incoming, 1),
-        preferred_element_type=float_type,
-    ).astype(half_type)
-    mixture = lax.psum_scatter(
-        mixture.reshape(length, model_width), "seq", scatter_dimension=0, tiled=True
-    ).astype(float_type)
-    output = (residual + mixture).astype(half_type)
-    out_grad_seq = seq_gather(out_grad, seq_size, 2)
-    grad_out_local = jnp.einsum(
-        "th,td->hd", attended_heads, out_grad_seq, preferred_element_type=float_type
-    )
-    attended_grad = jnp.einsum(
-        "td,hd->th", out_grad_seq, out_rows, preferred_element_type=float_type
-    ).astype(half_type)
-    grad_cube = attended_grad.reshape(blocks, block_rows, heads_local, head_size)
-
-    def attend_back(running, pieces):
-        key_acc, value_acc = running
-        query_block, segment_block, grad_block, log_block = pieces
-        scores = block_scores(query_block, segment_block)
-        soft_values = jnp.exp(scores - log_block[..., None])
-        prob_grad = jnp.einsum(
-            "qhd,khd->hqk", grad_block, value_cube, preferred_element_type=float_type
-        )
-        center = jnp.sum(soft_values * prob_grad, -1, keepdims=True)
-        score_grad = (soft_values * (prob_grad - center)).astype(half_type)
-        query_grad = (
-            jnp.einsum("hqk,khd->qhd", score_grad, key_cube, preferred_element_type=float_type)
-            * score_scale
-        )
-        key_acc = (
-            key_acc
-            + jnp.einsum("hqk,qhd->khd", score_grad, query_block, preferred_element_type=float_type)
-            * score_scale
-        )
-        value_acc = value_acc + jnp.einsum(
-            "hqk,qhd->khd",
-            soft_values.astype(half_type),
-            grad_block,
-            preferred_element_type=float_type,
-        )
-        return ((key_acc, value_acc), query_grad.astype(half_type))
-
-    empty_acc = jnp.zeros((length, heads_local, head_size), float_type)
-    (key_acc, value_acc), query_grads = lax.scan(
-        attend_back, (empty_acc, empty_acc), (query_cube, segment_blocks, grad_cube, log_sums)
-    )
-    query_back = query_grads.reshape(length, local_width)
-    key_back = key_acc.reshape(length, local_width).astype(half_type)
-    value_back = value_acc.reshape(length, local_width).astype(half_type)
-    query_unit_grad = rotate(query_back.astype(float_type), cosine_table, -sine_table, head_size)
-    key_unit_grad = rotate(key_back.astype(float_type), cosine_table, -sine_table, head_size)
-    gain_query_grad = jnp.sum(query_unit_grad * unit_query, axis=0)
-    gain_key_grad = jnp.sum(key_unit_grad * unit_key, axis=0)
-    query_scaled = query_unit_grad * gain_cols[2]
-    key_scaled = key_unit_grad * gain_cols[3]
-    centers = seq_sum(
-        (jnp.sum(query_scaled * unit_query, -1), jnp.sum(key_scaled * unit_key, -1)), seq_size, 3
-    )
-    query_raw_grad = (
-        inverse_query * (query_scaled - unit_query * (centers[0] / model_width)[:, None])
-    ).astype(half_type)
-    key_raw_grad = (
-        inverse_key * (key_scaled - unit_key * (centers[1] / model_width)[:, None])
-    ).astype(half_type)
-    raw_grads = jnp.concatenate([query_raw_grad, key_raw_grad, value_back], 1)
-    raw_blocks = raw_grads.reshape(seq_size, tok_rows, 3 * local_width)
-    normed_grad = seq_reduce(raw_blocks, qkv_cols, model_width, True, 5)
-    grad_qkv_local = jnp.einsum("td,th->dh", normed_seq, raw_grads, preferred_element_type=float_type)
-    gain_first_grad = jnp.sum(normed_grad * unit_first, axis=0)
-    input_grad = residual_grad + norm_back(normed_grad * gain_rows[0], unit_first, inverse_first)
-    zero_row = jnp.zeros((model_width,), float_type)
-    gain_query_full = lax.dynamic_update_slice_in_dim(zero_row, gain_query_grad, column_start, 0)
-    gain_key_full = lax.dynamic_update_slice_in_dim(zero_row, gain_key_grad, column_start, 0)
-    gain_grads = jnp.stack([gain_first_grad, gain_second_grad, gain_query_full, gain_key_full])
-    small = jnp.concatenate([gain_grads, jnp.zeros_like(gain_grads), grad_router_local])
-    small = total_sum(small, seq_size, split, 6)
-    gain_sums, router_grad = small[:4], small[8:].T
-    qkv_owned = lax.psum_scatter(
-        grad_qkv_local.astype(half_type), "fsdp", scatter_dimension=0, tiled=True
-    ).astype(float_type)
-    out_owned = lax.psum_scatter(
-        grad_out_local.astype(half_type), "fsdp", scatter_dimension=1, tiled=True
-    ).astype(float_type)
+    input_grad, gain_grads, qkv_owned, out_owned, mixed_rows, gate_landing = back(
+        sizes,
+        out_grad,
+        tokens,
+        residual_grad,
+        (gain_rows, gain_cols, gain_second_grad),
+        (
+            cosine_wide,
+            sine_wide,
+            segment_ids.reshape(-1, 1),
+            segment_ids.reshape(1, -1),
+            query_heads,
+            key_heads,
+            value_heads,
+            unit_pair,
+            square_sums,
+            log_wide,
+            attended_heads,
+            qkv_stack,
+            out_stack,
+        ),
+        (normed_seq, hidden, down_full, grad_gate_full),
+        2,
+    )
+    output, small, up_landing = close(
+        sizes, mixed_rows, combine, residual, gain_grads, router_grad, grad_up_full, 3
+    )
+
+    def owned(landing):
+        shape = (split // experts_local, experts_local, *landing.shape[1:])
+        return landing.astype(float_type).reshape(shape).sum(0)
+
     return (
         output,
         input_grad,
-        gain_sums,
-        qkv_owned[:, :local_width],
-        qkv_owned[:, local_width : 2 * local_width],
-        qkv_owned[:, 2 * local_width :],
+        small[:4],
+        qkv_owned[0],
+        qkv_owned[1],
+        qkv_owned[2],
         out_owned,
-        router_grad,
-        to_shards(grad_gate_full, 0),
-        to_shards(grad_up_full, 0),
-        to_shards(grad_down_full, 1),
+        small[8:].T,
+        owned(gate_landing),
+        owned(up_landing),
+        owned(down_landing),
     )
 
 

time: 889 us -> 692 us (0.78)
  waiting for transfers between devices: 128 us -> 0 us
  Pallas kernels: 561 us -> 655 us
  matrix products: 49.2 us -> 0 us
  local copies, waits for them, and re-layouts: 57.4 us -> 10.9 us
  other arithmetic: 58.7 us -> 21.8 us
  starting transfers between devices: 14.8 us -> 0 us
  between operations: 14.7 us -> 0.9 us
    ppermute x12 -> x0, waiting for transfers between devices: 128 us -> none  [the longest x3 73.8 us: shards(): lax.ppermute(piece, 'fsdp', [(one, one ^ move) for one in range(split)])]
    pallas_call x4 -> x2, Pallas kernels: 132 us -> 224 us  [the longest x1 161 us: back(): pl.pallas_call(functools.partial(back_kernel, sizes), out_shape=(shape((t...]
    dot_general x15 -> x0, matrix products: 49.2 us -> none  [the longest x1 8.19 us: shards(): jnp.einsum('mpsf,fd->mpsd', hidden, down_full, preferred_element_type=flo...]
    dynamic_update_slice x12 -> x0, other arithmetic: 17.1 us -> none  [to_shards(): owned = lax.dynamic_update_index_in_dim(owned, piece, expert, 0)]
    ppermute x12 -> x0, starting transfers between devices: 14.6 us -> none  [the longest x9 11.1 us: to_shards(): piece = lax.ppermute(piece, 'fsdp', links)]
  transfers between devices with their start and end apart: 15 -> 0, of which waited for: 6 -> 0; matrix products, arithmetic and copies ran while one was open for 16% -> 0% of each run, Pallas kernels for 10% -> 0%
where the time goes in v5:
time: 692 us; the launch traced here: 688 us
  Pallas kernels  655 us (95%)
  other arithmetic  21.8 us (3%)
  local copies, waits for them, and re-layouts  10.9 us (2%)
    pallas_call x1, Pallas kernels, front(): pl.pallas_call(functools.partial(front_kernel, sizes), out_shape=(shape((...  253 us
    pallas_call x1, Pallas kernels, experts(): pl.pallas_call(functools.partial(experts_kernel, sizes), out_shape=(shape...  178 us
    pallas_call x1, Pallas kernels, back(): pl.pallas_call(functools.partial(back_kernel, sizes), out_shape=(shape((t...  161 us
    pallas_call x1, Pallas kernels, close(): pl.pallas_call(functools.partial(close_kernel, sizes), out_shape=(shape((...  63 us
    convert_element_type x3, other arithmetic, owned(): return landing.astype(float_type).reshape(shape).sum(0)  15.8 us

profile of v5, /device:TPU:0, one launch (start us, length us, event | category | flops | bytes accessed | tf_op | source)
XLA Modules:
  0.0 688.4 jit_solution(269218422602959107)
XLA Ops:
  0.7 0.7 add_select_fusion
  1.4 1.3 add_bitcast_fusion.choice_ref
  2.7 0.7 convert_element_type.25.gains_ref
  3.4 0.6 constant_dynamic-slice_fusion.gain_cols_ref
  4.0 1.0 reshape.89
  4.9 0.7 pad_bitcast_fusion.router_ref
  5.7 1.7 copy.25.seg_col_ref
  7.4 1.9 fusion
  9.3 1.3 pad_maximum_fusion
  10.6 0.0 copy-done.6
  10.6 252.9 %shard_map.221 = (bf16[1024,2048]{1,0:T(8,128)(2,1)}, bf16[3,2048,256]{2,1,0:T(8,128)(2,1)}, bf16[4,256,512]{2,1,0:T(8,128)(2,1)}, bf16[1024,256]{1,0:T(8,128)(2...) custom-call(bf16[128,2048]{1,0:T(8,128)(2,1)} %tokens_ref.3, ...), custom_call_target="tpu_custom_call" | custom-call | flops 4294967296 | bytes 524288000 | tf_op jit(solution)/shard_map/pallas_call | solution.py:623
  263.5 177.8 %shard_map.222 = (f32[128,2048]{1,0:T(8,128)}, bf16[128,2048]{1,0:T(8,128)(2,1)}, f32[8,2048]{1,0:T(8,128)}, f32[32,2048]{1,0:T(8,128)}, bf16[4,320,256]{2,1,0:T...) custom-call(bf16[1024,2048]{1,0:T(8,128)(2,1)} %get-tuple-element.59, ...), custom_call_target="tpu_custom_call" | custom-call | flops 42949672960 | bytes 524288000 | tf_op jit(solution)/shard_map/pallas_call | solution.py:1156
  441.3 161.1 %shard_map.223 = (f32[128,2048]{1,0:T(8,128)}, f32[8,2048]{1,0:T(8,128)}, f32[3,512,256]{2,1,0:T(8,128)}, f32[256,512]{1,0:T(8,128)}, bf16[4,320,2048]{2,1,0:T(8,128)(2,1)}, /*index=5*/bf16[4,512,1024]{2,1,0:T(8,128)(2,1)}) custom-call(bf16[128,2048]{1,0:T(8,128)(2,1)} %get-tuple-element.67.out_grad_ref, bf16[128,2048]{1,0:T(8,128)(2,1)} %tokens_ref.3, ...), custom_call_target="tpu_custom_call" | custom-call | flops 8589934592 | bytes 524288000 | tf_op jit(solution)/shard_map/pallas_call | solution.py:1536
  602.4 0.0 copy-start.2
  602.4 63.0 %shard_map.224 = (bf16[128,2048]{1,0:T(8,128)(2,1)}, f32[40,2048]{1,0:T(8,128)}, bf16[4,512,1024]{2,1,0:T(8,128)(2,1)}) custom-call(bf16[4,320,2048]{2,1,0:T(8,128)(2,1)} %get-tuple-element.82.mixed_rows_ref, bf16[4,320,256]{2,1,0:T(8,128)(2,1)} %get-tuple-element.83.combine_ref, f32[128,2048]{1,0:T(8,128)} %get-tuple-element.63.residual_ref, ...), custom_call_target="tpu_custom_call" | custom-call | tf_op jit(solution)/shard_map/pallas_call | solution.py:1727
  665.5 1.5 slice.36
  666.9 1.7 slice_bitcast_fusion.3
  668.6 1.2 slice_bitcast_fusion
  669.8 6.8 convert_element_type.28
  676.6 4.4 convert_element_type.27
  681.0 4.6 convert_element_type.29
  685.6 0.8 copy.30
  686.4 1.0 copy.31
  687.4 0.8 copy.32
  (14 shorter events, 0.0 us)
Async XLA Ops:
  3.4 7.2 %copy-start.6 = (f32[4,2048]{1,0:T(4,128)}, f32[4,2048]{1,0:T(4,128)S(1)}, u32[]{:S(2)}) copy-start(f32[4,2048]{1,0:T(4,128)S(1)} %convert_element_type.25.gains_ref) | copy-start | bytes 98308
  602.4 66.2 %copy-start.2 = (f32[3,512,256]{2,1,0:T(8,128)S(1)}, f32[3,512,256]{2,1,0:T(8,128)}, u32[]{:S(2)}) copy-start(f32[3,512,256]{2,1,0:T(8,128)} %get-tuple-element.90) | copy-start | bytes 4718596
  669.8 6.8 copy-start.1
  676.6 4.4 copy-start
  681.0 4.6 copy-start.5
  681.0 5.4 copy-start.3
  681.0 6.4 copy-start.4

commit v6 on v5

--- a/solution.py
+++ b/solution.py
@@ -2,6 +2,7 @@
 
 import jax
 import jax.numpy as jnp
+import numpy as np
 from jax import lax
 from jax.experimental import pallas as pl
 from jax.experimental.pallas import tpu as pltpu
@@ -17,11 +18,15 @@
 HIGHEST = lax.Precision.HIGHEST
 
 
-def rope_tables(positions, head_size):
+def rope_tables(length, head_size):
     half_dim = head_size // 2
-    frequency = THETA ** (-jnp.arange(half_dim, dtype=jnp.float32) / half_dim)
-    angles = positions.astype(jnp.float32)[:, None] * frequency[None, :]
-    return (jnp.cos(angles), jnp.sin(angles))
+    frequency = THETA ** (-np.arange(half_dim, dtype=np.float64) / half_dim)
+    angles = np.arange(length, dtype=np.float64)[:, None] * frequency.astype(np.float32)
+    cosine, sine = np.cos(angles), np.sin(angles)
+    return (
+        jnp.asarray(np.concatenate([cosine, cosine], 1), jnp.float32),
+        jnp.asarray(np.concatenate([-sine, sine], 1), jnp.float32),
+    )
 
 
 class ChainGather:
@@ -278,12 +283,12 @@
 def front_kernel(
     sizes,
     tokens_ref,
-    gains_ref,
-    gain_cols_ref,
+    gains_in_ref,
     cos_ref,
     sin_ref,
-    seg_col_ref,
     seg_row_ref,
+    ids_ref,
+    slots_ref,
     cotangent_ref,
     wq_ref,
     wk_ref,
@@ -292,7 +297,6 @@
     w_gate_ref,
     w_up_ref,
     w_down_ref,
-    choice_ref,
     normed_out,
     qkv_out,
     rows_out,
@@ -304,6 +308,8 @@
     log_ref,
     attended_ref,
     residual_ref,
+    gains_ref,
+    seg_col_ref,
     routed_out,
     cotangent_rows,
     gate_full,
@@ -315,7 +321,11 @@
     qkv,
     rows_full,
     routed_own,
+    choice_own,
+    cotangent_pair,
     cotangent_all,
+    mate_choices,
+    mate_onehot,
     placed,
     raw,
     sums_own,
@@ -327,6 +337,11 @@
     sums_recv,
     choice_send,
     choice_recv,
+    mate_send,
+    mate_recv,
+    cross_local,
+    cross_send,
+    cross_recv,
     placed_local,
     placed_send,
     placed_recv,
@@ -350,8 +365,11 @@
 
     inputs = tokens_ref[...].astype(f32)
     inverse = lax.rsqrt(jnp.mean(inputs * inputs, -1, keepdims=True) + EPSILON)
-    own_rows = pl.ds(pl.multiple_of(me * tok_rows, tok_rows), tok_rows)
+    gains_ref[...] = gains_in_ref[...].astype(f32)
     routed_own[...] = (inputs * inverse * gains_ref[0:1, :]).astype(half)
+    crossed = split == experts_local == 4
+    half_width = model_width // 2
+    x_mate, y_mate = {"fsdp": partner_of(mine, 1)}, {"fsdp": partner_of(mine, 2)}
     greet_all(size, split)
 
     def gather(index, x_ref, out_ref):
@@ -367,9 +385,41 @@
     first = gather(0, routed_own, normed)
     first.start()
 
+    cross_rows = pl.ds(tok_rows, tok_rows)
+    lower, upper = pl.ds(0, half_width), pl.ds(half_width, half_width)
+
+    def cross_copy(index):
+        cols = (lower, upper)[index]
+        return pltpu.make_async_remote_copy(
+            src_ref=cotangent_ref.at[:, cols],
+            dst_ref=cotangent_pair.at[cross_rows, cols],
+            send_sem=cross_send.at[index],
+            recv_sem=cross_recv.at[index],
+            device_id=(x_mate, y_mate)[index],
+        )
+
+    if crossed:
+        cross_own = pltpu.make_async_copy(
+            cotangent_ref, cotangent_pair.at[pl.ds(0, tok_rows)], cross_local
+        )
+        cross_copy(0).start()
+        cross_copy(1).start()
+        cross_own.start()
+
+    top_count = ids_ref.shape[1]
+    same = lax.broadcasted_iota(jnp.int32, (top_count, top_count), 0) == (
+        lax.broadcasted_iota(jnp.int32, (top_count, top_count), 1)
+    )
+    ids_row = row_sums(ids_ref[...].astype(f32), same.astype(f32))
+    slots_row = row_sums(slots_ref[...].astype(f32), same.astype(f32))
+    choice_own[0:top_count, :] = ids_row.astype(jnp.int32)
+    choice_own[top_count : 2 * top_count, :] = jnp.where(
+        slots_row < CAP, ids_row * CAP + slots_row, -1e6
+    ).astype(jnp.int32)
+
     def choice_copy(shift):
         return pltpu.make_async_remote_copy(
-            src_ref=choice_ref,
+            src_ref=choice_own,
             dst_ref=choices.at[me],
             send_sem=choice_send.at[shift],
             recv_sem=choice_recv.at[shift],
@@ -394,13 +444,38 @@
             device_id={"fsdp": lax.rem(mine + shift, split)},
         )
 
+    def landed_half(index, owner, side):
+        if index == 3:
+            rows = local_width // 2
+            return rows_full.at[owner, pl.ds(side * rows, rows)]
+        rows = part // 2
+        start = pl.multiple_of(owner * part + side * rows, rows)
+        return qkv.at[index, pl.ds(start, rows)]
+
+    def relay_copy(index, step):
+        if step < 2:
+            source, target = shard_pairs[index]
+        else:
+            source = target = landed_half(index, partner_of(mine, step - 1), step - 2)
+        return pltpu.make_async_remote_copy(
+            src_ref=source,
+            dst_ref=target,
+            send_sem=shard_send.at[index, step],
+            recv_sem=shard_recv.at[index, step],
+            device_id=(x_mate, y_mate, y_mate, x_mate)[step],
+        )
+
     def shard_own(index):
         source, target = shard_pairs[index]
         return pltpu.make_async_copy(source, target, shard_local.at[index])
 
     for index in range(4):
-        for shift in range(1, split):
-            shard_copy(index, shift).start()
+        if split == 4:
+            relay_copy(index, 0).start()
+            relay_copy(index, 1).start()
+        else:
+            for shift in range(1, split):
+                shard_copy(index, shift).start()
         shard_own(index).start()
 
     def expert_pair(index, dest):
@@ -425,11 +500,21 @@
         source, target = expert_pair(index, mine)
         return pltpu.make_async_copy(source, target, expert_local.at[index])
 
-    first.steps()
+    for distance in range(1, chips):
+        first.step(distance)
+        if split == 4 and distance == min(2, chips - 1):
+            for index in range(4):
+                for step in range(2):
+                    relay_copy(index, step).wait_recv()
+                    relay_copy(index, step + 2).start()
     for index in range(4):
         shard_own(index).wait()
-        for shift in range(1, split):
-            shard_copy(index, shift).wait_recv()
+        if split == 4:
+            relay_copy(index, 2).wait_recv()
+            relay_copy(index, 3).wait_recv()
+        else:
+            for shift in range(1, split):
+                shard_copy(index, shift).wait_recv()
     for index in range(3):
         for shift in range(1, split):
             expert_copy(index, shift).start()
@@ -437,8 +522,14 @@
     first.landed()
     for shift in range(1, size):
         choice_copy(shift).start()
-    choices[me] = choice_ref[...]
-    second = gather(1, cotangent_ref, cotangent_all)
+    choices[me] = choice_own[...]
+    if crossed:
+        cross_own.wait()
+        cross_copy(0).wait()
+        cross_copy(1).wait()
+        second = gather(1, cotangent_pair, cotangent_all)
+    else:
+        second = gather(1, cotangent_ref, cotangent_all)
     second.start()
     keeps = [
         pltpu.make_async_copy(normed, normed_out, out_sem.at[0]),
@@ -448,6 +539,7 @@
     for keep in keeps:
         keep.start()
 
+    own_cols = pl.ds(pl.multiple_of(me * local_width, local_width), local_width)
     block = min(512, length)
     lanes = lax.broadcasted_iota(jnp.int32, (8, local_width), 0)
     first_row, second_row = (lanes == 0).astype(f32), (lanes == 1).astype(f32)
@@ -478,16 +570,36 @@
     for shift in range(1, size):
         sums_copy(shift).wait()
     sums_ref[...] = jnp.sum(sums_in[...], 0)
+    for shift in range(1, size):
+        choice_copy(shift).wait()
+
+    def mate_copy(index):
+        return pltpu.make_async_remote_copy(
+            src_ref=choices,
+            dst_ref=mate_choices.at[index],
+            send_sem=mate_send.at[index],
+            recv_sem=mate_recv.at[index],
+            device_id=(x_mate, y_mate)[index],
+        )
+
+    if crossed:
+        mate_copy(0).start()
+        mate_copy(1).start()
+    segments = seg_row_ref[...].astype(f32)
+    narrow = first_row[:, 0:128]
 
     @pl.loop(0, length // block)
     def _(step):
         rows = pl.ds(pl.multiple_of(step * block, block), block)
         square_sums = sums_ref[:, rows]
+        seg_col_ref[rows, :] = column_of(
+            jnp.broadcast_to(seg_row_ref[:, rows].astype(f32), (8, block)), narrow
+        )
         for index, pick, target in ((0, first_row, q_ref), (1, second_row, k_ref)):
             scale = lax.rsqrt(column_of(square_sums, pick) / model_width + EPSILON)
             unit = raw[index, rows, :] * scale
             unit_ref[index, rows, :] = unit
-            scaled = unit * gain_cols_ref[2 + index : 3 + index, :]
+            scaled = unit * gains_ref[2 + index : 3 + index, own_cols]
             for number in range(heads):
                 cols = slice(number * head, (number + 1) * head)
                 piece = scaled[:, cols]
@@ -511,7 +623,7 @@
                 preferred_element_type=f32,
             )
             scores = scores * (head**-0.5)
-            scores = jnp.where(seg_col_ref[rows, :] == seg_row_ref[...], scores, MASKED)
+            scores = jnp.where(seg_col_ref[rows, 0:1] == segments, scores, MASKED)
             peak = jnp.max(scores, -1, keepdims=True)
             grown = jnp.exp(scores - peak)
             weight = jnp.sum(grown, -1, keepdims=True)
@@ -543,72 +655,127 @@
     routed_own[...] = (residual * inverse * gains_ref[1:2, :]).astype(half)
     third = gather(2, routed_own, routed_out)
     third.start()
-    third.steps()
-    third.landed()
 
     second.landed()
-    for shift in range(1, size):
-        choice_copy(shift).wait()
     double = 2 * CAP
     member = lax.rem(mine, experts_local)
-    top_count = choice_ref.shape[0] // 2
     slot_row = lax.broadcasted_iota(jnp.int32, (double, tok_rows), 0)
+    if crossed:
+        mate_copy(0).wait()
+        mate_copy(1).wait()
+
+    def one_hot(places, target, rows, expert):
+        base = (me * experts_local + expert) * CAP
+        for side in range(2):
+            want = jnp.where(slot_row // CAP == side, slot_row - side * CAP + base, -1)
+            hit = want == places(side)[top_count : top_count + 1, :]
+            for choice in range(1, top_count):
+                hit = hit | (want == places(side)[top_count + choice : top_count + choice + 1, :])
+            cols = slice(side * tok_rows, (side + 1) * tok_rows)
+            target[rows, cols] = jnp.where(hit, 1.0, 0.0).astype(half)
+
+    def slot_range(move):
+        return slice(move * double, (move + 1) * double)
 
     @pl.loop(0, size // 2)
     def _(pair):
         for move in range(experts_local):
-            base = (me * experts_local + partner_of(member, move)) * CAP
-            for side in range(2):
-                want = jnp.where(slot_row // CAP == side, slot_row - side * CAP + base, -1)
-                places = choices[pair * 2 + side]
-                hit = want == places[top_count : top_count + 1, :]
-                for choice in range(1, top_count):
-                    hit = hit | (want == places[top_count + choice : top_count + choice + 1, :])
-                cols = slice(side * tok_rows, (side + 1) * tok_rows)
-                onehot_ref[pair, move * double : (move + 1) * double, cols] = jnp.where(
-                    hit, 1.0, 0.0
-                ).astype(half)
-        start = pl.multiple_of(pair * 2 * tok_rows, 2 * tok_rows)
-        made = jnp.dot(
-            onehot_ref[pair], cotangent_all[pl.ds(start, 2 * tok_rows), :], preferred_element_type=f32
-        ).astype(half)
-        for move in range(experts_local):
-            placed[move, pair] = made[move * double : (move + 1) * double]
-
-    def placed_copy(move):
+            one_hot(
+                lambda side: choices[pair * 2 + side],
+                onehot_ref.at[pair],
+                slot_range(move),
+                partner_of(member, move),
+            )
+        if crossed:
+            start = pl.multiple_of(pair * 4 * tok_rows, 4 * tok_rows)
+            four = cotangent_all[pl.ds(start, 4 * tok_rows), :]
+            own = jnp.concatenate(
+                [four[0:tok_rows], four[2 * tok_rows : 3 * tok_rows]], 0
+            )
+            mates = jnp.concatenate(
+                [four[tok_rows : 2 * tok_rows], four[3 * tok_rows : 4 * tok_rows]], 0
+            )
+            made = jnp.dot(onehot_ref[pair], own, preferred_element_type=f32).astype(half)
+            placed[0, pair] = made[slot_range(0)]
+            placed[1, pair, :, upper] = made[slot_range(1), half_width:]
+            placed[2, pair, :, lower] = made[slot_range(2), :half_width]
+            for index in range(2):
+                for row, expert in enumerate((member, partner_of(member, 2 - index))):
+                    one_hot(
+                        lambda side: mate_choices[index, pair * 2 + side],
+                        mate_onehot.at[index],
+                        slot_range(row),
+                        expert,
+                    )
+                cols = (lower, upper)[index]
+                taken = mates[:, :half_width] if index == 0 else mates[:, half_width:]
+                made = jnp.dot(mate_onehot[index], taken, preferred_element_type=f32).astype(half)
+                placed[index + 1, pair, :, cols] = made[slot_range(0)]
+                placed[3, pair, :, cols] = made[slot_range(1)]
+        else:
+            start = pl.multiple_of(pair * 2 * tok_rows, 2 * tok_rows)
+            made = jnp.dot(
+                onehot_ref[pair],
+                cotangent_all[pl.ds(start, 2 * tok_rows), :],
+                preferred_element_type=f32,
+            ).astype(half)
+            for move in range(experts_local):
+                placed[move, pair] = made[slot_range(move)]
+
+    def placed_copy(index):
+        if crossed:
+            move, cols = ((1, upper), (2, lower), (3, upper), (3, lower))[index]
+            source, target = placed.at[move, :, :, cols], cotangent_rows.at[move, :, :, cols]
+            mate = (x_mate, y_mate)[index % 2]
+        else:
+            source, target = placed.at[index], cotangent_rows.at[index]
+            mate = {"fsdp": partner_of(mine, index)}
         return pltpu.make_async_remote_copy(
-            src_ref=placed.at[move],
-            dst_ref=cotangent_rows.at[move],
-            send_sem=placed_send.at[move],
-            recv_sem=placed_recv.at[move],
-            device_id={"fsdp": partner_of(mine, move)},
-        )
-
-    for move in range(experts_local - 1, 0, -1):
-        placed_copy(move).start()
-    placed_own = pltpu.make_async_copy(placed.at[0], cotangent_rows.at[0], placed_local)
-    placed_own.start()
-
+            src_ref=source,
+            dst_ref=target,
+            send_sem=placed_send.at[index],
+            recv_sem=placed_recv.at[index],
+            device_id=mate,
+        )
+
+    if crossed:
+        placed_pieces = [
+            (placed.at[0], cotangent_rows.at[0]),
+            (placed.at[1, :, :, lower], cotangent_rows.at[1, :, :, lower]),
+            (placed.at[2, :, :, upper], cotangent_rows.at[2, :, :, upper]),
+        ]
+    else:
+        placed_pieces = [(placed.at[0], cotangent_rows.at[0])]
+    placed_sends = [placed_copy(index) for index in range(0 if crossed else 1, experts_local)]
+    placed_owns = [
+        pltpu.make_async_copy(source, target, placed_local.at[index])
+        for index, (source, target) in enumerate(placed_pieces)
+    ]
+    for copy in placed_sends + placed_owns:
+        copy.start()
+    third.steps()
+    third.landed()
     reduce.sent()
     second.sent()
     third.sent()
     for index in range(4):
-        for shift in range(1, split):
-            shard_copy(index, shift).wait_send()
+        if split == 4:
+            for step in range(4):
+                relay_copy(index, step).wait_send()
+        else:
+            for shift in range(1, split):
+                shard_copy(index, shift).wait_send()
     for keep in keeps:
         keep.wait()
-    placed_own.wait()
-    for move in range(1, experts_local):
-        placed_copy(move).wait()
+    for copy in placed_sends + placed_owns:
+        copy.wait()
     for index in range(3):
         expert_own(index).wait()
         for shift in range(1, split):
             expert_copy(index, shift).wait()
 
 
-def front(
-    sizes, tokens, gain_rows, gain_cols, cos, sin, segment_ids, cotangent, weights, choice, which
-):
+def front(sizes, tokens, gains, cos, sin, segment_row, ids, slots, cotangent, weights, which):
     size, split, chips, experts_local = sizes
     w_query, w_key, w_value, w_out, w_gate, w_up, w_down = weights
     tok_rows, model_width = tokens.shape
@@ -620,6 +787,8 @@
     anywhere = pl.BlockSpec(memory_space=pl.ANY)
     kind = pltpu.SemaphoreType.DMA
     shape = jax.ShapeDtypeStruct
+    crossed = split == experts_local == 4
+    choices = (size, 2 * ids.shape[1], tok_rows)
     return pl.pallas_call(
         functools.partial(front_kernel, sizes),
         out_shape=(
@@ -634,22 +803,28 @@
             shape((length, local_width), f32),
             shape((length, local_width), half),
             shape((tok_rows, model_width), f32),
+            shape(gains.shape, f32),
+            shape((length, 128), f32),
             shape((length, model_width), half),
             shape((experts_local, size // 2, 2 * CAP, model_width), half),
             shape((model_width, hidden_width), half),
             shape((model_width, hidden_width), half),
             shape((hidden_width, model_width), half),
-            shape((size, *choice.shape), choice.dtype),
+            shape((size, 2 * ids.shape[1], tok_rows), jnp.int32),
             shape((size // 2, experts_local * 2 * CAP, 2 * tok_rows), half),
         ),
-        in_specs=[vmem] * 7 + [anywhere] * 8 + [vmem],
-        out_specs=tuple([anywhere] * 3 + [vmem] * 8 + [anywhere] * 5 + [vmem] * 2),
+        in_specs=[vmem] * 7 + [anywhere] * 8,
+        out_specs=tuple([anywhere] * 3 + [vmem] * 10 + [anywhere] * 5 + [vmem] * 2),
         scratch_shapes=[
             pltpu.VMEM((length, model_width), half),
             pltpu.VMEM((3, model_width, local_width), half),
             pltpu.VMEM((split, *w_out.shape), half),
             pltpu.VMEM((tok_rows, model_width), half),
-            pltpu.VMEM((length, model_width), half),
+            pltpu.VMEM((2 * ids.shape[1], tok_rows), jnp.int32),
+            pltpu.VMEM((2 * tok_rows if crossed else 16, model_width), half),
+            pltpu.VMEM(((2 if crossed else 1) * length, model_width), half),
+            pltpu.VMEM((2, *(choices if crossed else (1, 8, 128))), jnp.int32),
+            pltpu.VMEM((2, 4 * CAP if crossed else 16, 2 * tok_rows), half),
             pltpu.VMEM((experts_local, size // 2, 2 * CAP, model_width), half),
             pltpu.VMEM((2, length, local_width), f32),
             pltpu.VMEM((8, length), f32),
@@ -661,7 +836,12 @@
             kind((size,)),
             kind((size,)),
             kind((size,)),
+            kind((2,)),
+            kind((2,)),
             kind,
+            kind((2,)),
+            kind((2,)),
+            kind((3,)),
             kind((experts_local,)),
             kind((experts_local,)),
             kind((4,)),
@@ -682,17 +862,9 @@
             transcendentals=0,
         ),
     )(
-        tokens,
-        gain_rows,
-        gain_cols,
-        cos,
-        sin,
-        segment_ids.reshape(-1, 1),
-        segment_ids.reshape(1, -1),
-        cotangent,
-        *weights,
-        choice,
-    )
+        tokens, gains, cos, sin, segment_row, ids, slots, cotangent, *weights
+    )
+
 
 class ShardSend:
     def __init__(self, split, source, landing, local_sem, sends, arrivals):
@@ -1233,7 +1405,6 @@
     tokens_ref,
     residual_grad_ref,
     gains_ref,
-    gain_cols_ref,
     second_gain_ref,
     cos_ref,
     sin_ref,
@@ -1254,7 +1425,9 @@
     grad_gate_ref,
     input_grad_ref,
     gains_out_ref,
-    qkv_grad_ref,
+    query_w_grad_ref,
+    key_w_grad_ref,
+    value_w_grad_ref,
     out_w_grad_ref,
     mixed_rows,
     gate_landing,
@@ -1322,6 +1495,8 @@
         gate_recv,
     )
 
+    gate_send_all.start()
+
     down_load.wait()
     hidden_load.wait()
     width_step = min(512, model_width)
@@ -1354,7 +1529,6 @@
         if move:
             rows_copy(move).start()
     own_rows.start()
-    gate_send_all.start()
     gather.steps()
     gather.landed()
 
@@ -1385,6 +1559,7 @@
 
     wide = min(256, length) if length <= 1024 else 128
     scale = head**-0.5
+    segments = seg_row_ref[...].astype(f32)
     for number in range(heads):
         cols = slice(number * head, (number + 1) * head)
         key_total[...] = jnp.zeros_like(key_total)
@@ -1394,7 +1569,7 @@
         def _(step):
             rows = pl.ds(pl.multiple_of(step * wide, wide), wide)
             scores = cross_dot(q_ref[rows, cols], k_ref[:, cols]) * scale
-            scores = jnp.where(seg_col_ref[rows, :] == seg_row_ref[...], scores, MASKED)
+            scores = jnp.where(seg_col_ref[rows, 0:1] == segments, scores, MASKED)
             probs = jnp.exp(scores - log_ref[rows, cols][:, 0:1])
             grads = attended_grad[rows, cols]
             prob_grad = cross_dot(grads, v_ref[:, cols])
@@ -1429,7 +1604,7 @@
             gains_out_ref[2 + index : 3 + index, own_cols] += jnp.sum(
                 unit_grad * unit, 0, keepdims=True
             )
-            grown = unit_grad * gain_cols_ref[2 + index : 3 + index, :]
+            grown = unit_grad * gains_ref[2 + index : 3 + index, own_cols]
             scaled[index, rows, :] = grown
             found += row_sums(grown * unit, pick)
         centers_own[:, rows] = found
@@ -1507,11 +1682,11 @@
         total += out_landing[index].astype(f32)
     out_w_grad_ref[...] = total
     qkv_send_all.wait()
-    for index in range(3):
+    for index, target in enumerate((query_w_grad_ref, key_w_grad_ref, value_w_grad_ref)):
         total = qkv_landing[0, index].astype(f32)
         for piece in range(1, split):
             total += qkv_landing[piece, index].astype(f32)
-        qkv_grad_ref[index] = total
+        target[...] = total
     reduce.sent()
     own_rows.wait()
     for move in range(1, experts_local):
@@ -1523,7 +1698,7 @@
     size, split, chips, experts_local = sizes
     f32, half = jnp.float32, jnp.bfloat16
     tok_rows, model_width = tokens.shape
-    query_heads, qkv_stack, out_stack = kept[4], kept[11], kept[12]
+    query_heads = kept[4]
     length, local_width = query_heads.shape
     normed_seq, hidden, down_full, grad_gate = big_ones
     hidden_width = down_full.shape[0]
@@ -1538,13 +1713,15 @@
         out_shape=(
             shape((tok_rows, model_width), f32),
             shape((8, model_width), f32),
-            shape((3, part, local_width), f32),
+            shape((part, local_width), f32),
+            shape((part, local_width), f32),
+            shape((part, local_width), f32),
             shape((local_width, part), f32),
             shape((size // 2, experts_local * 2 * CAP, model_width), half),
             shape((split, part, hidden_width), half),
         ),
-        in_specs=[vmem] * 19 + [anywhere] * 4,
-        out_specs=tuple([vmem] * 4 + [anywhere] * 2),
+        in_specs=[vmem] * 18 + [anywhere] * 4,
+        out_specs=tuple([vmem] * 6 + [anywhere] * 2),
         scratch_shapes=[
             pltpu.VMEM(down_full.shape, half),
             pltpu.VMEM((length, model_width), half),
@@ -1601,7 +1778,8 @@
     router_ref,
     grad_up_ref,
     output_ref,
-    small_ref,
+    gains_out_ref,
+    router_out_ref,
     up_landing,
     total,
     small,
@@ -1707,7 +1885,9 @@
     for shift in range(1, size):
         collect(shift).wait()
     for index in range(size):
-        small_ref[:, index * slice_width : (index + 1) * slice_width] = final[index]
+        cols = slice(index * slice_width, (index + 1) * slice_width)
+        gains_out_ref[:, cols] = final[index, 0:4]
+        router_out_ref[:, cols] = final[index, 8:]
     reduce.sent()
     up_send_all.wait()
 
@@ -1728,11 +1908,12 @@
         functools.partial(close_kernel, sizes),
         out_shape=(
             shape((tok_rows, model_width), half),
-            shape((rows, model_width), f32),
+            shape((4, model_width), f32),
+            shape(router_grad.shape, f32),
             shape((split, part, hidden_width), half),
         ),
         in_specs=[vmem] * 5 + [anywhere],
-        out_specs=(vmem, vmem, anywhere),
+        out_specs=(vmem, vmem, vmem, anywhere),
         scratch_shapes=[
             pltpu.VMEM((tok_rows, model_width), f32),
             pltpu.VMEM((rows, model_width), f32),
@@ -1773,27 +1954,14 @@
     cotangent,
 ):
     half_type = jnp.bfloat16
-    float_type = jnp.float32
-    tok_rows = tokens.shape[0]
     model_width = tokens.shape[1]
-    expert_total = w_router.shape[1]
-    top_count = expert_ids.shape[1]
-    head_size = HEAD_DIM
-    local_width = w_query.shape[1]
-    capacity = CAP
-    column_start = lax.axis_index("seq") * local_width
     experts_local = w_gate.shape[0]
     seq_size = lax.axis_size("seq")
     split = lax.axis_size("fsdp")
-    places = jnp.where(expert_slots < capacity, expert_ids * capacity + expert_slots, -(10**6))
-    gain_rows = norm_gains.astype(float_type)
-    gain_cols = lax.dynamic_slice_in_dim(gain_rows, column_start, local_width, 1)
-    length = seq_size * tok_rows
+    length = seq_size * tokens.shape[0]
     sizes = (seq_size, split, seq_size // 2, experts_local)
-    positions = jnp.arange(length, dtype=jnp.int32)
-    cosine_table, sine_table = rope_tables(positions, head_size)
-    cosine_wide = jnp.concatenate([cosine_table, cosine_table], 1)
-    sine_wide = jnp.concatenate([-sine_table, sine_table], 1)
+    cosine_wide, sine_wide = rope_tables(length, HEAD_DIM)
+    segment_row = segment_ids.reshape(1, -1)
     (
         normed_seq,
         qkv_stack,
@@ -1806,6 +1974,8 @@
         log_wide,
         attended_heads,
         residual,
+        gain_rows,
+        segment_cols,
         routed_seq,
         cotangent_rows,
         gate_full,
@@ -1816,14 +1986,14 @@
     ) = front(
         sizes,
         tokens,
-        gain_rows,
-        gain_cols,
+        norm_gains,
         cosine_wide,
         sine_wide,
-        segment_ids,
+        segment_row,
+        expert_ids,
+        expert_slots,
         cotangent,
         (w_query, w_key, w_value, w_out, w_gate, w_up, w_down),
-        jnp.concatenate([expert_ids, places], 1).T,
         0,
     )
     router_rows = jnp.zeros((seq_size, 8, model_width), half_type)
@@ -1854,17 +2024,26 @@
         (gate_full, up_full, down_full),
         1,
     )
-    input_grad, gain_grads, qkv_owned, out_owned, mixed_rows, gate_landing = back(
+    (
+        input_grad,
+        gain_grads,
+        query_owned,
+        key_owned,
+        value_owned,
+        out_owned,
+        mixed_rows,
+        gate_landing,
+    ) = back(
         sizes,
         out_grad,
         tokens,
         residual_grad,
-        (gain_rows, gain_cols, gain_second_grad),
+        (gain_rows, gain_second_grad),
         (
             cosine_wide,
             sine_wide,
-            segment_ids.reshape(-1, 1),
-            segment_ids.reshape(1, -1),
+            segment_cols,
+            segment_row,
             query_heads,
             key_heads,
             value_heads,
@@ -1878,23 +2057,23 @@
         (normed_seq, hidden, down_full, grad_gate_full),
         2,
     )
-    output, small, up_landing = close(
+    output, gain_sums, router_sums, up_landing = close(
         sizes, mixed_rows, combine, residual, gain_grads, router_grad, grad_up_full, 3
     )
 
     def owned(landing):
         shape = (split // experts_local, experts_local, *landing.shape[1:])
-        return landing.astype(float_type).reshape(shape).sum(0)
+        return landing.astype(jnp.float32).reshape(shape).sum(0)
 
     return (
         output,
         input_grad,
-        small[:4],
-        qkv_owned[0],
-        qkv_owned[1],
-        qkv_owned[2],
+        gain_sums,
+        query_owned,
+        key_owned,
+        value_owned,
         out_owned,
-        small[8:].T,
+        router_sums.T,
         owned(gate_landing),
         owned(up_landing),
         owned(down_landing),

time: 692 us -> 661 us (0.955)
  Pallas kernels: 655 us -> 624 us
    pallas_call x1, Pallas kernels: 253 us -> 225 us  [front(): pl.pallas_call(functools.partial(front_kernel, sizes), out_shape=(shape((...]
    convert_element_type x5 -> x3, other arithmetic: 16.5 us -> 15.8 us  [owned(): return landing.astype(jnp.float32).reshape(shape).sum(0)]
where the time goes in v6:
time: 661 us; the launch traced here: 652 us
  Pallas kernels  624 us (94%)
  other arithmetic  15.8 us (2%)
  local copies, waits for them, and re-layouts  10.8 us (2%)
    pallas_call x1, Pallas kernels, front(): pl.pallas_call(functools.partial(front_kernel, sizes), out_shape=(shape((...  225 us
    pallas_call x1, Pallas kernels, experts(): pl.pallas_call(functools.partial(experts_kernel, sizes), out_shape=(shape...  178 us
    pallas_call x1, Pallas kernels, back(): pl.pallas_call(functools.partial(back_kernel, sizes), out_shape=(shape((t...  157 us
    pallas_call x1, Pallas kernels, close(): pl.pallas_call(functools.partial(close_kernel, sizes), out_shape=(shape((...  63.6 us
    convert_element_type x3, other arithmetic, owned(): return landing.astype(jnp.float32).reshape(shape).sum(0)  15.8 us

profile of v6, /device:TPU:0, one launch (start us, length us, event | category | flops | bytes accessed | tf_op | source)
XLA Modules:
  0.0 652.2 jit_solution(11666754551912204392)
XLA Ops:
  0.6 1.4 copy.27.ids_ref
  2.1 1.4 copy.28.slots_ref
  3.5 1.0 reshape.73
  4.4 0.7 pad_bitcast_fusion.router_ref
  5.2 225.5 %shard_map.239 = (bf16[1024,2048]{1,0:T(8,128)(2,1)}, bf16[3,2048,256]{2,1,0:T(8,128)(2,1)}, bf16[4,256,512]{2,1,0:T(8,128)(2,1)}, bf16[1024,256]{1,0:T(8,128)(2...) custom-call(bf16[128,2048]{1,0:T(8,128)(2,1)} %tokens_ref.3, ...), custom_call_target="tpu_custom_call" | custom-call | flops 4294967296 | bytes 524288000 | tf_op jit(solution)/shard_map/pallas_call | solution.py:792
  230.6 178.0 %shard_map.240 = (f32[128,2048]{1,0:T(8,128)}, bf16[128,2048]{1,0:T(8,128)(2,1)}, f32[8,2048]{1,0:T(8,128)}, f32[32,2048]{1,0:T(8,128)}, bf16[4,320,256]{2,1,0:T...) custom-call(bf16[1024,2048]{1,0:T(8,128)(2,1)} %get-tuple-element.64, ...), custom_call_target="tpu_custom_call" | custom-call | flops 42949672960 | bytes 524288000 | tf_op jit(solution)/shard_map/pallas_call | solution.py:1328
  408.7 157.3 %shard_map.241 = (f32[128,2048]{1,0:T(8,128)}, f32[8,2048]{1,0:T(8,128)}, f32[512,256]{1,0:T(8,128)}, f32[512,256]{1,0:T(8,128)}, f32[512,256]{1,0:T(8,128)}, /*...) custom-call(bf16[128,2048]{1,0:T(8,128)(2,1)} %get-tuple-element.73.out_grad_ref, ...), custom_call_target="tpu_custom_call" | custom-call | flops 8589934592 | bytes 524288000 | tf_op jit(solution)/shard_map/pallas_call | solution.py:1711
  566.0 63.6 %shard_map.242 = (bf16[128,2048]{1,0:T(8,128)(2,1)}, f32[4,2048]{1,0:T(4,128)}, f32[32,2048]{1,0:T(8,128)}, bf16[4,512,1024]{2,1,0:T(8,128)(2,1)}) custom-call(bf16[4,320,2048]{2,1,0:T(8,128)(2,1)} %get-tuple-element.89.mixed_rows_ref, bf16[4,320,256]{2,1,0:T(8,128)(2,1)} %get-tuple-element.90.combine_ref, f32[128,2048]{1,0:T(8,128)} %get-tuple-element.69.residual_ref, ...), custom_call_target="tpu_custom_call" | custom-call | tf_op jit(solution)/shard_map/pallas_call | solution.py:1907
  629.6 0.0 copy-start.1
  629.6 6.8 %convert_element_type.10 = f32[4,512,1024]{2,1,0:T(8,128)} convert(bf16[4,512,1024]{2,1,0:T(8,128)(2,1)} %get-tuple-element.103) | non-fusion elementwise | flops 2097152 | bytes 12582912 | tf_op jit(solution)/shard_map/convert_element_type | solution.py:2066
  636.4 0.0 copy-done.1
  636.4 4.4 convert_element_type.9
  640.9 4.6 convert_element_type.11
  645.5 0.0 copy-done.7
  645.5 0.0 copy-start.8
  645.5 0.8 copy.37
  646.3 1.0 copy.38
  647.3 0.6 copy.39
  647.9 0.8 copy.40
  648.7 0.8 copy.41
  649.5 0.0 copy-done.4
  649.5 0.8 copy.42
  650.3 0.8 copy.43
  651.1 0.7 copy.44
  (15 shorter events, 0.0 us)
Async XLA Ops:
  629.6 6.8 %copy-start.1 = (bf16[4,512,1024]{2,1,0:T(8,128)(2,1)S(1)}, bf16[4,512,1024]{2,1,0:T(8,128)(2,1)}, u32[]{:S(2)}) copy-start(bf16[4,512,1024]{2,1,0:T(8,128)(2,1)} %get-tuple-element.102) | copy-start | bytes 12582916
  636.4 4.4 copy-start
  640.9 4.6 copy-start.7
  640.9 5.4 copy-start.2
  640.9 6.4 copy-start.9
  640.9 7.0 %copy-start.6 = (f32[512,256]{1,0:T(8,128)S(1)}, f32[512,256]{1,0:T(8,128)}, u32[]{:S(2)}) copy-start(f32[512,256]{1,0:T(8,128)} %get-tuple-element.119) | copy-start | bytes 1572868
  645.5 3.2 copy-start.5
  645.5 4.0 copy-start.4
  645.5 4.8 copy-start.3
  645.5 5.6 copy-start.8

commit v7 on v6

--- a/solution.py
+++ b/solution.py
@@ -300,13 +300,13 @@
     normed_out,
     qkv_out,
     rows_out,
-    q_ref,
-    k_ref,
-    v_ref,
-    unit_ref,
+    q_out,
+    k_out,
+    v_out,
+    unit_out,
+    log_out,
+    attended_out,
     sums_ref,
-    log_ref,
-    attended_ref,
     residual_ref,
     gains_ref,
     seg_col_ref,
@@ -317,6 +317,12 @@
     down_full,
     choices,
     onehot_ref,
+    q_ref,
+    k_ref,
+    v_ref,
+    unit_ref,
+    log_ref,
+    attended_ref,
     normed,
     qkv,
     rows_full,
@@ -639,6 +645,19 @@
     for distance in range(heads + 2, chips):
         second.step(distance)
 
+    for index, (source, target) in enumerate(
+        (
+            (q_ref, q_out),
+            (k_ref, k_out),
+            (v_ref, v_out),
+            (unit_ref, unit_out),
+            (log_ref, log_out),
+            (attended_ref, attended_out),
+        )
+    ):
+        keeps.append(pltpu.make_async_copy(source, target, out_sem.at[3 + index]))
+        keeps[-1].start()
+
     reduce = ChainReduce(chips, residual_ref, reduce_buffers)
 
     def product(index, store):
@@ -799,9 +818,9 @@
             shape((length, local_width), half),
             shape((length, local_width), half),
             shape((2, length, local_width), f32),
-            shape((8, length), f32),
             shape((length, local_width), f32),
             shape((length, local_width), half),
+            shape((8, length), f32),
             shape((tok_rows, model_width), f32),
             shape(gains.shape, f32),
             shape((length, 128), f32),
@@ -814,8 +833,14 @@
             shape((size // 2, experts_local * 2 * CAP, 2 * tok_rows), half),
         ),
         in_specs=[vmem] * 7 + [anywhere] * 8,
-        out_specs=tuple([anywhere] * 3 + [vmem] * 10 + [anywhere] * 5 + [vmem] * 2),
+        out_specs=tuple([anywhere] * 9 + [vmem] * 4 + [anywhere] * 5 + [vmem] * 2),
         scratch_shapes=[
+            pltpu.VMEM((length, local_width), half),
+            pltpu.VMEM((length, local_width), half),
+            pltpu.VMEM((length, local_width), half),
+            pltpu.VMEM((2, length, local_width), f32),
+            pltpu.VMEM((length, local_width), f32),
+            pltpu.VMEM((length, local_width), half),
             pltpu.VMEM((length, model_width), half),
             pltpu.VMEM((3, model_width, local_width), half),
             pltpu.VMEM((split, *w_out.shape), half),
@@ -850,7 +875,7 @@
             kind((3,)),
             kind((3, split)),
             kind((3, split)),
-            kind((3,)),
+            kind((9,)),
             *ChainReduce.scratch(chips, tok_rows, model_width),
         ],
         compiler_params=pltpu.CompilerParams(
@@ -927,7 +952,6 @@
     out_grad_ref,
     gain_ref,
     router_grad_ref,
-    combine_ref,
     hidden_out,
     grad_gate_ref,
     grad_up_ref,
@@ -1046,7 +1070,6 @@
             )
             slot_rows = pl.ds(move * double, double)
             weighted = onehot_ref[pair, slot_rows, :].astype(f32) * weights
-            combine_ref[pair, slot_rows, :] = weighted.astype(half)
             gates_out[move, pair] = row_sums(weighted, ones)
 
         @pl.when((pair + 1 < pairs) & (slots == 1))
@@ -1131,7 +1154,8 @@
             sigmoid = 1.0 / (1.0 + jnp.exp(-pre))
             active = pre * sigmoid
             made = (active * up).astype(half)
-            hidden[move, :, :, cols] = made.reshape(pairs, double, cols_step)
+            weighted = made.astype(f32) * scales[:, 0:1]
+            hidden[move, :, :, cols] = weighted.astype(half).reshape(pairs, double, cols_step)
             dots = made.astype(f32) * plain
             for pair in range(pairs):
                 dots_out[move, pair] += row_sums(
@@ -1143,10 +1167,6 @@
             up_grad[move, :, :, cols] = (
                 (scaled * active).astype(half).reshape(pairs, double, cols_step)
             )
-
-        for pair in range(pairs):
-            scale = scales[pair * double : (pair + 1) * double, 0:1]
-            upstream[move, pair] = (upstream[move, pair].astype(f32) * scale).astype(half)
 
         if move:
             dots_copy(move).start()
@@ -1332,14 +1352,13 @@
             shape((tok_rows, model_width), half),
             shape((8, model_width), f32),
             shape((size * experts_local, model_width), f32),
-            shape(onehot.shape, half),
             shape(narrow_rows, half),
             shape(gate_full.shape, half),
             shape(up_full.shape, half),
             shape((split, hidden_width, model_width // split), half),
         ),
         in_specs=[anywhere, vmem, vmem, anywhere] + [vmem] * 4 + [anywhere] * 3,
-        out_specs=tuple([vmem] * 5 + [anywhere] * 4),
+        out_specs=tuple([vmem] * 4 + [anywhere] * 4),
         scratch_shapes=[
             pltpu.VMEM(gate_full.shape, half),
             pltpu.VMEM(up_full.shape, half),
@@ -1402,35 +1421,48 @@
 def back_kernel(
     sizes,
     out_grad_ref,
-    tokens_ref,
-    residual_grad_ref,
     gains_ref,
     second_gain_ref,
-    cos_ref,
-    sin_ref,
-    seg_col_ref,
     seg_row_ref,
-    q_ref,
-    k_ref,
-    v_ref,
-    unit_ref,
     sums_ref,
-    log_ref,
-    attended_ref,
-    qkv_ref,
-    rows_full_ref,
+    *refs,
+):
+    kept_count = 13
+    kept, refs = refs[:kept_count], refs[kept_count:]
+    back_body(sizes, out_grad_ref, gains_ref, second_gain_ref, seg_row_ref, sums_ref, kept, *refs)
+
+
+def back_body(
+    sizes,
+    out_grad_ref,
+    gains_ref,
+    second_gain_ref,
+    seg_row_ref,
+    sums_ref,
+    kept,
     normed_ref,
     hidden_ref,
     down_ref,
     grad_gate_ref,
     input_grad_ref,
     gains_out_ref,
-    query_w_grad_ref,
-    key_w_grad_ref,
-    value_w_grad_ref,
     out_w_grad_ref,
     mixed_rows,
     gate_landing,
+    qkv_out,
+    rows_full_ref,
+    attended_ref,
+    q_ref,
+    k_ref,
+    v_ref,
+    seg_col_ref,
+    log_ref,
+    cos_ref,
+    sin_ref,
+    unit_ref,
+    qkv_ref,
+    tokens_ref,
+    residual_grad_ref,
     down_full,
     out_grads,
     attended_grad,
@@ -1443,7 +1475,6 @@
     centers_own,
     centers_in,
     qkv_stage,
-    qkv_landing,
     out_stage,
     out_landing,
     load_sem,
@@ -1458,9 +1489,7 @@
     rows_recv,
     centers_send,
     centers_recv,
-    qkv_local,
-    qkv_send,
-    qkv_recv,
+    kept_sem,
     out_local,
     out_send,
     out_recv,
@@ -1469,7 +1498,7 @@
     size, split, chips, experts_local = sizes
     f32, half = jnp.float32, jnp.bfloat16
     me, mine = lax.axis_index("seq"), lax.axis_index("fsdp")
-    tok_rows, model_width = tokens_ref.shape
+    tok_rows, model_width = out_grad_ref.shape
     length, local_width = q_ref.shape
     hidden_width = down_ref.shape[0]
     part = model_width // split
@@ -1483,6 +1512,25 @@
     hidden_load = pltpu.make_async_copy(hidden_ref, hidden, load_sem.at[1])
     down_load.start()
     hidden_load.start()
+    targets = (
+        rows_full_ref,
+        attended_ref,
+        q_ref,
+        k_ref,
+        v_ref,
+        seg_col_ref,
+        log_ref,
+        cos_ref,
+        sin_ref,
+        unit_ref,
+        qkv_ref,
+        tokens_ref,
+        residual_grad_ref,
+    )
+    kept_loads = [
+        pltpu.make_async_copy(source, target, kept_sem.at[index])
+        for index, (source, target) in enumerate(zip(kept, targets))
+    ]
     greet_all(size, split)
     gather = ChainGather(chips, out_grad_ref, out_grads, gather_local, gather_send, gather_recv)
     gather.start()
@@ -1496,6 +1544,8 @@
     )
 
     gate_send_all.start()
+    for load in kept_loads:
+        load.start()
 
     down_load.wait()
     hidden_load.wait()
@@ -1530,6 +1580,8 @@
             rows_copy(move).start()
     own_rows.start()
     gather.steps()
+    for load in kept_loads:
+        load.wait()
     gather.landed()
 
     block = min(512, length)
@@ -1648,9 +1700,7 @@
             total += cross_dot(raw_grads[2, rows, :], qkv_ref[2, cols, :])
             store(cols, total)
 
-    qkv_send_all = ShardSend(
-        split, lambda dest: qkv_stage.at[dest], qkv_landing, qkv_local, qkv_send, qkv_recv
-    )
+    qkv_keep = pltpu.make_async_copy(qkv_stage, qkv_out, load_sem.at[1])
 
     def between():
         normed_load.wait()
@@ -1662,7 +1712,7 @@
             for index in range(3):
                 qkv_stage[piece, index] = turned_dot(left, raw_grads[index]).astype(half)
 
-        qkv_send_all.start()
+        qkv_keep.start()
 
     reduce.run(product, between)
 
@@ -1681,12 +1731,7 @@
     for index in range(1, split):
         total += out_landing[index].astype(f32)
     out_w_grad_ref[...] = total
-    qkv_send_all.wait()
-    for index, target in enumerate((query_w_grad_ref, key_w_grad_ref, value_w_grad_ref)):
-        total = qkv_landing[0, index].astype(f32)
-        for piece in range(1, split):
-            total += qkv_landing[piece, index].astype(f32)
-        target[...] = total
+    qkv_keep.wait()
     reduce.sent()
     own_rows.wait()
     for move in range(1, experts_local):
@@ -1694,12 +1739,11 @@
     gate_send_all.wait()
 
 
-def back(sizes, out_grad, tokens, residual_grad, gains, kept, big_ones, which):
+def back(sizes, out_grad, small, kept, big_ones, which):
     size, split, chips, experts_local = sizes
     f32, half = jnp.float32, jnp.bfloat16
-    tok_rows, model_width = tokens.shape
-    query_heads = kept[4]
-    length, local_width = query_heads.shape
+    tok_rows, model_width = out_grad.shape
+    length, local_width = kept[1].shape
     normed_seq, hidden, down_full, grad_gate = big_ones
     hidden_width = down_full.shape[0]
     part = model_width // split
@@ -1713,16 +1757,15 @@
         out_shape=(
             shape((tok_rows, model_width), f32),
             shape((8, model_width), f32),
-            shape((part, local_width), f32),
-            shape((part, local_width), f32),
-            shape((part, local_width), f32),
             shape((local_width, part), f32),
             shape((size // 2, experts_local * 2 * CAP, model_width), half),
             shape((split, part, hidden_width), half),
+            shape((split, 3, part, local_width), half),
         ),
-        in_specs=[vmem] * 18 + [anywhere] * 4,
-        out_specs=tuple([vmem] * 6 + [anywhere] * 2),
+        in_specs=[vmem] * 5 + [anywhere] * (len(kept) + 4),
+        out_specs=tuple([vmem] * 3 + [anywhere] * 3),
         scratch_shapes=[
+            *[pltpu.VMEM(one.shape, one.dtype) for one in kept],
             pltpu.VMEM(down_full.shape, half),
             pltpu.VMEM((length, model_width), half),
             pltpu.VMEM((length, local_width), half),
@@ -1734,7 +1777,6 @@
             pltpu.VMEM((3, length, local_width), half),
             pltpu.VMEM((8, length), f32),
             pltpu.VMEM((size, 8, length), f32),
-            pltpu.VMEM((split, 3, part, local_width), half),
             pltpu.VMEM((split, 3, part, local_width), half),
             pltpu.VMEM((split, local_width, part), half),
             pltpu.VMEM((split, local_width, part), half),
@@ -1750,9 +1792,7 @@
             few,
             kind((size,)),
             kind((size,)),
-            kind,
-            fsdp,
-            fsdp,
+            kind((len(kept),)),
             kind,
             fsdp,
             fsdp,
@@ -1766,21 +1806,33 @@
             bytes_accessed=500 * 2**20,
             transcendentals=0,
         ),
-    )(out_grad, tokens, residual_grad, *gains, *kept, *big_ones)
+    )(out_grad, *small, *kept, *big_ones)
 
 
 def close_kernel(
     sizes,
-    mixed_rows_ref,
-    combine_ref,
-    residual_ref,
+    onehot_ref,
     gains_ref,
     router_ref,
+    mixed_rows_any,
+    residual_any,
+    qkv_any,
     grad_up_ref,
     output_ref,
     gains_out_ref,
     router_out_ref,
+    query_w_grad_ref,
+    key_w_grad_ref,
+    value_w_grad_ref,
     up_landing,
+    mixed_rows_ref,
+    residual_ref,
+    qkv_ref,
+    qkv_in,
+    qkv_sum,
+    load_sem,
+    qkv_send,
+    qkv_recv,
     total,
     small,
     first,
@@ -1804,6 +1856,14 @@
     part = model_width // split
     slice_width = model_width // size
     experts_all = router_ref.shape[0]
+    loads = [
+        pltpu.make_async_copy(source, target, load_sem.at[index])
+        for index, (source, target) in enumerate(
+            ((qkv_any, qkv_ref), (mixed_rows_any, mixed_rows_ref), (residual_any, residual_ref))
+        )
+    ]
+    for load in loads:
+        load.start()
     small[0:8, :] = gains_ref[...]
     small[8 : 8 + experts_all, :] = router_ref[...]
     greet_all(size, split)
@@ -1815,6 +1875,44 @@
         up_send,
         up_recv,
     )
+    loads[0].wait()
+
+    half_part = qkv_ref.shape[2] // 2
+    lower, upper = pl.ds(0, half_part), pl.ds(half_part, half_part)
+    mates = (partner_of(mine, 1), partner_of(mine, 2), partner_of(mine, 3)) if split == 4 else ()
+
+    def qkv_copy(index):
+        side = index % 2
+        rows = (lower, upper)[side]
+        if index < 4:
+            dest = mates[side] if index < 2 else mates[2]
+            source, mate = qkv_ref.at[dest, :, rows], mates[side]
+        else:
+            source, mate = qkv_sum.at[side], mates[1 - side]
+        return pltpu.make_async_remote_copy(
+            src_ref=source,
+            dst_ref=qkv_in.at[index],
+            send_sem=qkv_send.at[index],
+            recv_sem=qkv_recv.at[index],
+            device_id={"fsdp": mate},
+        )
+
+    def qkv_shift(shift):
+        dest = lax.rem(mine + shift, split)
+        return pltpu.make_async_remote_copy(
+            src_ref=qkv_ref.at[dest],
+            dst_ref=qkv_in.at[shift],
+            send_sem=qkv_send.at[shift],
+            recv_sem=qkv_recv.at[shift],
+            device_id={"fsdp": dest},
+        )
+
+    if split == 4:
+        for index in range(4):
+            qkv_copy(index).start()
+    else:
+        for shift in range(1, split):
+            qkv_shift(shift).start()
     up_send_all.start()
 
     def columns(index):
@@ -1857,7 +1955,7 @@
 
     def product(index, store):
         side = pl.ds(pl.multiple_of(lax.rem(index, 2) * tok_rows, tok_rows), tok_rows)
-        left = combine_ref[index // 2, :, side]
+        left = onehot_ref[index // 2, :, side]
 
         @pl.loop(0, model_width // width_step)
         def _(step):
@@ -1871,7 +1969,17 @@
         for shift in range(1, split):
             share(shift).start()
 
+    loads[1].wait()
     reduce.run(product, between)
+    if split == 4:
+        for side in range(2):
+            qkv_copy(2 + side).wait_recv()
+            rows = (lower, upper)[side]
+            qkv_sum[side] = (
+                qkv_ref[mates[1 - side], :, rows].astype(f32) + qkv_in[2 + side].astype(f32)
+            ).astype(qkv_sum.dtype)
+            qkv_copy(4 + side).start()
+    loads[2].wait()
     for shift in range(1, split):
         share(shift).wait_recv()
     final[me] = jnp.sum(second[...], 0)
@@ -1888,11 +1996,33 @@
         cols = slice(index * slice_width, (index + 1) * slice_width)
         gains_out_ref[:, cols] = final[index, 0:4]
         router_out_ref[:, cols] = final[index, 8:]
+    targets = (query_w_grad_ref, key_w_grad_ref, value_w_grad_ref)
+    if split == 4:
+        for side in range(2):
+            for index in (side, 2 + side, 5 - side):
+                copy = qkv_copy(index)
+                copy.wait() if index < 2 or index > 3 else copy.wait_send()
+        for side in range(2):
+            rows = (lower, upper)[side]
+            for index, target in enumerate(targets):
+                target[rows, :] = (
+                    qkv_ref[mine, index, rows].astype(f32)
+                    + qkv_in[side, index].astype(f32)
+                    + qkv_in[4 + side, index].astype(f32)
+                )
+    else:
+        for shift in range(1, split):
+            qkv_shift(shift).wait()
+        for index, target in enumerate(targets):
+            sums = qkv_ref[mine, index].astype(f32)
+            for shift in range(1, split):
+                sums += qkv_in[shift, index].astype(f32)
+            target[...] = sums
     reduce.sent()
     up_send_all.wait()
 
 
-def close(sizes, mixed_rows, combine, residual, gains, router_grad, grad_up, which):
+def close(sizes, onehot, gains, router_grad, mixed_rows, residual, qkv_parts, grad_up, which):
     size, split, chips, experts_local = sizes
     f32, half = jnp.float32, jnp.bfloat16
     tok_rows, model_width = residual.shape
@@ -1904,17 +2034,29 @@
     kind = pltpu.SemaphoreType.DMA
     shape = jax.ShapeDtypeStruct
     seq, fsdp = kind((size,)), kind((split,))
+    share = qkv_parts.shape[2:]
     return pl.pallas_call(
         functools.partial(close_kernel, sizes),
         out_shape=(
             shape((tok_rows, model_width), half),
             shape((4, model_width), f32),
             shape(router_grad.shape, f32),
+            shape(share, f32),
+            shape(share, f32),
+            shape(share, f32),
             shape((split, part, hidden_width), half),
         ),
-        in_specs=[vmem] * 5 + [anywhere],
-        out_specs=(vmem, vmem, vmem, anywhere),
+        in_specs=[vmem] * 3 + [anywhere] * 4,
+        out_specs=tuple([vmem] * 6 + [anywhere]),
         scratch_shapes=[
+            pltpu.VMEM(mixed_rows.shape, half),
+            pltpu.VMEM(residual.shape, f32),
+            pltpu.VMEM(qkv_parts.shape, half),
+            pltpu.VMEM((6, 3, share[0] // 2, share[1]) if split == 4 else qkv_parts.shape, half),
+            pltpu.VMEM((2, 3, share[0] // 2, share[1]), half),
+            kind((3,)),
+            kind((max(6, split),)),
+            kind((max(6, split),)),
             pltpu.VMEM((tok_rows, model_width), f32),
             pltpu.VMEM((rows, model_width), f32),
             pltpu.VMEM((size, rows, slice_width), f32),
@@ -1934,7 +2076,54 @@
         compiler_params=pltpu.CompilerParams(
             collective_id=which, has_side_effects=True, vmem_limit_bytes=56 * 2**20
         ),
-    )(mixed_rows, combine, residual, gains, router_grad, grad_up)
+    )(onehot, gains, router_grad, mixed_rows, residual, qkv_parts, grad_up)
+
+
+def finish_kernel(count, *refs):
+    sources, targets = refs[: len(refs) // 2], refs[len(refs) // 2 :]
+    for source, target in zip(sources[:count], targets[:count]):
+        target[...] = source[...]
+    for source, target in zip(sources[count:], targets[count:]):
+        total = source[0].astype(target.dtype)
+        for index in range(1, source.shape[0]):
+            total += source[index].astype(target.dtype)
+        target[...] = total
+
+
+def finish(results, landings, experts_local):
+    halves = 2
+    steps = experts_local * halves
+    in_specs, out_specs, shapes = [], [], []
+    for one in results:
+        rows = one.shape[0] // steps
+        spec = pl.BlockSpec((rows, one.shape[1]), lambda step: (step, 0))
+        if one.shape[0] % (steps * 16):
+            spec = pl.BlockSpec(one.shape, lambda step: (0, 0))
+        in_specs.append(spec)
+        out_specs.append(spec)
+        shapes.append(jax.ShapeDtypeStruct(one.shape, one.dtype))
+    grouped = []
+    for one in landings:
+        groups = one.shape[0] // experts_local
+        grouped.append(one.reshape(groups, experts_local, *one.shape[1:]))
+        block = (one.shape[1] // halves, one.shape[2])
+        in_specs.append(
+            pl.BlockSpec(
+                (groups, 1, *block), lambda step: (0, step // halves, step % halves, 0)
+            )
+        )
+        out_specs.append(
+            pl.BlockSpec((1, *block), lambda step: (step // halves, step % halves, 0))
+        )
+        shapes.append(jax.ShapeDtypeStruct((experts_local, *one.shape[1:]), jnp.float32))
+    return pl.pallas_call(
+        functools.partial(finish_kernel, len(results)),
+        grid=(steps,),
+        in_specs=in_specs,
+        out_specs=out_specs,
+        out_shape=shapes,
+        compiler_params=pltpu.CompilerParams(vmem_limit_bytes=63 * 2**20),
+    )(*results, *grouped)
 
 
 def shards(
@@ -1970,9 +2159,9 @@
         key_heads,
         value_heads,
         unit_pair,
-        square_sums,
         log_wide,
         attended_heads,
+        square_sums,
         residual,
         gain_rows,
         segment_cols,
@@ -2006,7 +2195,6 @@
         out_grad,
         gain_second_grad,
         router_grad,
-        combine,
         hidden,
         grad_gate_full,
         grad_up_full,
@@ -2024,47 +2212,57 @@
         (gate_full, up_full, down_full),
         1,
     )
+    input_grad, gain_grads, out_owned, mixed_rows, gate_landing, qkv_parts = back(
+        sizes,
+        out_grad,
+        (gain_rows, gain_second_grad, segment_row, square_sums),
+        (
+            out_stack,
+            attended_heads,
+            query_heads,
+            key_heads,
+            value_heads,
+            segment_cols,
+            log_wide,
+            cosine_wide,
+            sine_wide,
+            unit_pair,
+            qkv_stack,
+            tokens,
+            residual_grad,
+        ),
+        (normed_seq, hidden, down_full, grad_gate_full),
+        2,
+    )
+    output, gain_sums, router_sums, query_owned, key_owned, value_owned, up_landing = close(
+        sizes, onehot, gain_grads, router_grad, mixed_rows, residual, qkv_parts, grad_up_full, 3
+    )
     (
+        output,
         input_grad,
-        gain_grads,
+        gain_sums,
         query_owned,
         key_owned,
         value_owned,
         out_owned,
-        mixed_rows,
-        gate_landing,
-    ) = back(
-        sizes,
-        out_grad,
-        tokens,
-        residual_grad,
-        (gain_rows, gain_second_grad),
+        router_sums,
+        gate_owned,
+        up_owned,
+        down_owned,
+    ) = finish(
         (
-            cosine_wide,
-            sine_wide,
-            segment_cols,
-            segment_row,
-            query_heads,
-            key_heads,
-            value_heads,
-            unit_pair,
-            square_sums,
-            log_wide,
-            attended_heads,
-            qkv_stack,
-            out_stack,
+            output,
+            input_grad,
+            gain_sums,
+            query_owned,
+            key_owned,
+            value_owned,
+            out_owned,
+            router_sums,
         ),
-        (normed_seq, hidden, down_full, grad_gate_full),
-        2,
-    )
-    output, gain_sums, router_sums, up_landing = close(
-        sizes, mixed_rows, combine, residual, gain_grads, router_grad, grad_up_full, 3
-    )
-
-    def owned(landing):
-        shape = (split // experts_local, experts_local, *landing.shape[1:])
-        return landing.astype(jnp.float32).reshape(shape).sum(0)
-
+        (gate_landing, up_landing, down_landing),
+        experts_local,
+    )
     return (
         output,
         input_grad,
@@ -2074,9 +2272,9 @@
         value_owned,
         out_owned,
         router_sums.T,
-        owned(gate_landing),
-        owned(up_landing),
-        owned(down_landing),
+        gate_owned,
+        up_owned,
+        down_owned,
     )
 
 

time: 661 us -> 627 us (0.949); the launches traced: 652 us -> 626 us
  other arithmetic: 15.8 us -> 0 us
    pallas_call x1, Pallas kernels: 157 us -> 122 us  [back(): pl.pallas_call(functools.partial(back_kernel, sizes), out_shape=(shape((t...]
    pallas_call x1, Pallas kernels: 63.6 us -> 80.2 us  [close(): pl.pallas_call(functools.partial(close_kernel, sizes), out_shape=(shape((...]
    pallas_call x0 -> x1, Pallas kernels: none -> 16.6 us  [finish(): pl.pallas_call(functools.partial(finish_kernel, len(results)), grid=(step...]
    convert_element_type x3 -> x0, other arithmetic: 15.8 us -> none  [owned(): return landing.astype(jnp.float32).reshape(shape).sum(0)]
where the time goes in v7:
time: 627 us; the launch traced here: 626 us
  Pallas kernels  621 us (99%)
    pallas_call x1, Pallas kernels, front(): pl.pallas_call(functools.partial(front_kernel, sizes), out_shape=(shape((...  224 us
    pallas_call x1, Pallas kernels, experts(): pl.pallas_call(functools.partial(experts_kernel, sizes), out_shape=(shape...  179 us
    pallas_call x1, Pallas kernels, back(): pl.pallas_call(functools.partial(back_kernel, sizes), out_shape=(shape((t...  122 us
    pallas_call x1, Pallas kernels, close(): pl.pallas_call(functools.partial(close_kernel, sizes), out_shape=(shape((...  80.2 us
    pallas_call x1, Pallas kernels, finish(): pl.pallas_call(functools.partial(finish_kernel, len(results)), grid=(step...  16.6 us

profile of v7, /device:TPU:0, one launch (start us, length us, event | category | flops | bytes accessed | tf_op | source)
XLA Modules:
  0.0 626.4 jit_solution(1285154658427628588)
XLA Ops:
  0.6 1.4 copy.27.ids_ref
  2.1 1.4 copy.28.slots_ref
  3.5 1.0 reshape.73
  4.4 0.7 pad_bitcast_fusion.router_ref
  5.2 223.9 %shard_map.239 = (bf16[1024,2048]{1,0:T(8,128)(2,1)}, bf16[3,2048,256]{2,1,0:T(8,128)(2,1)}, bf16[4,256,512]{2,1,0:T(8,128)(2,1)}, bf16[1024,256]{1,0:T(8,128)(2...) custom-call(bf16[128,2048]{1,0:T(8,128)(2,1)} %refs_11_.1, ...), custom_call_target="tpu_custom_call" | custom-call | flops 4294967296 | bytes 524288000 | tf_op jit(solution)/shard_map/pallas_call | solution.py:811
  229.1 178.6 %shard_map.240 = (f32[128,2048]{1,0:T(8,128)}, bf16[128,2048]{1,0:T(8,128)(2,1)}, f32[8,2048]{1,0:T(8,128)}, f32[32,2048]{1,0:T(8,128)}, bf16[4,4,80,1024]{3,2,1...) custom-call(bf16[1024,2048]{1,0:T(8,128)(2,1)} %get-tuple-element.76.routed_, ...), custom_call_target="tpu_custom_call" | custom-call | flops 42949672960 | bytes 524288000 | tf_op jit(solution)/shard_map/pallas_call | solution.py:1348
  407.8 121.7 %shard_map.241 = (f32[128,2048]{1,0:T(8,128)}, f32[8,2048]{1,0:T(8,128)}, f32[256,512]{1,0:T(8,128)}, bf16[4,320,2048]{2,1,0:T(8,128)(2,1)}, bf16[4,512,1024]{2,...) custom-call(bf16[128,2048]{1,0:T(8,128)(2,1)} %get-tuple-element.84.out_grad_ref, f32[4,2048]{1,0:T(4,128)} %get-tuple-element.79.gains_ref, ...), custom_call_target="tpu_custom_call" | custom-call | flops 8589934592 | bytes 524288000 | tf_op jit(solution)/shard_map/pallas_call | solution.py:1755
  529.4 80.2 %shard_map.242 = (bf16[128,2048]{1,0:T(8,128)(2,1)}, f32[4,2048]{1,0:T(4,128)}, f32[32,2048]{1,0:T(8,128)}, f32[512,256]{1,0:T(8,128)}, f32[512,256]{1,0:T(8,128...) custom-call(bf16[4,320,256]{2,1,0:T(8,128)(2,1)} %get-tuple-element.75.onehot_ref, ...), custom_call_target="tpu_custom_call" | custom-call | tf_op jit(solution)/shard_map/pallas_call | solution.py:2038
  609.7 16.6 %shard_map.243 = (bf16[128,2048]{1,0:T(8,128)(2,1)}, f32[128,2048]{1,0:T(8,128)}, f32[4,2048]{1,0:T(4,128)}, f32[512,256]{1,0:T(8,128)}, f32[512,256]{1,0:T(8,12...) custom-call(bf16[128,2048]{1,0:T(8,128)(2,1)} %get-tuple-element.105, ...), custom_call_target="tpu_custom_call" | custom-call | tf_op jit(solution)/shard_map/pallas_call | solution.py:2119

commit v8 on v7

--- a/solution.py
+++ b/solution.py
@@ -179,7 +179,7 @@
         dest = self.chip + (1 - 2 * lax.rem(index, 2)) * distance
         return dest, (dest >= 0) & (dest < self.chips)
 
-    def run(self, product, between=None):
+    def run(self, product, between=None, hook=None):
         chips, chip, core, total = self.chips, self.chip, self.core, self.total
         sibling = chip * 2 + 1 - core
 
@@ -201,6 +201,8 @@
         @pl.loop(0, 2 * chips - 1)
         def _(index):
             dest, inside = self.place(index)
+            if hook:
+                hook(index)
 
             @pl.when(inside)
             def _():
@@ -311,12 +313,14 @@
     gains_ref,
     seg_col_ref,
     routed_out,
-    cotangent_rows,
+    routed_cross,
+    placed_out,
     gate_full,
     up_full,
     down_full,
     choices,
     onehot_ref,
+    mate_onehot,
     q_ref,
     k_ref,
     v_ref,
@@ -331,7 +335,6 @@
     cotangent_pair,
     cotangent_all,
     mate_choices,
-    mate_onehot,
     placed,
     raw,
     sums_own,
@@ -349,8 +352,6 @@
     cross_send,
     cross_recv,
     placed_local,
-    placed_send,
-    placed_recv,
     shard_local,
     shard_send,
     shard_recv,
@@ -372,7 +373,8 @@
     inputs = tokens_ref[...].astype(f32)
     inverse = lax.rsqrt(jnp.mean(inputs * inputs, -1, keepdims=True) + EPSILON)
     gains_ref[...] = gains_in_ref[...].astype(f32)
-    routed_own[...] = (inputs * inverse * gains_ref[0:1, :]).astype(half)
+    routed_half = routed_own.at[pl.ds(0, tok_rows)]
+    routed_half[...] = (inputs * inverse * gains_ref[0:1, :]).astype(half)
     crossed = split == experts_local == 4
     half_width = model_width // 2
     x_mate, y_mate = {"fsdp": partner_of(mine, 1)}, {"fsdp": partner_of(mine, 2)}
@@ -388,20 +390,23 @@
             gather_recv.at[index],
         )
 
-    first = gather(0, routed_own, normed)
+    first = gather(0, routed_half, normed)
     first.start()
 
     cross_rows = pl.ds(tok_rows, tok_rows)
     lower, upper = pl.ds(0, half_width), pl.ds(half_width, half_width)
 
     def cross_copy(index):
-        cols = (lower, upper)[index]
+        cols = (lower, upper)[index % 2]
+        source, target = (
+            (cotangent_ref, cotangent_pair) if index < 2 else (routed_half, routed_own)
+        )
         return pltpu.make_async_remote_copy(
-            src_ref=cotangent_ref.at[:, cols],
-            dst_ref=cotangent_pair.at[cross_rows, cols],
+            src_ref=source.at[:, cols],
+            dst_ref=target.at[cross_rows, cols],
             send_sem=cross_send.at[index],
             recv_sem=cross_recv.at[index],
-            device_id=(x_mate, y_mate)[index],
+            device_id=(x_mate, y_mate)[index % 2],
         )
 
     if crossed:
@@ -521,10 +526,13 @@
         else:
             for shift in range(1, split):
                 shard_copy(index, shift).wait_recv()
-    for index in range(3):
+
+    def expert_start(index):
         for shift in range(1, split):
             expert_copy(index, shift).start()
         expert_own(index).start()
+
+    expert_start(0)
     first.landed()
     for shift in range(1, size):
         choice_copy(shift).start()
@@ -639,12 +647,7 @@
             ).astype(half)
             log_ref[rows, cols] = jnp.broadcast_to(peak + jnp.log(weight), (wide, head))
 
-        if number + 2 < chips:
-            second.step(number + 2)
-
-    for distance in range(heads + 2, chips):
-        second.step(distance)
-
+    expert_start(1)
     for index, (source, target) in enumerate(
         (
             (q_ref, q_out),
@@ -666,14 +669,27 @@
             cols = pl.ds(piece * part, part)
             store(cols, jnp.dot(left, rows_full[piece], preferred_element_type=f32))
 
-    reduce.run(product)
+    def hook(index):
+        for distance in range(2, chips - 1):
+
+            @pl.when(index == 2 * distance)
+            def _():
+                second.step(distance)
+
+    reduce.run(product, hook=hook)
     residual = tokens_ref[...].astype(f32) + reduce.total[...]
     residual_ref[...] = residual
     inverse = lax.rsqrt(jnp.mean(residual * residual, -1, keepdims=True) + EPSILON)
     first.sent()
-    routed_own[...] = (residual * inverse * gains_ref[1:2, :]).astype(half)
-    third = gather(2, routed_own, routed_out)
+    routed_half[...] = (residual * inverse * gains_ref[1:2, :]).astype(half)
+    if crossed:
+        cross_copy(2).start()
+        cross_copy(3).start()
+    third = gather(2, routed_half, routed_out)
     third.start()
+    if chips > 2:
+        second.step(chips - 1)
+    expert_start(2)
 
     second.landed()
     double = 2 * CAP
@@ -722,13 +738,15 @@
                 for row, expert in enumerate((member, partner_of(member, 2 - index))):
                     one_hot(
                         lambda side: mate_choices[index, pair * 2 + side],
-                        mate_onehot.at[index],
+                        mate_onehot.at[pair, index],
                         slot_range(row),
                         expert,
                     )
                 cols = (lower, upper)[index]
                 taken = mates[:, :half_width] if index == 0 else mates[:, half_width:]
-                made = jnp.dot(mate_onehot[index], taken, preferred_element_type=f32).astype(half)
+                made = jnp.dot(
+                    mate_onehot[pair, index], taken, preferred_element_type=f32
+                ).astype(half)
                 placed[index + 1, pair, :, cols] = made[slot_range(0)]
                 placed[3, pair, :, cols] = made[slot_range(1)]
         else:
@@ -741,39 +759,17 @@
             for move in range(experts_local):
                 placed[move, pair] = made[slot_range(move)]
 
-    def placed_copy(index):
-        if crossed:
-            move, cols = ((1, upper), (2, lower), (3, upper), (3, lower))[index]
-            source, target = placed.at[move, :, :, cols], cotangent_rows.at[move, :, :, cols]
-            mate = (x_mate, y_mate)[index % 2]
-        else:
-            source, target = placed.at[index], cotangent_rows.at[index]
-            mate = {"fsdp": partner_of(mine, index)}
-        return pltpu.make_async_remote_copy(
-            src_ref=source,
-            dst_ref=target,
-            send_sem=placed_send.at[index],
-            recv_sem=placed_recv.at[index],
-            device_id=mate,
-        )
-
-    if crossed:
-        placed_pieces = [
-            (placed.at[0], cotangent_rows.at[0]),
-            (placed.at[1, :, :, lower], cotangent_rows.at[1, :, :, lower]),
-            (placed.at[2, :, :, upper], cotangent_rows.at[2, :, :, upper]),
-        ]
-    else:
-        placed_pieces = [(placed.at[0], cotangent_rows.at[0])]
-    placed_sends = [placed_copy(index) for index in range(0 if crossed else 1, experts_local)]
-    placed_owns = [
-        pltpu.make_async_copy(source, target, placed_local.at[index])
-        for index, (source, target) in enumerate(placed_pieces)
-    ]
-    for copy in placed_sends + placed_owns:
-        copy.start()
+    placed_keep = pltpu.make_async_copy(placed, placed_out, placed_local.at[0])
+    placed_keep.start()
     third.steps()
     third.landed()
+    if crossed:
+        cross_copy(2).wait()
+        cross_copy(3).wait()
+        cross_keep = pltpu.make_async_copy(
+            routed_own.at[cross_rows], routed_cross, placed_local.at[1]
+        )
+        cross_keep.start()
     reduce.sent()
     second.sent()
     third.sent()
@@ -786,8 +782,9 @@
                 shard_copy(index, shift).wait_send()
     for keep in keeps:
         keep.wait()
-    for copy in placed_sends + placed_owns:
-        copy.wait()
+    placed_keep.wait()
+    if crossed:
+        cross_keep.wait()
     for index in range(3):
         expert_own(index).wait()
         for shift in range(1, split):
@@ -825,15 +822,17 @@
             shape(gains.shape, f32),
             shape((length, 128), f32),
             shape((length, model_width), half),
+            shape((tok_rows, model_width), half),
             shape((experts_local, size // 2, 2 * CAP, model_width), half),
             shape((model_width, hidden_width), half),
             shape((model_width, hidden_width), half),
             shape((hidden_width, model_width), half),
             shape((size, 2 * ids.shape[1], tok_rows), jnp.int32),
             shape((size // 2, experts_local * 2 * CAP, 2 * tok_rows), half),
+            shape((size // 2 if crossed else 1, 2, 4 * CAP, 2 * tok_rows), half),
         ),
         in_specs=[vmem] * 7 + [anywhere] * 8,
-        out_specs=tuple([anywhere] * 9 + [vmem] * 4 + [anywhere] * 5 + [vmem] * 2),
+        out_specs=tuple([anywhere] * 9 + [vmem] * 4 + [anywhere] * 6 + [vmem] * 3),
         scratch_shapes=[
             pltpu.VMEM((length, local_width), half),
             pltpu.VMEM((length, local_width), half),
@@ -844,12 +843,11 @@
             pltpu.VMEM((length, model_width), half),
             pltpu.VMEM((3, model_width, local_width), half),
             pltpu.VMEM((split, *w_out.shape), half),
-            pltpu.VMEM((tok_rows, model_width), half),
+            pltpu.VMEM((2 * tok_rows, model_width), half),
             pltpu.VMEM((2 * ids.shape[1], tok_rows), jnp.int32),
             pltpu.VMEM((2 * tok_rows if crossed else 16, model_width), half),
             pltpu.VMEM(((2 if crossed else 1) * length, model_width), half),
             pltpu.VMEM((2, *(choices if crossed else (1, 8, 128))), jnp.int32),
-            pltpu.VMEM((2, 4 * CAP if crossed else 16, 2 * tok_rows), half),
             pltpu.VMEM((experts_local, size // 2, 2 * CAP, model_width), half),
             pltpu.VMEM((2, length, local_width), f32),
             pltpu.VMEM((8, length), f32),
@@ -864,11 +862,9 @@
             kind((2,)),
             kind((2,)),
             kind,
+            kind((4,)),
+            kind((4,)),
             kind((2,)),
-            kind((2,)),
-            kind((3,)),
-            kind((experts_local,)),
-            kind((experts_local,)),
             kind((4,)),
             kind((4, split)),
             kind((4, split)),
@@ -938,9 +934,11 @@
 def experts_kernel(
     sizes,
     routed_ref,
+    routed_cross_ref,
     choices_ref,
     onehot_ref,
-    cotangent_rows_ref,
+    mate_onehot_ref,
+    placed_ref,
     router_ref,
     gains_ref,
     residual_ref,
@@ -956,6 +954,7 @@
     grad_gate_ref,
     grad_up_ref,
     down_landing,
+    routed_mates,
     gate_full,
     up_full,
     down_full,
@@ -978,6 +977,11 @@
     load_sem,
     pair_sem,
     keep_sem,
+    gather_local,
+    gather_send,
+    gather_recv,
+    upstream_send,
+    upstream_recv,
     rows_send,
     rows_recv,
     gates_send,
@@ -1003,6 +1007,9 @@
     rows_of = pairs * double
     part = model_width // split
     member = lax.rem(mine, experts_local)
+    crossed = split == experts_local == 4
+    half_width = model_width // 2
+    lower, upper = pl.ds(0, half_width), pl.ds(half_width, half_width)
 
     loads = [
         pltpu.make_async_copy(source, target, load_sem.at[index])
@@ -1011,24 +1018,64 @@
                 (gate_ref, gate_full),
                 (up_ref, up_full),
                 (down_ref, down_full),
-                (cotangent_rows_ref, upstream),
             )
         )
     ]
+    if crossed:
+        pieces = (
+            (placed_ref.at[0], upstream.at[0]),
+            (placed_ref.at[1, :, :, lower], upstream.at[1, :, :, lower]),
+            (placed_ref.at[2, :, :, upper], upstream.at[2, :, :, upper]),
+        )
+    else:
+        pieces = ((placed_ref.at[0], upstream.at[0]),)
+    loads += [
+        pltpu.make_async_copy(source, target, load_sem.at[3 + index])
+        for index, (source, target) in enumerate(pieces)
+    ]
 
     slots = pair_rows.shape[0]
 
-    def pair_load(pair):
+    def pair_load(source, pair):
         slot = lax.rem(pair, slots)
         start = pl.multiple_of(pair * wide, wide)
         return pltpu.make_async_copy(
-            routed_ref.at[pl.ds(start, wide)], pair_rows.at[slot], pair_sem.at[slot]
-        )
-
-    pair_load(0).start()
+            source.at[pl.ds(start, wide)], pair_rows.at[slot], pair_sem.at[slot]
+        )
+
+    pair_load(routed_ref, 0).start()
     for load in loads:
         load.start()
     greet_all(size, split)
+
+    def mate(move):
+        return {"fsdp": partner_of(mine, move)}
+
+    def upstream_piece(move, index, cols, target):
+        return pltpu.make_async_remote_copy(
+            src_ref=placed_ref.at[move, :, :, cols],
+            dst_ref=upstream.at[move, :, :, cols],
+            send_sem=upstream_send.at[index],
+            recv_sem=upstream_recv.at[index],
+            device_id=mate(target),
+        )
+
+    def halves_of(piece, move):
+        if not crossed:
+            return [piece(move, move, pl.ds(0, model_width), move)]
+        if move == 3:
+            return [piece(3, 3, upper, 1), piece(3, 0, lower, 2)]
+        return [piece(move, move, (upper, lower)[move - 1], move)]
+
+    order = [1, 2, 3] if crossed else list(range(experts_local - 1, 0, -1))
+    if crossed:
+        gather = ChainGather(
+            chips, routed_cross_ref, routed_mates, gather_local, gather_send, gather_recv
+        )
+        gather.start()
+    for move in order:
+        for copy in halves_of(upstream_piece, move):
+            copy.start()
 
     padded = size * 8
     expert_row = lax.broadcasted_iota(jnp.int32, (padded, tok_rows), 0)
@@ -1039,11 +1086,11 @@
 
     @pl.loop(0, pairs)
     def _(pair):
-        pair_load(pair).wait()
+        pair_load(routed_ref, pair).wait()
 
         @pl.when((pair + 1 < pairs) & (slots > 1))
         def _():
-            pair_load(pair + 1).start()
+            pair_load(routed_ref, pair + 1).start()
 
         rows = pair_rows[lax.rem(pair, slots)]
         logits = lax.dot_general(
@@ -1060,10 +1107,15 @@
         placed = jnp.dot(onehot_ref[pair], rows, preferred_element_type=f32).astype(half)
         for move in range(experts_local):
             piece = placed[move * double : (move + 1) * double]
-            if move:
+            if move == 0:
+                arrived[0, pair] = piece
+            elif not crossed:
                 outgoing[move - 1, pair] = piece
-            else:
-                arrived[0, pair] = piece
+            elif move < 3:
+                cols = (upper, lower)[move - 1]
+                outgoing[move - 1, pair, :, cols] = (
+                    piece[:, half_width:] if move == 1 else piece[:, :half_width]
+                )
             row = me * 8 + partner_of(member, move)
             weights = jnp.concatenate(
                 [gates[pair * 2, pl.ds(row, 1), :], gates[pair * 2 + 1, pl.ds(row, 1), :]], 1
@@ -1074,18 +1126,15 @@
 
         @pl.when((pair + 1 < pairs) & (slots == 1))
         def _():
-            pair_load(pair + 1).start()
-
-    def mate(move):
-        return {"fsdp": partner_of(mine, move)}
-
-    def rows_copy(move):
+            pair_load(routed_ref, pair + 1).start()
+
+    def rows_piece(move, index, cols, target):
         return pltpu.make_async_remote_copy(
-            src_ref=outgoing.at[move - 1],
-            dst_ref=arrived.at[move],
-            send_sem=rows_send.at[move],
-            recv_sem=rows_recv.at[move],
-            device_id=mate(move),
+            src_ref=outgoing.at[move - 1, :, :, cols],
+            dst_ref=arrived.at[move, :, :, cols],
+            send_sem=rows_send.at[index],
+            recv_sem=rows_recv.at[index],
+            device_id=mate(target),
         )
 
     def gates_copy(move):
@@ -1118,13 +1167,43 @@
             device_id=mate(move),
         )
 
-    order = list(range(experts_local - 1, 0, -1))
     for move in order:
         gates_copy(move).start()
-        rows_copy(move).start()
+        if not crossed or move < 3:
+            for copy in halves_of(rows_piece, move):
+                copy.start()
     gates_in[0] = gates_out[0]
     for load in loads:
         load.wait()
+    if crossed:
+        gather.step(1)
+
+    def mates_rows():
+        for distance in range(3, chips):
+            gather.step(distance)
+        gather.landed()
+        pair_load(routed_mates, 0).start()
+
+        @pl.loop(0, pairs)
+        def _(pair):
+            pair_load(routed_mates, pair).wait()
+
+            @pl.when(pair + 1 < pairs)
+            def _():
+                pair_load(routed_mates, pair + 1).start()
+
+            for index, cols in enumerate((lower, upper)):
+                made = jnp.dot(
+                    mate_onehot_ref[pair, index],
+                    pair_rows[lax.rem(pair, slots), :, cols],
+                    preferred_element_type=f32,
+                ).astype(half)
+                arrived[index + 1, pair, :, cols] = made[0:double]
+                outgoing[2, pair, :, cols] = made[double:]
+
+        for copy in halves_of(rows_piece, 3):
+            copy.start()
+        gather.sent()
 
     cols_step = min(256, hidden_width)
     width_step = min(512, model_width)
@@ -1132,7 +1211,8 @@
     for move in [0] + order:
         if move:
             gates_copy(move).wait()
-            rows_copy(move).wait()
+            for copy in halves_of(rows_piece, move) + halves_of(upstream_piece, move):
+                copy.wait()
         for pair in range(pairs):
             scales[pair * double : (pair + 1) * double, :] = column_of(
                 gates_in[move, pair], spread
@@ -1172,6 +1252,8 @@
             dots_copy(move).start()
         else:
             dots_in[0] = dots_out[0]
+            if crossed and chips > 2:
+                gather.step(2)
 
         @pl.loop(0, model_width // width_step)
         def _(index):
@@ -1196,6 +1278,8 @@
 
         if move:
             back_copy(move).start()
+        elif crossed:
+            mates_rows()
 
     own_rows = pl.ds(pl.multiple_of(me * tok_rows, tok_rows), tok_rows)
     own_load = pltpu.make_async_copy(
@@ -1321,9 +1405,11 @@
 def experts(
     sizes,
     routed_seq,
+    routed_cross,
     choices,
     onehot,
-    cotangent_rows,
+    mate_onehot,
+    placed,
     router_rows,
     gain_rows,
     residual,
@@ -1342,6 +1428,7 @@
     kind = pltpu.SemaphoreType.DMA
     shape = jax.ShapeDtypeStruct
     few = kind((experts_local,))
+    crossed = split == experts_local == 4
     wide_rows = (experts_local, pairs, double, model_width)
     narrow_rows = (experts_local, pairs, double, hidden_width)
     flags = (experts_local, pairs, 8, double)
@@ -1356,9 +1443,10 @@
             shape(gate_full.shape, half),
             shape(up_full.shape, half),
             shape((split, hidden_width, model_width // split), half),
+            shape(routed_seq.shape if crossed else (16, model_width), half),
         ),
-        in_specs=[anywhere, vmem, vmem, anywhere] + [vmem] * 4 + [anywhere] * 3,
-        out_specs=tuple([vmem] * 4 + [anywhere] * 4),
+        in_specs=[anywhere] * 2 + [vmem] * 3 + [anywhere] + [vmem] * 4 + [anywhere] * 3,
+        out_specs=tuple([vmem] * 4 + [anywhere] * 5),
         scratch_shapes=[
             pltpu.VMEM(gate_full.shape, half),
             pltpu.VMEM(up_full.shape, half),
@@ -1379,9 +1467,14 @@
             pltpu.VMEM((size, 8, tok_rows), f32),
             pltpu.VMEM((size, 8, tok_rows), f32),
             pltpu.VMEM((pairs * double, 128), f32),
-            kind((4,)),
+            kind((6,)),
             kind((2,)),
             kind,
+            kind,
+            kind((3, chips)),
+            kind((2, chips)),
+            few,
+            few,
             few,
             few,
             few,
@@ -1406,9 +1499,11 @@
         ),
     )(
         routed_seq,
+        routed_cross,
         choices,
         onehot,
-        cotangent_rows,
+        mate_onehot,
+        placed,
         router_rows,
         gain_rows,
         residual,
@@ -2166,12 +2261,14 @@
         gain_rows,
         segment_cols,
         routed_seq,
-        cotangent_rows,
+        routed_cross,
+        placed,
         gate_full,
         up_full,
         down_full,
         choices,
         onehot,
+        mate_onehot,
     ) = front(
         sizes,
         tokens,
@@ -2199,12 +2296,15 @@
         grad_gate_full,
         grad_up_full,
         down_landing,
+        _,
     ) = experts(
         sizes,
         routed_seq,
+        routed_cross,
         choices,
         onehot,
-        cotangent_rows,
+        mate_onehot,
+        placed,
         router_rows,
         gain_rows,
         residual,

time: 627 us -> 605 us (0.965)
  Pallas kernels: 621 us -> 599 us
    pallas_call x1, Pallas kernels: 224 us -> 198 us  [front(): pl.pallas_call(functools.partial(front_kernel, sizes), out_shape=(shape((...]
where the time goes in v8:
time: 605 us; the launch traced here: 604 us
  Pallas kernels  599 us (99%)
    pallas_call x1, Pallas kernels, front(): pl.pallas_call(functools.partial(front_kernel, sizes), out_shape=(shape((...  198 us
    pallas_call x1, Pallas kernels, experts(): pl.pallas_call(functools.partial(experts_kernel, sizes), out_shape=(shape...  181 us
    pallas_call x1, Pallas kernels, back(): pl.pallas_call(functools.partial(back_kernel, sizes), out_shape=(shape((t...  122 us
    pallas_call x1, Pallas kernels, close(): pl.pallas_call(functools.partial(close_kernel, sizes), out_shape=(shape((...  80.9 us
    pallas_call x1, Pallas kernels, finish(): pl.pallas_call(functools.partial(finish_kernel, len(results)), grid=(step...  16.6 us

profile of v8, /device:TPU:0, one launch (start us, length us, event | category | flops | bytes accessed | tf_op | source)
XLA Modules:
  0.0 604.2 jit_solution(13318215709868832468)
XLA Ops:
  0.6 1.4 copy.27.ids_ref
  2.1 1.4 copy.28.slots_ref
  3.5 1.0 reshape.73
  4.4 0.7 pad_bitcast_fusion.router_ref
  5.2 198.4 %shard_map.239 = (bf16[1024,2048]{1,0:T(8,128)(2,1)}, bf16[3,2048,256]{2,1,0:T(8,128)(2,1)}, bf16[4,256,512]{2,1,0:T(8,128)(2,1)}, bf16[1024,256]{1,0:T(8,128)(2...) custom-call(bf16[128,2048]{1,0:T(8,128)(2,1)} %refs_11_.1, ...), custom_call_target="tpu_custom_call" | custom-call | flops 4294967296 | bytes 524288000 | tf_op jit(solution)/shard_map/pallas_call | solution.py:808
  203.6 181.3 %shard_map.240 = (f32[128,2048]{1,0:T(8,128)}, bf16[128,2048]{1,0:T(8,128)(2,1)}, f32[8,2048]{1,0:T(8,128)}, f32[32,2048]{1,0:T(8,128)}, bf16[4,4,80,1024]{3,2,1...) custom-call(bf16[1024,2048]{1,0:T(8,128)(2,1)} %get-tuple-element.78, ...), custom_call_target="tpu_custom_call" | custom-call | flops 42949672960 | bytes 524288000 | tf_op jit(solution)/shard_map/pallas_call | solution.py:1435
  384.9 121.6 %shard_map.241 = (f32[128,2048]{1,0:T(8,128)}, f32[8,2048]{1,0:T(8,128)}, f32[256,512]{1,0:T(8,128)}, bf16[4,320,2048]{2,1,0:T(8,128)(2,1)}, bf16[4,512,1024]{2,...) custom-call(bf16[128,2048]{1,0:T(8,128)(2,1)} %get-tuple-element.88.out_grad_ref, f32[4,2048]{1,0:T(4,128)} %get-tuple-element.83.gains_ref, ...), custom_call_target="tpu_custom_call" | custom-call | flops 8589934592 | bytes 524288000 | tf_op jit(solution)/shard_map/pallas_call | solution.py:1850
  506.6 80.9 %shard_map.242 = (bf16[128,2048]{1,0:T(8,128)(2,1)}, f32[4,2048]{1,0:T(4,128)}, f32[32,2048]{1,0:T(8,128)}, f32[512,256]{1,0:T(8,128)}, f32[512,256]{1,0:T(8,128...) custom-call(bf16[4,320,256]{2,1,0:T(8,128)(2,1)} %get-tuple-element.77.onehot_ref, ...), custom_call_target="tpu_custom_call" | custom-call | tf_op jit(solution)/shard_map/pallas_call | solution.py:2133
  587.5 16.6 %shard_map.243 = (bf16[128,2048]{1,0:T(8,128)(2,1)}, f32[128,2048]{1,0:T(8,128)}, f32[4,2048]{1,0:T(4,128)}, f32[512,256]{1,0:T(8,128)}, f32[512,256]{1,0:T(8,12...) custom-call(bf16[128,2048]{1,0:T(8,128)(2,1)} %get-tuple-element.109, ...), custom_call_target="tpu_custom_call" | custom-call | tf_op jit(solution)/shard_map/pallas_call | solution.py:2214

commit v9 on v8

--- a/solution.py
+++ b/solution.py
@@ -417,16 +417,12 @@
         cross_copy(1).start()
         cross_own.start()
 
-    top_count = ids_ref.shape[1]
-    same = lax.broadcasted_iota(jnp.int32, (top_count, top_count), 0) == (
-        lax.broadcasted_iota(jnp.int32, (top_count, top_count), 1)
-    )
-    ids_row = row_sums(ids_ref[...].astype(f32), same.astype(f32))
-    slots_row = row_sums(slots_ref[...].astype(f32), same.astype(f32))
-    choice_own[0:top_count, :] = ids_row.astype(jnp.int32)
+    top_count = ids_ref.shape[0]
+    ids_row, slots_row = ids_ref[...], slots_ref[...]
+    choice_own[0:top_count, :] = ids_row
     choice_own[top_count : 2 * top_count, :] = jnp.where(
-        slots_row < CAP, ids_row * CAP + slots_row, -1e6
-    ).astype(jnp.int32)
+        slots_row < CAP, ids_row * CAP + slots_row, -(10**6)
+    )
 
     def choice_copy(shift):
         return pltpu.make_async_remote_copy(
@@ -804,7 +800,7 @@
     kind = pltpu.SemaphoreType.DMA
     shape = jax.ShapeDtypeStruct
     crossed = split == experts_local == 4
-    choices = (size, 2 * ids.shape[1], tok_rows)
+    choices = (size, 2 * ids.shape[0], tok_rows)
     return pl.pallas_call(
         functools.partial(front_kernel, sizes),
         out_shape=(
@@ -827,7 +823,7 @@
             shape((model_width, hidden_width), half),
             shape((model_width, hidden_width), half),
             shape((hidden_width, model_width), half),
-            shape((size, 2 * ids.shape[1], tok_rows), jnp.int32),
+            shape((size, 2 * ids.shape[0], tok_rows), jnp.int32),
             shape((size // 2, experts_local * 2 * CAP, 2 * tok_rows), half),
             shape((size // 2 if crossed else 1, 2, 4 * CAP, 2 * tok_rows), half),
         ),
@@ -844,7 +840,7 @@
             pltpu.VMEM((3, model_width, local_width), half),
             pltpu.VMEM((split, *w_out.shape), half),
             pltpu.VMEM((2 * tok_rows, model_width), half),
-            pltpu.VMEM((2 * ids.shape[1], tok_rows), jnp.int32),
+            pltpu.VMEM((2 * ids.shape[0], tok_rows), jnp.int32),
             pltpu.VMEM((2 * tok_rows if crossed else 16, model_width), half),
             pltpu.VMEM(((2 if crossed else 1) * length, model_width), half),
             pltpu.VMEM((2, *(choices if crossed else (1, 8, 128))), jnp.int32),
@@ -2186,7 +2182,7 @@
 
 
 def finish(results, landings, experts_local):
-    halves = 2
+    halves = 1
     steps = experts_local * halves
     in_specs, out_specs, shapes = [], [], []
     for one in results:
@@ -2276,8 +2272,8 @@
         cosine_wide,
         sine_wide,
         segment_row,
-        expert_ids,
-        expert_slots,
+        expert_ids.T,
+        expert_slots.T,
         cotangent,
         (w_query, w_key, w_value, w_out, w_gate, w_up, w_down),
         0,

time: 605 us -> 601 us (level)
  no operation moved by 1% of the time
where the time goes in v9:
time: 601 us
  Pallas kernels  598 us (100%)
    pallas_call x1, Pallas kernels, front(): pl.pallas_call(functools.partial(front_kernel, sizes), out_shape=(shape((...  198 us
    pallas_call x1, Pallas kernels, experts(): pl.pallas_call(functools.partial(experts_kernel, sizes), out_shape=(shape...  181 us
    pallas_call x1, Pallas kernels, back(): pl.pallas_call(functools.partial(back_kernel, sizes), out_shape=(shape((t...  122 us
    pallas_call x1, Pallas kernels, close(): pl.pallas_call(functools.partial(close_kernel, sizes), out_shape=(shape((...  81 us
    pallas_call x1, Pallas kernels, finish(): pl.pallas_call(functools.partial(finish_kernel, len(results)), grid=(step...  15.8 us

profile of v9, /device:TPU:0, one launch (start us, length us, event | category | flops | bytes accessed | tf_op | source)
XLA Modules:
  0.0 600.7 jit_solution(16000829293426449731)
XLA Ops:
  0.6 1.0 reshape.73
  1.6 0.7 pad_bitcast_fusion.router_ref
  2.4 198.4 %shard_map.239 = (bf16[1024,2048]{1,0:T(8,128)(2,1)}, bf16[3,2048,256]{2,1,0:T(8,128)(2,1)}, bf16[4,256,512]{2,1,0:T(8,128)(2,1)}, bf16[1024,256]{1,0:T(8,128)(2...) custom-call(bf16[128,2048]{1,0:T(8,128)(2,1)} %refs_11_.1, ...), custom_call_target="tpu_custom_call" | custom-call | flops 4294967296 | bytes 524288000 | tf_op jit(solution)/shard_map/pallas_call | solution.py:804
  200.8 181.3 %shard_map.240 = (f32[128,2048]{1,0:T(8,128)}, bf16[128,2048]{1,0:T(8,128)(2,1)}, f32[8,2048]{1,0:T(8,128)}, f32[32,2048]{1,0:T(8,128)}, bf16[4,4,80,1024]{3,2,1...) custom-call(bf16[1024,2048]{1,0:T(8,128)(2,1)} %get-tuple-element.78, ...), custom_call_target="tpu_custom_call" | custom-call | flops 42949672960 | bytes 524288000 | tf_op jit(solution)/shard_map/pallas_call | solution.py:1431
  382.1 121.6 %shard_map.241 = (f32[128,2048]{1,0:T(8,128)}, f32[8,2048]{1,0:T(8,128)}, f32[256,512]{1,0:T(8,128)}, bf16[4,320,2048]{2,1,0:T(8,128)(2,1)}, bf16[4,512,1024]{2,...) custom-call(bf16[128,2048]{1,0:T(8,128)(2,1)} %get-tuple-element.88.out_grad_ref, f32[4,2048]{1,0:T(4,128)} %get-tuple-element.83.gains_ref, ...), custom_call_target="tpu_custom_call" | custom-call | flops 8589934592 | bytes 524288000 | tf_op jit(solution)/shard_map/pallas_call | solution.py:1846
  503.7 81.0 %shard_map.242 = (bf16[128,2048]{1,0:T(8,128)(2,1)}, f32[4,2048]{1,0:T(4,128)}, f32[32,2048]{1,0:T(8,128)}, f32[512,256]{1,0:T(8,128)}, f32[512,256]{1,0:T(8,128...) custom-call(bf16[4,320,256]{2,1,0:T(8,128)(2,1)} %get-tuple-element.77.onehot_ref, ...), custom_call_target="tpu_custom_call" | custom-call | tf_op jit(solution)/shard_map/pallas_call | solution.py:2129
  584.7 15.8 %shard_map.243 = (bf16[128,2048]{1,0:T(8,128)(2,1)}, f32[128,2048]{1,0:T(8,128)}, f32[4,2048]{1,0:T(4,128)}, f32[512,256]{1,0:T(8,128)}, f32[512,256]{1,0:T(8,12...) custom-call(bf16[128,2048]{1,0:T(8,128)(2,1)} %get-tuple-element.109, ...), custom_call_target="tpu_custom_call" | custom-call | tf_op jit(solution)/shard_map/pallas_call | solution.py:2210

commit v10 on v9

--- a/solution.py
+++ b/solution.py
@@ -309,7 +309,7 @@
     log_out,
     attended_out,
     sums_ref,
-    residual_ref,
+    residual_out,
     gains_ref,
     seg_col_ref,
     routed_out,
@@ -321,6 +321,7 @@
     choices,
     onehot_ref,
     mate_onehot,
+    residual_ref,
     q_ref,
     k_ref,
     v_ref,
@@ -675,6 +676,8 @@
     reduce.run(product, hook=hook)
     residual = tokens_ref[...].astype(f32) + reduce.total[...]
     residual_ref[...] = residual
+    keeps.append(pltpu.make_async_copy(residual_ref, residual_out, out_sem.at[9]))
+    keeps[-1].start()
     inverse = lax.rsqrt(jnp.mean(residual * residual, -1, keepdims=True) + EPSILON)
     first.sent()
     routed_half[...] = (residual * inverse * gains_ref[1:2, :]).astype(half)
@@ -828,8 +831,11 @@
             shape((size // 2 if crossed else 1, 2, 4 * CAP, 2 * tok_rows), half),
         ),
         in_specs=[vmem] * 7 + [anywhere] * 8,
-        out_specs=tuple([anywhere] * 9 + [vmem] * 4 + [anywhere] * 6 + [vmem] * 3),
+        out_specs=tuple(
+            [anywhere] * 9 + [vmem, anywhere, vmem, vmem] + [anywhere] * 6 + [vmem] * 3
+        ),
         scratch_shapes=[
+            pltpu.VMEM((tok_rows, model_width), f32),
             pltpu.VMEM((length, local_width), half),
             pltpu.VMEM((length, local_width), half),
             pltpu.VMEM((length, local_width), half),
@@ -867,7 +873,7 @@
             kind((3,)),
             kind((3, split)),
             kind((3, split)),
-            kind((9,)),
+            kind((10,)),
             *ChainReduce.scratch(chips, tok_rows, model_width),
         ],
         compiler_params=pltpu.CompilerParams(
@@ -933,12 +939,12 @@
     routed_cross_ref,
     choices_ref,
     onehot_ref,
-    mate_onehot_ref,
+    mate_onehot_any,
     placed_ref,
     router_ref,
     gains_ref,
-    residual_ref,
-    cotangent_ref,
+    residual_any,
+    cotangent_any,
     gate_ref,
     up_ref,
     down_ref,
@@ -951,6 +957,10 @@
     grad_up_ref,
     down_landing,
     routed_mates,
+    mate_onehot_ref,
+    residual_ref,
+    cotangent_ref,
+    late_sem,
     gate_full,
     up_full,
     down_full,
@@ -1042,6 +1052,18 @@
     pair_load(routed_ref, 0).start()
     for load in loads:
         load.start()
+    late_loads = [
+        pltpu.make_async_copy(source, target, late_sem.at[index])
+        for index, (source, target) in enumerate(
+            (
+                (mate_onehot_any, mate_onehot_ref),
+                (residual_any, residual_ref),
+                (cotangent_any, cotangent_ref),
+            )
+        )
+    ]
+    for load in late_loads:
+        load.start()
     greet_all(size, split)
 
     def mate(move):
@@ -1070,8 +1092,9 @@
         )
         gather.start()
     for move in order:
-        for copy in halves_of(upstream_piece, move):
-            copy.start()
+        if not crossed or move < 3:
+            for copy in halves_of(upstream_piece, move):
+                copy.start()
 
     padded = size * 8
     expert_row = lax.broadcasted_iota(jnp.int32, (padded, tok_rows), 0)
@@ -1168,8 +1191,11 @@
         if not crossed or move < 3:
             for copy in halves_of(rows_piece, move):
                 copy.start()
+    if crossed:
+        for copy in halves_of(upstream_piece, 3):
+            copy.start()
     gates_in[0] = gates_out[0]
-    for load in loads:
+    for load in loads + late_loads:
         load.wait()
     if crossed:
         gather.step(1)
@@ -1441,9 +1467,13 @@
             shape((split, hidden_width, model_width // split), half),
             shape(routed_seq.shape if crossed else (16, model_width), half),
         ),
-        in_specs=[anywhere] * 2 + [vmem] * 3 + [anywhere] + [vmem] * 4 + [anywhere] * 3,
+        in_specs=[anywhere] * 2 + [vmem] * 2 + [anywhere] * 2 + [vmem] * 2 + [anywhere] * 5,
         out_specs=tuple([vmem] * 4 + [anywhere] * 5),
         scratch_shapes=[
+            pltpu.VMEM(mate_onehot.shape, half),
+            pltpu.VMEM(residual.shape, f32),
+            pltpu.VMEM(cotangent.shape, half),
+            kind((3,)),
             pltpu.VMEM(gate_full.shape, half),
             pltpu.VMEM(up_full.shape, half),
             pltpu.VMEM(down_full.shape, half),

time: 601 us -> 599 us (level)
  no operation moved by 1% of the time
where the time goes in v10:
time: 599 us; the launch traced here: 598 us
  Pallas kernels  596 us (99%)
    pallas_call x1, Pallas kernels, front(): pl.pallas_call(functools.partial(front_kernel, sizes), out_shape=(shape((...  198 us
    pallas_call x1, Pallas kernels, experts(): pl.pallas_call(functools.partial(experts_kernel, sizes), out_shape=(shape...  179 us
    pallas_call x1, Pallas kernels, back(): pl.pallas_call(functools.partial(back_kernel, sizes), out_shape=(shape((t...  122 us
    pallas_call x1, Pallas kernels, close(): pl.pallas_call(functools.partial(close_kernel, sizes), out_shape=(shape((...  80.6 us
    pallas_call x1, Pallas kernels, finish(): pl.pallas_call(functools.partial(finish_kernel, len(results)), grid=(step...  15.8 us

profile of v10, /device:TPU:0, one launch (start us, length us, event | category | flops | bytes accessed | tf_op | source)
XLA Modules:
  0.0 598.1 jit_solution(9268284789440348483)
XLA Ops:
  0.6 1.0 reshape.73
  1.6 0.7 pad_bitcast_fusion.router_ref
  2.4 198.1 %shard_map.239 = (bf16[1024,2048]{1,0:T(8,128)(2,1)}, bf16[3,2048,256]{2,1,0:T(8,128)(2,1)}, bf16[4,256,512]{2,1,0:T(8,128)(2,1)}, bf16[1024,256]{1,0:T(8,128)(2...) custom-call(bf16[128,2048]{1,0:T(8,128)(2,1)} %refs_11_.1, ...), custom_call_target="tpu_custom_call" | custom-call | flops 4294967296 | bytes 524288000 | tf_op jit(solution)/shard_map/pallas_call | solution.py:807
  200.4 179.3 %shard_map.240 = (f32[128,2048]{1,0:T(8,128)}, bf16[128,2048]{1,0:T(8,128)(2,1)}, f32[8,2048]{1,0:T(8,128)}, f32[32,2048]{1,0:T(8,128)}, bf16[4,4,80,1024]{3,2,1...) custom-call(bf16[1024,2048]{1,0:T(8,128)(2,1)} %get-tuple-element.78, ...), custom_call_target="tpu_custom_call" | custom-call | flops 42949672960 | bytes 524288000 | tf_op jit(solution)/shard_map/pallas_call | solution.py:1457
  379.8 121.7 %shard_map.241 = (f32[128,2048]{1,0:T(8,128)}, f32[8,2048]{1,0:T(8,128)}, f32[256,512]{1,0:T(8,128)}, bf16[4,320,2048]{2,1,0:T(8,128)(2,1)}, bf16[4,512,1024]{2,...) custom-call(bf16[128,2048]{1,0:T(8,128)(2,1)} %get-tuple-element.88.out_grad_ref, f32[4,2048]{1,0:T(4,128)} %get-tuple-element.83.gains_ref, ...), custom_call_target="tpu_custom_call" | custom-call | flops 8589934592 | bytes 524288000 | tf_op jit(solution)/shard_map/pallas_call | solution.py:1876
  501.5 80.6 %shard_map.242 = (bf16[128,2048]{1,0:T(8,128)(2,1)}, f32[4,2048]{1,0:T(4,128)}, f32[32,2048]{1,0:T(8,128)}, f32[512,256]{1,0:T(8,128)}, f32[512,256]{1,0:T(8,128...) custom-call(bf16[4,320,256]{2,1,0:T(8,128)(2,1)} %get-tuple-element.77.onehot_ref, ...), custom_call_target="tpu_custom_call" | custom-call | tf_op jit(solution)/shard_map/pallas_call | solution.py:2159
  582.1 15.8 %shard_map.243 = (bf16[128,2048]{1,0:T(8,128)(2,1)}, f32[128,2048]{1,0:T(8,128)}, f32[4,2048]{1,0:T(4,128)}, f32[512,256]{1,0:T(8,128)}, f32[512,256]{1,0:T(8,12...) custom-call(bf16[128,2048]{1,0:T(8,128)(2,1)} %get-tuple-element.109, ...), custom_call_target="tpu_custom_call" | custom-call | tf_op jit(solution)/shard_map/pallas_call | solution.py:2240

commit v11 on v10

--- a/solution.py
+++ b/solution.py
@@ -311,7 +311,7 @@
     sums_ref,
     residual_out,
     gains_ref,
-    seg_col_ref,
+    seg_col_out,
     routed_out,
     routed_cross,
     placed_out,
@@ -319,6 +319,9 @@
     up_full,
     down_full,
     choices,
+    onehot_out,
+    mate_out,
+    seg_col_ref,
     onehot_ref,
     mate_onehot,
     residual_ref,
@@ -653,6 +656,7 @@
             (unit_ref, unit_out),
             (log_ref, log_out),
             (attended_ref, attended_out),
+            (seg_col_ref, seg_col_out),
         )
     ):
         keeps.append(pltpu.make_async_copy(source, target, out_sem.at[3 + index]))
@@ -676,7 +680,7 @@
     reduce.run(product, hook=hook)
     residual = tokens_ref[...].astype(f32) + reduce.total[...]
     residual_ref[...] = residual
-    keeps.append(pltpu.make_async_copy(residual_ref, residual_out, out_sem.at[9]))
+    keeps.append(pltpu.make_async_copy(residual_ref, residual_out, out_sem.at[10]))
     keeps[-1].start()
     inverse = lax.rsqrt(jnp.mean(residual * residual, -1, keepdims=True) + EPSILON)
     first.sent()
@@ -760,6 +764,9 @@
 
     placed_keep = pltpu.make_async_copy(placed, placed_out, placed_local.at[0])
     placed_keep.start()
+    for index, (source, target) in enumerate(((onehot_ref, onehot_out), (mate_onehot, mate_out))):
+        keeps.append(pltpu.make_async_copy(source, target, out_sem.at[11 + index]))
+        keeps[-1].start()
     third.steps()
     third.landed()
     if crossed:
@@ -832,9 +839,12 @@
         ),
         in_specs=[vmem] * 7 + [anywhere] * 8,
         out_specs=tuple(
-            [anywhere] * 9 + [vmem, anywhere, vmem, vmem] + [anywhere] * 6 + [vmem] * 3
+            [anywhere] * 9 + [vmem, anywhere, vmem, anywhere] + [anywhere] * 6 + [vmem, anywhere, anywhere]
         ),
         scratch_shapes=[
+            pltpu.VMEM((length, 128), f32),
+            pltpu.VMEM((size // 2, experts_local * 2 * CAP, 2 * tok_rows), half),
+            pltpu.VMEM((size // 2 if crossed else 1, 2, 4 * CAP, 2 * tok_rows), half),
             pltpu.VMEM((tok_rows, model_width), f32),
             pltpu.VMEM((length, local_width), half),
             pltpu.VMEM((length, local_width), half),
@@ -873,7 +883,7 @@
             kind((3,)),
             kind((3, split)),
             kind((3, split)),
-            kind((10,)),
+            kind((13,)),
             *ChainReduce.scratch(chips, tok_rows, model_width),
         ],
         compiler_params=pltpu.CompilerParams(

time: 599 us -> 598 us (level)
  no operation moved by 1% of the time
where the time goes in v11:
time: 598 us
  Pallas kernels  595 us (99%)
    pallas_call x1, Pallas kernels, front(): pl.pallas_call(functools.partial(front_kernel, sizes), out_shape=(shape((...  197 us
    pallas_call x1, Pallas kernels, experts(): pl.pallas_call(functools.partial(experts_kernel, sizes), out_shape=(shape...  179 us
    pallas_call x1, Pallas kernels, back(): pl.pallas_call(functools.partial(back_kernel, sizes), out_shape=(shape((t...  122 us
    pallas_call x1, Pallas kernels, close(): pl.pallas_call(functools.partial(close_kernel, sizes), out_shape=(shape((...  80.7 us
    pallas_call x1, Pallas kernels, finish(): pl.pallas_call(functools.partial(finish_kernel, len(results)), grid=(step...  15.8 us

profile of v11, /device:TPU:0, one launch (start us, length us, event | category | flops | bytes accessed | tf_op | source)
XLA Modules:
  0.0 597.7 jit_solution(7221583153379965586)
XLA Ops:
  0.6 1.0 reshape.73
  1.6 0.7 pad_bitcast_fusion.router_ref
  2.4 197.5 %shard_map.239 = (bf16[1024,2048]{1,0:T(8,128)(2,1)}, bf16[3,2048,256]{2,1,0:T(8,128)(2,1)}, bf16[4,256,512]{2,1,0:T(8,128)(2,1)}, bf16[1024,256]{1,0:T(8,128)(2...) custom-call(bf16[128,2048]{1,0:T(8,128)(2,1)} %refs_11_.1, ...), custom_call_target="tpu_custom_call" | custom-call | flops 4294967296 | bytes 524288000 | tf_op jit(solution)/shard_map/pallas_call | solution.py:814
  199.8 179.3 %shard_map.240 = (f32[128,2048]{1,0:T(8,128)}, bf16[128,2048]{1,0:T(8,128)(2,1)}, f32[8,2048]{1,0:T(8,128)}, f32[32,2048]{1,0:T(8,128)}, bf16[4,4,80,1024]{3,2,1...) custom-call(bf16[1024,2048]{1,0:T(8,128)(2,1)} %get-tuple-element.78, ...), custom_call_target="tpu_custom_call" | custom-call | flops 42949672960 | bytes 524288000 | tf_op jit(solution)/shard_map/pallas_call | solution.py:1467
  379.2 121.8 %shard_map.241 = (f32[128,2048]{1,0:T(8,128)}, f32[8,2048]{1,0:T(8,128)}, f32[256,512]{1,0:T(8,128)}, bf16[4,320,2048]{2,1,0:T(8,128)(2,1)}, bf16[4,512,1024]{2,...) custom-call(bf16[128,2048]{1,0:T(8,128)(2,1)} %get-tuple-element.88.out_grad_ref, f32[4,2048]{1,0:T(4,128)} %get-tuple-element.83.gains_ref, ...), custom_call_target="tpu_custom_call" | custom-call | flops 8589934592 | bytes 524288000 | tf_op jit(solution)/shard_map/pallas_call | solution.py:1886
  501.0 80.7 %shard_map.242 = (bf16[128,2048]{1,0:T(8,128)(2,1)}, f32[4,2048]{1,0:T(4,128)}, f32[32,2048]{1,0:T(8,128)}, f32[512,256]{1,0:T(8,128)}, f32[512,256]{1,0:T(8,128...) custom-call(bf16[4,320,256]{2,1,0:T(8,128)(2,1)} %get-tuple-element.77.onehot_ref, ...), custom_call_target="tpu_custom_call" | custom-call | tf_op jit(solution)/shard_map/pallas_call | solution.py:2169
  581.7 15.8 %shard_map.243 = (bf16[128,2048]{1,0:T(8,128)(2,1)}, f32[128,2048]{1,0:T(8,128)}, f32[4,2048]{1,0:T(4,128)}, f32[512,256]{1,0:T(8,128)}, f32[512,256]{1,0:T(8,12...) custom-call(bf16[128,2048]{1,0:T(8,128)(2,1)} %get-tuple-element.109, ...), custom_call_target="tpu_custom_call" | custom-call | tf_op jit(solution)/shard_map/pallas_call | solution.py:2250
